TPU v7x, 32 devices: a whole 2x2x4 slice. The times are simulated.
32 devices in a mesh: groups: 2 (over y), dp: 4 (over z), tensor: 4 (over x, core).
Axes of the slice: x: 2, y: 2, z: 4, core: 2. Of those that a mesh axis runs over, the one named last changes fastest.
Arguments:
- activations: bfloat16 [4096, 4096], P(('groups', 'dp'), 'tensor'), parts along dimension 0, may hold values from -6 to 6
- out_grads: bfloat16 [4096, 14336], P(('groups', 'dp'), 'tensor'), parts along dimension 0, may hold values from -6 to 6
- proj_in: bfloat16 [4096, 64], P('tensor'), may hold values from -0.09375 to 0.09375
- proj_out: bfloat16 [14336, 64], P('tensor'), may hold values from -0.046875 to 0.046875
- doc_lengths: int32 [8, 32], P(('groups', 'dp')), parts along dimension 0, may hold values from 1 to 48, 512 in all within a row
- doc_owner: int32 [256, 1], P(('groups', 'dp')), parts along dimension 0, may hold values from 0 to 3; in each aligned block of 32 rows (0 to 31, 32 to 63, ...) at most 16 rows name the same one
- query_grads: float32 [256, 4096], P(('groups', 'dp'), 'tensor'), parts along dimension 0, may hold values from -24 to 24
- query_ids: int32 [256], P('groups'), parts along dimension 0, may hold values from 0 to 127
Outputs:
- store: float32 [512, 4096], P(('groups', 'dp'), 'tensor'), parts along dimension 0
- scores: float32 [512, 128], P(('groups', 'dp')), parts along dimension 0
There are 2 independent parts, one for each index of `groups`. A program takes and returns all parts, laid end to end along the dimension named above; an argument that names none is the same for every part. Nothing has to cross between parts.
Inputs may be any that keep to these rules, and one draw needn't show every extreme that they name: `doc_owner`: among the 32 documents of one index of dp no owner appears more than 16 times. `doc_lengths`: each row sums to 512; its largest entry is 48.
All inputs are finite; a program needn't handle non-finite values.
Results may differ from a plain program's by a relative error of at most 0.0003.
Values sent between devices are 32-bit elements; how exact they have to be, the bound alone decides.
No kernel may reach another device: no remote copies, remote signals or barrier semaphores. Data moves between devices by JAX's collectives and lax.ppermute only.
A program may use at most 64 MiB of HBM per device.

v0:
```python
import jax
import jax.numpy as jnp
from jax import lax
from jax.sharding import PartitionSpec as P

precise = lax.Precision.HIGHEST


def token_docs(lengths_row, row_count):
    doc_ends = jnp.cumsum(lengths_row, dtype=jnp.int32)
    position = lax.iota(jnp.int32, row_count)
    doc_index = jnp.sum(
        (position[:, None] >= doc_ends[None, :]).astype(jnp.int32), axis=1, dtype=jnp.int32
    )
    return (doc_index[:, None] == lax.iota(jnp.int32, doc_ends.shape[0])[None, :]).astype(
        jnp.float32
    )


def doc_outer(member, left_cols, right_cols):
    spread = (member[:, :, None] * left_cols[:, None, :]).reshape(member.shape[0], -1)
    product = lax.dot_general(
        spread,
        right_cols,
        (((0,), (0,)), ((), ())),
        precision=precise,
        preferred_element_type=jnp.float32,
    )
    return product.reshape(member.shape[1], -1)


def score_rows(rows_in, queries):
    return lax.dot_general(
        rows_in,
        queries,
        (((1,), (1,)), ((), ())),
        precision=precise,
        preferred_element_type=jnp.float32,
    )


def local(
    activations, out_grads, proj_in, proj_out, doc_lengths, doc_owner, query_grads, query_ids
):
    tensor_size = lax.axis_size("tensor")
    data_size = lax.axis_size("dp")
    tensor_pos = lax.axis_index("tensor")
    tok_rows = activations.shape[0]
    rank_k = proj_in.shape[1]
    width_rows = rank_k // tensor_size
    projected = lax.psum(
        jnp.concatenate(
            [
                jnp.dot(activations, proj_in, preferred_element_type=jnp.float32),
                jnp.dot(out_grads, proj_out, preferred_element_type=jnp.float32),
            ],
            axis=1,
        ),
        "tensor",
    )
    member = token_docs(doc_lengths[0], tok_rows)
    my_rows = lax.dynamic_slice_in_dim(
        projected[:, rank_k:], tensor_pos * width_rows, width_rows, 1
    )
    doc_grads = doc_outer(member, my_rows, projected[:, :rank_k])
    all_rows = lax.all_gather(query_grads, "dp", axis=0, tiled=True)
    queries = jnp.take(all_rows, query_ids, axis=0)
    docs_dev = doc_grads.shape[0]
    capacity = max(2, 2 * docs_dev // data_size)
    owners = doc_owner[:, 0]
    owner_hot = (owners[:, None] == lax.iota(jnp.int32, data_size)[None, :]).astype(jnp.int32)
    before = jnp.cumsum(owner_hot, axis=0, dtype=jnp.int32) - owner_hot
    doc_rank = jnp.sum(before * owner_hot, axis=1, dtype=jnp.int32)
    doc_slot = owners * capacity + doc_rank
    dispatch = (lax.iota(jnp.int32, data_size * capacity)[:, None] == doc_slot[None, :]).astype(
        jnp.float32
    )
    send_rows = jnp.dot(
        dispatch, doc_grads, precision=precise, preferred_element_type=jnp.float32
    ).reshape(data_size, capacity, -1)
    score_scale = 1.0 / (rank_k * rank_k)
    own_scores = lax.psum(score_rows(doc_grads, queries), "tensor")
    send_scores = jnp.dot(
        dispatch, own_scores, precision=precise, preferred_element_type=jnp.float32
    ).reshape(data_size, capacity, -1)
    stored, scores = (
        lax.all_to_all(send_rows, "dp", split_axis=0, concat_axis=0, tiled=True),
        lax.all_to_all(send_scores, "dp", split_axis=0, concat_axis=0, tiled=True),
    )
    stored = stored.reshape(data_size * capacity, -1)
    scores = scores.reshape(data_size * capacity, -1)
    return (stored, scores * score_scale)


def solution(mesh):
    return jax.shard_map(
        local,
        mesh=mesh,
        in_specs=(
            P(("groups", "dp"), "tensor"),
            P(("groups", "dp"), "tensor"),
            P("tensor", None),
            P("tensor", None),
            P(("groups", "dp"), None),
            P(("groups", "dp"), None),
            P(("groups", "dp"), "tensor"),
            P("groups"),
        ),
        out_specs=(P(("groups", "dp"), "tensor"), P(("groups", "dp"), None)),
        check_vma=False,
    )
```

profile of v0, /device:TPU:0, one launch (start us, length us, event | category | flops | bytes accessed | tf_op | source)
XLA Modules:
  0.0 91.4 jit_solution(9827481589700518067)
XLA Ops:
  7.3 1.1 %copy-done = bf16[512,1024]{1,0:T(8,128)(2,1)S(1)} copy-done((bf16[512,1024]{1,0:T(8,128)(2,1)S(1)}, bf16[512,1024]{1,0:T(8,128)(2,1)}, u32[]{:S(2)}) %copy-start) | copy-done | bytes 1048600
  8.4 1.3 %fusion.15 = f32[512,64]{0,1:T(8,128)S(1)} fusion(bf16[512,1024]{1,0:T(8,128)(2,1)S(1)} %copy-done, bf16[1024,64]{0,1:T(8,128)(2,1)} %param.10), kind=kOutput, calls=%fused_computation.31 | convolution fusion | flops 67108864 | bytes 1310720 | tf_op jit(solution)/shard_map/dot_general | solution.py:54
  9.7 3.3 %fusion.16 = f32[512,64]{0,1:T(8,128)S(1)} fusion(bf16[512,3584]{1,0:T(8,128)(2,1)} %param.9, bf16[3584,64]{0,1:T(8,128)(2,1)} %param.11), kind=kOutput, calls=%fused_computation.32 | convolution fusion | flops 234881024 | bytes 4259840 | tf_op jit(solution)/shard_map/dot_general | solution.py:55
  13.1 0.7 pad_maximum_fusion
  14.0 0.1 reduce
  14.3 17.4 %all_gather.3 = f32[128,1024]{1,0:T(8,128)S(1)} all-gather(f32[32,1024]{1,0:T(8,128)S(1)} %copy-done.1), channel_id=1, replica_groups=mesh['groups'=2,'dp'=4,'tensor'=4] {'dp'}, dimensions={0}, use_global_device_ids=true | all-gather | bytes 655360 | tf_op jit(solution)/shard_map/all_gather | solution.py:66
  31.8 0.2 select_reduce_fusion
  32.0 0.8 gather_fusion
  32.8 15.9 %all-reduce.2.cloned.1.call-done = f32[512,128]{0,1:T(8,128)} async-done(((f32[512,128]{0,1:T(8,128)}), f32[512,128]{0,1:T(8,128)}) %all-reduce.2.cloned.1.call-update) | async-done | bytes 262160 | tf_op jit(solution)/shard_map/psum | solution.py:51
  48.7 0.9 slice.10
  49.6 0.1 broadcast_multiply_fusion
  49.7 1.9 %fusion.4 = f32[512,64]{1,0:T(8,128)S(1)} fusion(f32[512,512]{0,1:T(8,128)S(1)} %bitcast.15, f32[512,128]{0,1:T(8,128)} %all-reduce.2.cloned.1.call-done), kind=kOutput, calls=%fused_computation.7 | convolution fusion | flops 201326592 | bytes 1310720 | tf_op jit(solution)/shard_map/dot_general | solution.py:22
  51.6 0.1 reshape.101
  51.7 0.1 reshape.113
  51.9 0.7 fusion
  52.6 10.1 %psum.15 = f32[32,128]{1,0:T(8,128)S(1)} all-reduce(f32[32,128]{1,0:T(8,128)S(1)} %fusion), channel_id=1, replica_groups=mesh['groups'=2,'dp'=4,'tensor'=4] {'tensor'}, use_global_device_ids=true, to_apply=%region_5.6 | all-reduce | flops 4096 | bytes 32768 | tf_op jit(solution)/shard_map/psum | solution.py:82
  62.7 0.8 fusion.7
  63.4 4.6 %all-to-all-start.1 = ((f32[4,16,128]{2,1,0:T(8,128)}), f32[4,16,128]{2,1,0:T(8,128)S(1)}, u32[]{:S(2)}, u32[]{:S(2)}) async-start(f32[4,16,128]{2,1,0:T(8,128)} %bitcast.4), calls=%async_computation.1 | async-start | bytes 65536 | tf_op jit(solution)/shard_map/all_to_all | solution.py:88
  68.0 1.0 %fusion.8 = f32[4,16,1024]{2,1,0:T(8,128)} fusion(f32[32,1024,1]{1,0,2:T(8,128)S(1)} %reshape.113, s32[32]{0:T(128)S(1)} %multiply_add_fusion.1, s32[4,16]{1,0:T(4,128)S(1)} %multiply_add_fusion), kind=kOutput, calls=%fused_computation.15 | convolution fusion | flops 25167872 | bytes 393600 | tf_op jit(solution)/shard_map/dot_general | solution.py:78
  69.1 4.6 %all-to-all-done.1 = f32[4,16,128]{2,1,0:T(8,128)S(1)} async-done(((f32[4,16,128]{2,1,0:T(8,128)}), f32[4,16,128]{2,1,0:T(8,128)S(1)}, u32[]{:S(2)}, u32[]{:S(2)}) %all-to-all-start.1) | async-done | bytes 32800 | tf_op jit(solution)/shard_map/all_to_all | solution.py:88
  73.7 3.4 %all-to-all-start = ((f32[4,16,1024]{2,1,0:T(8,128)}), f32[4,16,1024]{2,1,0:T(8,128)S(1)}, u32[]{:S(2)}, u32[]{:S(2)}) async-start(f32[4,16,1024]{2,1,0:T(8,128)} %fusion.8), calls=%async_computation | async-start | bytes 524288 | tf_op jit(solution)/shard_map/all_to_all | solution.py:87
  77.1 0.6 broadcast_multiply_fusion.1
  77.7 6.1 %all-to-all-done = f32[4,16,1024]{2,1,0:T(8,128)S(1)} async-done(((f32[4,16,1024]{2,1,0:T(8,128)}), f32[4,16,1024]{2,1,0:T(8,128)S(1)}, u32[]{:S(2)}, u32[]{:S(2)}) %all-to-all-start) | async-done | bytes 262176 | tf_op jit(solution)/shard_map/all_to_all | solution.py:87
  83.9 0.7 copy.19
  (23 shorter events, 0.5 us)
Async XLA Ops:
  7.2 1.2 %copy-start = (bf16[512,1024]{1,0:T(8,128)(2,1)S(1)}, bf16[512,1024]{1,0:T(8,128)(2,1)}, u32[]{:S(2)}) copy-start(bf16[512,1024]{1,0:T(8,128)(2,1)} %param.8) | copy-start | bytes 3145732
  7.2 6.7 %copy-start.4 = (s32[128]{0:T(128)S(1)}, s32[128]{0:T(128)}, u32[]{:S(2)}) copy-start(s32[128]{0:T(128)} %param.15) | copy-start | bytes 1540
  7.2 6.7 %copy-start.3 = (s32[1,32]{1,0:T(1,128)S(1)}, s32[1,32]{1,0:T(1,128)}, u32[]{:S(2)}) copy-start(s32[1,32]{1,0:T(1,128)} %param.12) | copy-start | bytes 388
  7.2 7.1 %copy-start.1 = (f32[32,1024]{1,0:T(8,128)S(1)}, f32[32,1024]{1,0:T(8,128)}, u32[]{:S(2)}) copy-start(f32[32,1024]{1,0:T(8,128)} %param.14) | copy-start | bytes 393220
  7.2 24.4 %copy-start.2 = (s32[32,1]{0,1:T(1,128)S(1)}, s32[32,1]{0,1:T(1,128)}, u32[]{:S(2)}) copy-start(s32[32,1]{0,1:T(1,128)} %param.13) | copy-start | bytes 388
  7.2 41.4 %all-reduce.2.cloned.1.call-start = ((), (), s32[]{:S(2)}) async-start(), calls=%async_computation.2 | async-start | bytes 524288 | tf_op jit(solution)/shard_map/psum | solution.py:51
  63.4 10.3 %all-to-all-start.1 = ((f32[4,16,128]{2,1,0:T(8,128)}), f32[4,16,128]{2,1,0:T(8,128)S(1)}, u32[]{:S(2)}, u32[]{:S(2)}) async-start(f32[4,16,128]{2,1,0:T(8,128)} %bitcast.4), calls=%async_computation.1 | async-start | bytes 65536 | tf_op jit(solution)/shard_map/all_to_all | solution.py:88
  73.7 10.2 %all-to-all-start = ((f32[4,16,1024]{2,1,0:T(8,128)}), f32[4,16,1024]{2,1,0:T(8,128)S(1)}, u32[]{:S(2)}, u32[]{:S(2)}) async-start(f32[4,16,1024]{2,1,0:T(8,128)} %fusion.8), calls=%async_computation | async-start | bytes 524288 | tf_op jit(solution)/shard_map/all_to_all | solution.py:87
Sparse Core Ops, SparseCore 0:
  14.0 34.6 all-reduce.1
where the time goes:
time: 91.8 us; the launch traced here: 91.4 us
  blocking collectives  27.5 us (30%)
  waiting for transfers between devices  26.7 us (29%)
  between operations  14.2 us (15%)
  matrix products  9.03 us (10%)
  starting transfers between devices  8.04 us (9%)
  local copies, waits for them, and re-layouts  3.92 us (4%)
  other arithmetic  2.09 us (2%)
    all_gather x1, blocking collectives, local(): all_rows = lax.all_gather(query_grads, 'dp', axis=0, tiled=True)  17.4 us
    psum x1, waiting for transfers between devices, local(): lax.psum(jnp.concatenate([jnp.dot(activations, proj_in, preferred_element...  15.9 us
    psum x1, blocking collectives, local(): own_scores = lax.psum(score_rows(doc_grads, queries), 'tensor')  10.1 us
    all_to_all x1, waiting for transfers between devices, local(): lax.all_to_all(send_rows, 'dp', split_axis=0, concat_axis=0, tiled=True)  6.12 us
    all_to_all x1, waiting for transfers between devices, local(): lax.all_to_all(send_scores, 'dp', split_axis=0, concat_axis=0, tiled=True)  4.64 us
    all_to_all x1, starting transfers between devices, local(): lax.all_to_all(send_scores, 'dp', split_axis=0, concat_axis=0, tiled=True)  4.6 us
    all_to_all x1, starting transfers between devices, local(): lax.all_to_all(send_rows, 'dp', split_axis=0, concat_axis=0, tiled=True)  3.41 us
    dot_general x1, matrix products, local(): jnp.dot(out_grads, proj_out, preferred_element_type=jnp.float32)  3.34 us
  transfers between devices with their start and end apart: 3, of which 3 were waited for; matrix products, arithmetic and copies ran while one was open for 3% of the time, Pallas kernels for 0%

commit v1 on v0

v1 whole, which is shorter than its diff:
```python
import functools

import jax
import jax.numpy as jnp
from jax import lax
from jax.experimental import pallas as pl
from jax.experimental.pallas import tpu as pltpu
from jax.sharding import PartitionSpec as P

F32 = jnp.float32
BF16 = jnp.bfloat16
MIB = 1024 * 1024
NT = (((1,), (1,)), ((), ()))
MOST_SHIFTS = 8


def params(mib):
    return pltpu.CompilerParams(vmem_limit_bytes=mib * MIB)


def cost(flops, nbytes):
    return pl.CostEstimate(flops=flops, bytes_accessed=nbytes, transcendentals=0)


def halves(x):
    high = x.astype(BF16)
    return high, (x - high.astype(F32)).astype(BF16)


def mm(a, b, dims=(((1,), (0,)), ((), ()))):
    return lax.dot_general(a, b, dims, preferred_element_type=F32)


def pick(parity, even, odd):
    return jnp.where(parity == 0, even, odd)


def x_kernel(act_ref, proj_ref, keep_ref, send_ref):
    parity = lax.rem(lax.axis_index("tensor"), 2)
    full = mm(act_ref[...], proj_ref[...], NT).T
    half = full.shape[0] // 2
    keep_ref[...] = pick(parity, full[:half], full[half:])
    send_ref[...] = pick(parity, full[half:], full[:half])


def g_kernel(width, act_ref, proj_ref, keep_ref, send_ref):
    parity = lax.rem(lax.axis_index("tensor"), 2)
    full = mm(act_ref[...], proj_ref[...], NT).T
    for i in range(full.shape[0] // (2 * width)):
        even = full[2 * i * width : (2 * i + 1) * width]
        odd = full[(2 * i + 1) * width : (2 * i + 2) * width]
        keep_ref[i * width : (i + 1) * width, :] = pick(parity, even, odd)
        send_ref[i * width : (i + 1) * width, :] = pick(parity, odd, even)


def project(kernel, act, proj_t, tile):
    tokens, depth = act.shape
    rank = proj_t.shape[0]
    out = jax.ShapeDtypeStruct((rank // 2, tokens), F32)
    spec = pl.BlockSpec((rank // 2, tile), lambda i: (0, i))
    return pl.pallas_call(
        kernel,
        grid=(tokens // tile,),
        in_specs=[
            pl.BlockSpec((tile, depth), lambda i: (i, 0)),
            pl.BlockSpec((rank, depth), lambda i: (0, 0)),
        ],
        out_specs=[spec, spec],
        out_shape=[out, out],
        compiler_params=params(24),
        cost_estimate=cost(8 * tokens * depth * rank, 2 * depth * (tokens + rank)),
    )(act, proj_t)


def mask_kernel(owners, relative, cap, lengths_ref, owner_ref, mask_ref):
    docs = lengths_ref.shape[1]
    slots, tokens = mask_ref.shape
    me = lax.axis_index("dp") if relative else 0
    row = lax.broadcasted_iota(jnp.int32, (docs, docs), 0)
    col = lax.broadcasted_iota(jnp.int32, (docs, docs), 1)
    len_row = lengths_ref[...].astype(F32)
    own_row = lax.rem(owner_ref[...] - me + owners, owners).astype(F32)

    def column(values):
        return jnp.sum(jnp.where(row == col, values, 0.0), axis=1, keepdims=True)

    ends = jnp.sum(jnp.where(row <= col, column(len_row), 0.0), axis=0, keepdims=True)
    rank = jnp.sum(
        jnp.where((row < col) & (column(own_row) == own_row), 1.0, 0.0), axis=0, keepdims=True
    )
    slot_row = own_row * cap + rank
    slot = lax.broadcasted_iota(jnp.int32, (slots, docs), 0).astype(F32)
    hot = slot == slot_row
    first = jnp.sum(jnp.where(hot, ends - len_row, 0.0), axis=1, keepdims=True)
    last = jnp.sum(jnp.where(hot, ends, 0.0), axis=1, keepdims=True)
    token = lax.broadcasted_iota(jnp.int32, (slots, tokens), 1).astype(F32)
    mask_ref[...] = jnp.where((token >= first) & (token < last), 1.0, 0.0)


def slot_mask(lengths, owner_row, tokens, owners, cap, relative):
    return pl.pallas_call(
        functools.partial(mask_kernel, owners, relative, cap),
        out_shape=jax.ShapeDtypeStruct((owners * cap, tokens), F32),
        cost_estimate=cost(0, 4 * owners * cap * tokens),
    )(lengths, owner_row)


def query_kernel(shards, *refs):
    ids_ref, pieces, out_ref = refs[0], refs[1:-1], refs[-1]
    queries = ids_ref.shape[1]
    me = lax.axis_index("dp")
    row = lax.broadcasted_iota(jnp.int32, (queries, queries), 0)
    col = lax.broadcasted_iota(jnp.int32, (queries, queries), 1)
    ids = jnp.sum(
        jnp.where(row == col, ids_ref[...].astype(F32), 0.0), axis=1, keepdims=True
    )
    high_sum, low_sum = None, None
    for k, piece in enumerate(pieces):
        rows = piece.shape[0]
        base = lax.rem(me - k + shards, shards) * rows if len(pieces) > 1 else 0
        place = (lax.broadcasted_iota(jnp.int32, (queries, rows), 1) + base).astype(F32)
        hot = jnp.where(ids == place, 1.0, 0.0).astype(BF16)
        high, low = halves(piece[...])
        high_part, low_part = mm(hot, high), mm(hot, low)
        high_sum = high_part if high_sum is None else high_sum + high_part
        low_sum = low_part if low_sum is None else low_sum + low_part
    out_ref[:queries, :] = high_sum.astype(BF16)
    out_ref[queries:, :] = low_sum.astype(BF16)


def pick_queries(ids_row, pieces, shards):
    queries, feats = ids_row.shape[1], pieces[0].shape[1]
    pool = pieces[0].shape[0] * len(pieces)
    return pl.pallas_call(
        functools.partial(query_kernel, shards),
        out_shape=jax.ShapeDtypeStruct((2 * queries, feats), BF16),
        compiler_params=params(24),
        cost_estimate=cost(4 * queries * pool * feats, 4 * pool * feats),
    )(ids_row, *pieces)


def outer_kernel(x_ref, g_ref, mask_ref, query_ref, *outs):
    *blocks, scores_ref = outs
    width = g_ref.shape[0]
    rank = x_ref.shape[0]
    slots = mask_ref.shape[0]
    queries = query_ref.shape[0] // 2
    x_high, x_low = halves(x_ref[...])
    x_both = jnp.concatenate([x_high, x_low], axis=0)
    g_high = g_ref[...].astype(BF16).astype(F32)
    g_low = g_ref[...] - g_high
    mask = mask_ref[...]

    def part(g, i):
        return (mask * g[i : i + 1, :]).astype(BF16)

    columns = []
    for i in range(width):
        both = mm(part(g_high, i), x_both, NT) + mm(part(g_low, i), x_both, NT)
        columns.append(both[:, :rank] + both[:, rank:])
    grads = jnp.concatenate(columns, axis=1)
    cap = blocks[0].shape[0]
    for k, block in enumerate(blocks):
        block[...] = grads[k * cap : (k + 1) * cap, :]
    high, low = halves(grads)
    query = query_ref[...]
    products = mm(jnp.concatenate([high, low], axis=0), query, NT)
    scores_ref[...] = (
        products[:slots, :queries] + products[:slots, queries:] + products[slots:, :queries]
    )


def outer(x_t, g_t, mask, query, owners):
    slots, tokens = mask.shape
    width, rank = g_t.shape[0], x_t.shape[0]
    queries = query.shape[0] // 2
    cap = slots // owners
    return pl.pallas_call(
        outer_kernel,
        out_shape=[jax.ShapeDtypeStruct((cap, width * rank), F32)] * owners
        + [jax.ShapeDtypeStruct((slots, queries), F32)],
        compiler_params=params(24),
        cost_estimate=cost(16 * slots * width * tokens * rank, 4 * slots * width * rank),
    )(x_t, g_t, mask, query)


def place_kernel(scale, *refs):
    ins, (store_ref, scores_ref) = refs[:-2], refs[-2:]
    count = len(ins) // 2
    me = lax.axis_index("dp")
    cap = ins[0].shape[0]
    for k in range(count):
        spot = pl.ds(pl.multiple_of(lax.rem(me - k + count, count) * cap, cap), cap)
        store_ref[spot, :] = ins[k][...]
        scores_ref[spot, :] = ins[count + k][...] * scale


def place(rows, scores, scale):
    slots = rows[0].shape[0] * len(rows)
    return pl.pallas_call(
        functools.partial(place_kernel, scale),
        out_shape=[
            jax.ShapeDtypeStruct((slots, rows[0].shape[1]), F32),
            jax.ShapeDtypeStruct((slots, scores[0].shape[1]), F32),
        ],
        compiler_params=params(16),
        cost_estimate=cost(0, 8 * slots * rows[0].shape[1]),
    )(*rows, *scores)


def flip(x, bit, size):
    return lax.ppermute(x, "tensor", [(i, i ^ bit) for i in range(size)])


def shift(x, by, size):
    return lax.ppermute(x, "dp", [(i, (i + by) % size) for i in range(size)])


def local(
    activations, out_grads, proj_in, proj_out, doc_lengths, doc_owner, query_grads, query_ids
):
    tensor_size = lax.axis_size("tensor")
    data_size = lax.axis_size("dp")
    tensor_pos = lax.axis_index("tensor")
    tokens = activations.shape[0]
    rank = proj_in.shape[1]
    width = rank // tensor_size
    docs = doc_owner.shape[0]
    cap = max(2, 2 * docs // data_size)
    direct = data_size <= MOST_SHIFTS

    if direct:
        pieces = [query_grads] + [shift(query_grads, k, data_size) for k in range(1, data_size)]
    else:
        pieces = [lax.all_gather(query_grads, "dp", axis=0, tiled=True)]

    x_keep, x_send = project(x_kernel, activations, proj_in.T, tokens)
    x_got = flip(x_send, 1, tensor_size)
    g_keep, g_send = project(
        functools.partial(g_kernel, width), out_grads, proj_out.T, tokens // 4
    )
    g_got = flip(g_send, 1, tensor_size)
    x_half = x_keep + x_got
    g_part = (g_keep + g_got).reshape(-1, width, tokens)
    bit = 2
    while bit < tensor_size:
        x_got = flip(x_half, bit, tensor_size)
        pairs = g_part.reshape(-1, 2, width, tokens)
        upper = (tensor_pos // bit) % 2
        mine = lax.dynamic_index_in_dim(pairs, upper, 1, keepdims=False)
        other = lax.dynamic_index_in_dim(pairs, 1 - upper, 1, keepdims=False)
        g_part = mine + flip(other, bit, tensor_size)
        x_half = x_half + x_got
        bit *= 2
    x_other = flip(x_half, 1, tensor_size)
    odd = (tensor_pos % 2) == 1
    x_full = jnp.concatenate(
        [jnp.where(odd, x_other, x_half), jnp.where(odd, x_half, x_other)], axis=0
    )
    g_mine = g_part.reshape(width, tokens)

    mask = slot_mask(doc_lengths, doc_owner.T, tokens, data_size, cap, direct)
    query = pick_queries(query_ids[None, :], pieces, data_size)
    *blocks, partial = outer(x_full, g_mine, mask, query, data_size)
    scale = 1.0 / (rank * rank)
    if direct:
        rows = [blocks[0]] + [shift(blocks[k], k, data_size) for k in range(1, data_size)]
        bit = 1
        while bit < tensor_size:
            partial = partial + flip(partial, bit, tensor_size)
            bit *= 2
        scored = [partial[k * cap : (k + 1) * cap] for k in range(data_size)]
        scored = [scored[0]] + [shift(scored[k], k, data_size) for k in range(1, data_size)]
        store, scores = place(rows, scored, scale)
        return store, scores
    rows = lax.all_to_all(jnp.stack(blocks), "dp", split_axis=0, concat_axis=0, tiled=True)
    summed = lax.psum(partial, "tensor").reshape(data_size, cap, -1)
    scores = lax.all_to_all(summed, "dp", split_axis=0, concat_axis=0, tiled=True)
    slots = data_size * cap
    return rows.reshape(slots, -1), scores.reshape(slots, -1) * scale


def solution(mesh):
    return jax.shard_map(
        local,
        mesh=mesh,
        in_specs=(
            P(("groups", "dp"), "tensor"),
            P(("groups", "dp"), "tensor"),
            P("tensor", None),
            P("tensor", None),
            P(("groups", "dp"), None),
            P(("groups", "dp"), None),
            P(("groups", "dp"), "tensor"),
            P("groups"),
        ),
        out_specs=(P(("groups", "dp"), "tensor"), P(("groups", "dp"), None)),
        check_vma=False,
    )
```

time: 91.8 us -> 45.6 us (0.50)
  blocking collectives: 27.5 us -> 0 us
  waiting for transfers between devices: 26.7 us -> 9.18 us
  starting transfers between devices: 8.04 us -> 22 us
  between operations: 14.2 us -> 0.8 us
  matrix products: 9.03 us -> 0 us
  Pallas kernels: 0 us -> 7.13 us
  local copies, waits for them, and re-layouts: 3.92 us -> 6.11 us
  other arithmetic: 2.09 us -> 0.08 us
    ppermute x0 -> x16, starting transfers between devices: none -> 22 us  [the longest x9 16.7 us: shift(): return lax.ppermute(x, 'dp', [(i, (i + by) % size) for i in range(size)])]
    all_gather x1 -> x0, blocking collectives: 17.4 us -> none  [local(): all_rows = lax.all_gather(query_grads, 'dp', axis=0, tiled=True)]
    psum x1 -> x0, waiting for transfers between devices: 15.9 us -> none  [local(): lax.psum(jnp.concatenate([jnp.dot(activations, proj_in, preferred_element...]
    all_to_all x2 -> x0, waiting for transfers between devices: 10.8 us -> none  [the longest x1 6.12 us: local(): lax.all_to_all(send_rows, 'dp', split_axis=0, concat_axis=0, tiled=True)]
    psum x1 -> x0, blocking collectives: 10.1 us -> none  [local(): own_scores = lax.psum(score_rows(doc_grads, queries), 'tensor')]
    ppermute x0 -> x16, waiting for transfers between devices: none -> 9.18 us  [the longest x9 7.97 us: shift(): return lax.ppermute(x, 'dp', [(i, (i + by) % size) for i in range(size)])]
    dot_general x6 -> x0, matrix products: 9.03 us -> none  [the longest x1 3.34 us: local(): jnp.dot(out_grads, proj_out, preferred_element_type=jnp.float32)]
    all_to_all x2 -> x0, starting transfers between devices: 8.01 us -> none  [the longest x1 4.6 us: local(): lax.all_to_all(send_scores, 'dp', split_axis=0, concat_axis=0, tiled=True)]
  transfers between devices with their start and end apart: 3 -> 16, of which waited for: 3 -> 5; matrix products, arithmetic and copies ran while one was open for 3% -> 0% of each run, Pallas kernels for 0% -> 9%
where the time goes in v1:
time: 45.6 us; the launch traced here: 45.3 us
  starting transfers between devices  22 us (48%)
  waiting for transfers between devices  9.18 us (20%)
  Pallas kernels  7.13 us (16%)
  local copies, waits for them, and re-layouts  6.11 us (13%)
  between operations  0.8 us (2%)
    ppermute x9, starting transfers between devices, shift(): return lax.ppermute(x, 'dp', [(i, (i + by) % size) for i in range(size)])  16.7 us
    ppermute x9, waiting for transfers between devices, shift(): return lax.ppermute(x, 'dp', [(i, (i + by) % size) for i in range(size)])  7.97 us
    unnamed x14, local copies, waits for them, and re-layouts  6.09 us
    ppermute x7, starting transfers between devices, flip(): return lax.ppermute(x, 'tensor', [(i, i ^ bit) for i in range(size)])  5.35 us
    pallas_call x2, Pallas kernels, project(): pl.pallas_call(kernel, grid=(tokens // tile,), in_specs=[pl.BlockSpec((ti...  2.23 us
    pallas_call x1, Pallas kernels, outer(): pl.pallas_call(outer_kernel, out_shape=[jax.ShapeDtypeStruct((cap, width...  1.87 us
    pallas_call x1, Pallas kernels, slot_mask(): pl.pallas_call(functools.partial(mask_kernel, owners, relative, cap), out...  1.53 us
    ppermute x7, waiting for transfers between devices, flip(): return lax.ppermute(x, 'tensor', [(i, i ^ bit) for i in range(size)])  1.21 us
  transfers between devices with their start and end apart: 16, of which 5 were waited for; matrix products, arithmetic and copies ran while one was open for 0% of the time, Pallas kernels for 9%

profile of v1, /device:TPU:0, one launch (start us, length us, event | category | flops | bytes accessed | tf_op | source)
XLA Modules:
  0.0 45.3 jit_solution(14700280602438920635)
XLA Ops:
  0.7 1.2 %copy-done.1 = bf16[512,1024]{1,0:T(8,128)(2,1)S(1)} copy-done((bf16[512,1024]{1,0:T(8,128)(2,1)S(1)}, bf16[512,1024]{1,0:T(8,128)(2,1)}, u32[]{:S(2)}) %copy-start.1) | copy-done | bytes 1048600
  1.9 0.9 %copy-done.3 = bf16[1024,64]{0,1:T(8,128)(2,1)S(1)} copy-done((bf16[1024,64]{0,1:T(8,128)(2,1)S(1)}, bf16[1024,64]{0,1:T(8,128)(2,1)}, u32[]{:S(2)}) %copy-start.3) | copy-done | bytes 131096
  3.8 2.0 %copy-done = bf16[512,3584]{1,0:T(8,128)(2,1)S(1)} copy-done((bf16[512,3584]{1,0:T(8,128)(2,1)S(1)}, bf16[512,3584]{1,0:T(8,128)(2,1)}, u32[]{:S(2)}) %copy-start) | copy-done | bytes 3670040
  5.8 1.0 %copy-done.2 = bf16[3584,64]{0,1:T(8,128)(2,1)S(1)} copy-done((bf16[3584,64]{0,1:T(8,128)(2,1)S(1)}, bf16[3584,64]{0,1:T(8,128)(2,1)}, u32[]{:S(2)}) %copy-start.2) | copy-done | bytes 458776
  6.8 1.8 %shard_map.96 = (f32[32,512]{1,0:T(8,128)S(1)}, f32[32,512]{1,0:T(8,128)S(1)}) custom-call(bf16[512,3584]{1,0:T(8,128)(2,1)S(1)} %copy-done, bf16[64,3584]{1,0:T(8,128)(2,1)S(1)} %bitcast.13), custom_call_target="tpu_custom_call" | custom-call | flops 939524096 | bytes 4128768 | tf_op jit(solution)/shard_map/pallas_call | solution.py:61
  8.7 3.0 %collective-permute-start.1 = (f32[32,512]{1,0:T(8,128)S(1)}, f32[32,512]{1,0:T(8,128)S(1)}, u32[]{:S(2)}, u32[]{:S(2)}) collective-permute-start(f32[32,512]{1,0:T(8,128)S(1)} %add.35), channel_id=1, source_target_pairs={{0,2},{1,3},{2,0},{3,1},{4,6},{5,7},{6,4},{7,5},{8,10},{9,11},{10,... | collective-permute-start | bytes 196616 | tf_op jit(solution)/shard_map/ppermute | solution.py:212
  11.8 0.9 %collective-permute-start.4 = (f32[1,16,512]{2,1,0:T(8,128)S(1)}, f32[1,16,512]{2,1,0:T(8,128)S(1)}, u32[]{:S(2)}, u32[]{:S(2)}) collective-permute-start(f32[1,16,512]{2,1,0:T(8,128)S(1)} %dynamic-slice_bitcast_fusion), channel_id=1, source_target_pairs={{0,2},{1,3},{2,0},{3,1},{4,6},{5,7},{6,4},{7,5},{8,10},{9,11},{10,... | collective-permute-start | bytes 98312 | tf_op jit(solution)/shard_map/ppermute | solution.py:212
  12.7 1.6 %collective-permute-start.5 = (f32[32,1024]{1,0:T(8,128)S(1)}, f32[32,1024]{1,0:T(8,128)S(1)}, u32[]{:S(2)}, u32[]{:S(2)}) collective-permute-start(f32[32,1024]{1,0:T(8,128)S(1)} %copy-done.5), channel_id=1, source_target_pairs={{0,4},{4,8},{8,12},{12,0},{1,5},{5,9},{9,13},{13,1},{2,6},{6,10},{... | collective-permute-start | bytes 393224 | tf_op jit(solution)/shard_map/ppermute | solution.py:216
  14.2 2.6 %collective-permute-start.6 = (f32[32,1024]{1,0:T(8,128)S(1)}, f32[32,1024]{1,0:T(8,128)S(1)}, u32[]{:S(2)}, u32[]{:S(2)}) collective-permute-start(f32[32,1024]{1,0:T(8,128)S(1)} %copy-done.5), channel_id=1, source_target_pairs={{0,8},{4,12},{8,0},{12,4},{1,9},{5,13},{9,1},{13,5},{2,10},{6,14},... | collective-permute-start | bytes 393224 | tf_op jit(solution)/shard_map/ppermute | solution.py:216
  16.8 1.4 %collective-permute-start.7 = (f32[32,1024]{1,0:T(8,128)S(1)}, f32[32,1024]{1,0:T(8,128)S(1)}, u32[]{:S(2)}, u32[]{:S(2)}) collective-permute-start(f32[32,1024]{1,0:T(8,128)S(1)} %copy-done.5), channel_id=1, source_target_pairs={{0,12},{4,0},{8,4},{12,8},{1,13},{5,1},{9,5},{13,9},{2,14},{6,2},{... | collective-permute-start | bytes 393224 | tf_op jit(solution)/shard_map/ppermute | solution.py:216
  18.2 1.5 %shard_map.97.mask_ref = f32[64,512]{1,0:T(8,128)} custom-call(s32[1,32]{1,0:T(1,128)} %lengths_ref.1, s32[1,32]{1,0:T(1,128)} %bitcast.18), custom_call_target="tpu_custom_call" | custom-call | bytes 131072 | tf_op jit(solution)/shard_map/pallas_call | solution.py:101
  19.8 1.1 %collective-permute-done.5.refs_2_ = f32[32,1024]{1,0:T(8,128)S(1)} collective-permute-done((f32[32,1024]{1,0:T(8,128)S(1)}, f32[32,1024]{1,0:T(8,128)S(1)}, u32[]{:S(2)}, u32[]{:S(2)}) %collective-permute-start.5) | collective-permute-done | bytes 131104 | tf_op jit(solution)/shard_map/ppermute | solution.py:216
  20.9 4.8 %collective-permute-done.6.refs_3_ = f32[32,1024]{1,0:T(8,128)S(1)} collective-permute-done((f32[32,1024]{1,0:T(8,128)S(1)}, f32[32,1024]{1,0:T(8,128)S(1)}, u32[]{:S(2)}, u32[]{:S(2)}) %collective-permute-start.6) | collective-permute-done | bytes 131104 | tf_op jit(solution)/shard_map/ppermute | solution.py:216
  25.7 0.8 %shard_map.98.query_ref = bf16[256,1024]{1,0:T(8,128)(2,1)S(1)} custom-call(s32[1,128]{1,0:T(1,128)S(1)} %bitcast.15, f32[32,1024]{1,0:T(8,128)S(1)} %copy-done.5, f32[32,1024]{1,0:T(8,128)S(1)} %collective-permute-done.5.refs_2_, f32[32,1024]{1,0:T(8,128)S(1)} %collective-permute-done.6.refs_3_, f32[32,1024]{1,0:T(8,128)S(1)} %collective-permute-done.7.refs_4_), custom_call_target="tpu_custom_call" | custom-call | flops 67108864 | bytes 524288 | tf_op jit(solution)/shard_map/pallas_call | solution.py:134
  26.5 0.9 %copy-done.4 = f32[64,512]{1,0:T(8,128)S(1)} copy-done((f32[64,512]{1,0:T(8,128)S(1)}, f32[64,512]{1,0:T(8,128)}, u32[]{:S(2)}) %copy-start.4) | copy-done | bytes 131096
  27.4 1.9 %shard_map.99 = (f32[16,1024]{1,0:T(8,128)S(1)}, f32[16,1024]{1,0:T(8,128)S(1)}, f32[16,1024]{1,0:T(8,128)S(1)}, f32[16,1024]{1,0:T(8,128)S(1)}, f32[64,128]{1,0:T(8,128)S(1)}) custom-call(f32[64,512]{1,0:T(8,128)S(1)} %pad_maximum_fusion.x_ref, f32[16,512]{1,0:T(8,128)S(1)} %fusion.g_ref, f32[64,512]{1,0:T(8,128)S(1)} %copy-done.4, ...), custom_call_target="tpu_custom_call" | custom-call | flops 536870912 | bytes 262144 | tf_op jit(solution)/shard_map/pallas_call | solution.py:178
  29.4 1.2 %collective-permute-done.11 = f32[64,128]{1,0:T(8,128)S(1)} collective-permute-done((f32[64,128]{1,0:T(8,128)S(1)}, f32[64,128]{1,0:T(8,128)S(1)}, u32[]{:S(2)}, u32[]{:S(2)}) %collective-permute-start.11) | collective-permute-done | bytes 32800 | tf_op jit(solution)/shard_map/ppermute | solution.py:212
  30.6 0.7 %collective-permute-start.12 = (f32[64,128]{1,0:T(8,128)S(1)}, f32[64,128]{1,0:T(8,128)S(1)}, u32[]{:S(2)}, u32[]{:S(2)}) collective-permute-start(f32[64,128]{1,0:T(8,128)S(1)} %add.42), channel_id=1, source_target_pairs={{0,2},{1,3},{2,0},{3,1},{4,6},{5,7},{6,4},{7,5},{8,10},{9,11},{10,... | collective-permute-start | bytes 98312 | tf_op jit(solution)/shard_map/ppermute | solution.py:212
  31.3 4.3 %collective-permute-start.10 = (f32[16,1024]{1,0:T(8,128)S(1)}, f32[16,1024]{1,0:T(8,128)S(1)}, u32[]{:S(2)}, u32[]{:S(2)}) collective-permute-start(f32[16,1024]{1,0:T(8,128)S(1)} %get-tuple-element.18), channel_id=1, source_target_pairs={{0,12},{4,0},{8,4},{12,8},{1,13},{5,1},{9,5},{13,9},{2,14},{6,2},{... | collective-permute-start | bytes 196616 | tf_op jit(solution)/shard_map/ppermute | solution.py:216
  36.2 3.9 %collective-permute-start.13 = (f32[16,128]{1,0:T(8,128)S(1)}, f32[16,128]{1,0:T(8,128)S(1)}, u32[]{:S(2)}, u32[]{:S(2)}) collective-permute-start(f32[16,128]{1,0:T(8,128)S(1)} %get-tuple-element.24), channel_id=1, source_target_pairs={{0,4},{4,8},{8,12},{12,0},{1,5},{5,9},{9,13},{13,1},{2,6},{6,10},{... | collective-permute-start | bytes 24584 | tf_op jit(solution)/shard_map/ppermute | solution.py:216
  40.0 2.4 %collective-permute-start.15 = (f32[16,128]{1,0:T(8,128)S(1)}, f32[16,128]{1,0:T(8,128)S(1)}, u32[]{:S(2)}, u32[]{:S(2)}) collective-permute-start(f32[16,128]{1,0:T(8,128)S(1)} %get-tuple-element.22), channel_id=1, source_target_pairs={{0,12},{4,0},{8,4},{12,8},{1,13},{5,1},{9,5},{13,9},{2,14},{6,2},{... | collective-permute-start | bytes 24584 | tf_op jit(solution)/shard_map/ppermute | solution.py:216
  42.5 1.0 %collective-permute-done.9.refs_2_ = f32[16,1024]{1,0:T(8,128)S(1)} collective-permute-done((f32[16,1024]{1,0:T(8,128)S(1)}, f32[16,1024]{1,0:T(8,128)S(1)}, u32[]{:S(2)}, u32[]{:S(2)}) %collective-permute-start.9) | collective-permute-done | bytes 65568 | tf_op jit(solution)/shard_map/ppermute | solution.py:216
  43.5 1.1 %collective-permute-done.14.refs_6_ = f32[16,128]{1,0:T(8,128)S(1)} collective-permute-done((f32[16,128]{1,0:T(8,128)S(1)}, f32[16,128]{1,0:T(8,128)S(1)}, u32[]{:S(2)}, u32[]{:S(2)}) %collective-permute-start.14) | collective-permute-done | bytes 8224 | tf_op jit(solution)/shard_map/ppermute | solution.py:216
  44.6 0.7 %shard_map.100 = (f32[64,1024]{1,0:T(8,128)}, f32[64,128]{1,0:T(8,128)}) custom-call(f32[16,1024]{1,0:T(8,128)S(1)} %get-tuple-element.15.refs_0_, f32[16,1024]{1,0:T(8,128)S(1)} %collective-permute-done.8.refs_1_, f32[16,1024]{1,0:T(8,128)S(1)} %collective-permute-done.9.refs_2_, f32[16,1024]{1,0:T(8,128)S(1)} %collective-permute-done.10.refs_3_, ...), custom_call_target="tpu_custom_call" | custom-call | bytes 524288 | tf_op jit(solution)/shard_map/pallas_call | solution.py:200
  (38 shorter events, 1.9 us)
Async XLA Ops:
  0.6 25.1 %copy-start.6 = (s32[128]{0:T(128)S(1)}, s32[128]{0:T(128)}, u32[]{:S(2)}) copy-start(s32[128]{0:T(128)} %param.15) | copy-start | bytes 1540
  0.6 1.2 %copy-start.1 = (bf16[512,1024]{1,0:T(8,128)(2,1)S(1)}, bf16[512,1024]{1,0:T(8,128)(2,1)}, u32[]{:S(2)}) copy-start(bf16[512,1024]{1,0:T(8,128)(2,1)} %act_ref.2) | copy-start | bytes 3145732
  1.9 0.9 %copy-start.3 = (bf16[1024,64]{0,1:T(8,128)(2,1)S(1)}, bf16[1024,64]{0,1:T(8,128)(2,1)}, u32[]{:S(2)}) copy-start(bf16[1024,64]{0,1:T(8,128)(2,1)} %param.10) | copy-start | bytes 393220
  2.8 9.9 %copy-start.5 = (f32[32,1024]{1,0:T(8,128)S(1)}, f32[32,1024]{1,0:T(8,128)}, u32[]{:S(2)}) copy-start(f32[32,1024]{1,0:T(8,128)} %refs_1_.1) | copy-start | bytes 393220
  3.2 5.5 %collective-permute-start = (f32[32,512]{1,0:T(8,128)S(1)}, f32[32,512]{1,0:T(8,128)S(1)}, u32[]{:S(2)}, u32[]{:S(2)}) collective-permute-start(f32[32,512]{1,0:T(8,128)S(1)} %get-tuple-element.12), channel_id=1, source_target_pairs={{0,1},{1,0},{2,3},{3,2},{4,5},{5,4},{6,7},{7,6},{8,9},{9,8},{10,11... | collective-permute-start | bytes 196616 | tf_op jit(solution)/shard_map/ppermute | solution.py:212
  3.8 2.0 %copy-start = (bf16[512,3584]{1,0:T(8,128)(2,1)S(1)}, bf16[512,3584]{1,0:T(8,128)(2,1)}, u32[]{:S(2)}) copy-start(bf16[512,3584]{1,0:T(8,128)(2,1)} %act_ref.3) | copy-start | bytes 11010052
  5.8 1.0 %copy-start.2 = (bf16[3584,64]{0,1:T(8,128)(2,1)S(1)}, bf16[3584,64]{0,1:T(8,128)(2,1)}, u32[]{:S(2)}) copy-start(bf16[3584,64]{0,1:T(8,128)(2,1)} %param.11) | copy-start | bytes 1376260
  8.6 3.1 %collective-permute-start.3 = (f32[32,512]{1,0:T(8,128)S(1)}, f32[32,512]{1,0:T(8,128)S(1)}, u32[]{:S(2)}, u32[]{:S(2)}) collective-permute-start(f32[32,512]{1,0:T(8,128)S(1)} %get-tuple-element.14), channel_id=1, source_target_pairs={{0,1},{1,0},{2,3},{3,2},{4,5},{5,4},{6,7},{7,6},{8,9},{9,8},{10,11... | collective-permute-start | bytes 196616 | tf_op jit(solution)/shard_map/ppermute | solution.py:212
  8.7 11.0 %collective-permute-start.1 = (f32[32,512]{1,0:T(8,128)S(1)}, f32[32,512]{1,0:T(8,128)S(1)}, u32[]{:S(2)}, u32[]{:S(2)}) collective-permute-start(f32[32,512]{1,0:T(8,128)S(1)} %add.35), channel_id=1, source_target_pairs={{0,2},{1,3},{2,0},{3,1},{4,6},{5,7},{6,4},{7,5},{8,10},{9,11},{10,... | collective-permute-start | bytes 196616 | tf_op jit(solution)/shard_map/ppermute | solution.py:212
  11.8 8.0 %collective-permute-start.4 = (f32[1,16,512]{2,1,0:T(8,128)S(1)}, f32[1,16,512]{2,1,0:T(8,128)S(1)}, u32[]{:S(2)}, u32[]{:S(2)}) collective-permute-start(f32[1,16,512]{2,1,0:T(8,128)S(1)} %dynamic-slice_bitcast_fusion), channel_id=1, source_target_pairs={{0,2},{1,3},{2,0},{3,1},{4,6},{5,7},{6,4},{7,5},{8,10},{9,11},{10,... | collective-permute-start | bytes 98312 | tf_op jit(solution)/shard_map/ppermute | solution.py:212
  12.7 8.2 %collective-permute-start.5 = (f32[32,1024]{1,0:T(8,128)S(1)}, f32[32,1024]{1,0:T(8,128)S(1)}, u32[]{:S(2)}, u32[]{:S(2)}) collective-permute-start(f32[32,1024]{1,0:T(8,128)S(1)} %copy-done.5), channel_id=1, source_target_pairs={{0,4},{4,8},{8,12},{12,0},{1,5},{5,9},{9,13},{13,1},{2,6},{6,10},{... | collective-permute-start | bytes 393224 | tf_op jit(solution)/shard_map/ppermute | solution.py:216
  14.2 11.5 %collective-permute-start.6 = (f32[32,1024]{1,0:T(8,128)S(1)}, f32[32,1024]{1,0:T(8,128)S(1)}, u32[]{:S(2)}, u32[]{:S(2)}) collective-permute-start(f32[32,1024]{1,0:T(8,128)S(1)} %copy-done.5), channel_id=1, source_target_pairs={{0,8},{4,12},{8,0},{12,4},{1,9},{5,13},{9,1},{13,5},{2,10},{6,14},... | collective-permute-start | bytes 393224 | tf_op jit(solution)/shard_map/ppermute | solution.py:216
  16.8 8.9 %collective-permute-start.7 = (f32[32,1024]{1,0:T(8,128)S(1)}, f32[32,1024]{1,0:T(8,128)S(1)}, u32[]{:S(2)}, u32[]{:S(2)}) collective-permute-start(f32[32,1024]{1,0:T(8,128)S(1)} %copy-done.5), channel_id=1, source_target_pairs={{0,12},{4,0},{8,4},{12,8},{1,13},{5,1},{9,5},{13,9},{2,14},{6,2},{... | collective-permute-start | bytes 393224 | tf_op jit(solution)/shard_map/ppermute | solution.py:216
  19.7 6.7 %collective-permute-start.2 = (f32[32,512]{1,0:T(8,128)S(1)}, f32[32,512]{1,0:T(8,128)S(1)}, u32[]{:S(2)}, u32[]{:S(2)}) collective-permute-start(f32[32,512]{1,0:T(8,128)S(1)} %add.36), channel_id=1, source_target_pairs={{0,1},{1,0},{2,3},{3,2},{4,5},{5,4},{6,7},{7,6},{8,9},{9,8},{10,11... | collective-permute-start | bytes 196616 | tf_op jit(solution)/shard_map/ppermute | solution.py:212
  26.5 0.9 %copy-start.4 = (f32[64,512]{1,0:T(8,128)S(1)}, f32[64,512]{1,0:T(8,128)}, u32[]{:S(2)}) copy-start(f32[64,512]{1,0:T(8,128)} %shard_map.97.mask_ref) | copy-start | bytes 393220
  29.3 1.3 %collective-permute-start.11 = (f32[64,128]{1,0:T(8,128)S(1)}, f32[64,128]{1,0:T(8,128)S(1)}, u32[]{:S(2)}, u32[]{:S(2)}) collective-permute-start(f32[64,128]{1,0:T(8,128)S(1)} %get-tuple-element.19), channel_id=1, source_target_pairs={{0,1},{1,0},{2,3},{3,2},{4,5},{5,4},{6,7},{7,6},{8,9},{9,8},{10,11... | collective-permute-start | bytes 98312 | tf_op jit(solution)/shard_map/ppermute | solution.py:212
  30.6 5.6 %collective-permute-start.12 = (f32[64,128]{1,0:T(8,128)S(1)}, f32[64,128]{1,0:T(8,128)S(1)}, u32[]{:S(2)}, u32[]{:S(2)}) collective-permute-start(f32[64,128]{1,0:T(8,128)S(1)} %add.42), channel_id=1, source_target_pairs={{0,2},{1,3},{2,0},{3,1},{4,6},{5,7},{6,4},{7,5},{8,10},{9,11},{10,... | collective-permute-start | bytes 98312 | tf_op jit(solution)/shard_map/ppermute | solution.py:212
  31.3 8.8 %collective-permute-start.10 = (f32[16,1024]{1,0:T(8,128)S(1)}, f32[16,1024]{1,0:T(8,128)S(1)}, u32[]{:S(2)}, u32[]{:S(2)}) collective-permute-start(f32[16,1024]{1,0:T(8,128)S(1)} %get-tuple-element.18), channel_id=1, source_target_pairs={{0,12},{4,0},{8,4},{12,8},{1,13},{5,1},{9,5},{13,9},{2,14},{6,2},{... | collective-permute-start | bytes 196616 | tf_op jit(solution)/shard_map/ppermute | solution.py:216
  35.6 6.9 %collective-permute-start.8 = (f32[16,1024]{1,0:T(8,128)S(1)}, f32[16,1024]{1,0:T(8,128)S(1)}, u32[]{:S(2)}, u32[]{:S(2)}) collective-permute-start(f32[16,1024]{1,0:T(8,128)S(1)} %get-tuple-element.16), channel_id=1, source_target_pairs={{0,4},{4,8},{8,12},{12,0},{1,5},{5,9},{9,13},{13,1},{2,6},{6,10},{... | collective-permute-start | bytes 196616 | tf_op jit(solution)/shard_map/ppermute | solution.py:216
  35.6 7.9 %collective-permute-start.9 = (f32[16,1024]{1,0:T(8,128)S(1)}, f32[16,1024]{1,0:T(8,128)S(1)}, u32[]{:S(2)}, u32[]{:S(2)}) collective-permute-start(f32[16,1024]{1,0:T(8,128)S(1)} %get-tuple-element.17), channel_id=1, source_target_pairs={{0,8},{4,12},{8,0},{12,4},{1,9},{5,13},{9,1},{13,5},{2,10},{6,14},... | collective-permute-start | bytes 196616 | tf_op jit(solution)/shard_map/ppermute | solution.py:216
  36.2 7.4 %collective-permute-start.13 = (f32[16,128]{1,0:T(8,128)S(1)}, f32[16,128]{1,0:T(8,128)S(1)}, u32[]{:S(2)}, u32[]{:S(2)}) collective-permute-start(f32[16,128]{1,0:T(8,128)S(1)} %get-tuple-element.24), channel_id=1, source_target_pairs={{0,4},{4,8},{8,12},{12,0},{1,5},{5,9},{9,13},{13,1},{2,6},{6,10},{... | collective-permute-start | bytes 24584 | tf_op jit(solution)/shard_map/ppermute | solution.py:216
  40.0 4.5 %collective-permute-start.14 = (f32[16,128]{1,0:T(8,128)S(1)}, f32[16,128]{1,0:T(8,128)S(1)}, u32[]{:S(2)}, u32[]{:S(2)}) collective-permute-start(f32[16,128]{1,0:T(8,128)S(1)} %get-tuple-element.23), channel_id=1, source_target_pairs={{0,8},{4,12},{8,0},{12,4},{1,9},{5,13},{9,1},{13,5},{2,10},{6,14},... | collective-permute-start | bytes 24584 | tf_op jit(solution)/shard_map/ppermute | solution.py:216
  40.0 4.5 %collective-permute-start.15 = (f32[16,128]{1,0:T(8,128)S(1)}, f32[16,128]{1,0:T(8,128)S(1)}, u32[]{:S(2)}, u32[]{:S(2)}) collective-permute-start(f32[16,128]{1,0:T(8,128)S(1)} %get-tuple-element.22), channel_id=1, source_target_pairs={{0,12},{4,0},{8,4},{12,8},{1,13},{5,1},{9,5},{13,9},{2,14},{6,2},{... | collective-permute-start | bytes 24584 | tf_op jit(solution)/shard_map/ppermute | solution.py:216

commit v2 on v0

v2 whole, which is shorter than its diff:
```python
import functools

import jax
import jax.numpy as jnp
from jax import lax
from jax.experimental import pallas as pl
from jax.experimental.pallas import tpu as pltpu
from jax.sharding import PartitionSpec as P

F32 = jnp.float32
BF16 = jnp.bfloat16
MIB = 1024 * 1024
NT = (((1,), (1,)), ((), ()))
MOST_DIRECT = 8
TILES = 4


def params(mib):
    return pltpu.CompilerParams(vmem_limit_bytes=mib * MIB)


def cost(flops, nbytes):
    return pl.CostEstimate(flops=flops, bytes_accessed=nbytes, transcendentals=0)


def halves(x):
    high = x.astype(BF16)
    return high, (x - high.astype(F32)).astype(BF16)


def mm(a, b, dims=(((1,), (0,)), ((), ()))):
    return lax.dot_general(a, b, dims, preferred_element_type=F32)


def copies(pairs, sems):
    made = [pltpu.make_async_copy(src, dst, sems.at[i]) for i, (src, dst) in enumerate(pairs)]
    for copy in made:
        copy.start()
    return made


def slot_mask(owners, relative, cap, lengths, owner, slots, tokens):
    docs = lengths.shape[1]
    row = lax.broadcasted_iota(jnp.int32, (docs, docs), 0)
    col = lax.broadcasted_iota(jnp.int32, (docs, docs), 1)
    len_row = lengths.astype(F32)
    place_row = owner ^ lax.axis_index("dp") if relative else owner
    own_row = place_row.astype(F32)

    def column(values):
        return jnp.sum(jnp.where(row == col, values, 0.0), axis=1, keepdims=True)

    ends = jnp.sum(jnp.where(row <= col, column(len_row), 0.0), axis=0, keepdims=True)
    rank = jnp.sum(
        jnp.where((row < col) & (column(own_row) == own_row), 1.0, 0.0), axis=0, keepdims=True
    )
    slot = lax.broadcasted_iota(jnp.int32, (slots, docs), 0).astype(F32)
    hot = slot == own_row * cap + rank
    first = jnp.sum(jnp.where(hot, ends - len_row, 0.0), axis=1, keepdims=True)
    last = jnp.sum(jnp.where(hot, ends, 0.0), axis=1, keepdims=True)
    token = lax.broadcasted_iota(jnp.int32, (slots, tokens), 1).astype(F32)
    return jnp.where((token >= first) & (token < last), 1.0, 0.0)


def project_kernel(
    owners, relative, cap, width, act_hbm, grad_hbm, in_hbm, out_hbm, len_hbm, own_hbm,
    keep_ref, send_ref, mask_ref, act, grad, proj_in, proj_out, lens, owner, turned, sems,
):
    tokens = act.shape[0]
    rank = proj_in.shape[0]
    half = rank // 2
    tile = tokens // TILES
    tiles = [pl.ds(i * tile, tile) for i in range(TILES)]
    pairs = [(len_hbm, lens), (own_hbm, owner), (in_hbm, proj_in), (act_hbm, act)]
    pairs += [(out_hbm, proj_out)]
    pairs += [(grad_hbm.at[t, :], grad.at[t, :]) for t in tiles]
    made = copies(pairs, sems)
    made[0].wait()
    made[1].wait()
    mask_ref[...] = slot_mask(
        owners, relative, cap, lens[...], owner[...], mask_ref.shape[0], tokens
    )
    me = lax.axis_index("tensor")
    parity = lax.rem(me, 2)
    made[2].wait()
    made[3].wait()
    x_t = mm(act[...], proj_in[...], NT).T
    keep_ref[:half, :] = jnp.where(parity == 0, x_t[:half], x_t[half:])
    send_ref[:half, :] = jnp.where(parity == 0, x_t[half:], x_t[:half])
    made[4].wait()
    for i, t in enumerate(tiles):
        made[5 + i].wait()
        turned[:, t] = mm(grad[t, :], proj_out[...], NT).T
    spot = half
    for apart in range(rank // width - 2, -1, -2):
        for ref, who in ((keep_ref, me ^ apart), (send_ref, me ^ (apart ^ 1))):
            block = pl.ds(pl.multiple_of(who * width, width), width)
            ref[spot : spot + width, :] = turned[block, :]
        spot += width


def project(act, grad, in_t, out_t, lengths, owner_row, owners, cap, width, relative):
    tokens, rank = act.shape[0], in_t.shape[0]
    depth = act.shape[1] + grad.shape[1]
    part = jax.ShapeDtypeStruct((rank, tokens), F32)
    hbm = pl.BlockSpec(memory_space=pl.ANY)
    vmem = pl.BlockSpec(memory_space=pltpu.VMEM)
    return pl.pallas_call(
        functools.partial(project_kernel, owners, relative, cap, width),
        in_specs=[hbm] * 6,
        out_specs=[vmem] * 3,
        out_shape=[part, part, jax.ShapeDtypeStruct((owners * cap, tokens), F32)],
        scratch_shapes=[
            pltpu.VMEM(act.shape, BF16),
            pltpu.VMEM(grad.shape, BF16),
            pltpu.VMEM(in_t.shape, BF16),
            pltpu.VMEM(out_t.shape, BF16),
            pltpu.VMEM(lengths.shape, jnp.int32),
            pltpu.VMEM(owner_row.shape, jnp.int32),
            pltpu.VMEM((rank, tokens), F32),
            pltpu.SemaphoreType.DMA((5 + TILES,)),
        ],
        compiler_params=params(24),
        cost_estimate=cost(2 * tokens * depth * rank, 2 * depth * (tokens + rank)),
    )(
        *(
            pltpu.with_memory_space_constraint(x, pltpu.HBM)
            for x in (act, grad, in_t, out_t, lengths, owner_row)
        )
    )


def outer_kernel(x_ref, x_other_ref, g_ref, mask_ref, *blocks):
    width = g_ref.shape[0]
    rank = 2 * x_ref.shape[0]
    odd = lax.rem(lax.axis_index("tensor"), 2) == 1
    own, other = x_ref[...], x_other_ref[...]
    x_full = jnp.concatenate([jnp.where(odd, other, own), jnp.where(odd, own, other)], axis=0)
    x_both = jnp.concatenate(halves(x_full), axis=0)
    g_high = g_ref[...].astype(BF16).astype(F32)
    g_low = g_ref[...] - g_high
    mask = mask_ref[...]
    cap = blocks[0].shape[0]

    def product(i):
        total = None
        for g in (g_high, g_low):
            term = mm((mask * g[i : i + 1, :]).astype(BF16), x_both, NT)
            total = term if total is None else total + term
        return total[:, :rank] + total[:, rank:]

    step = max(1, 128 // rank)
    for i in range(0, width, step):
        columns = jnp.concatenate([product(i + j) for j in range(step)], axis=1)
        for k, block in enumerate(blocks):
            block[:, i * rank : (i + step) * rank] = columns[k * cap : (k + 1) * cap, :]


def outer(x_half, x_other, g_t, mask, owners):
    slots, tokens = mask.shape
    width, rank = g_t.shape[0], 2 * x_half.shape[0]
    cap = slots // owners
    return pl.pallas_call(
        outer_kernel,
        out_shape=[jax.ShapeDtypeStruct((cap, width * rank), F32)] * owners,
        compiler_params=params(24),
        cost_estimate=cost(8 * slots * width * tokens * rank, 4 * slots * width * rank),
    )(x_half, x_other, g_t, mask)


def score_kernel(count, early, size, gaps, relative, ids_ref, *refs):
    rows, pieces, scores_ref = refs[:count], refs[count:-1], refs[-1]
    queries = ids_ref.shape[1]
    me = lax.axis_index("dp")
    cap = rows[0].shape[0]
    high, low = halves(jnp.concatenate([r[:cap, :] for r in rows], axis=0))
    slots = high.shape[0]
    both = jnp.concatenate([high, low], axis=0)
    parts = [piece[...] for piece in pieces]
    parts += [rows[1][cap + i * size : cap + (i + 1) * size, :] for i in range(len(gaps) - early)]
    total = None
    for gap, piece in zip(gaps, parts):
        held = piece.shape[0]
        products = mm(both, jnp.concatenate(halves(piece), axis=0), NT)
        part = products[:slots, :held] + products[:slots, held:] + products[slots:, :held]
        base = (me ^ gap) * held if len(gaps) > 1 else 0
        place = lax.broadcasted_iota(jnp.int32, (held, queries), 0) + base
        hot = jnp.where(place == ids_ref[...], 1.0, 0.0).astype(BF16)
        top, rest = halves(part)
        last = (part - top.astype(F32) - rest.astype(F32)).astype(BF16)
        for term in (top, rest, last):
            picked = mm(term, hot)
            total = picked if total is None else total + picked
    for k in range(count):
        spot = pl.ds(pl.multiple_of((me ^ k) * cap, cap), cap) if relative else pl.ds(k * cap, cap)
        scores_ref[spot, :] = total[k * cap : (k + 1) * cap, :]


def score(ids_row, rows, pieces, gaps, relative):
    slots = rows[0].shape[0] * len(rows)
    queries = ids_row.shape[1]
    size, feats = pieces[0].shape
    flops = 6 * slots * size * len(gaps) * feats
    return pl.pallas_call(
        functools.partial(score_kernel, len(rows), len(pieces), size, gaps, relative),
        out_shape=jax.ShapeDtypeStruct((slots, queries), F32),
        compiler_params=params(24),
        cost_estimate=cost(flops, 4 * size * len(gaps) * feats),
    )(ids_row, *rows, *pieces)


def place_kernel(*refs):
    rows, store_ref = refs[:-1], refs[-1]
    me = lax.axis_index("dp")
    cap = rows[0].shape[0]
    for k, row in enumerate(rows):
        store_ref[pl.ds(pl.multiple_of((me ^ k) * cap, cap), cap), :] = row[:cap, :]


def place(rows):
    slots, feats = rows[0].shape[0] * len(rows), rows[0].shape[1]
    return pl.pallas_call(
        place_kernel,
        out_shape=jax.ShapeDtypeStruct((slots, feats), F32),
        compiler_params=params(16),
        cost_estimate=cost(0, 8 * slots * feats),
    )(*rows)


def swap(x, axis, gap):
    return lax.ppermute(x, axis, [(i, i ^ gap) for i in range(lax.axis_size(axis))])


def gather_pieces(piece):
    pieces, gaps = [piece], [0]
    bit = lax.axis_size("dp") // 2
    while bit > 1:
        pieces, gaps = pieces + [swap(p, "dp", bit) for p in pieces], gaps + [g ^ bit for g in gaps]
        bit //= 2
    return pieces, gaps


def local(
    activations, out_grads, proj_in, proj_out, doc_lengths, doc_owner, query_grads, query_ids
):
    tensor_size = lax.axis_size("tensor")
    data_size = lax.axis_size("dp")
    tokens = activations.shape[0]
    rank = proj_in.shape[1]
    half = rank // 2
    width = rank // tensor_size
    docs = doc_owner.shape[0]
    cap = max(2, 2 * docs // data_size)
    direct = data_size <= MOST_DIRECT

    if direct:
        pieces, gaps = gather_pieces(query_grads)
        mate = swap(query_grads, "dp", 1)
    else:
        pieces, gaps = [lax.all_gather(query_grads, "dp", axis=0, tiled=True)], [0]

    keep, send, mask = project(
        activations, out_grads, proj_in.T, proj_out.T, doc_lengths, doc_owner.T,
        data_size, cap, width, direct,
    )
    part = keep + swap(send, "tensor", 1)
    bit = tensor_size // 2
    while bit > 1:
        cut = half + (part.shape[0] - half) // 2
        got = swap(part[:cut], "tensor", bit)
        part = jnp.concatenate([part[:half] + got[:half], part[cut:] + got[half:]], axis=0)
        bit //= 2
    x_half, g_mine = part[:half], part[half:]
    x_other = swap(x_half, "tensor", 1)
    blocks = outer(x_half, x_other, g_mine, mask, data_size)
    if direct:
        near = swap(jnp.concatenate([blocks[1], *pieces[1:]], axis=0), "dp", 1)
        far = [swap(blocks[k], "dp", k) for k in range(2, data_size)]
        rows = [blocks[0], near, *far]
        pieces, gaps = [*pieces, mate], [*gaps, 1, *(g ^ 1 for g in gaps[1:])]
        store = place(rows)
    else:
        rows = [lax.all_to_all(jnp.stack(blocks), "dp", 0, 0, tiled=True).reshape(-1, width * rank)]
        store = rows[0]
    scores = score(query_ids[None, :], rows, pieces, gaps, direct)
    bit = 1
    while bit < tensor_size:
        scores = scores + swap(scores, "tensor", bit)
        bit *= 2
    return store, scores * (1.0 / (rank * rank))


def solution(mesh):
    return jax.shard_map(
        local,
        mesh=mesh,
        in_specs=(
            P(("groups", "dp"), "tensor"),
            P(("groups", "dp"), "tensor"),
            P("tensor", None),
            P("tensor", None),
            P(("groups", "dp"), None),
            P(("groups", "dp"), None),
            P(("groups", "dp"), "tensor"),
            P("groups"),
        ),
        out_specs=(P(("groups", "dp"), "tensor"), P(("groups", "dp"), None)),
        check_vma=False,
    )
```

time: 91.8 us -> 40 us (0.44)
  blocking collectives: 27.5 us -> 0 us
  between operations: 14.2 us -> 0.71 us
  matrix products: 9.03 us -> 0 us
  waiting for transfers between devices: 26.7 us -> 18.1 us
  Pallas kernels: 0 us -> 8.11 us
  starting transfers between devices: 8.04 us -> 12.2 us
  local copies, waits for them, and re-layouts: 3.92 us -> 0.02 us
  other arithmetic: 2.09 us -> 0.68 us
    ppermute x0 -> x10, waiting for transfers between devices: none -> 18.1 us  [swap(): lax.ppermute(x, axis, [(i, i ^ gap) for i in range(lax.axis_size(axis))])]
    all_gather x1 -> x0, blocking collectives: 17.4 us -> none  [local(): all_rows = lax.all_gather(query_grads, 'dp', axis=0, tiled=True)]
    psum x1 -> x0, waiting for transfers between devices: 15.9 us -> none  [local(): lax.psum(jnp.concatenate([jnp.dot(activations, proj_in, preferred_element...]
    ppermute x0 -> x10, starting transfers between devices: none -> 12.2 us  [swap(): lax.ppermute(x, axis, [(i, i ^ gap) for i in range(lax.axis_size(axis))])]
    all_to_all x2 -> x0, waiting for transfers between devices: 10.8 us -> none  [the longest x1 6.12 us: local(): lax.all_to_all(send_rows, 'dp', split_axis=0, concat_axis=0, tiled=True)]
    psum x1 -> x0, blocking collectives: 10.1 us -> none  [local(): own_scores = lax.psum(score_rows(doc_grads, queries), 'tensor')]
    dot_general x6 -> x0, matrix products: 9.03 us -> none  [the longest x1 3.34 us: local(): jnp.dot(out_grads, proj_out, preferred_element_type=jnp.float32)]
    pallas_call x0 -> x4, Pallas kernels: none -> 8.11 us  [the longest x1 4.6 us: project(): pl.pallas_call(functools.partial(project_kernel, owners, relative, cap, w...]
  transfers between devices with their start and end apart: 3 -> 10, of which waited for: 3 -> 8; matrix products, arithmetic and copies ran while one was open for 3% -> 0% of each run, Pallas kernels for 0% -> 6%
where the time goes in v2:
time: 40 us; the launch traced here: 39.8 us
  waiting for transfers between devices  18.1 us (45%)
  starting transfers between devices  12.2 us (30%)
  Pallas kernels  8.11 us (20%)
  between operations  0.71 us (2%)
  other arithmetic  0.68 us (2%)
    ppermute x10, waiting for transfers between devices, swap(): lax.ppermute(x, axis, [(i, i ^ gap) for i in range(lax.axis_size(axis))])  18.1 us
    ppermute x10, starting transfers between devices, swap(): lax.ppermute(x, axis, [(i, i ^ gap) for i in range(lax.axis_size(axis))])  12.2 us
    pallas_call x1, Pallas kernels, project(): pl.pallas_call(functools.partial(project_kernel, owners, relative, cap, w...  4.6 us
    pallas_call x1, Pallas kernels, outer(): pl.pallas_call(outer_kernel, out_shape=[jax.ShapeDtypeStruct((cap, width...  1.71 us
    pallas_call x1, Pallas kernels, score(): pl.pallas_call(functools.partial(score_kernel, len(rows), len(pieces), si...  1.08 us
  transfers between devices with their start and end apart: 10, of which 8 were waited for; matrix products, arithmetic and copies ran while one was open for 0% of the time, Pallas kernels for 6%

profile of v2, /device:TPU:0, one launch (start us, length us, event | category | flops | bytes accessed | tf_op | source)
XLA Modules:
  0.0 39.8 jit_solution(8113405382877982747)
XLA Ops:
  0.7 4.6 %shard_map.95 = (f32[64,512]{1,0:T(8,128)S(1)}, f32[64,512]{1,0:T(8,128)S(1)}, f32[64,512]{1,0:T(8,128)S(1)}) custom-call(bf16[512,1024]{1,0:T(8,128)(2,1)} %act_hbm.1, bf16[512,3584]{1,0:T(8,128)(2,1)} %grad_hbm.1, bf16[64,1024]{1,0:T(8,128)(2,1)} %bitcast.6, bf16[64,3584]{1,0:T(8,128)(2,1)} %bitcast.5, s32[1,32]{1,0:T(1,128)} %len_hbm.1, s32[1,32]{1,0:T(1,128)} %bitcast.7), custom_call_target="tpu_custom_call" | custom-call | flops 301989888 | bytes 5308416 | tf_op jit(solution)/shard_map/pallas_call | solution.py:108
  5.3 0.5 %collective-permute-start = (f32[64,512]{1,0:T(8,128)S(1)}, f32[64,512]{1,0:T(8,128)S(1)}, u32[]{:S(2)}, u32[]{:S(2)}) collective-permute-start(f32[64,512]{1,0:T(8,128)S(1)} %get-tuple-element.10), channel_id=1, source_target_pairs={{0,1},{1,0},{2,3},{3,2},{4,5},{5,4},{6,7},{7,6},{8,9},{9,8},{10,11... | collective-permute-start | bytes 393224 | tf_op jit(solution)/shard_map/ppermute | solution.py:231
  5.8 1.0 %collective-permute-done = f32[64,512]{1,0:T(8,128)S(1)} collective-permute-done((f32[64,512]{1,0:T(8,128)S(1)}, f32[64,512]{1,0:T(8,128)S(1)}, u32[]{:S(2)}, u32[]{:S(2)}) %collective-permute-start) | collective-permute-done | bytes 131104 | tf_op jit(solution)/shard_map/ppermute | solution.py:231
  6.8 2.9 %collective-permute-start.1 = (f32[48,512]{1,0:T(8,128)S(1)}, f32[48,512]{1,0:T(8,128)S(1)}, u32[]{:S(2)}, u32[]{:S(2)}) collective-permute-start(f32[48,512]{1,0:T(8,128)S(1)} %slice.21), channel_id=1, source_target_pairs={{0,2},{1,3},{2,0},{3,1},{4,6},{5,7},{6,4},{7,5},{8,10},{9,11},{10,... | collective-permute-start | bytes 294920 | tf_op jit(solution)/shard_map/ppermute | solution.py:231
  9.7 2.6 %collective-permute-start.3 = (f32[32,1024]{1,0:T(8,128)S(1)}, f32[32,1024]{1,0:T(8,128)S(1)}, u32[]{:S(2)}, u32[]{:S(2)}) collective-permute-start(f32[32,1024]{1,0:T(8,128)S(1)} %copy-done), channel_id=1, source_target_pairs={{0,8},{4,12},{8,0},{12,4},{1,9},{5,13},{9,1},{13,5},{2,10},{6,14},... | collective-permute-start | bytes 393224 | tf_op jit(solution)/shard_map/ppermute | solution.py:231
  12.3 0.5 %collective-permute-done.1 = f32[48,512]{1,0:T(8,128)S(1)} collective-permute-done((f32[48,512]{1,0:T(8,128)S(1)}, f32[48,512]{1,0:T(8,128)S(1)}, u32[]{:S(2)}, u32[]{:S(2)}) %collective-permute-start.1) | collective-permute-done | bytes 98336 | tf_op jit(solution)/shard_map/ppermute | solution.py:231
  12.8 0.1 collective-permute-start.2
  12.9 1.2 %collective-permute-done.2.x_other_ref = f32[32,512]{1,0:T(8,128)S(1)} collective-permute-done((f32[32,512]{1,0:T(8,128)S(1)}, f32[32,512]{1,0:T(8,128)S(1)}, u32[]{:S(2)}, u32[]{:S(2)}) %collective-permute-start.2) | collective-permute-done | bytes 65568 | tf_op jit(solution)/shard_map/ppermute | solution.py:231
  14.2 1.7 %shard_map.96 = (f32[16,1024]{1,0:T(8,128)S(1)}, f32[16,1024]{1,0:T(8,128)S(1)}, f32[16,1024]{1,0:T(8,128)S(1)}, f32[16,1024]{1,0:T(8,128)S(1)}) custom-call(f32[32,512]{1,0:T(8,128)S(1)} %slice_add_fusion.x_ref, f32[32,512]{1,0:T(8,128)S(1)} %collective-permute-done.2.x_other_ref, f32[16,512]{1,0:T(8,128)S(1)} %slice_add_fusion.1.g_ref, ...), custom_call_target="tpu_custom_call" | custom-call | flops 268435456 | bytes 262144 | tf_op jit(solution)/shard_map/pallas_call | solution.py:163
  15.9 2.8 %collective-permute-done.3.refs_5_ = f32[32,1024]{1,0:T(8,128)S(1)} collective-permute-done((f32[32,1024]{1,0:T(8,128)S(1)}, f32[32,1024]{1,0:T(8,128)S(1)}, u32[]{:S(2)}, u32[]{:S(2)}) %collective-permute-start.3) | collective-permute-done | bytes 131104 | tf_op jit(solution)/shard_map/ppermute | solution.py:231
  18.7 0.7 %collective-permute-start.4 = (f32[48,1024]{1,0:T(8,128)S(1)}, f32[48,1024]{1,0:T(8,128)S(1)}, u32[]{:S(2)}, u32[]{:S(2)}) collective-permute-start(f32[48,1024]{1,0:T(8,128)S(1)} %pad_maximum_fusion), channel_id=1, source_target_pairs={{0,4},{4,0},{8,12},{12,8},{1,5},{5,1},{9,13},{13,9},{2,6},{6,2},{1... | collective-permute-start | bytes 589832 | tf_op jit(solution)/shard_map/ppermute | solution.py:231
  19.4 1.4 %collective-permute-start.7 = (f32[32,1024]{1,0:T(8,128)S(1)}, f32[32,1024]{1,0:T(8,128)S(1)}, u32[]{:S(2)}, u32[]{:S(2)}) collective-permute-start(f32[32,1024]{1,0:T(8,128)S(1)} %copy-done), channel_id=1, source_target_pairs={{0,4},{4,0},{8,12},{12,8},{1,5},{5,1},{9,13},{13,9},{2,6},{6,2},{1... | collective-permute-start | bytes 393224 | tf_op jit(solution)/shard_map/ppermute | solution.py:231
  20.8 2.1 %collective-permute-start.5 = (f32[16,1024]{1,0:T(8,128)S(1)}, f32[16,1024]{1,0:T(8,128)S(1)}, u32[]{:S(2)}, u32[]{:S(2)}) collective-permute-start(f32[16,1024]{1,0:T(8,128)S(1)} %get-tuple-element.14), channel_id=1, source_target_pairs={{0,8},{4,12},{8,0},{12,4},{1,9},{5,13},{9,1},{13,5},{2,10},{6,14},... | collective-permute-start | bytes 196616 | tf_op jit(solution)/shard_map/ppermute | solution.py:231
  22.9 1.4 %collective-permute-start.6 = (f32[16,1024]{1,0:T(8,128)S(1)}, f32[16,1024]{1,0:T(8,128)S(1)}, u32[]{:S(2)}, u32[]{:S(2)}) collective-permute-start(f32[16,1024]{1,0:T(8,128)S(1)} %get-tuple-element.15), channel_id=1, source_target_pairs={{0,12},{4,8},{8,4},{12,0},{1,13},{5,9},{9,5},{13,1},{2,14},{6,10},... | collective-permute-start | bytes 196616 | tf_op jit(solution)/shard_map/ppermute | solution.py:231
  24.3 4.5 %collective-permute-done.7.refs_6_ = f32[32,1024]{1,0:T(8,128)S(1)} collective-permute-done((f32[32,1024]{1,0:T(8,128)S(1)}, f32[32,1024]{1,0:T(8,128)S(1)}, u32[]{:S(2)}, u32[]{:S(2)}) %collective-permute-start.7) | collective-permute-done | bytes 131104 | tf_op jit(solution)/shard_map/ppermute | solution.py:231
  28.8 0.0 collective-permute-done.5.refs_2_
  28.8 4.2 %collective-permute-done.6.refs_3_ = f32[16,1024]{1,0:T(8,128)S(1)} collective-permute-done((f32[16,1024]{1,0:T(8,128)S(1)}, f32[16,1024]{1,0:T(8,128)S(1)}, u32[]{:S(2)}, u32[]{:S(2)}) %collective-permute-start.6) | collective-permute-done | bytes 65568 | tf_op jit(solution)/shard_map/ppermute | solution.py:231
  33.0 0.0 collective-permute-done.4.refs_1_
  33.0 1.1 %shard_map.98 = f32[64,128]{1,0:T(8,128)S(1)} custom-call(s32[1,128]{1,0:T(1,128)S(1)} %bitcast.4, f32[16,1024]{1,0:T(8,128)S(1)} %get-tuple-element.12.refs_0_, f32[48,1024]{1,0:T(8,128)S(1)} %collective-permute-done.4.refs_1_, f32[16,1024]{1,0:T(8,128)S(1)} %collective-permute-done.5.refs_2_, f32[16,1024]{1,0:T(8,128)S(1)} %collective-permute-done.6.refs_3_, ...), custom_call_target="tpu_custom_call" | custom-call | flops 50331648 | bytes 524288 | tf_op jit(solution)/shard_map/pallas_call | solution.py:204
  34.1 1.2 %collective-permute-done.8 = f32[64,128]{1,0:T(8,128)S(1)} collective-permute-done((f32[64,128]{1,0:T(8,128)S(1)}, f32[64,128]{1,0:T(8,128)S(1)}, u32[]{:S(2)}, u32[]{:S(2)}) %collective-permute-start.8) | collective-permute-done | bytes 32800 | tf_op jit(solution)/shard_map/ppermute | solution.py:231
  35.3 0.5 %collective-permute-start.9 = (f32[64,128]{1,0:T(8,128)S(1)}, f32[64,128]{1,0:T(8,128)S(1)}, u32[]{:S(2)}, u32[]{:S(2)}) collective-permute-start(f32[64,128]{1,0:T(8,128)S(1)} %add.18), channel_id=1, source_target_pairs={{0,2},{1,3},{2,0},{3,1},{4,6},{5,7},{6,4},{7,5},{8,10},{9,11},{10,... | collective-permute-start | bytes 98312 | tf_op jit(solution)/shard_map/ppermute | solution.py:231
  35.8 0.7 %shard_map.97 = f32[64,1024]{1,0:T(8,128)} custom-call(f32[16,1024]{1,0:T(8,128)S(1)} %get-tuple-element.12.refs_0_, f32[48,1024]{1,0:T(8,128)S(1)} %collective-permute-done.4.refs_1_, f32[16,1024]{1,0:T(8,128)S(1)} %collective-permute-done.5.refs_2_, f32[16,1024]{1,0:T(8,128)S(1)} %collective-permute-done.6.refs_3_), custom_call_target="tpu_custom_call" | custom-call | bytes 524288 | tf_op jit(solution)/shard_map/pallas_call | solution.py:222
  36.5 2.6 %collective-permute-done.9 = f32[64,128]{1,0:T(8,128)S(1)} collective-permute-done((f32[64,128]{1,0:T(8,128)S(1)}, f32[64,128]{1,0:T(8,128)S(1)}, u32[]{:S(2)}, u32[]{:S(2)}) %collective-permute-start.9) | collective-permute-done | bytes 32800 | tf_op jit(solution)/shard_map/ppermute | solution.py:231
  39.2 0.6 %add_multiply_fusion = f32[64,128]{1,0:T(8,128)} fusion(f32[64,128]{1,0:T(8,128)S(1)} %add.18, f32[64,128]{1,0:T(8,128)S(1)} %collective-permute-done.9), kind=kLoop, calls=%fused_computation.3 | loop fusion | flops 16384 | bytes 98304 | tf_op jit(solution)/shard_map/mul | solution.py:290
  (11 shorter events, 0.1 us)
Async XLA Ops:
  0.6 9.1 %copy-start = (f32[32,1024]{1,0:T(8,128)S(1)}, f32[32,1024]{1,0:T(8,128)}, u32[]{:S(2)}) copy-start(f32[32,1024]{1,0:T(8,128)} %refs_4_.1) | copy-start | bytes 393220
  0.6 32.3 %copy-start.1 = (s32[128]{0:T(128)S(1)}, s32[128]{0:T(128)}, u32[]{:S(2)}) copy-start(s32[128]{0:T(128)} %param.15) | copy-start | bytes 1540
  5.3 1.5 %collective-permute-start = (f32[64,512]{1,0:T(8,128)S(1)}, f32[64,512]{1,0:T(8,128)S(1)}, u32[]{:S(2)}, u32[]{:S(2)}) collective-permute-start(f32[64,512]{1,0:T(8,128)S(1)} %get-tuple-element.10), channel_id=1, source_target_pairs={{0,1},{1,0},{2,3},{3,2},{4,5},{5,4},{6,7},{7,6},{8,9},{9,8},{10,11... | collective-permute-start | bytes 393224 | tf_op jit(solution)/shard_map/ppermute | solution.py:231
  6.8 6.0 %collective-permute-start.1 = (f32[48,512]{1,0:T(8,128)S(1)}, f32[48,512]{1,0:T(8,128)S(1)}, u32[]{:S(2)}, u32[]{:S(2)}) collective-permute-start(f32[48,512]{1,0:T(8,128)S(1)} %slice.21), channel_id=1, source_target_pairs={{0,2},{1,3},{2,0},{3,1},{4,6},{5,7},{6,4},{7,5},{8,10},{9,11},{10,... | collective-permute-start | bytes 294920 | tf_op jit(solution)/shard_map/ppermute | solution.py:231
  9.7 9.0 %collective-permute-start.3 = (f32[32,1024]{1,0:T(8,128)S(1)}, f32[32,1024]{1,0:T(8,128)S(1)}, u32[]{:S(2)}, u32[]{:S(2)}) collective-permute-start(f32[32,1024]{1,0:T(8,128)S(1)} %copy-done), channel_id=1, source_target_pairs={{0,8},{4,12},{8,0},{12,4},{1,9},{5,13},{9,1},{13,5},{2,10},{6,14},... | collective-permute-start | bytes 393224 | tf_op jit(solution)/shard_map/ppermute | solution.py:231
  12.8 1.3 %collective-permute-start.2 = (f32[32,512]{1,0:T(8,128)S(1)}, f32[32,512]{1,0:T(8,128)S(1)}, u32[]{:S(2)}, u32[]{:S(2)}) collective-permute-start(f32[32,512]{1,0:T(8,128)S(1)} %slice_add_fusion.x_ref), channel_id=1, source_target_pairs={{0,1},{1,0},{2,3},{3,2},{4,5},{5,4},{6,7},{7,6},{8,9},{9,8},{10,11... | collective-permute-start | bytes 196616 | tf_op jit(solution)/shard_map/ppermute | solution.py:231
  18.7 14.3 %collective-permute-start.4 = (f32[48,1024]{1,0:T(8,128)S(1)}, f32[48,1024]{1,0:T(8,128)S(1)}, u32[]{:S(2)}, u32[]{:S(2)}) collective-permute-start(f32[48,1024]{1,0:T(8,128)S(1)} %pad_maximum_fusion), channel_id=1, source_target_pairs={{0,4},{4,0},{8,12},{12,8},{1,5},{5,1},{9,13},{13,9},{2,6},{6,2},{1... | collective-permute-start | bytes 589832 | tf_op jit(solution)/shard_map/ppermute | solution.py:231
  19.4 9.4 %collective-permute-start.7 = (f32[32,1024]{1,0:T(8,128)S(1)}, f32[32,1024]{1,0:T(8,128)S(1)}, u32[]{:S(2)}, u32[]{:S(2)}) collective-permute-start(f32[32,1024]{1,0:T(8,128)S(1)} %copy-done), channel_id=1, source_target_pairs={{0,4},{4,0},{8,12},{12,8},{1,5},{5,1},{9,13},{13,9},{2,6},{6,2},{1... | collective-permute-start | bytes 393224 | tf_op jit(solution)/shard_map/ppermute | solution.py:231
  20.8 8.0 %collective-permute-start.5 = (f32[16,1024]{1,0:T(8,128)S(1)}, f32[16,1024]{1,0:T(8,128)S(1)}, u32[]{:S(2)}, u32[]{:S(2)}) collective-permute-start(f32[16,1024]{1,0:T(8,128)S(1)} %get-tuple-element.14), channel_id=1, source_target_pairs={{0,8},{4,12},{8,0},{12,4},{1,9},{5,13},{9,1},{13,5},{2,10},{6,14},... | collective-permute-start | bytes 196616 | tf_op jit(solution)/shard_map/ppermute | solution.py:231
  22.9 10.1 %collective-permute-start.6 = (f32[16,1024]{1,0:T(8,128)S(1)}, f32[16,1024]{1,0:T(8,128)S(1)}, u32[]{:S(2)}, u32[]{:S(2)}) collective-permute-start(f32[16,1024]{1,0:T(8,128)S(1)} %get-tuple-element.15), channel_id=1, source_target_pairs={{0,12},{4,8},{8,4},{12,0},{1,13},{5,9},{9,5},{13,1},{2,14},{6,10},... | collective-permute-start | bytes 196616 | tf_op jit(solution)/shard_map/ppermute | solution.py:231
  34.0 1.2 %collective-permute-start.8 = (f32[64,128]{1,0:T(8,128)S(1)}, f32[64,128]{1,0:T(8,128)S(1)}, u32[]{:S(2)}, u32[]{:S(2)}) collective-permute-start(f32[64,128]{1,0:T(8,128)S(1)} %shard_map.98), channel_id=1, source_target_pairs={{0,1},{1,0},{2,3},{3,2},{4,5},{5,4},{6,7},{7,6},{8,9},{9,8},{10,11... | collective-permute-start | bytes 98312 | tf_op jit(solution)/shard_map/ppermute | solution.py:231
  35.3 3.9 %collective-permute-start.9 = (f32[64,128]{1,0:T(8,128)S(1)}, f32[64,128]{1,0:T(8,128)S(1)}, u32[]{:S(2)}, u32[]{:S(2)}) collective-permute-start(f32[64,128]{1,0:T(8,128)S(1)} %add.18), channel_id=1, source_target_pairs={{0,2},{1,3},{2,0},{3,1},{4,6},{5,7},{6,4},{7,5},{8,10},{9,11},{10,... | collective-permute-start | bytes 98312 | tf_op jit(solution)/shard_map/ppermute | solution.py:231

commit v3 on v2

--- a/solution.py
+++ b/solution.py
@@ -12,7 +12,7 @@
 MIB = 1024 * 1024
 NT = (((1,), (1,)), ((), ()))
 MOST_DIRECT = 8
-TILES = 4
+CHUNKS = 2
 
 
 def params(mib):
@@ -69,28 +69,31 @@
     tokens = act.shape[0]
     rank = proj_in.shape[0]
     half = rank // 2
-    tile = tokens // TILES
-    tiles = [pl.ds(i * tile, tile) for i in range(TILES)]
-    pairs = [(len_hbm, lens), (own_hbm, owner), (in_hbm, proj_in), (act_hbm, act)]
-    pairs += [(out_hbm, proj_out)]
-    pairs += [(grad_hbm.at[t, :], grad.at[t, :]) for t in tiles]
-    made = copies(pairs, sems)
-    made[0].wait()
-    made[1].wait()
-    mask_ref[...] = slot_mask(
-        owners, relative, cap, lens[...], owner[...], mask_ref.shape[0], tokens
-    )
+    chunk = grad.shape[1] // CHUNKS
+    chunks = [pl.ds(i * chunk, chunk) for i in range(CHUNKS)]
+    pairs = [(in_hbm, proj_in), (act_hbm, act), (out_hbm, proj_out)]
+    pairs += [(grad_hbm.at[:, c], grad.at[:, c]) for c in chunks]
+    pairs += [(len_hbm, lens), (own_hbm, owner)]
+    in_copy, act_copy, out_copy, *grad_copies, len_copy, own_copy = copies(pairs, sems)
     me = lax.axis_index("tensor")
     parity = lax.rem(me, 2)
-    made[2].wait()
-    made[3].wait()
+    in_copy.wait()
+    act_copy.wait()
     x_t = mm(act[...], proj_in[...], NT).T
     keep_ref[:half, :] = jnp.where(parity == 0, x_t[:half], x_t[half:])
     send_ref[:half, :] = jnp.where(parity == 0, x_t[half:], x_t[:half])
-    made[4].wait()
-    for i, t in enumerate(tiles):
-        made[5 + i].wait()
-        turned[:, t] = mm(grad[t, :], proj_out[...], NT).T
+    len_copy.wait()
+    own_copy.wait()
+    mask_ref[...] = slot_mask(
+        owners, relative, cap, lens[...], owner[...], mask_ref.shape[0], tokens
+    )
+    out_copy.wait()
+    total = None
+    for c, copy in zip(chunks, grad_copies):
+        copy.wait()
+        term = mm(grad[:, c], proj_out[:, c], NT)
+        total = term if total is None else total + term
+    turned[...] = total.T
     spot = half
     for apart in range(rank // width - 2, -1, -2):
         for ref, who in ((keep_ref, me ^ apart), (send_ref, me ^ (apart ^ 1))):
@@ -118,7 +121,7 @@
             pltpu.VMEM(lengths.shape, jnp.int32),
             pltpu.VMEM(owner_row.shape, jnp.int32),
             pltpu.VMEM((rank, tokens), F32),
-            pltpu.SemaphoreType.DMA((5 + TILES,)),
+            pltpu.SemaphoreType.DMA((5 + CHUNKS,)),
         ],
         compiler_params=params(24),
         cost_estimate=cost(2 * tokens * depth * rank, 2 * depth * (tokens + rank)),
@@ -143,11 +146,10 @@
     cap = blocks[0].shape[0]
 
     def product(i):
-        total = None
-        for g in (g_high, g_low):
-            term = mm((mask * g[i : i + 1, :]).astype(BF16), x_both, NT)
-            total = term if total is None else total + term
-        return total[:, :rank] + total[:, rank:]
+        pair = [(mask * g[i : i + 1, :]).astype(BF16) for g in (g_high, g_low)]
+        both = mm(jnp.concatenate(pair, axis=0), x_both, NT)
+        slots = mask.shape[0]
+        return both[:slots, :rank] + both[:slots, rank:] + both[slots:, :rank]
 
     step = max(1, 128 // rank)
     for i in range(0, width, step):
@@ -164,8 +166,35 @@
         outer_kernel,
         out_shape=[jax.ShapeDtypeStruct((cap, width * rank), F32)] * owners,
         compiler_params=params(24),
-        cost_estimate=cost(8 * slots * width * tokens * rank, 4 * slots * width * rank),
+        cost_estimate=cost(0, 0),
     )(x_half, x_other, g_t, mask)
+
+
+def join_kernel(block_ref, *refs):
+    *pieces, _, joined_ref, _ = refs
+    cap = block_ref.shape[0]
+    joined_ref[:cap, :] = block_ref[...]
+    for i, piece in enumerate(pieces):
+        size = piece.shape[0]
+        joined_ref[cap + i * size : cap + (i + 1) * size, :] = piece[...]
+
+
+def join(block, pieces, mate):
+    rows = block.shape[0] + sum(p.shape[0] for p in pieces)
+    vmem = pl.BlockSpec(memory_space=pltpu.VMEM)
+    anywhere = pl.BlockSpec(memory_space=pl.ANY)
+    return pl.pallas_call(
+        join_kernel,
+        in_specs=[vmem] * (1 + len(pieces)) + [anywhere],
+        out_specs=[vmem, anywhere],
+        out_shape=[
+            jax.ShapeDtypeStruct((rows, block.shape[1]), F32),
+            jax.ShapeDtypeStruct(mate.shape, mate.dtype),
+        ],
+        input_output_aliases={1 + len(pieces): 1},
+        compiler_params=params(16),
+        cost_estimate=cost(0, 0),
+    )(block, *pieces, mate)
 
 
 def score_kernel(count, early, size, gaps, relative, ids_ref, *refs):
@@ -178,19 +207,18 @@
     both = jnp.concatenate([high, low], axis=0)
     parts = [piece[...] for piece in pieces]
     parts += [rows[1][cap + i * size : cap + (i + 1) * size, :] for i in range(len(gaps) - early)]
-    total = None
-    for gap, piece in zip(gaps, parts):
-        held = piece.shape[0]
-        products = mm(both, jnp.concatenate(halves(piece), axis=0), NT)
-        part = products[:slots, :held] + products[:slots, held:] + products[slots:, :held]
-        base = (me ^ gap) * held if len(gaps) > 1 else 0
-        place = lax.broadcasted_iota(jnp.int32, (held, queries), 0) + base
-        hot = jnp.where(place == ids_ref[...], 1.0, 0.0).astype(BF16)
-        top, rest = halves(part)
-        last = (part - top.astype(F32) - rest.astype(F32)).astype(BF16)
-        for term in (top, rest, last):
-            picked = mm(term, hot)
-            total = picked if total is None else total + picked
+    held = parts[0].shape[0]
+    pool = jnp.concatenate(parts, axis=0)
+    products = mm(both, jnp.concatenate(halves(pool), axis=0), NT)
+    split = pool.shape[0]
+    part = products[:slots, :split] + products[:slots, split:] + products[slots:, :split]
+    row = lax.broadcasted_iota(jnp.int32, (held, queries), 0)
+    places = [row + ((me ^ gap) * held if len(gaps) > 1 else 0) for gap in gaps]
+    hot = (jnp.concatenate(places, axis=0) == ids_ref[...]).astype(F32).astype(BF16)
+    top, rest = halves(part)
+    last = (part - top.astype(F32) - rest.astype(F32)).astype(BF16)
+    picked = mm(jnp.concatenate([top, rest, last], axis=0), hot)
+    total = picked[:slots] + picked[slots : 2 * slots] + picked[2 * slots :]
     for k in range(count):
         spot = pl.ds(pl.multiple_of((me ^ k) * cap, cap), cap) if relative else pl.ds(k * cap, cap)
         scores_ref[spot, :] = total[k * cap : (k + 1) * cap, :]
@@ -274,7 +302,8 @@
     x_other = swap(x_half, "tensor", 1)
     blocks = outer(x_half, x_other, g_mine, mask, data_size)
     if direct:
-        near = swap(jnp.concatenate([blocks[1], *pieces[1:]], axis=0), "dp", 1)
+        joined, mate = join(blocks[1], pieces[1:], mate)
+        near = swap(joined, "dp", 1)
         far = [swap(blocks[k], "dp", k) for k in range(2, data_size)]
         rows = [blocks[0], near, *far]
         pieces, gaps = [*pieces, mate], [*gaps, 1, *(g ^ 1 for g in gaps[1:])]

time: 40 us -> 36.1 us (0.903)
  waiting for transfers between devices: 18.1 us -> 15.7 us
  Pallas kernels: 8.11 us -> 6.14 us
  starting transfers between devices: 12.2 us -> 12.7 us
    ppermute x10, waiting for transfers between devices: 18.1 us -> 15.7 us  [swap(): lax.ppermute(x, axis, [(i, i ^ gap) for i in range(lax.axis_size(axis))])]
    pallas_call x1, Pallas kernels: 1.71 us -> 0.84 us  [outer(): pl.pallas_call(outer_kernel, out_shape=[jax.ShapeDtypeStruct((cap, width...]
    pallas_call x1, Pallas kernels: 1.08 us -> 0.44 us  [score(): pl.pallas_call(functools.partial(score_kernel, len(rows), len(pieces), si...]
    ppermute x10, starting transfers between devices: 12.2 us -> 12.7 us  [swap(): lax.ppermute(x, axis, [(i, i ^ gap) for i in range(lax.axis_size(axis))])]
    pallas_call x1, Pallas kernels: 4.6 us -> 4.12 us  [project(): pl.pallas_call(functools.partial(project_kernel, owners, relative, cap, w...]
  transfers between devices with their start and end apart: 10 -> 10, of which waited for: 8 -> 8; matrix products, arithmetic and copies ran while one was open for 0% -> 0% of each run, Pallas kernels for 6% -> 4%
where the time goes in v3:
time: 36.1 us; the launch traced here: 36 us
  waiting for transfers between devices  15.7 us (43%)
  starting transfers between devices  12.7 us (35%)
  Pallas kernels  6.14 us (17%)
  between operations  0.72 us (2%)
  other arithmetic  0.66 us (2%)
    ppermute x10, waiting for transfers between devices, swap(): lax.ppermute(x, axis, [(i, i ^ gap) for i in range(lax.axis_size(axis))])  15.7 us
    ppermute x10, starting transfers between devices, swap(): lax.ppermute(x, axis, [(i, i ^ gap) for i in range(lax.axis_size(axis))])  12.7 us
    pallas_call x1, Pallas kernels, project(): pl.pallas_call(functools.partial(project_kernel, owners, relative, cap, w...  4.12 us
    pallas_call x1, Pallas kernels, outer(): pl.pallas_call(outer_kernel, out_shape=[jax.ShapeDtypeStruct((cap, width...  0.84 us
    pallas_call x1, Pallas kernels, place(): pl.pallas_call(place_kernel, out_shape=jax.ShapeDtypeStruct((slots, feats...  0.73 us
  transfers between devices with their start and end apart: 10, of which 8 were waited for; matrix products, arithmetic and copies ran while one was open for 0% of the time, Pallas kernels for 4%

profile of v3, /device:TPU:0, one launch (start us, length us, event | category | flops | bytes accessed | tf_op | source)
XLA Modules:
  0.0 36.0 jit_solution(18275693014613235622)
XLA Ops:
  0.7 4.1 %shard_map.95 = (f32[64,512]{1,0:T(8,128)S(1)}, f32[64,512]{1,0:T(8,128)S(1)}, f32[64,512]{1,0:T(8,128)S(1)}) custom-call(bf16[512,1024]{1,0:T(8,128)(2,1)} %act_hbm.1, bf16[512,3584]{1,0:T(8,128)(2,1)} %grad_hbm.1, bf16[64,1024]{1,0:T(8,128)(2,1)} %bitcast.6, bf16[64,3584]{1,0:T(8,128)(2,1)} %bitcast.5, s32[1,32]{1,0:T(1,128)} %len_hbm.1, s32[1,32]{1,0:T(1,128)} %bitcast.7), custom_call_target="tpu_custom_call" | custom-call | flops 301989888 | bytes 5308416 | tf_op jit(solution)/shard_map/pallas_call | solution.py:111
  4.8 0.5 %collective-permute-start = (f32[64,512]{1,0:T(8,128)S(1)}, f32[64,512]{1,0:T(8,128)S(1)}, u32[]{:S(2)}, u32[]{:S(2)}) collective-permute-start(f32[64,512]{1,0:T(8,128)S(1)} %get-tuple-element.12), channel_id=1, source_target_pairs={{0,1},{1,0},{2,3},{3,2},{4,5},{5,4},{6,7},{7,6},{8,9},{9,8},{10,11... | collective-permute-start | bytes 393224 | tf_op jit(solution)/shard_map/ppermute | solution.py:259
  5.3 1.0 %collective-permute-done = f32[64,512]{1,0:T(8,128)S(1)} collective-permute-done((f32[64,512]{1,0:T(8,128)S(1)}, f32[64,512]{1,0:T(8,128)S(1)}, u32[]{:S(2)}, u32[]{:S(2)}) %collective-permute-start) | collective-permute-done | bytes 131104 | tf_op jit(solution)/shard_map/ppermute | solution.py:259
  6.3 2.9 %collective-permute-start.1 = (f32[48,512]{1,0:T(8,128)S(1)}, f32[48,512]{1,0:T(8,128)S(1)}, u32[]{:S(2)}, u32[]{:S(2)}) collective-permute-start(f32[48,512]{1,0:T(8,128)S(1)} %slice.21), channel_id=1, source_target_pairs={{0,2},{1,3},{2,0},{3,1},{4,6},{5,7},{6,4},{7,5},{8,10},{9,11},{10,... | collective-permute-start | bytes 294920 | tf_op jit(solution)/shard_map/ppermute | solution.py:259
  9.2 2.6 %collective-permute-start.3 = (f32[32,1024]{1,0:T(8,128)S(1)}, f32[32,1024]{1,0:T(8,128)S(1)}, u32[]{:S(2)}, u32[]{:S(2)}) collective-permute-start(f32[32,1024]{1,0:T(8,128)S(1)} %copy-done), channel_id=1, source_target_pairs={{0,8},{4,12},{8,0},{12,4},{1,9},{5,13},{9,1},{13,5},{2,10},{6,14},... | collective-permute-start | bytes 393224 | tf_op jit(solution)/shard_map/ppermute | solution.py:259
  11.8 1.6 %collective-permute-start.4 = (f32[32,1024]{1,0:T(8,128)S(1)}, f32[32,1024]{1,0:T(8,128)S(1)}, u32[]{:S(2)}, u32[]{:S(2)}) collective-permute-start(f32[32,1024]{1,0:T(8,128)S(1)} %copy-done), channel_id=1, source_target_pairs={{0,4},{4,0},{8,12},{12,8},{1,5},{5,1},{9,13},{13,9},{2,6},{6,2},{1... | collective-permute-start | bytes 393224 | tf_op jit(solution)/shard_map/ppermute | solution.py:259
  13.4 0.0 collective-permute-done.1
  13.4 0.1 collective-permute-start.2
  13.5 1.2 %collective-permute-done.2.x_other_ref = f32[32,512]{1,0:T(8,128)S(1)} collective-permute-done((f32[32,512]{1,0:T(8,128)S(1)}, f32[32,512]{1,0:T(8,128)S(1)}, u32[]{:S(2)}, u32[]{:S(2)}) %collective-permute-start.2) | collective-permute-done | bytes 65568 | tf_op jit(solution)/shard_map/ppermute | solution.py:259
  14.7 0.8 %shard_map.96 = (f32[16,1024]{1,0:T(8,128)S(1)}, f32[16,1024]{1,0:T(8,128)S(1)}, f32[16,1024]{1,0:T(8,128)S(1)}, f32[16,1024]{1,0:T(8,128)S(1)}) custom-call(f32[32,512]{1,0:T(8,128)S(1)} %slice_add_fusion.x_ref, f32[32,512]{1,0:T(8,128)S(1)} %collective-permute-done.2.x_other_ref, f32[16,512]{1,0:T(8,128)S(1)} %slice_add_fusion.1.g_ref, ...), custom_call_target="tpu_custom_call" | custom-call | tf_op jit(solution)/shard_map/pallas_call | solution.py:165
  15.6 2.7 %collective-permute-done.3.refs_0_.refs_5_ = f32[32,1024]{1,0:T(8,128)S(1)} collective-permute-done((f32[32,1024]{1,0:T(8,128)S(1)}, f32[32,1024]{1,0:T(8,128)S(1)}, u32[]{:S(2)}, u32[]{:S(2)}) %collective-permute-start.3) | collective-permute-done | bytes 131104 | tf_op jit(solution)/shard_map/ppermute | solution.py:259
  18.3 0.2 collective-permute-done.4.refs_1_
  18.5 1.5 %collective-permute-start.5 = (f32[48,1024]{1,0:T(8,128)S(1)}, f32[48,1024]{1,0:T(8,128)S(1)}, u32[]{:S(2)}, u32[]{:S(2)}) collective-permute-start(f32[48,1024]{1,0:T(8,128)S(1)} %get-tuple-element.16), channel_id=1, source_target_pairs={{0,4},{4,0},{8,12},{12,8},{1,5},{5,1},{9,13},{13,9},{2,6},{6,2},{1... | collective-permute-start | bytes 589832 | tf_op jit(solution)/shard_map/ppermute | solution.py:259
  20.0 2.4 %collective-permute-start.6 = (f32[16,1024]{1,0:T(8,128)S(1)}, f32[16,1024]{1,0:T(8,128)S(1)}, u32[]{:S(2)}, u32[]{:S(2)}) collective-permute-start(f32[16,1024]{1,0:T(8,128)S(1)} %get-tuple-element.17), channel_id=1, source_target_pairs={{0,8},{4,12},{8,0},{12,4},{1,9},{5,13},{9,1},{13,5},{2,10},{6,14},... | collective-permute-start | bytes 196616 | tf_op jit(solution)/shard_map/ppermute | solution.py:259
  22.4 0.6 %collective-permute-start.7 = (f32[16,1024]{1,0:T(8,128)S(1)}, f32[16,1024]{1,0:T(8,128)S(1)}, u32[]{:S(2)}, u32[]{:S(2)}) collective-permute-start(f32[16,1024]{1,0:T(8,128)S(1)} %get-tuple-element.18), channel_id=1, source_target_pairs={{0,12},{4,8},{8,4},{12,0},{1,13},{5,9},{9,5},{13,1},{2,14},{6,10},... | collective-permute-start | bytes 196616 | tf_op jit(solution)/shard_map/ppermute | solution.py:259
  23.0 2.7 %collective-permute-done.6.refs_2_ = f32[16,1024]{1,0:T(8,128)S(1)} collective-permute-done((f32[16,1024]{1,0:T(8,128)S(1)}, f32[16,1024]{1,0:T(8,128)S(1)}, u32[]{:S(2)}, u32[]{:S(2)}) %collective-permute-start.6) | collective-permute-done | bytes 65568 | tf_op jit(solution)/shard_map/ppermute | solution.py:259
  25.7 4.0 %collective-permute-done.7.refs_3_ = f32[16,1024]{1,0:T(8,128)S(1)} collective-permute-done((f32[16,1024]{1,0:T(8,128)S(1)}, f32[16,1024]{1,0:T(8,128)S(1)}, u32[]{:S(2)}, u32[]{:S(2)}) %collective-permute-start.7) | collective-permute-done | bytes 65568 | tf_op jit(solution)/shard_map/ppermute | solution.py:259
  29.7 0.4 %shard_map.99 = f32[64,128]{1,0:T(8,128)S(1)} custom-call(s32[1,128]{1,0:T(1,128)S(1)} %bitcast.4, f32[16,1024]{1,0:T(8,128)S(1)} %get-tuple-element.14.refs_0_, f32[48,1024]{1,0:T(8,128)S(1)} %collective-permute-done.5.refs_1_, f32[16,1024]{1,0:T(8,128)S(1)} %collective-permute-done.6.refs_2_, f32[16,1024]{1,0:T(8,128)S(1)} %collective-permute-done.7.refs_3_, ...), custom_call_target="tpu_custom_call" | custom-call | flops 50331648 | bytes 524288 | tf_op jit(solution)/shard_map/pallas_call | solution.py:232
  30.1 0.1 collective-permute-start.8
  30.2 1.2 %collective-permute-done.8 = f32[64,128]{1,0:T(8,128)S(1)} collective-permute-done((f32[64,128]{1,0:T(8,128)S(1)}, f32[64,128]{1,0:T(8,128)S(1)}, u32[]{:S(2)}, u32[]{:S(2)}) %collective-permute-start.8) | collective-permute-done | bytes 32800 | tf_op jit(solution)/shard_map/ppermute | solution.py:259
  31.4 0.5 %collective-permute-start.9 = (f32[64,128]{1,0:T(8,128)S(1)}, f32[64,128]{1,0:T(8,128)S(1)}, u32[]{:S(2)}, u32[]{:S(2)}) collective-permute-start(f32[64,128]{1,0:T(8,128)S(1)} %add.18), channel_id=1, source_target_pairs={{0,2},{1,3},{2,0},{3,1},{4,6},{5,7},{6,4},{7,5},{8,10},{9,11},{10,... | collective-permute-start | bytes 98312 | tf_op jit(solution)/shard_map/ppermute | solution.py:259
  32.0 0.7 %shard_map.98 = f32[64,1024]{1,0:T(8,128)} custom-call(f32[16,1024]{1,0:T(8,128)S(1)} %get-tuple-element.14.refs_0_, f32[48,1024]{1,0:T(8,128)S(1)} %collective-permute-done.5.refs_1_, f32[16,1024]{1,0:T(8,128)S(1)} %collective-permute-done.6.refs_2_, f32[16,1024]{1,0:T(8,128)S(1)} %collective-permute-done.7.refs_3_), custom_call_target="tpu_custom_call" | custom-call | bytes 524288 | tf_op jit(solution)/shard_map/pallas_call | solution.py:250
  32.7 2.6 %collective-permute-done.9 = f32[64,128]{1,0:T(8,128)S(1)} collective-permute-done((f32[64,128]{1,0:T(8,128)S(1)}, f32[64,128]{1,0:T(8,128)S(1)}, u32[]{:S(2)}, u32[]{:S(2)}) %collective-permute-start.9) | collective-permute-done | bytes 32800 | tf_op jit(solution)/shard_map/ppermute | solution.py:259
  35.3 0.6 %add_multiply_fusion = f32[64,128]{1,0:T(8,128)} fusion(f32[64,128]{1,0:T(8,128)S(1)} %add.18, f32[64,128]{1,0:T(8,128)S(1)} %collective-permute-done.9), kind=kLoop, calls=%fused_computation.2 | loop fusion | flops 16384 | bytes 98304 | tf_op jit(solution)/shard_map/mul | solution.py:319
  (11 shorter events, 0.1 us)
Async XLA Ops:
  0.6 8.6 %copy-start = (f32[32,1024]{1,0:T(8,128)S(1)}, f32[32,1024]{1,0:T(8,128)}, u32[]{:S(2)}) copy-start(f32[32,1024]{1,0:T(8,128)} %refs_4_.1) | copy-start | bytes 393220
  0.6 29.0 %copy-start.1 = (s32[128]{0:T(128)S(1)}, s32[128]{0:T(128)}, u32[]{:S(2)}) copy-start(s32[128]{0:T(128)} %param.15) | copy-start | bytes 1540
  4.8 1.5 %collective-permute-start = (f32[64,512]{1,0:T(8,128)S(1)}, f32[64,512]{1,0:T(8,128)S(1)}, u32[]{:S(2)}, u32[]{:S(2)}) collective-permute-start(f32[64,512]{1,0:T(8,128)S(1)} %get-tuple-element.12), channel_id=1, source_target_pairs={{0,1},{1,0},{2,3},{3,2},{4,5},{5,4},{6,7},{7,6},{8,9},{9,8},{10,11... | collective-permute-start | bytes 393224 | tf_op jit(solution)/shard_map/ppermute | solution.py:259
  6.3 7.1 %collective-permute-start.1 = (f32[48,512]{1,0:T(8,128)S(1)}, f32[48,512]{1,0:T(8,128)S(1)}, u32[]{:S(2)}, u32[]{:S(2)}) collective-permute-start(f32[48,512]{1,0:T(8,128)S(1)} %slice.21), channel_id=1, source_target_pairs={{0,2},{1,3},{2,0},{3,1},{4,6},{5,7},{6,4},{7,5},{8,10},{9,11},{10,... | collective-permute-start | bytes 294920 | tf_op jit(solution)/shard_map/ppermute | solution.py:259
  9.2 9.1 %collective-permute-start.3 = (f32[32,1024]{1,0:T(8,128)S(1)}, f32[32,1024]{1,0:T(8,128)S(1)}, u32[]{:S(2)}, u32[]{:S(2)}) collective-permute-start(f32[32,1024]{1,0:T(8,128)S(1)} %copy-done), channel_id=1, source_target_pairs={{0,8},{4,12},{8,0},{12,4},{1,9},{5,13},{9,1},{13,5},{2,10},{6,14},... | collective-permute-start | bytes 393224 | tf_op jit(solution)/shard_map/ppermute | solution.py:259
  11.8 6.7 %collective-permute-start.4 = (f32[32,1024]{1,0:T(8,128)S(1)}, f32[32,1024]{1,0:T(8,128)S(1)}, u32[]{:S(2)}, u32[]{:S(2)}) collective-permute-start(f32[32,1024]{1,0:T(8,128)S(1)} %copy-done), channel_id=1, source_target_pairs={{0,4},{4,0},{8,12},{12,8},{1,5},{5,1},{9,13},{13,9},{2,6},{6,2},{1... | collective-permute-start | bytes 393224 | tf_op jit(solution)/shard_map/ppermute | solution.py:259
  13.4 1.3 %collective-permute-start.2 = (f32[32,512]{1,0:T(8,128)S(1)}, f32[32,512]{1,0:T(8,128)S(1)}, u32[]{:S(2)}, u32[]{:S(2)}) collective-permute-start(f32[32,512]{1,0:T(8,128)S(1)} %slice_add_fusion.x_ref), channel_id=1, source_target_pairs={{0,1},{1,0},{2,3},{3,2},{4,5},{5,4},{6,7},{7,6},{8,9},{9,8},{10,11... | collective-permute-start | bytes 196616 | tf_op jit(solution)/shard_map/ppermute | solution.py:259
  18.5 11.2 %collective-permute-start.5 = (f32[48,1024]{1,0:T(8,128)S(1)}, f32[48,1024]{1,0:T(8,128)S(1)}, u32[]{:S(2)}, u32[]{:S(2)}) collective-permute-start(f32[48,1024]{1,0:T(8,128)S(1)} %get-tuple-element.16), channel_id=1, source_target_pairs={{0,4},{4,0},{8,12},{12,8},{1,5},{5,1},{9,13},{13,9},{2,6},{6,2},{1... | collective-permute-start | bytes 589832 | tf_op jit(solution)/shard_map/ppermute | solution.py:259
  20.0 5.7 %collective-permute-start.6 = (f32[16,1024]{1,0:T(8,128)S(1)}, f32[16,1024]{1,0:T(8,128)S(1)}, u32[]{:S(2)}, u32[]{:S(2)}) collective-permute-start(f32[16,1024]{1,0:T(8,128)S(1)} %get-tuple-element.17), channel_id=1, source_target_pairs={{0,8},{4,12},{8,0},{12,4},{1,9},{5,13},{9,1},{13,5},{2,10},{6,14},... | collective-permute-start | bytes 196616 | tf_op jit(solution)/shard_map/ppermute | solution.py:259
  22.4 7.3 %collective-permute-start.7 = (f32[16,1024]{1,0:T(8,128)S(1)}, f32[16,1024]{1,0:T(8,128)S(1)}, u32[]{:S(2)}, u32[]{:S(2)}) collective-permute-start(f32[16,1024]{1,0:T(8,128)S(1)} %get-tuple-element.18), channel_id=1, source_target_pairs={{0,12},{4,8},{8,4},{12,0},{1,13},{5,9},{9,5},{13,1},{2,14},{6,10},... | collective-permute-start | bytes 196616 | tf_op jit(solution)/shard_map/ppermute | solution.py:259
  30.1 1.3 %collective-permute-start.8 = (f32[64,128]{1,0:T(8,128)S(1)}, f32[64,128]{1,0:T(8,128)S(1)}, u32[]{:S(2)}, u32[]{:S(2)}) collective-permute-start(f32[64,128]{1,0:T(8,128)S(1)} %shard_map.99), channel_id=1, source_target_pairs={{0,1},{1,0},{2,3},{3,2},{4,5},{5,4},{6,7},{7,6},{8,9},{9,8},{10,11... | collective-permute-start | bytes 98312 | tf_op jit(solution)/shard_map/ppermute | solution.py:259
  31.4 3.9 %collective-permute-start.9 = (f32[64,128]{1,0:T(8,128)S(1)}, f32[64,128]{1,0:T(8,128)S(1)}, u32[]{:S(2)}, u32[]{:S(2)}) collective-permute-start(f32[64,128]{1,0:T(8,128)S(1)} %add.18), channel_id=1, source_target_pairs={{0,2},{1,3},{2,0},{3,1},{4,6},{5,7},{6,4},{7,5},{8,10},{9,11},{10,... | collective-permute-start | bytes 98312 | tf_op jit(solution)/shard_map/ppermute | solution.py:259

commit v4 on v3

--- a/solution.py
+++ b/solution.py
@@ -79,7 +79,7 @@
     parity = lax.rem(me, 2)
     in_copy.wait()
     act_copy.wait()
-    x_t = mm(act[...], proj_in[...], NT).T
+    x_t = mm(proj_in[...], act[...], NT)
     keep_ref[:half, :] = jnp.where(parity == 0, x_t[:half], x_t[half:])
     send_ref[:half, :] = jnp.where(parity == 0, x_t[half:], x_t[:half])
     len_copy.wait()
@@ -91,9 +91,9 @@
     total = None
     for c, copy in zip(chunks, grad_copies):
         copy.wait()
-        term = mm(grad[:, c], proj_out[:, c], NT)
+        term = mm(proj_out[:, c], grad[:, c], NT)
         total = term if total is None else total + term
-    turned[...] = total.T
+    turned[...] = total
     spot = half
     for apart in range(rank // width - 2, -1, -2):
         for ref, who in ((keep_ref, me ^ apart), (send_ref, me ^ (apart ^ 1))):

time: 36.1 us -> 35.9 us (level)
  no operation moved by 1% of the time
where the time goes in v4:
time: 35.9 us; the launch traced here: 35.8 us
  waiting for transfers between devices  15.7 us (44%)
  starting transfers between devices  12.7 us (35%)
  Pallas kernels  5.96 us (17%)
  between operations  0.72 us (2%)
  other arithmetic  0.66 us (2%)
    ppermute x10, waiting for transfers between devices, swap(): lax.ppermute(x, axis, [(i, i ^ gap) for i in range(lax.axis_size(axis))])  15.7 us
    ppermute x10, starting transfers between devices, swap(): lax.ppermute(x, axis, [(i, i ^ gap) for i in range(lax.axis_size(axis))])  12.7 us
    pallas_call x1, Pallas kernels, project(): pl.pallas_call(functools.partial(project_kernel, owners, relative, cap, w...  3.93 us
    pallas_call x1, Pallas kernels, outer(): pl.pallas_call(outer_kernel, out_shape=[jax.ShapeDtypeStruct((cap, width...  0.84 us
    pallas_call x1, Pallas kernels, place(): pl.pallas_call(place_kernel, out_shape=jax.ShapeDtypeStruct((slots, feats...  0.73 us
  transfers between devices with their start and end apart: 10, of which 8 were waited for; matrix products, arithmetic and copies ran while one was open for 0% of the time, Pallas kernels for 4%

profile of v4, /device:TPU:0, one launch (start us, length us, event | category | flops | bytes accessed | tf_op | source)
XLA Modules:
  0.0 35.8 jit_solution(5440644262855481303)
XLA Ops:
  0.7 3.9 %shard_map.95 = (f32[64,512]{1,0:T(8,128)S(1)}, f32[64,512]{1,0:T(8,128)S(1)}, f32[64,512]{1,0:T(8,128)S(1)}) custom-call(bf16[512,1024]{1,0:T(8,128)(2,1)} %act_hbm.1, bf16[512,3584]{1,0:T(8,128)(2,1)} %grad_hbm.1, bf16[64,1024]{1,0:T(8,128)(2,1)} %bitcast.6, bf16[64,3584]{1,0:T(8,128)(2,1)} %bitcast.5, s32[1,32]{1,0:T(1,128)} %len_hbm.1, s32[1,32]{1,0:T(1,128)} %bitcast.7), custom_call_target="tpu_custom_call" | custom-call | flops 301989888 | bytes 5308416 | tf_op jit(solution)/shard_map/pallas_call | solution.py:111
  4.6 0.5 %collective-permute-start = (f32[64,512]{1,0:T(8,128)S(1)}, f32[64,512]{1,0:T(8,128)S(1)}, u32[]{:S(2)}, u32[]{:S(2)}) collective-permute-start(f32[64,512]{1,0:T(8,128)S(1)} %get-tuple-element.12), channel_id=1, source_target_pairs={{0,1},{1,0},{2,3},{3,2},{4,5},{5,4},{6,7},{7,6},{8,9},{9,8},{10,11... | collective-permute-start | bytes 393224 | tf_op jit(solution)/shard_map/ppermute | solution.py:259
  5.1 1.0 %collective-permute-done = f32[64,512]{1,0:T(8,128)S(1)} collective-permute-done((f32[64,512]{1,0:T(8,128)S(1)}, f32[64,512]{1,0:T(8,128)S(1)}, u32[]{:S(2)}, u32[]{:S(2)}) %collective-permute-start) | collective-permute-done | bytes 131104 | tf_op jit(solution)/shard_map/ppermute | solution.py:259
  6.1 2.9 %collective-permute-start.1 = (f32[48,512]{1,0:T(8,128)S(1)}, f32[48,512]{1,0:T(8,128)S(1)}, u32[]{:S(2)}, u32[]{:S(2)}) collective-permute-start(f32[48,512]{1,0:T(8,128)S(1)} %slice.21), channel_id=1, source_target_pairs={{0,2},{1,3},{2,0},{3,1},{4,6},{5,7},{6,4},{7,5},{8,10},{9,11},{10,... | collective-permute-start | bytes 294920 | tf_op jit(solution)/shard_map/ppermute | solution.py:259
  9.1 2.6 %collective-permute-start.3 = (f32[32,1024]{1,0:T(8,128)S(1)}, f32[32,1024]{1,0:T(8,128)S(1)}, u32[]{:S(2)}, u32[]{:S(2)}) collective-permute-start(f32[32,1024]{1,0:T(8,128)S(1)} %copy-done), channel_id=1, source_target_pairs={{0,8},{4,12},{8,0},{12,4},{1,9},{5,13},{9,1},{13,5},{2,10},{6,14},... | collective-permute-start | bytes 393224 | tf_op jit(solution)/shard_map/ppermute | solution.py:259
  11.6 1.6 %collective-permute-start.4 = (f32[32,1024]{1,0:T(8,128)S(1)}, f32[32,1024]{1,0:T(8,128)S(1)}, u32[]{:S(2)}, u32[]{:S(2)}) collective-permute-start(f32[32,1024]{1,0:T(8,128)S(1)} %copy-done), channel_id=1, source_target_pairs={{0,4},{4,0},{8,12},{12,8},{1,5},{5,1},{9,13},{13,9},{2,6},{6,2},{1... | collective-permute-start | bytes 393224 | tf_op jit(solution)/shard_map/ppermute | solution.py:259
  13.2 0.0 collective-permute-done.1
  13.2 0.1 collective-permute-start.2
  13.3 1.2 %collective-permute-done.2.x_other_ref = f32[32,512]{1,0:T(8,128)S(1)} collective-permute-done((f32[32,512]{1,0:T(8,128)S(1)}, f32[32,512]{1,0:T(8,128)S(1)}, u32[]{:S(2)}, u32[]{:S(2)}) %collective-permute-start.2) | collective-permute-done | bytes 65568 | tf_op jit(solution)/shard_map/ppermute | solution.py:259
  14.6 0.8 %shard_map.96 = (f32[16,1024]{1,0:T(8,128)S(1)}, f32[16,1024]{1,0:T(8,128)S(1)}, f32[16,1024]{1,0:T(8,128)S(1)}, f32[16,1024]{1,0:T(8,128)S(1)}) custom-call(f32[32,512]{1,0:T(8,128)S(1)} %slice_add_fusion.x_ref, f32[32,512]{1,0:T(8,128)S(1)} %collective-permute-done.2.x_other_ref, f32[16,512]{1,0:T(8,128)S(1)} %slice_add_fusion.1.g_ref, ...), custom_call_target="tpu_custom_call" | custom-call | tf_op jit(solution)/shard_map/pallas_call | solution.py:165
  15.4 2.7 %collective-permute-done.3.refs_0_.refs_5_ = f32[32,1024]{1,0:T(8,128)S(1)} collective-permute-done((f32[32,1024]{1,0:T(8,128)S(1)}, f32[32,1024]{1,0:T(8,128)S(1)}, u32[]{:S(2)}, u32[]{:S(2)}) %collective-permute-start.3) | collective-permute-done | bytes 131104 | tf_op jit(solution)/shard_map/ppermute | solution.py:259
  18.1 0.2 collective-permute-done.4.refs_1_
  18.3 1.5 %collective-permute-start.5 = (f32[48,1024]{1,0:T(8,128)S(1)}, f32[48,1024]{1,0:T(8,128)S(1)}, u32[]{:S(2)}, u32[]{:S(2)}) collective-permute-start(f32[48,1024]{1,0:T(8,128)S(1)} %get-tuple-element.16), channel_id=1, source_target_pairs={{0,4},{4,0},{8,12},{12,8},{1,5},{5,1},{9,13},{13,9},{2,6},{6,2},{1... | collective-permute-start | bytes 589832 | tf_op jit(solution)/shard_map/ppermute | solution.py:259
  19.8 2.4 %collective-permute-start.6 = (f32[16,1024]{1,0:T(8,128)S(1)}, f32[16,1024]{1,0:T(8,128)S(1)}, u32[]{:S(2)}, u32[]{:S(2)}) collective-permute-start(f32[16,1024]{1,0:T(8,128)S(1)} %get-tuple-element.17), channel_id=1, source_target_pairs={{0,8},{4,12},{8,0},{12,4},{1,9},{5,13},{9,1},{13,5},{2,10},{6,14},... | collective-permute-start | bytes 196616 | tf_op jit(solution)/shard_map/ppermute | solution.py:259
  22.2 0.6 %collective-permute-start.7 = (f32[16,1024]{1,0:T(8,128)S(1)}, f32[16,1024]{1,0:T(8,128)S(1)}, u32[]{:S(2)}, u32[]{:S(2)}) collective-permute-start(f32[16,1024]{1,0:T(8,128)S(1)} %get-tuple-element.18), channel_id=1, source_target_pairs={{0,12},{4,8},{8,4},{12,0},{1,13},{5,9},{9,5},{13,1},{2,14},{6,10},... | collective-permute-start | bytes 196616 | tf_op jit(solution)/shard_map/ppermute | solution.py:259
  22.8 2.7 %collective-permute-done.6.refs_2_ = f32[16,1024]{1,0:T(8,128)S(1)} collective-permute-done((f32[16,1024]{1,0:T(8,128)S(1)}, f32[16,1024]{1,0:T(8,128)S(1)}, u32[]{:S(2)}, u32[]{:S(2)}) %collective-permute-start.6) | collective-permute-done | bytes 65568 | tf_op jit(solution)/shard_map/ppermute | solution.py:259
  25.5 4.0 %collective-permute-done.7.refs_3_ = f32[16,1024]{1,0:T(8,128)S(1)} collective-permute-done((f32[16,1024]{1,0:T(8,128)S(1)}, f32[16,1024]{1,0:T(8,128)S(1)}, u32[]{:S(2)}, u32[]{:S(2)}) %collective-permute-start.7) | collective-permute-done | bytes 65568 | tf_op jit(solution)/shard_map/ppermute | solution.py:259
  29.5 0.4 %shard_map.99 = f32[64,128]{1,0:T(8,128)S(1)} custom-call(s32[1,128]{1,0:T(1,128)S(1)} %bitcast.4, f32[16,1024]{1,0:T(8,128)S(1)} %get-tuple-element.14.refs_0_, f32[48,1024]{1,0:T(8,128)S(1)} %collective-permute-done.5.refs_1_, f32[16,1024]{1,0:T(8,128)S(1)} %collective-permute-done.6.refs_2_, f32[16,1024]{1,0:T(8,128)S(1)} %collective-permute-done.7.refs_3_, ...), custom_call_target="tpu_custom_call" | custom-call | flops 50331648 | bytes 524288 | tf_op jit(solution)/shard_map/pallas_call | solution.py:232
  30.0 0.1 collective-permute-start.8
  30.0 1.2 %collective-permute-done.8 = f32[64,128]{1,0:T(8,128)S(1)} collective-permute-done((f32[64,128]{1,0:T(8,128)S(1)}, f32[64,128]{1,0:T(8,128)S(1)}, u32[]{:S(2)}, u32[]{:S(2)}) %collective-permute-start.8) | collective-permute-done | bytes 32800 | tf_op jit(solution)/shard_map/ppermute | solution.py:259
  31.2 0.5 %collective-permute-start.9 = (f32[64,128]{1,0:T(8,128)S(1)}, f32[64,128]{1,0:T(8,128)S(1)}, u32[]{:S(2)}, u32[]{:S(2)}) collective-permute-start(f32[64,128]{1,0:T(8,128)S(1)} %add.18), channel_id=1, source_target_pairs={{0,2},{1,3},{2,0},{3,1},{4,6},{5,7},{6,4},{7,5},{8,10},{9,11},{10,... | collective-permute-start | bytes 98312 | tf_op jit(solution)/shard_map/ppermute | solution.py:259
  31.8 0.7 %shard_map.98 = f32[64,1024]{1,0:T(8,128)} custom-call(f32[16,1024]{1,0:T(8,128)S(1)} %get-tuple-element.14.refs_0_, f32[48,1024]{1,0:T(8,128)S(1)} %collective-permute-done.5.refs_1_, f32[16,1024]{1,0:T(8,128)S(1)} %collective-permute-done.6.refs_2_, f32[16,1024]{1,0:T(8,128)S(1)} %collective-permute-done.7.refs_3_), custom_call_target="tpu_custom_call" | custom-call | bytes 524288 | tf_op jit(solution)/shard_map/pallas_call | solution.py:250
  32.5 2.7 %collective-permute-done.9 = f32[64,128]{1,0:T(8,128)S(1)} collective-permute-done((f32[64,128]{1,0:T(8,128)S(1)}, f32[64,128]{1,0:T(8,128)S(1)}, u32[]{:S(2)}, u32[]{:S(2)}) %collective-permute-start.9) | collective-permute-done | bytes 32800 | tf_op jit(solution)/shard_map/ppermute | solution.py:259
  35.2 0.6 %add_multiply_fusion = f32[64,128]{1,0:T(8,128)} fusion(f32[64,128]{1,0:T(8,128)S(1)} %add.18, f32[64,128]{1,0:T(8,128)S(1)} %collective-permute-done.9), kind=kLoop, calls=%fused_computation.2 | loop fusion | flops 16384 | bytes 98304 | tf_op jit(solution)/shard_map/mul | solution.py:319
  (11 shorter events, 0.1 us)
Async XLA Ops:
  0.6 8.4 %copy-start = (f32[32,1024]{1,0:T(8,128)S(1)}, f32[32,1024]{1,0:T(8,128)}, u32[]{:S(2)}) copy-start(f32[32,1024]{1,0:T(8,128)} %refs_4_.1) | copy-start | bytes 393220
  0.6 28.9 %copy-start.1 = (s32[128]{0:T(128)S(1)}, s32[128]{0:T(128)}, u32[]{:S(2)}) copy-start(s32[128]{0:T(128)} %param.15) | copy-start | bytes 1540
  4.6 1.5 %collective-permute-start = (f32[64,512]{1,0:T(8,128)S(1)}, f32[64,512]{1,0:T(8,128)S(1)}, u32[]{:S(2)}, u32[]{:S(2)}) collective-permute-start(f32[64,512]{1,0:T(8,128)S(1)} %get-tuple-element.12), channel_id=1, source_target_pairs={{0,1},{1,0},{2,3},{3,2},{4,5},{5,4},{6,7},{7,6},{8,9},{9,8},{10,11... | collective-permute-start | bytes 393224 | tf_op jit(solution)/shard_map/ppermute | solution.py:259
  6.1 7.1 %collective-permute-start.1 = (f32[48,512]{1,0:T(8,128)S(1)}, f32[48,512]{1,0:T(8,128)S(1)}, u32[]{:S(2)}, u32[]{:S(2)}) collective-permute-start(f32[48,512]{1,0:T(8,128)S(1)} %slice.21), channel_id=1, source_target_pairs={{0,2},{1,3},{2,0},{3,1},{4,6},{5,7},{6,4},{7,5},{8,10},{9,11},{10,... | collective-permute-start | bytes 294920 | tf_op jit(solution)/shard_map/ppermute | solution.py:259
  9.1 9.1 %collective-permute-start.3 = (f32[32,1024]{1,0:T(8,128)S(1)}, f32[32,1024]{1,0:T(8,128)S(1)}, u32[]{:S(2)}, u32[]{:S(2)}) collective-permute-start(f32[32,1024]{1,0:T(8,128)S(1)} %copy-done), channel_id=1, source_target_pairs={{0,8},{4,12},{8,0},{12,4},{1,9},{5,13},{9,1},{13,5},{2,10},{6,14},... | collective-permute-start | bytes 393224 | tf_op jit(solution)/shard_map/ppermute | solution.py:259
  11.6 6.7 %collective-permute-start.4 = (f32[32,1024]{1,0:T(8,128)S(1)}, f32[32,1024]{1,0:T(8,128)S(1)}, u32[]{:S(2)}, u32[]{:S(2)}) collective-permute-start(f32[32,1024]{1,0:T(8,128)S(1)} %copy-done), channel_id=1, source_target_pairs={{0,4},{4,0},{8,12},{12,8},{1,5},{5,1},{9,13},{13,9},{2,6},{6,2},{1... | collective-permute-start | bytes 393224 | tf_op jit(solution)/shard_map/ppermute | solution.py:259
  13.2 1.3 %collective-permute-start.2 = (f32[32,512]{1,0:T(8,128)S(1)}, f32[32,512]{1,0:T(8,128)S(1)}, u32[]{:S(2)}, u32[]{:S(2)}) collective-permute-start(f32[32,512]{1,0:T(8,128)S(1)} %slice_add_fusion.x_ref), channel_id=1, source_target_pairs={{0,1},{1,0},{2,3},{3,2},{4,5},{5,4},{6,7},{7,6},{8,9},{9,8},{10,11... | collective-permute-start | bytes 196616 | tf_op jit(solution)/shard_map/ppermute | solution.py:259
  18.3 11.2 %collective-permute-start.5 = (f32[48,1024]{1,0:T(8,128)S(1)}, f32[48,1024]{1,0:T(8,128)S(1)}, u32[]{:S(2)}, u32[]{:S(2)}) collective-permute-start(f32[48,1024]{1,0:T(8,128)S(1)} %get-tuple-element.16), channel_id=1, source_target_pairs={{0,4},{4,0},{8,12},{12,8},{1,5},{5,1},{9,13},{13,9},{2,6},{6,2},{1... | collective-permute-start | bytes 589832 | tf_op jit(solution)/shard_map/ppermute | solution.py:259
  19.8 5.7 %collective-permute-start.6 = (f32[16,1024]{1,0:T(8,128)S(1)}, f32[16,1024]{1,0:T(8,128)S(1)}, u32[]{:S(2)}, u32[]{:S(2)}) collective-permute-start(f32[16,1024]{1,0:T(8,128)S(1)} %get-tuple-element.17), channel_id=1, source_target_pairs={{0,8},{4,12},{8,0},{12,4},{1,9},{5,13},{9,1},{13,5},{2,10},{6,14},... | collective-permute-start | bytes 196616 | tf_op jit(solution)/shard_map/ppermute | solution.py:259
  22.2 7.3 %collective-permute-start.7 = (f32[16,1024]{1,0:T(8,128)S(1)}, f32[16,1024]{1,0:T(8,128)S(1)}, u32[]{:S(2)}, u32[]{:S(2)}) collective-permute-start(f32[16,1024]{1,0:T(8,128)S(1)} %get-tuple-element.18), channel_id=1, source_target_pairs={{0,12},{4,8},{8,4},{12,0},{1,13},{5,9},{9,5},{13,1},{2,14},{6,10},... | collective-permute-start | bytes 196616 | tf_op jit(solution)/shard_map/ppermute | solution.py:259
  30.0 1.3 %collective-permute-start.8 = (f32[64,128]{1,0:T(8,128)S(1)}, f32[64,128]{1,0:T(8,128)S(1)}, u32[]{:S(2)}, u32[]{:S(2)}) collective-permute-start(f32[64,128]{1,0:T(8,128)S(1)} %shard_map.99), channel_id=1, source_target_pairs={{0,1},{1,0},{2,3},{3,2},{4,5},{5,4},{6,7},{7,6},{8,9},{9,8},{10,11... | collective-permute-start | bytes 98312 | tf_op jit(solution)/shard_map/ppermute | solution.py:259
  31.2 3.9 %collective-permute-start.9 = (f32[64,128]{1,0:T(8,128)S(1)}, f32[64,128]{1,0:T(8,128)S(1)}, u32[]{:S(2)}, u32[]{:S(2)}) collective-permute-start(f32[64,128]{1,0:T(8,128)S(1)} %add.18), channel_id=1, source_target_pairs={{0,2},{1,3},{2,0},{3,1},{4,6},{5,7},{6,4},{7,5},{8,10},{9,11},{10,... | collective-permute-start | bytes 98312 | tf_op jit(solution)/shard_map/ppermute | solution.py:259

commit v5 on v4

--- a/solution.py
+++ b/solution.py
@@ -124,7 +124,7 @@
             pltpu.SemaphoreType.DMA((5 + CHUNKS,)),
         ],
         compiler_params=params(24),
-        cost_estimate=cost(2 * tokens * depth * rank, 2 * depth * (tokens + rank)),
+        cost_estimate=cost(0, 0),
     )(
         *(
             pltpu.with_memory_space_constraint(x, pltpu.HBM)
@@ -133,7 +133,48 @@
     )
 
 
-def outer_kernel(x_ref, x_other_ref, g_ref, mask_ref, *blocks):
+def fold_kernel(keeps, gots, low, high, cuts, *refs):
+    kept = jnp.concatenate([r[...] for r in refs[:keeps]], axis=0)
+    got = jnp.concatenate([r[...] for r in refs[keeps : keeps + gots]], axis=0)
+    if low < high:
+        kept = jnp.concatenate([kept[:low], kept[high:]], axis=0)
+    total = kept + got
+    for first, last, out in zip(cuts, cuts[1:], refs[keeps + gots :]):
+        out[...] = total[first:last]
+
+
+def fold(keeps, gots, low, high, cuts):
+    tokens = keeps[0].shape[1]
+    return list(
+        pl.pallas_call(
+            functools.partial(fold_kernel, len(keeps), len(gots), low, high, tuple(cuts)),
+            out_shape=[
+                jax.ShapeDtypeStruct((last - first, tokens), F32)
+                for first, last in zip(cuts, cuts[1:])
+            ],
+            compiler_params=params(16),
+            cost_estimate=cost(0, 0),
+        )(*keeps, *gots)
+    )
+
+
+def sum_tensor(keep, send, half, width):
+    rows = keep.shape[0]
+    bit = lax.axis_size("tensor")
+    low, high = rows, rows
+    keeps, gots = [keep], [swap(send, "tensor", 1)]
+    while bit > 2:
+        bit //= 2
+        cut = half + (rows - half) // 2
+        parts = fold(keeps, gots, low, high, [0, cut // 16 * 8, cut, rows])
+        gots = [swap(p, "tensor", bit) for p in parts[:2]]
+        keeps, low, high = parts, half, cut
+        rows -= cut - half
+    return fold(keeps, gots, low, high, [0, half, half + width])
+
+
+def outer_kernel(owners, x_ref, x_other_ref, g_ref, mask_ref, *refs):
+    blocks = refs[-owners:]
     width = g_ref.shape[0]
     rank = 2 * x_ref.shape[0]
     odd = lax.rem(lax.axis_index("tensor"), 2) == 1
@@ -158,16 +199,18 @@
             block[:, i * rank : (i + step) * rank] = columns[k * cap : (k + 1) * cap, :]
 
 
-def outer(x_half, x_other, g_t, mask, owners):
+def outer(x_half, x_other, g_t, mask, owners, pieces):
     slots, tokens = mask.shape
     width, rank = g_t.shape[0], 2 * x_half.shape[0]
     cap = slots // owners
     return pl.pallas_call(
-        outer_kernel,
+        functools.partial(outer_kernel, owners),
+        in_specs=[pl.BlockSpec(memory_space=pltpu.VMEM)] * 4
+        + [pl.BlockSpec(memory_space=pl.ANY)] * len(pieces),
         out_shape=[jax.ShapeDtypeStruct((cap, width * rank), F32)] * owners,
         compiler_params=params(24),
-        cost_estimate=cost(0, 0),
-    )(x_half, x_other, g_t, mask)
+        cost_estimate=cost(8 * slots * width * tokens * rank, 4 * slots * width * rank),
+    )(x_half, x_other, g_t, mask, *pieces)
 
 
 def join_kernel(block_ref, *refs):
@@ -291,16 +334,9 @@
         activations, out_grads, proj_in.T, proj_out.T, doc_lengths, doc_owner.T,
         data_size, cap, width, direct,
     )
-    part = keep + swap(send, "tensor", 1)
-    bit = tensor_size // 2
-    while bit > 1:
-        cut = half + (part.shape[0] - half) // 2
-        got = swap(part[:cut], "tensor", bit)
-        part = jnp.concatenate([part[:half] + got[:half], part[cut:] + got[half:]], axis=0)
-        bit //= 2
-    x_half, g_mine = part[:half], part[half:]
+    x_half, g_mine = sum_tensor(keep, send, half, width)
     x_other = swap(x_half, "tensor", 1)
-    blocks = outer(x_half, x_other, g_mine, mask, data_size)
+    blocks = outer(x_half, x_other, g_mine, mask, data_size, pieces[1:])
     if direct:
         joined, mate = join(blocks[1], pieces[1:], mate)
         near = swap(joined, "dp", 1)

time: 35.9 us -> 34.6 us (0.964)
  waiting for transfers between devices: 15.7 us -> 13.2 us
  starting transfers between devices: 12.7 us -> 13.9 us
    ppermute x10 -> x11, waiting for transfers between devices: 15.7 us -> 13.2 us  [swap(): lax.ppermute(x, axis, [(i, i ^ gap) for i in range(lax.axis_size(axis))])]
    ppermute x10 -> x11, starting transfers between devices: 12.7 us -> 13.9 us  [swap(): lax.ppermute(x, axis, [(i, i ^ gap) for i in range(lax.axis_size(axis))])]
    pallas_call x1 -> x3, Pallas kernels: 0.84 us -> 0.87 us  [the longest x1 0.85 us: outer(): pl.pallas_call(functools.partial(outer_kernel, owners), in_specs=[pl.Bloc...]
  transfers between devices with their start and end apart: 10 -> 11, of which waited for: 8 -> 8; matrix products, arithmetic and copies ran while one was open for 0% -> 0% of each run, Pallas kernels for 4% -> 5%
where the time goes in v5:
time: 34.6 us; the launch traced here: 34.4 us
  starting transfers between devices  13.9 us (40%)
  waiting for transfers between devices  13.2 us (38%)
  Pallas kernels  5.99 us (17%)
  between operations  0.71 us (2%)
  other arithmetic  0.63 us (2%)
    ppermute x11, starting transfers between devices, swap(): lax.ppermute(x, axis, [(i, i ^ gap) for i in range(lax.axis_size(axis))])  13.9 us
    ppermute x11, waiting for transfers between devices, swap(): lax.ppermute(x, axis, [(i, i ^ gap) for i in range(lax.axis_size(axis))])  13.2 us
    pallas_call x1, Pallas kernels, project(): pl.pallas_call(functools.partial(project_kernel, owners, relative, cap, w...  3.93 us
    pallas_call x1, Pallas kernels, outer(): pl.pallas_call(functools.partial(outer_kernel, owners), in_specs=[pl.Bloc...  0.85 us
    pallas_call x1, Pallas kernels, place(): pl.pallas_call(place_kernel, out_shape=jax.ShapeDtypeStruct((slots, feats...  0.73 us
  transfers between devices with their start and end apart: 11, of which 8 were waited for; matrix products, arithmetic and copies ran while one was open for 0% of the time, Pallas kernels for 5%

profile of v5, /device:TPU:0, one launch (start us, length us, event | category | flops | bytes accessed | tf_op | source)
XLA Modules:
  0.0 34.4 jit_solution(1505895243780486000)
XLA Ops:
  0.7 3.9 %shard_map.95 = (f32[64,512]{1,0:T(8,128)S(1)}, f32[64,512]{1,0:T(8,128)S(1)}, f32[64,512]{1,0:T(8,128)S(1)}) custom-call(bf16[512,1024]{1,0:T(8,128)(2,1)} %act_hbm.1, bf16[512,3584]{1,0:T(8,128)(2,1)} %grad_hbm.1, bf16[64,1024]{1,0:T(8,128)(2,1)} %bitcast.6, bf16[64,3584]{1,0:T(8,128)(2,1)} %bitcast.5, s32[1,32]{1,0:T(1,128)} %len_hbm.1, s32[1,32]{1,0:T(1,128)} %bitcast.7), custom_call_target="tpu_custom_call" | custom-call | tf_op jit(solution)/shard_map/pallas_call | solution.py:111
  4.6 0.5 %collective-permute-start = (f32[64,512]{1,0:T(8,128)S(1)}, f32[64,512]{1,0:T(8,128)S(1)}, u32[]{:S(2)}, u32[]{:S(2)}) collective-permute-start(f32[64,512]{1,0:T(8,128)S(1)} %get-tuple-element.17), channel_id=1, source_target_pairs={{0,1},{1,0},{2,3},{3,2},{4,5},{5,4},{6,7},{7,6},{8,9},{9,8},{10,11... | collective-permute-start | bytes 393224 | tf_op jit(solution)/shard_map/ppermute | solution.py:302
  5.1 3.7 %collective-permute-start.4 = (f32[32,1024]{1,0:T(8,128)S(1)}, f32[32,1024]{1,0:T(8,128)S(1)}, u32[]{:S(2)}, u32[]{:S(2)}) collective-permute-start(f32[32,1024]{1,0:T(8,128)S(1)} %copy-done), channel_id=1, source_target_pairs={{0,8},{4,12},{8,0},{12,4},{1,9},{5,13},{9,1},{13,5},{2,10},{6,14},... | collective-permute-start | bytes 393224 | tf_op jit(solution)/shard_map/ppermute | solution.py:302
  8.8 1.6 %collective-permute-start.1 = (f32[24,512]{1,0:T(8,128)S(1)}, f32[24,512]{1,0:T(8,128)S(1)}, u32[]{:S(2)}, u32[]{:S(2)}) collective-permute-start(f32[24,512]{1,0:T(8,128)S(1)} %get-tuple-element.18.refs_0_), channel_id=1, source_target_pairs={{0,2},{1,3},{2,0},{3,1},{4,6},{5,7},{6,4},{7,5},{8,10},{9,11},{10,... | collective-permute-start | bytes 147464 | tf_op jit(solution)/shard_map/ppermute | solution.py:302
  10.4 0.5 %collective-permute-start.2 = (f32[24,512]{1,0:T(8,128)S(1)}, f32[24,512]{1,0:T(8,128)S(1)}, u32[]{:S(2)}, u32[]{:S(2)}) collective-permute-start(f32[24,512]{1,0:T(8,128)S(1)} %get-tuple-element.19.refs_1_), channel_id=1, source_target_pairs={{0,2},{1,3},{2,0},{3,1},{4,6},{5,7},{6,4},{7,5},{8,10},{9,11},{10,... | collective-permute-start | bytes 147464 | tf_op jit(solution)/shard_map/ppermute | solution.py:302
  10.9 1.6 %collective-permute-start.5 = (f32[32,1024]{1,0:T(8,128)S(1)}, f32[32,1024]{1,0:T(8,128)S(1)}, u32[]{:S(2)}, u32[]{:S(2)}) collective-permute-start(f32[32,1024]{1,0:T(8,128)S(1)} %copy-done), channel_id=1, source_target_pairs={{0,4},{4,0},{8,12},{12,8},{1,5},{5,1},{9,13},{13,9},{2,6},{6,2},{1... | collective-permute-start | bytes 393224 | tf_op jit(solution)/shard_map/ppermute | solution.py:302
  12.5 0.7 %collective-permute-done.1.refs_3_ = f32[24,512]{1,0:T(8,128)S(1)} collective-permute-done((f32[24,512]{1,0:T(8,128)S(1)}, f32[24,512]{1,0:T(8,128)S(1)}, u32[]{:S(2)}, u32[]{:S(2)}) %collective-permute-start.1) | collective-permute-done | bytes 49184 | tf_op jit(solution)/shard_map/ppermute | solution.py:302
  13.2 1.3 %collective-permute-done.2.refs_4_ = f32[24,512]{1,0:T(8,128)S(1)} collective-permute-done((f32[24,512]{1,0:T(8,128)S(1)}, f32[24,512]{1,0:T(8,128)S(1)}, u32[]{:S(2)}, u32[]{:S(2)}) %collective-permute-start.2) | collective-permute-done | bytes 49184 | tf_op jit(solution)/shard_map/ppermute | solution.py:302
  14.5 0.1 collective-permute-start.3
  14.5 1.2 %collective-permute-done.4.refs_0_.refs_5_ = f32[32,1024]{1,0:T(8,128)S(1)} collective-permute-done((f32[32,1024]{1,0:T(8,128)S(1)}, f32[32,1024]{1,0:T(8,128)S(1)}, u32[]{:S(2)}, u32[]{:S(2)}) %collective-permute-start.4) | collective-permute-done | bytes 131104 | tf_op jit(solution)/shard_map/ppermute | solution.py:302
  15.8 0.8 %shard_map.98 = (f32[16,1024]{1,0:T(8,128)S(1)}, f32[16,1024]{1,0:T(8,128)S(1)}, f32[16,1024]{1,0:T(8,128)S(1)}, f32[16,1024]{1,0:T(8,128)S(1)}) custom-call(f32[32,512]{1,0:T(8,128)S(1)} %get-tuple-element.21.x_ref, f32[32,512]{1,0:T(8,128)S(1)} %collective-permute-done.3.x_other_ref, f32[16,512]{1,0:T(8,128)S(1)} %get-tuple-element.22.g_ref, ...), custom_call_target="tpu_custom_call" | custom-call | flops 268435456 | bytes 262144 | tf_op jit(solution)/shard_map/pallas_call | solution.py:206
  16.6 0.9 %collective-permute-done.5.refs_1_ = f32[32,1024]{1,0:T(8,128)S(1)} collective-permute-done((f32[32,1024]{1,0:T(8,128)S(1)}, f32[32,1024]{1,0:T(8,128)S(1)}, u32[]{:S(2)}, u32[]{:S(2)}) %collective-permute-start.5) | collective-permute-done | bytes 131104 | tf_op jit(solution)/shard_map/ppermute | solution.py:302
  17.6 0.8 %collective-permute-start.6 = (f32[48,1024]{1,0:T(8,128)S(1)}, f32[48,1024]{1,0:T(8,128)S(1)}, u32[]{:S(2)}, u32[]{:S(2)}) collective-permute-start(f32[48,1024]{1,0:T(8,128)S(1)} %get-tuple-element.26), channel_id=1, source_target_pairs={{0,4},{4,0},{8,12},{12,8},{1,5},{5,1},{9,13},{13,9},{2,6},{6,2},{1... | collective-permute-start | bytes 589832 | tf_op jit(solution)/shard_map/ppermute | solution.py:302
  18.3 3.2 %collective-permute-start.7 = (f32[16,1024]{1,0:T(8,128)S(1)}, f32[16,1024]{1,0:T(8,128)S(1)}, u32[]{:S(2)}, u32[]{:S(2)}) collective-permute-start(f32[16,1024]{1,0:T(8,128)S(1)} %get-tuple-element.27), channel_id=1, source_target_pairs={{0,8},{4,12},{8,0},{12,4},{1,9},{5,13},{9,1},{13,5},{2,10},{6,14},... | collective-permute-start | bytes 196616 | tf_op jit(solution)/shard_map/ppermute | solution.py:302
  21.5 0.5 %collective-permute-start.8 = (f32[16,1024]{1,0:T(8,128)S(1)}, f32[16,1024]{1,0:T(8,128)S(1)}, u32[]{:S(2)}, u32[]{:S(2)}) collective-permute-start(f32[16,1024]{1,0:T(8,128)S(1)} %get-tuple-element.28), channel_id=1, source_target_pairs={{0,12},{4,8},{8,4},{12,0},{1,13},{5,9},{9,5},{13,1},{2,14},{6,10},... | collective-permute-start | bytes 196616 | tf_op jit(solution)/shard_map/ppermute | solution.py:302
  22.0 2.9 %collective-permute-done.7.refs_2_ = f32[16,1024]{1,0:T(8,128)S(1)} collective-permute-done((f32[16,1024]{1,0:T(8,128)S(1)}, f32[16,1024]{1,0:T(8,128)S(1)}, u32[]{:S(2)}, u32[]{:S(2)}) %collective-permute-start.7) | collective-permute-done | bytes 65568 | tf_op jit(solution)/shard_map/ppermute | solution.py:302
  24.9 3.3 %collective-permute-done.8.refs_3_ = f32[16,1024]{1,0:T(8,128)S(1)} collective-permute-done((f32[16,1024]{1,0:T(8,128)S(1)}, f32[16,1024]{1,0:T(8,128)S(1)}, u32[]{:S(2)}, u32[]{:S(2)}) %collective-permute-start.8) | collective-permute-done | bytes 65568 | tf_op jit(solution)/shard_map/ppermute | solution.py:302
  28.2 0.4 %shard_map.101 = f32[64,128]{1,0:T(8,128)S(1)} custom-call(s32[1,128]{1,0:T(1,128)S(1)} %bitcast.4, f32[16,1024]{1,0:T(8,128)S(1)} %get-tuple-element.24.refs_0_, f32[48,1024]{1,0:T(8,128)S(1)} %collective-permute-done.6.refs_1_, f32[16,1024]{1,0:T(8,128)S(1)} %collective-permute-done.7.refs_2_, f32[16,1024]{1,0:T(8,128)S(1)} %collective-permute-done.8.refs_3_, ...), custom_call_target="tpu_custom_call" | custom-call | flops 50331648 | bytes 524288 | tf_op jit(solution)/shard_map/pallas_call | solution.py:275
  28.6 0.1 collective-permute-start.9
  28.7 1.2 %collective-permute-done.9 = f32[64,128]{1,0:T(8,128)S(1)} collective-permute-done((f32[64,128]{1,0:T(8,128)S(1)}, f32[64,128]{1,0:T(8,128)S(1)}, u32[]{:S(2)}, u32[]{:S(2)}) %collective-permute-start.9) | collective-permute-done | bytes 32800 | tf_op jit(solution)/shard_map/ppermute | solution.py:302
  29.9 1.5 %collective-permute-start.10 = (f32[64,128]{1,0:T(8,128)S(1)}, f32[64,128]{1,0:T(8,128)S(1)}, u32[]{:S(2)}, u32[]{:S(2)}) collective-permute-start(f32[64,128]{1,0:T(8,128)S(1)} %add.6), channel_id=1, source_target_pairs={{0,2},{1,3},{2,0},{3,1},{4,6},{5,7},{6,4},{7,5},{8,10},{9,11},{10,... | collective-permute-start | bytes 98312 | tf_op jit(solution)/shard_map/ppermute | solution.py:302
  31.4 0.7 %shard_map.100 = f32[64,1024]{1,0:T(8,128)} custom-call(f32[16,1024]{1,0:T(8,128)S(1)} %get-tuple-element.24.refs_0_, f32[48,1024]{1,0:T(8,128)S(1)} %collective-permute-done.6.refs_1_, f32[16,1024]{1,0:T(8,128)S(1)} %collective-permute-done.7.refs_2_, f32[16,1024]{1,0:T(8,128)S(1)} %collective-permute-done.8.refs_3_), custom_call_target="tpu_custom_call" | custom-call | bytes 524288 | tf_op jit(solution)/shard_map/pallas_call | solution.py:293
  32.1 1.7 %collective-permute-done.10 = f32[64,128]{1,0:T(8,128)S(1)} collective-permute-done((f32[64,128]{1,0:T(8,128)S(1)}, f32[64,128]{1,0:T(8,128)S(1)}, u32[]{:S(2)}, u32[]{:S(2)}) %collective-permute-start.10) | collective-permute-done | bytes 32800 | tf_op jit(solution)/shard_map/ppermute | solution.py:302
  33.8 0.6 %add_multiply_fusion = f32[64,128]{1,0:T(8,128)} fusion(f32[64,128]{1,0:T(8,128)S(1)} %add.6, f32[64,128]{1,0:T(8,128)S(1)} %collective-permute-done.10), kind=kLoop, calls=%fused_computation | loop fusion | flops 16384 | bytes 98304 | tf_op jit(solution)/shard_map/mul | solution.py:355
  (11 shorter events, 0.1 us)
Async XLA Ops:
  0.6 4.5 %copy-start = (f32[32,1024]{1,0:T(8,128)S(1)}, f32[32,1024]{1,0:T(8,128)}, u32[]{:S(2)}) copy-start(f32[32,1024]{1,0:T(8,128)} %refs_4_.1) | copy-start | bytes 393220
  0.6 27.5 %copy-start.1 = (s32[128]{0:T(128)S(1)}, s32[128]{0:T(128)}, u32[]{:S(2)}) copy-start(s32[128]{0:T(128)} %param.15) | copy-start | bytes 1540
  4.6 4.2 %collective-permute-start = (f32[64,512]{1,0:T(8,128)S(1)}, f32[64,512]{1,0:T(8,128)S(1)}, u32[]{:S(2)}, u32[]{:S(2)}) collective-permute-start(f32[64,512]{1,0:T(8,128)S(1)} %get-tuple-element.17), channel_id=1, source_target_pairs={{0,1},{1,0},{2,3},{3,2},{4,5},{5,4},{6,7},{7,6},{8,9},{9,8},{10,11... | collective-permute-start | bytes 393224 | tf_op jit(solution)/shard_map/ppermute | solution.py:302
  5.1 10.7 %collective-permute-start.4 = (f32[32,1024]{1,0:T(8,128)S(1)}, f32[32,1024]{1,0:T(8,128)S(1)}, u32[]{:S(2)}, u32[]{:S(2)}) collective-permute-start(f32[32,1024]{1,0:T(8,128)S(1)} %copy-done), channel_id=1, source_target_pairs={{0,8},{4,12},{8,0},{12,4},{1,9},{5,13},{9,1},{13,5},{2,10},{6,14},... | collective-permute-start | bytes 393224 | tf_op jit(solution)/shard_map/ppermute | solution.py:302
  8.8 4.4 %collective-permute-start.1 = (f32[24,512]{1,0:T(8,128)S(1)}, f32[24,512]{1,0:T(8,128)S(1)}, u32[]{:S(2)}, u32[]{:S(2)}) collective-permute-start(f32[24,512]{1,0:T(8,128)S(1)} %get-tuple-element.18.refs_0_), channel_id=1, source_target_pairs={{0,2},{1,3},{2,0},{3,1},{4,6},{5,7},{6,4},{7,5},{8,10},{9,11},{10,... | collective-permute-start | bytes 147464 | tf_op jit(solution)/shard_map/ppermute | solution.py:302
  10.4 4.1 %collective-permute-start.2 = (f32[24,512]{1,0:T(8,128)S(1)}, f32[24,512]{1,0:T(8,128)S(1)}, u32[]{:S(2)}, u32[]{:S(2)}) collective-permute-start(f32[24,512]{1,0:T(8,128)S(1)} %get-tuple-element.19.refs_1_), channel_id=1, source_target_pairs={{0,2},{1,3},{2,0},{3,1},{4,6},{5,7},{6,4},{7,5},{8,10},{9,11},{10,... | collective-permute-start | bytes 147464 | tf_op jit(solution)/shard_map/ppermute | solution.py:302
  10.9 6.6 %collective-permute-start.5 = (f32[32,1024]{1,0:T(8,128)S(1)}, f32[32,1024]{1,0:T(8,128)S(1)}, u32[]{:S(2)}, u32[]{:S(2)}) collective-permute-start(f32[32,1024]{1,0:T(8,128)S(1)} %copy-done), channel_id=1, source_target_pairs={{0,4},{4,0},{8,12},{12,8},{1,5},{5,1},{9,13},{13,9},{2,6},{6,2},{1... | collective-permute-start | bytes 393224 | tf_op jit(solution)/shard_map/ppermute | solution.py:302
  14.5 1.3 %collective-permute-start.3 = (f32[32,512]{1,0:T(8,128)S(1)}, f32[32,512]{1,0:T(8,128)S(1)}, u32[]{:S(2)}, u32[]{:S(2)}) collective-permute-start(f32[32,512]{1,0:T(8,128)S(1)} %get-tuple-element.21.x_ref), channel_id=1, source_target_pairs={{0,1},{1,0},{2,3},{3,2},{4,5},{5,4},{6,7},{7,6},{8,9},{9,8},{10,11... | collective-permute-start | bytes 196616 | tf_op jit(solution)/shard_map/ppermute | solution.py:302
  17.6 10.6 %collective-permute-start.6 = (f32[48,1024]{1,0:T(8,128)S(1)}, f32[48,1024]{1,0:T(8,128)S(1)}, u32[]{:S(2)}, u32[]{:S(2)}) collective-permute-start(f32[48,1024]{1,0:T(8,128)S(1)} %get-tuple-element.26), channel_id=1, source_target_pairs={{0,4},{4,0},{8,12},{12,8},{1,5},{5,1},{9,13},{13,9},{2,6},{6,2},{1... | collective-permute-start | bytes 589832 | tf_op jit(solution)/shard_map/ppermute | solution.py:302
  18.3 6.6 %collective-permute-start.7 = (f32[16,1024]{1,0:T(8,128)S(1)}, f32[16,1024]{1,0:T(8,128)S(1)}, u32[]{:S(2)}, u32[]{:S(2)}) collective-permute-start(f32[16,1024]{1,0:T(8,128)S(1)} %get-tuple-element.27), channel_id=1, source_target_pairs={{0,8},{4,12},{8,0},{12,4},{1,9},{5,13},{9,1},{13,5},{2,10},{6,14},... | collective-permute-start | bytes 196616 | tf_op jit(solution)/shard_map/ppermute | solution.py:302
  21.5 6.6 %collective-permute-start.8 = (f32[16,1024]{1,0:T(8,128)S(1)}, f32[16,1024]{1,0:T(8,128)S(1)}, u32[]{:S(2)}, u32[]{:S(2)}) collective-permute-start(f32[16,1024]{1,0:T(8,128)S(1)} %get-tuple-element.28), channel_id=1, source_target_pairs={{0,12},{4,8},{8,4},{12,0},{1,13},{5,9},{9,5},{13,1},{2,14},{6,10},... | collective-permute-start | bytes 196616 | tf_op jit(solution)/shard_map/ppermute | solution.py:302
  28.6 1.3 %collective-permute-start.9 = (f32[64,128]{1,0:T(8,128)S(1)}, f32[64,128]{1,0:T(8,128)S(1)}, u32[]{:S(2)}, u32[]{:S(2)}) collective-permute-start(f32[64,128]{1,0:T(8,128)S(1)} %shard_map.101), channel_id=1, source_target_pairs={{0,1},{1,0},{2,3},{3,2},{4,5},{5,4},{6,7},{7,6},{8,9},{9,8},{10,11... | collective-permute-start | bytes 98312 | tf_op jit(solution)/shard_map/ppermute | solution.py:302
  29.9 3.9 %collective-permute-start.10 = (f32[64,128]{1,0:T(8,128)S(1)}, f32[64,128]{1,0:T(8,128)S(1)}, u32[]{:S(2)}, u32[]{:S(2)}) collective-permute-start(f32[64,128]{1,0:T(8,128)S(1)} %add.6), channel_id=1, source_target_pairs={{0,2},{1,3},{2,0},{3,1},{4,6},{5,7},{6,4},{7,5},{8,10},{9,11},{10,... | collective-permute-start | bytes 98312 | tf_op jit(solution)/shard_map/ppermute | solution.py:302

commit v6 on v4

--- a/solution.py
+++ b/solution.py
@@ -12,7 +12,6 @@
 MIB = 1024 * 1024
 NT = (((1,), (1,)), ((), ()))
 MOST_DIRECT = 8
-CHUNKS = 2
 
 
 def params(mib):
@@ -62,69 +61,46 @@
     return jnp.where((token >= first) & (token < last), 1.0, 0.0)
 
 
-def project_kernel(
-    owners, relative, cap, width, act_hbm, grad_hbm, in_hbm, out_hbm, len_hbm, own_hbm,
-    keep_ref, send_ref, mask_ref, act, grad, proj_in, proj_out, lens, owner, turned, sems,
+def x_kernel(
+    owners, relative, cap, act_hbm, grad_hbm, in_hbm, out_hbm, len_hbm, own_hbm,
+    x_ref, mask_ref, grad, proj_out, act, proj_in, lens, owner, sems,
 ):
-    tokens = act.shape[0]
-    rank = proj_in.shape[0]
-    half = rank // 2
-    chunk = grad.shape[1] // CHUNKS
-    chunks = [pl.ds(i * chunk, chunk) for i in range(CHUNKS)]
-    pairs = [(in_hbm, proj_in), (act_hbm, act), (out_hbm, proj_out)]
-    pairs += [(grad_hbm.at[:, c], grad.at[:, c]) for c in chunks]
-    pairs += [(len_hbm, lens), (own_hbm, owner)]
-    in_copy, act_copy, out_copy, *grad_copies, len_copy, own_copy = copies(pairs, sems)
-    me = lax.axis_index("tensor")
-    parity = lax.rem(me, 2)
+    pairs = [(in_hbm, proj_in), (act_hbm, act), (len_hbm, lens), (own_hbm, owner)]
+    pairs += [(out_hbm, proj_out), (grad_hbm, grad)]
+    in_copy, act_copy, len_copy, own_copy, out_copy, grad_copy = copies(pairs, sems)
+    len_copy.wait()
+    own_copy.wait()
+    mask_ref[...] = slot_mask(owners, relative, cap, lens[...], owner[...], *mask_ref.shape)
     in_copy.wait()
     act_copy.wait()
-    x_t = mm(proj_in[...], act[...], NT)
-    keep_ref[:half, :] = jnp.where(parity == 0, x_t[:half], x_t[half:])
-    send_ref[:half, :] = jnp.where(parity == 0, x_t[half:], x_t[:half])
-    len_copy.wait()
-    own_copy.wait()
-    mask_ref[...] = slot_mask(
-        owners, relative, cap, lens[...], owner[...], mask_ref.shape[0], tokens
-    )
+    x_ref[...] = mm(proj_in[...], act[...], NT)
     out_copy.wait()
-    total = None
-    for c, copy in zip(chunks, grad_copies):
-        copy.wait()
-        term = mm(proj_out[:, c], grad[:, c], NT)
-        total = term if total is None else total + term
-    turned[...] = total
-    spot = half
-    for apart in range(rank // width - 2, -1, -2):
-        for ref, who in ((keep_ref, me ^ apart), (send_ref, me ^ (apart ^ 1))):
-            block = pl.ds(pl.multiple_of(who * width, width), width)
-            ref[spot : spot + width, :] = turned[block, :]
-        spot += width
-
-
-def project(act, grad, in_t, out_t, lengths, owner_row, owners, cap, width, relative):
+    grad_copy.wait()
+
+
+def project_x(act, grad, in_t, out_t, lengths, owner_row, owners, cap, relative):
     tokens, rank = act.shape[0], in_t.shape[0]
-    depth = act.shape[1] + grad.shape[1]
-    part = jax.ShapeDtypeStruct((rank, tokens), F32)
     hbm = pl.BlockSpec(memory_space=pl.ANY)
     vmem = pl.BlockSpec(memory_space=pltpu.VMEM)
     return pl.pallas_call(
-        functools.partial(project_kernel, owners, relative, cap, width),
+        functools.partial(x_kernel, owners, relative, cap),
         in_specs=[hbm] * 6,
-        out_specs=[vmem] * 3,
-        out_shape=[part, part, jax.ShapeDtypeStruct((owners * cap, tokens), F32)],
+        out_specs=[vmem] * 4,
+        out_shape=[
+            jax.ShapeDtypeStruct((rank, tokens), F32),
+            jax.ShapeDtypeStruct((owners * cap, tokens), F32),
+            jax.ShapeDtypeStruct(grad.shape, BF16),
+            jax.ShapeDtypeStruct(out_t.shape, BF16),
+        ],
         scratch_shapes=[
             pltpu.VMEM(act.shape, BF16),
-            pltpu.VMEM(grad.shape, BF16),
             pltpu.VMEM(in_t.shape, BF16),
-            pltpu.VMEM(out_t.shape, BF16),
             pltpu.VMEM(lengths.shape, jnp.int32),
             pltpu.VMEM(owner_row.shape, jnp.int32),
-            pltpu.VMEM((rank, tokens), F32),
-            pltpu.SemaphoreType.DMA((5 + CHUNKS,)),
+            pltpu.SemaphoreType.DMA((6,)),
         ],
         compiler_params=params(24),
-        cost_estimate=cost(2 * tokens * depth * rank, 2 * depth * (tokens + rank)),
+        cost_estimate=cost(0, 0),
     )(
         *(
             pltpu.with_memory_space_constraint(x, pltpu.HBM)
@@ -133,15 +109,72 @@
     )
 
 
-def outer_kernel(x_ref, x_other_ref, g_ref, mask_ref, *blocks):
+def g_kernel(width, grad_ref, proj_ref, keep_ref, send_ref, full):
+    full[...] = mm(proj_ref[...], grad_ref[...], NT)
+    me = lax.axis_index("tensor")
+    count = full.shape[0] // width
+    for apart in range(count):
+        block = pl.ds(pl.multiple_of((me ^ apart) * width, width), width)
+        ref, spot = (keep_ref, apart) if apart < count // 2 else (send_ref, apart - count // 2)
+        ref[spot * width : (spot + 1) * width, :] = full[block, :]
+
+
+def project_g(grad, out_t, width):
+    tokens, rank = grad.shape[0], out_t.shape[0]
+    part = jax.ShapeDtypeStruct((rank // 2, tokens), F32)
+    return pl.pallas_call(
+        functools.partial(g_kernel, width),
+        out_shape=[part, part],
+        scratch_shapes=[pltpu.VMEM((rank, tokens), F32)],
+        compiler_params=params(24),
+        cost_estimate=cost(0, 0),
+    )(grad, out_t)
+
+
+def stack(refs):
+    return jnp.concatenate([r[...] for r in refs], axis=0)
+
+
+def fold_kernel(rank, owned, came, keep_ref, *refs):
+    first_ref, second_ref, kept_ref = refs[-3:]
+    got = stack(refs[owned : owned + came])
+    total = keep_ref[...] + got[rank:]
+    kept = kept_ref.shape[0]
+    kept_ref[...] = total[:kept]
+    x = stack(refs[:owned])[:rank] + got[:rank]
+    sent = jnp.concatenate([x, total[kept:]], axis=0)
+    cut = first_ref.shape[0]
+    first_ref[...] = sent[:cut]
+    second_ref[...] = sent[cut:]
+
+
+def fold(rank, keep, own, gots, pieces):
+    tokens = keep.shape[1]
+    kept = keep.shape[0] // 2
+    cut = (rank + kept) // 16 * 8
+    *sent, keep = pl.pallas_call(
+        functools.partial(fold_kernel, rank, len(own), len(gots)),
+        in_specs=[pl.BlockSpec(memory_space=pltpu.VMEM)] * (1 + len(own) + len(gots))
+        + [pl.BlockSpec(memory_space=pl.ANY)] * len(pieces),
+        out_shape=[
+            jax.ShapeDtypeStruct((rows, tokens), F32) for rows in (cut, rank + kept - cut, kept)
+        ],
+        compiler_params=params(16),
+        cost_estimate=cost(0, 0),
+    )(keep, *own, *gots, *pieces)
+    return keep, sent
+
+
+def outer_kernel(owners, sent, g_ref, mask_ref, *refs):
+    blocks = refs[-owners:]
     width = g_ref.shape[0]
-    rank = 2 * x_ref.shape[0]
-    odd = lax.rem(lax.axis_index("tensor"), 2) == 1
-    own, other = x_ref[...], x_other_ref[...]
-    x_full = jnp.concatenate([jnp.where(odd, other, own), jnp.where(odd, own, other)], axis=0)
+    own, got = stack(refs[:sent]), stack(refs[sent : 2 * sent])
+    rank = got.shape[0] - width
+    x_full = own[:rank] + got[:rank]
+    g_full = g_ref[...] + got[rank:]
     x_both = jnp.concatenate(halves(x_full), axis=0)
-    g_high = g_ref[...].astype(BF16).astype(F32)
-    g_low = g_ref[...] - g_high
+    g_high = g_full.astype(BF16).astype(F32)
+    g_low = g_full - g_high
     mask = mask_ref[...]
     cap = blocks[0].shape[0]
 
@@ -158,43 +191,33 @@
             block[:, i * rank : (i + step) * rank] = columns[k * cap : (k + 1) * cap, :]
 
 
-def outer(x_half, x_other, g_t, mask, owners):
+def outer(sent, gots, g, mask, owners, pieces):
     slots, tokens = mask.shape
-    width, rank = g_t.shape[0], 2 * x_half.shape[0]
+    width = g.shape[0]
+    rank = sum(p.shape[0] for p in sent) - width
     cap = slots // owners
     return pl.pallas_call(
-        outer_kernel,
+        functools.partial(outer_kernel, owners, len(sent)),
+        in_specs=[pl.BlockSpec(memory_space=pltpu.VMEM)] * (2 + 2 * len(sent))
+        + [pl.BlockSpec(memory_space=pl.ANY)] * len(pieces),
         out_shape=[jax.ShapeDtypeStruct((cap, width * rank), F32)] * owners,
         compiler_params=params(24),
-        cost_estimate=cost(0, 0),
-    )(x_half, x_other, g_t, mask)
-
-
-def join_kernel(block_ref, *refs):
-    *pieces, _, joined_ref, _ = refs
-    cap = block_ref.shape[0]
-    joined_ref[:cap, :] = block_ref[...]
-    for i, piece in enumerate(pieces):
-        size = piece.shape[0]
-        joined_ref[cap + i * size : cap + (i + 1) * size, :] = piece[...]
-
-
-def join(block, pieces, mate):
+        cost_estimate=cost(8 * slots * width * tokens * rank, 4 * slots * width * rank),
+    )(g, mask, *sent, *gots, *pieces)
+
+
+def join_kernel(*refs):
+    refs[-1][...] = stack(refs[:-1])
+
+
+def join(block, pieces):
     rows = block.shape[0] + sum(p.shape[0] for p in pieces)
-    vmem = pl.BlockSpec(memory_space=pltpu.VMEM)
-    anywhere = pl.BlockSpec(memory_space=pl.ANY)
     return pl.pallas_call(
         join_kernel,
-        in_specs=[vmem] * (1 + len(pieces)) + [anywhere],
-        out_specs=[vmem, anywhere],
-        out_shape=[
-            jax.ShapeDtypeStruct((rows, block.shape[1]), F32),
-            jax.ShapeDtypeStruct(mate.shape, mate.dtype),
-        ],
-        input_output_aliases={1 + len(pieces): 1},
+        out_shape=jax.ShapeDtypeStruct((rows, block.shape[1]), F32),
         compiler_params=params(16),
         cost_estimate=cost(0, 0),
-    )(block, *pieces, mate)
+    )(block, *pieces)
 
 
 def score_kernel(count, early, size, gaps, relative, ids_ref, *refs):
@@ -275,7 +298,6 @@
     data_size = lax.axis_size("dp")
     tokens = activations.shape[0]
     rank = proj_in.shape[1]
-    half = rank // 2
     width = rank // tensor_size
     docs = doc_owner.shape[0]
     cap = max(2, 2 * docs // data_size)
@@ -286,24 +308,23 @@
         mate = swap(query_grads, "dp", 1)
     else:
         pieces, gaps = [lax.all_gather(query_grads, "dp", axis=0, tiled=True)], [0]
-
-    keep, send, mask = project(
+        mate = pieces[0]
+
+    x, mask, grad, out_t = project_x(
         activations, out_grads, proj_in.T, proj_out.T, doc_lengths, doc_owner.T,
-        data_size, cap, width, direct,
+        data_size, cap, direct,
     )
-    part = keep + swap(send, "tensor", 1)
     bit = tensor_size // 2
+    x_got = swap(x, "tensor", bit)
+    keep, send = project_g(grad, out_t, width)
+    own, gots = [x], [x_got, swap(send, "tensor", bit)]
     while bit > 1:
-        cut = half + (part.shape[0] - half) // 2
-        got = swap(part[:cut], "tensor", bit)
-        part = jnp.concatenate([part[:half] + got[:half], part[cut:] + got[half:]], axis=0)
         bit //= 2
-    x_half, g_mine = part[:half], part[half:]
-    x_other = swap(x_half, "tensor", 1)
-    blocks = outer(x_half, x_other, g_mine, mask, data_size)
+        keep, own = fold(rank, keep, own, gots, pieces[1:])
+        gots = [swap(part, "tensor", bit) for part in own]
+    blocks = outer(own, gots, keep, mask, data_size, [mate])
     if direct:
-        joined, mate = join(blocks[1], pieces[1:], mate)
-        near = swap(joined, "dp", 1)
+        near = swap(join(blocks[1], pieces[1:]), "dp", 1)
         far = [swap(blocks[k], "dp", k) for k in range(2, data_size)]
         rows = [blocks[0], near, *far]
         pieces, gaps = [*pieces, mate], [*gaps, 1, *(g ^ 1 for g in gaps[1:])]

time: 35.9 us -> 35.7 us (level)
  waiting for transfers between devices: 15.7 us -> 14.9 us
  starting transfers between devices: 12.7 us -> 13.4 us
    ppermute x10 -> x11, waiting for transfers between devices: 15.7 us -> 14.9 us  [swap(): lax.ppermute(x, axis, [(i, i ^ gap) for i in range(lax.axis_size(axis))])]
    ppermute x10 -> x11, starting transfers between devices: 12.7 us -> 13.4 us  [swap(): lax.ppermute(x, axis, [(i, i ^ gap) for i in range(lax.axis_size(axis))])]
    pallas_call x3 -> x5, Pallas kernels: 4.79 us -> 4.8 us  [the longest x1 2.69 us: project_x(): pl.pallas_call(functools.partial(x_kernel, owners, relative, cap), in_spe...]
  transfers between devices with their start and end apart: 10 -> 11, of which waited for: 8 -> 7; matrix products, arithmetic and copies ran while one was open for 0% -> 0% of each run, Pallas kernels for 4% -> 6%
where the time goes in v6:
time: 35.7 us; the launch traced here: 35.6 us
  waiting for transfers between devices  14.9 us (42%)
  starting transfers between devices  13.4 us (38%)
  Pallas kernels  5.98 us (17%)
  between operations  0.71 us (2%)
  other arithmetic  0.63 us (2%)
    ppermute x11, waiting for transfers between devices, swap(): lax.ppermute(x, axis, [(i, i ^ gap) for i in range(lax.axis_size(axis))])  14.9 us
    ppermute x11, starting transfers between devices, swap(): lax.ppermute(x, axis, [(i, i ^ gap) for i in range(lax.axis_size(axis))])  13.4 us
    pallas_call x1, Pallas kernels, project_x(): pl.pallas_call(functools.partial(x_kernel, owners, relative, cap), in_spe...  2.69 us
    pallas_call x1, Pallas kernels, project_g(): pl.pallas_call(functools.partial(g_kernel, width), out_shape=[part, part]...  1.23 us
    pallas_call x1, Pallas kernels, outer(): pl.pallas_call(functools.partial(outer_kernel, owners, len(sent)), in_spe...  0.85 us
    pallas_call x1, Pallas kernels, place(): pl.pallas_call(place_kernel, out_shape=jax.ShapeDtypeStruct((slots, feats...  0.73 us
  transfers between devices with their start and end apart: 11, of which 7 were waited for; matrix products, arithmetic and copies ran while one was open for 0% of the time, Pallas kernels for 6%

profile of v6, /device:TPU:0, one launch (start us, length us, event | category | flops | bytes accessed | tf_op | source)
XLA Modules:
  0.0 35.6 jit_solution(5463659662622798024)
XLA Ops:
  0.6 2.7 %shard_map.95 = (f32[64,512]{1,0:T(8,128)S(1)}, f32[64,512]{1,0:T(8,128)S(1)}, bf16[512,3584]{1,0:T(8,128)(2,1)S(1)}, bf16[64,3584]{1,0:T(8,128)(2,1)S(1)}) custom-call(bf16[512,1024]{1,0:T(8,128)(2,1)} %act_hbm.1, bf16[512,3584]{1,0:T(8,128)(2,1)} %grad_hbm.1, bf16[64,1024]{1,0:T(8,128)(2,1)} %bitcast.6, bf16[64,3584]{1,0:T(8,128)(2,1)} %bitcast.5, ...), custom_call_target="tpu_custom_call" | custom-call | tf_op jit(solution)/shard_map/pallas_call | solution.py:85
  3.4 3.0 %collective-permute-start = (f32[64,512]{1,0:T(8,128)S(1)}, f32[64,512]{1,0:T(8,128)S(1)}, u32[]{:S(2)}, u32[]{:S(2)}) collective-permute-start(f32[64,512]{1,0:T(8,128)S(1)} %get-tuple-element.18.refs_0_), channel_id=1, source_target_pairs={{0,2},{1,3},{2,0},{3,1},{4,6},{5,7},{6,4},{7,5},{8,10},{9,11},{10,... | collective-permute-start | bytes 393224 | tf_op jit(solution)/shard_map/ppermute | solution.py:282
  6.4 2.6 %collective-permute-start.2 = (f32[32,1024]{1,0:T(8,128)S(1)}, f32[32,1024]{1,0:T(8,128)S(1)}, u32[]{:S(2)}, u32[]{:S(2)}) collective-permute-start(f32[32,1024]{1,0:T(8,128)S(1)} %copy-done), channel_id=1, source_target_pairs={{0,8},{4,12},{8,0},{12,4},{1,9},{5,13},{9,1},{13,5},{2,10},{6,14},... | collective-permute-start | bytes 393224 | tf_op jit(solution)/shard_map/ppermute | solution.py:282
  8.9 1.2 %shard_map.96 = (f32[32,512]{1,0:T(8,128)S(1)}, f32[32,512]{1,0:T(8,128)S(1)}) custom-call(bf16[512,3584]{1,0:T(8,128)(2,1)S(1)} %get-tuple-element.15.grad_ref, bf16[64,3584]{1,0:T(8,128)(2,1)S(1)} %get-tuple-element.16.proj_ref), custom_call_target="tpu_custom_call" | custom-call | tf_op jit(solution)/shard_map/pallas_call | solution.py:125
  10.2 0.6 %collective-permute-start.1 = (f32[32,512]{1,0:T(8,128)S(1)}, f32[32,512]{1,0:T(8,128)S(1)}, u32[]{:S(2)}, u32[]{:S(2)}) collective-permute-start(f32[32,512]{1,0:T(8,128)S(1)} %get-tuple-element.19), channel_id=1, source_target_pairs={{0,2},{1,3},{2,0},{3,1},{4,6},{5,7},{6,4},{7,5},{8,10},{9,11},{10,... | collective-permute-start | bytes 196616 | tf_op jit(solution)/shard_map/ppermute | solution.py:282
  10.8 1.6 %collective-permute-start.5 = (f32[32,1024]{1,0:T(8,128)S(1)}, f32[32,1024]{1,0:T(8,128)S(1)}, u32[]{:S(2)}, u32[]{:S(2)}) collective-permute-start(f32[32,1024]{1,0:T(8,128)S(1)} %copy-done), channel_id=1, source_target_pairs={{0,4},{4,0},{8,12},{12,8},{1,5},{5,1},{9,13},{13,9},{2,6},{6,2},{1... | collective-permute-start | bytes 393224 | tf_op jit(solution)/shard_map/ppermute | solution.py:282
  12.4 2.2 %collective-permute-done.1.refs_2_ = f32[32,512]{1,0:T(8,128)S(1)} collective-permute-done((f32[32,512]{1,0:T(8,128)S(1)}, f32[32,512]{1,0:T(8,128)S(1)}, u32[]{:S(2)}, u32[]{:S(2)}) %collective-permute-start.1) | collective-permute-done | bytes 65568 | tf_op jit(solution)/shard_map/ppermute | solution.py:282
  14.5 0.6 %collective-permute-done.2.refs_3_.refs_1_.refs_5_ = f32[32,1024]{1,0:T(8,128)S(1)} collective-permute-done((f32[32,1024]{1,0:T(8,128)S(1)}, f32[32,1024]{1,0:T(8,128)S(1)}, u32[]{:S(2)}, u32[]{:S(2)}) %collective-permute-start.2) | collective-permute-done | bytes 131104 | tf_op jit(solution)/shard_map/ppermute | solution.py:282
  15.2 0.1 collective-permute-start.3
  15.2 0.5 %collective-permute-start.4 = (f32[40,512]{1,0:T(8,128)S(1)}, f32[40,512]{1,0:T(8,128)S(1)}, u32[]{:S(2)}, u32[]{:S(2)}) collective-permute-start(f32[40,512]{1,0:T(8,128)S(1)} %get-tuple-element.23.refs_1_), channel_id=1, source_target_pairs={{0,1},{1,0},{2,3},{3,2},{4,5},{5,4},{6,7},{7,6},{8,9},{9,8},{10,11... | collective-permute-start | bytes 245768 | tf_op jit(solution)/shard_map/ppermute | solution.py:282
  15.7 1.1 %collective-permute-done.5.refs_4_.refs_6_ = f32[32,1024]{1,0:T(8,128)S(1)} collective-permute-done((f32[32,1024]{1,0:T(8,128)S(1)}, f32[32,1024]{1,0:T(8,128)S(1)}, u32[]{:S(2)}, u32[]{:S(2)}) %collective-permute-start.5) | collective-permute-done | bytes 131104 | tf_op jit(solution)/shard_map/ppermute | solution.py:282
  16.8 0.8 %shard_map.98 = (f32[16,1024]{1,0:T(8,128)S(1)}, f32[16,1024]{1,0:T(8,128)S(1)}, f32[16,1024]{1,0:T(8,128)S(1)}, f32[16,1024]{1,0:T(8,128)S(1)}) custom-call(f32[16,512]{1,0:T(8,128)S(1)} %get-tuple-element.20.g_ref, f32[64,512]{1,0:T(8,128)S(1)} %get-tuple-element.21.mask_ref, f32[40,512]{1,0:T(8,128)S(1)} %get-tuple-element.22.refs_0_, ...), custom_call_target="tpu_custom_call" | custom-call | flops 268435456 | bytes 262144 | tf_op jit(solution)/shard_map/pallas_call | solution.py:199
  17.7 0.9 %collective-permute-start.6 = (f32[48,1024]{1,0:T(8,128)S(1)}, f32[48,1024]{1,0:T(8,128)S(1)}, u32[]{:S(2)}, u32[]{:S(2)}) collective-permute-start(f32[48,1024]{1,0:T(8,128)S(1)} %shard_map.99), channel_id=1, source_target_pairs={{0,4},{4,0},{8,12},{12,8},{1,5},{5,1},{9,13},{13,9},{2,6},{6,2},{1... | collective-permute-start | bytes 589832 | tf_op jit(solution)/shard_map/ppermute | solution.py:282
  18.6 3.1 %collective-permute-start.7 = (f32[16,1024]{1,0:T(8,128)S(1)}, f32[16,1024]{1,0:T(8,128)S(1)}, u32[]{:S(2)}, u32[]{:S(2)}) collective-permute-start(f32[16,1024]{1,0:T(8,128)S(1)} %get-tuple-element.26), channel_id=1, source_target_pairs={{0,8},{4,12},{8,0},{12,4},{1,9},{5,13},{9,1},{13,5},{2,10},{6,14},... | collective-permute-start | bytes 196616 | tf_op jit(solution)/shard_map/ppermute | solution.py:282
  21.6 0.5 %collective-permute-start.8 = (f32[16,1024]{1,0:T(8,128)S(1)}, f32[16,1024]{1,0:T(8,128)S(1)}, u32[]{:S(2)}, u32[]{:S(2)}) collective-permute-start(f32[16,1024]{1,0:T(8,128)S(1)} %get-tuple-element.27), channel_id=1, source_target_pairs={{0,12},{4,8},{8,4},{12,0},{1,13},{5,9},{9,5},{13,1},{2,14},{6,10},... | collective-permute-start | bytes 196616 | tf_op jit(solution)/shard_map/ppermute | solution.py:282
  22.1 3.1 %collective-permute-done.7.refs_2_ = f32[16,1024]{1,0:T(8,128)S(1)} collective-permute-done((f32[16,1024]{1,0:T(8,128)S(1)}, f32[16,1024]{1,0:T(8,128)S(1)}, u32[]{:S(2)}, u32[]{:S(2)}) %collective-permute-start.7) | collective-permute-done | bytes 65568 | tf_op jit(solution)/shard_map/ppermute | solution.py:282
  25.3 4.1 %collective-permute-done.8.refs_3_ = f32[16,1024]{1,0:T(8,128)S(1)} collective-permute-done((f32[16,1024]{1,0:T(8,128)S(1)}, f32[16,1024]{1,0:T(8,128)S(1)}, u32[]{:S(2)}, u32[]{:S(2)}) %collective-permute-start.8) | collective-permute-done | bytes 65568 | tf_op jit(solution)/shard_map/ppermute | solution.py:282
  29.3 0.4 %shard_map.101 = f32[64,128]{1,0:T(8,128)S(1)} custom-call(s32[1,128]{1,0:T(1,128)S(1)} %bitcast.4, f32[16,1024]{1,0:T(8,128)S(1)} %get-tuple-element.24.refs_0_, f32[48,1024]{1,0:T(8,128)S(1)} %collective-permute-done.6.refs_1_, f32[16,1024]{1,0:T(8,128)S(1)} %collective-permute-done.7.refs_2_, f32[16,1024]{1,0:T(8,128)S(1)} %collective-permute-done.8.refs_3_, ...), custom_call_target="tpu_custom_call" | custom-call | flops 50331648 | bytes 524288 | tf_op jit(solution)/shard_map/pallas_call | solution.py:255
  29.8 0.1 collective-permute-start.9
  29.8 1.2 %collective-permute-done.9 = f32[64,128]{1,0:T(8,128)S(1)} collective-permute-done((f32[64,128]{1,0:T(8,128)S(1)}, f32[64,128]{1,0:T(8,128)S(1)}, u32[]{:S(2)}, u32[]{:S(2)}) %collective-permute-start.9) | collective-permute-done | bytes 32800 | tf_op jit(solution)/shard_map/ppermute | solution.py:282
  31.1 0.5 %collective-permute-start.10 = (f32[64,128]{1,0:T(8,128)S(1)}, f32[64,128]{1,0:T(8,128)S(1)}, u32[]{:S(2)}, u32[]{:S(2)}) collective-permute-start(f32[64,128]{1,0:T(8,128)S(1)} %add.6), channel_id=1, source_target_pairs={{0,2},{1,3},{2,0},{3,1},{4,6},{5,7},{6,4},{7,5},{8,10},{9,11},{10,... | collective-permute-start | bytes 98312 | tf_op jit(solution)/shard_map/ppermute | solution.py:282
  31.6 0.7 %shard_map.100 = f32[64,1024]{1,0:T(8,128)} custom-call(f32[16,1024]{1,0:T(8,128)S(1)} %get-tuple-element.24.refs_0_, f32[48,1024]{1,0:T(8,128)S(1)} %collective-permute-done.6.refs_1_, f32[16,1024]{1,0:T(8,128)S(1)} %collective-permute-done.7.refs_2_, f32[16,1024]{1,0:T(8,128)S(1)} %collective-permute-done.8.refs_3_), custom_call_target="tpu_custom_call" | custom-call | bytes 524288 | tf_op jit(solution)/shard_map/pallas_call | solution.py:273
  32.3 2.7 %collective-permute-done.10 = f32[64,128]{1,0:T(8,128)S(1)} collective-permute-done((f32[64,128]{1,0:T(8,128)S(1)}, f32[64,128]{1,0:T(8,128)S(1)}, u32[]{:S(2)}, u32[]{:S(2)}) %collective-permute-start.10) | collective-permute-done | bytes 32800 | tf_op jit(solution)/shard_map/ppermute | solution.py:282
  35.0 0.6 %add_multiply_fusion = f32[64,128]{1,0:T(8,128)} fusion(f32[64,128]{1,0:T(8,128)S(1)} %add.6, f32[64,128]{1,0:T(8,128)S(1)} %collective-permute-done.10), kind=kLoop, calls=%fused_computation | loop fusion | flops 16384 | bytes 98304 | tf_op jit(solution)/shard_map/mul | solution.py:340
  (11 shorter events, 0.1 us)
Async XLA Ops:
  0.6 5.7 %copy-start = (f32[32,1024]{1,0:T(8,128)S(1)}, f32[32,1024]{1,0:T(8,128)}, u32[]{:S(2)}) copy-start(f32[32,1024]{1,0:T(8,128)} %refs_4_.1) | copy-start | bytes 393220
  3.3 26.0 %copy-start.1 = (s32[128]{0:T(128)S(1)}, s32[128]{0:T(128)}, u32[]{:S(2)}) copy-start(s32[128]{0:T(128)} %param.15) | copy-start | bytes 1540
  3.4 11.2 %collective-permute-start = (f32[64,512]{1,0:T(8,128)S(1)}, f32[64,512]{1,0:T(8,128)S(1)}, u32[]{:S(2)}, u32[]{:S(2)}) collective-permute-start(f32[64,512]{1,0:T(8,128)S(1)} %get-tuple-element.18.refs_0_), channel_id=1, source_target_pairs={{0,2},{1,3},{2,0},{3,1},{4,6},{5,7},{6,4},{7,5},{8,10},{9,11},{10,... | collective-permute-start | bytes 393224 | tf_op jit(solution)/shard_map/ppermute | solution.py:282
  6.4 8.8 %collective-permute-start.2 = (f32[32,1024]{1,0:T(8,128)S(1)}, f32[32,1024]{1,0:T(8,128)S(1)}, u32[]{:S(2)}, u32[]{:S(2)}) collective-permute-start(f32[32,1024]{1,0:T(8,128)S(1)} %copy-done), channel_id=1, source_target_pairs={{0,8},{4,12},{8,0},{12,4},{1,9},{5,13},{9,1},{13,5},{2,10},{6,14},... | collective-permute-start | bytes 393224 | tf_op jit(solution)/shard_map/ppermute | solution.py:282
  10.2 4.3 %collective-permute-start.1 = (f32[32,512]{1,0:T(8,128)S(1)}, f32[32,512]{1,0:T(8,128)S(1)}, u32[]{:S(2)}, u32[]{:S(2)}) collective-permute-start(f32[32,512]{1,0:T(8,128)S(1)} %get-tuple-element.19), channel_id=1, source_target_pairs={{0,2},{1,3},{2,0},{3,1},{4,6},{5,7},{6,4},{7,5},{8,10},{9,11},{10,... | collective-permute-start | bytes 196616 | tf_op jit(solution)/shard_map/ppermute | solution.py:282
  10.8 6.0 %collective-permute-start.5 = (f32[32,1024]{1,0:T(8,128)S(1)}, f32[32,1024]{1,0:T(8,128)S(1)}, u32[]{:S(2)}, u32[]{:S(2)}) collective-permute-start(f32[32,1024]{1,0:T(8,128)S(1)} %copy-done), channel_id=1, source_target_pairs={{0,4},{4,0},{8,12},{12,8},{1,5},{5,1},{9,13},{13,9},{2,6},{6,2},{1... | collective-permute-start | bytes 393224 | tf_op jit(solution)/shard_map/ppermute | solution.py:282
  15.2 1.6 %collective-permute-start.3 = (f32[40,512]{1,0:T(8,128)S(1)}, f32[40,512]{1,0:T(8,128)S(1)}, u32[]{:S(2)}, u32[]{:S(2)}) collective-permute-start(f32[40,512]{1,0:T(8,128)S(1)} %get-tuple-element.22.refs_0_), channel_id=1, source_target_pairs={{0,1},{1,0},{2,3},{3,2},{4,5},{5,4},{6,7},{7,6},{8,9},{9,8},{10,11... | collective-permute-start | bytes 245768 | tf_op jit(solution)/shard_map/ppermute | solution.py:282
  15.2 1.6 %collective-permute-start.4 = (f32[40,512]{1,0:T(8,128)S(1)}, f32[40,512]{1,0:T(8,128)S(1)}, u32[]{:S(2)}, u32[]{:S(2)}) collective-permute-start(f32[40,512]{1,0:T(8,128)S(1)} %get-tuple-element.23.refs_1_), channel_id=1, source_target_pairs={{0,1},{1,0},{2,3},{3,2},{4,5},{5,4},{6,7},{7,6},{8,9},{9,8},{10,11... | collective-permute-start | bytes 245768 | tf_op jit(solution)/shard_map/ppermute | solution.py:282
  17.7 11.6 %collective-permute-start.6 = (f32[48,1024]{1,0:T(8,128)S(1)}, f32[48,1024]{1,0:T(8,128)S(1)}, u32[]{:S(2)}, u32[]{:S(2)}) collective-permute-start(f32[48,1024]{1,0:T(8,128)S(1)} %shard_map.99), channel_id=1, source_target_pairs={{0,4},{4,0},{8,12},{12,8},{1,5},{5,1},{9,13},{13,9},{2,6},{6,2},{1... | collective-permute-start | bytes 589832 | tf_op jit(solution)/shard_map/ppermute | solution.py:282
  18.6 6.7 %collective-permute-start.7 = (f32[16,1024]{1,0:T(8,128)S(1)}, f32[16,1024]{1,0:T(8,128)S(1)}, u32[]{:S(2)}, u32[]{:S(2)}) collective-permute-start(f32[16,1024]{1,0:T(8,128)S(1)} %get-tuple-element.26), channel_id=1, source_target_pairs={{0,8},{4,12},{8,0},{12,4},{1,9},{5,13},{9,1},{13,5},{2,10},{6,14},... | collective-permute-start | bytes 196616 | tf_op jit(solution)/shard_map/ppermute | solution.py:282
  21.6 7.7 %collective-permute-start.8 = (f32[16,1024]{1,0:T(8,128)S(1)}, f32[16,1024]{1,0:T(8,128)S(1)}, u32[]{:S(2)}, u32[]{:S(2)}) collective-permute-start(f32[16,1024]{1,0:T(8,128)S(1)} %get-tuple-element.27), channel_id=1, source_target_pairs={{0,12},{4,8},{8,4},{12,0},{1,13},{5,9},{9,5},{13,1},{2,14},{6,10},... | collective-permute-start | bytes 196616 | tf_op jit(solution)/shard_map/ppermute | solution.py:282
  29.8 1.3 %collective-permute-start.9 = (f32[64,128]{1,0:T(8,128)S(1)}, f32[64,128]{1,0:T(8,128)S(1)}, u32[]{:S(2)}, u32[]{:S(2)}) collective-permute-start(f32[64,128]{1,0:T(8,128)S(1)} %shard_map.101), channel_id=1, source_target_pairs={{0,1},{1,0},{2,3},{3,2},{4,5},{5,4},{6,7},{7,6},{8,9},{9,8},{10,11... | collective-permute-start | bytes 98312 | tf_op jit(solution)/shard_map/ppermute | solution.py:282
  31.1 3.9 %collective-permute-start.10 = (f32[64,128]{1,0:T(8,128)S(1)}, f32[64,128]{1,0:T(8,128)S(1)}, u32[]{:S(2)}, u32[]{:S(2)}) collective-permute-start(f32[64,128]{1,0:T(8,128)S(1)} %add.6), channel_id=1, source_target_pairs={{0,2},{1,3},{2,0},{3,1},{4,6},{5,7},{6,4},{7,5},{8,10},{9,11},{10,... | collective-permute-start | bytes 98312 | tf_op jit(solution)/shard_map/ppermute | solution.py:282

commit v7 on v6

--- a/solution.py
+++ b/solution.py
@@ -62,49 +62,44 @@
 
 
 def x_kernel(
-    owners, relative, cap, act_hbm, grad_hbm, in_hbm, out_hbm, len_hbm, own_hbm,
-    x_ref, mask_ref, grad, proj_out, act, proj_in, lens, owner, sems,
+    owners, relative, cap, act_hbm, in_hbm, len_hbm, own_hbm, x_ref, mask_ref,
+    act, proj_in, lens, owner, sems,
 ):
     pairs = [(in_hbm, proj_in), (act_hbm, act), (len_hbm, lens), (own_hbm, owner)]
-    pairs += [(out_hbm, proj_out), (grad_hbm, grad)]
-    in_copy, act_copy, len_copy, own_copy, out_copy, grad_copy = copies(pairs, sems)
+    in_copy, act_copy, len_copy, own_copy = copies(pairs, sems)
     len_copy.wait()
     own_copy.wait()
     mask_ref[...] = slot_mask(owners, relative, cap, lens[...], owner[...], *mask_ref.shape)
     in_copy.wait()
     act_copy.wait()
     x_ref[...] = mm(proj_in[...], act[...], NT)
-    out_copy.wait()
-    grad_copy.wait()
-
-
-def project_x(act, grad, in_t, out_t, lengths, owner_row, owners, cap, relative):
+
+
+def project_x(act, in_t, lengths, owner_row, owners, cap, relative):
     tokens, rank = act.shape[0], in_t.shape[0]
     hbm = pl.BlockSpec(memory_space=pl.ANY)
     vmem = pl.BlockSpec(memory_space=pltpu.VMEM)
     return pl.pallas_call(
         functools.partial(x_kernel, owners, relative, cap),
-        in_specs=[hbm] * 6,
-        out_specs=[vmem] * 4,
+        in_specs=[hbm] * 4,
+        out_specs=[vmem] * 2,
         out_shape=[
             jax.ShapeDtypeStruct((rank, tokens), F32),
             jax.ShapeDtypeStruct((owners * cap, tokens), F32),
-            jax.ShapeDtypeStruct(grad.shape, BF16),
-            jax.ShapeDtypeStruct(out_t.shape, BF16),
         ],
         scratch_shapes=[
             pltpu.VMEM(act.shape, BF16),
             pltpu.VMEM(in_t.shape, BF16),
             pltpu.VMEM(lengths.shape, jnp.int32),
             pltpu.VMEM(owner_row.shape, jnp.int32),
-            pltpu.SemaphoreType.DMA((6,)),
+            pltpu.SemaphoreType.DMA((4,)),
         ],
         compiler_params=params(24),
-        cost_estimate=cost(0, 0),
+        cost_estimate=cost(15 * 10**8, 0),
     )(
         *(
             pltpu.with_memory_space_constraint(x, pltpu.HBM)
-            for x in (act, grad, in_t, out_t, lengths, owner_row)
+            for x in (act, in_t, lengths, owner_row)
         )
     )
 
@@ -310,13 +305,12 @@
         pieces, gaps = [lax.all_gather(query_grads, "dp", axis=0, tiled=True)], [0]
         mate = pieces[0]
 
-    x, mask, grad, out_t = project_x(
-        activations, out_grads, proj_in.T, proj_out.T, doc_lengths, doc_owner.T,
-        data_size, cap, direct,
+    x, mask = project_x(
+        activations, proj_in.T, doc_lengths, doc_owner.T, data_size, cap, direct
     )
     bit = tensor_size // 2
     x_got = swap(x, "tensor", bit)
-    keep, send = project_g(grad, out_t, width)
+    keep, send = project_g(out_grads, proj_out.T, width)
     own, gots = [x], [x_got, swap(send, "tensor", bit)]
     while bit > 1:
         bit //= 2

time: 35.7 us -> 32.8 us (0.919)
  waiting for transfers between devices: 14.9 us -> 11.9 us
  Pallas kernels: 5.98 us -> 5.07 us
  starting transfers between devices: 13.4 us -> 14.3 us
    ppermute x11, waiting for transfers between devices: 14.9 us -> 11.9 us  [swap(): lax.ppermute(x, axis, [(i, i ^ gap) for i in range(lax.axis_size(axis))])]
    ppermute x11, starting transfers between devices: 13.4 us -> 14.3 us  [swap(): lax.ppermute(x, axis, [(i, i ^ gap) for i in range(lax.axis_size(axis))])]
    pallas_call x1, Pallas kernels: 2.69 us -> 1.81 us  [project_x(): pl.pallas_call(functools.partial(x_kernel, owners, relative, cap), in_spe...]
  transfers between devices with their start and end apart: 11 -> 11, of which waited for: 7 -> 8; matrix products, arithmetic and copies ran while one was open for 0% -> 0% of each run, Pallas kernels for 6% -> 12%
where the time goes in v7:
time: 32.8 us; the launch traced here: 32.7 us
  starting transfers between devices  14.3 us (44%)
  waiting for transfers between devices  11.9 us (36%)
  Pallas kernels  5.07 us (15%)
  between operations  0.73 us (2%)
  other arithmetic  0.63 us (2%)
    ppermute x11, starting transfers between devices, swap(): lax.ppermute(x, axis, [(i, i ^ gap) for i in range(lax.axis_size(axis))])  14.3 us
    ppermute x11, waiting for transfers between devices, swap(): lax.ppermute(x, axis, [(i, i ^ gap) for i in range(lax.axis_size(axis))])  11.9 us
    pallas_call x1, Pallas kernels, project_x(): pl.pallas_call(functools.partial(x_kernel, owners, relative, cap), in_spe...  1.81 us
    pallas_call x1, Pallas kernels, project_g(): pl.pallas_call(functools.partial(g_kernel, width), out_shape=[part, part]...  1.22 us
    pallas_call x1, Pallas kernels, outer(): pl.pallas_call(functools.partial(outer_kernel, owners, len(sent)), in_spe...  0.84 us
    pallas_call x1, Pallas kernels, place(): pl.pallas_call(place_kernel, out_shape=jax.ShapeDtypeStruct((slots, feats...  0.73 us
  transfers between devices with their start and end apart: 11, of which 8 were waited for; matrix products, arithmetic and copies ran while one was open for 0% of the time, Pallas kernels for 12%

profile of v7, /device:TPU:0, one launch (start us, length us, event | category | flops | bytes accessed | tf_op | source)
XLA Modules:
  0.0 32.7 jit_solution(7083929048116384677)
XLA Ops:
  0.7 4.1 %collective-permute-start.2 = (f32[32,1024]{1,0:T(8,128)}, f32[32,1024]{1,0:T(8,128)S(1)}, u32[]{:S(2)}, u32[]{:S(2)}) collective-permute-start(f32[32,1024]{1,0:T(8,128)} %refs_4_.1), channel_id=1, source_target_pairs={{0,8},{4,12},{8,0},{12,4},{1,9},{5,13},{9,1},{13,5},{2,10},{6,14},... | collective-permute-start | bytes 393224 | tf_op jit(solution)/shard_map/ppermute | solution.py:277
  4.8 1.8 %shard_map.96 = (f32[64,512]{1,0:T(8,128)S(1)}, f32[64,512]{1,0:T(8,128)S(1)}) custom-call(bf16[512,1024]{1,0:T(8,128)(2,1)} %act_hbm.1, bf16[64,1024]{1,0:T(8,128)(2,1)} %bitcast.6, s32[1,32]{1,0:T(1,128)} %len_hbm.1, s32[1,32]{1,0:T(1,128)} %bitcast.7), custom_call_target="tpu_custom_call" | custom-call | flops 1500000000 | tf_op jit(solution)/shard_map/pallas_call | solution.py:82
  6.6 1.6 %collective-permute-start = (f32[64,512]{1,0:T(8,128)S(1)}, f32[64,512]{1,0:T(8,128)S(1)}, u32[]{:S(2)}, u32[]{:S(2)}) collective-permute-start(f32[64,512]{1,0:T(8,128)S(1)} %get-tuple-element.14.refs_0_), channel_id=1, source_target_pairs={{0,2},{1,3},{2,0},{3,1},{4,6},{5,7},{6,4},{7,5},{8,10},{9,11},{10,... | collective-permute-start | bytes 393224 | tf_op jit(solution)/shard_map/ppermute | solution.py:277
  8.1 1.2 %shard_map.95 = (f32[32,512]{1,0:T(8,128)S(1)}, f32[32,512]{1,0:T(8,128)S(1)}) custom-call(bf16[512,3584]{1,0:T(8,128)(2,1)S(1)} %copy-done, bf16[64,3584]{1,0:T(8,128)(2,1)S(1)} %bitcast.4), custom_call_target="tpu_custom_call" | custom-call | tf_op jit(solution)/shard_map/pallas_call | solution.py:120
  9.4 0.6 %collective-permute-start.1 = (f32[32,512]{1,0:T(8,128)S(1)}, f32[32,512]{1,0:T(8,128)S(1)}, u32[]{:S(2)}, u32[]{:S(2)}) collective-permute-start(f32[32,512]{1,0:T(8,128)S(1)} %get-tuple-element.15), channel_id=1, source_target_pairs={{0,2},{1,3},{2,0},{3,1},{4,6},{5,7},{6,4},{7,5},{8,10},{9,11},{10,... | collective-permute-start | bytes 196616 | tf_op jit(solution)/shard_map/ppermute | solution.py:277
  10.0 1.6 %collective-permute-start.5 = (f32[32,1024]{1,0:T(8,128)S(1)}, f32[32,1024]{1,0:T(8,128)S(1)}, u32[]{:S(2)}, u32[]{:S(2)}) collective-permute-start(f32[32,1024]{1,0:T(8,128)S(1)} %copy-done.2), channel_id=1, source_target_pairs={{0,4},{4,0},{8,12},{12,8},{1,5},{5,1},{9,13},{13,9},{2,6},{6,2},{1... | collective-permute-start | bytes 393224 | tf_op jit(solution)/shard_map/ppermute | solution.py:277
  11.6 2.2 %collective-permute-done.1.refs_2_ = f32[32,512]{1,0:T(8,128)S(1)} collective-permute-done((f32[32,512]{1,0:T(8,128)S(1)}, f32[32,512]{1,0:T(8,128)S(1)}, u32[]{:S(2)}, u32[]{:S(2)}) %collective-permute-start.1) | collective-permute-done | bytes 65568 | tf_op jit(solution)/shard_map/ppermute | solution.py:277
  13.7 0.1 collective-permute-start.3
  13.8 0.5 %collective-permute-start.4 = (f32[40,512]{1,0:T(8,128)S(1)}, f32[40,512]{1,0:T(8,128)S(1)}, u32[]{:S(2)}, u32[]{:S(2)}) collective-permute-start(f32[40,512]{1,0:T(8,128)S(1)} %get-tuple-element.19.refs_1_), channel_id=1, source_target_pairs={{0,1},{1,0},{2,3},{3,2},{4,5},{5,4},{6,7},{7,6},{8,9},{9,8},{10,11... | collective-permute-start | bytes 245768 | tf_op jit(solution)/shard_map/ppermute | solution.py:277
  14.3 0.6 %collective-permute-done.5.refs_4_.refs_6_ = f32[32,1024]{1,0:T(8,128)S(1)} collective-permute-done((f32[32,1024]{1,0:T(8,128)S(1)}, f32[32,1024]{1,0:T(8,128)S(1)}, u32[]{:S(2)}, u32[]{:S(2)}) %collective-permute-start.5) | collective-permute-done | bytes 131104 | tf_op jit(solution)/shard_map/ppermute | solution.py:277
  14.9 0.1 collective-permute-done.3.refs_2_
  15.1 0.2 collective-permute-done.4.refs_3_
  15.2 0.8 %shard_map.98 = (f32[16,1024]{1,0:T(8,128)S(1)}, f32[16,1024]{1,0:T(8,128)S(1)}, f32[16,1024]{1,0:T(8,128)S(1)}, f32[16,1024]{1,0:T(8,128)S(1)}) custom-call(f32[16,512]{1,0:T(8,128)S(1)} %get-tuple-element.16.g_ref, f32[64,512]{1,0:T(8,128)S(1)} %get-tuple-element.17.mask_ref, f32[40,512]{1,0:T(8,128)S(1)} %get-tuple-element.18.refs_0_, ...), custom_call_target="tpu_custom_call" | custom-call | flops 268435456 | bytes 262144 | tf_op jit(solution)/shard_map/pallas_call | solution.py:194
  16.1 1.6 %collective-permute-start.6 = (f32[48,1024]{1,0:T(8,128)S(1)}, f32[48,1024]{1,0:T(8,128)S(1)}, u32[]{:S(2)}, u32[]{:S(2)}) collective-permute-start(f32[48,1024]{1,0:T(8,128)S(1)} %shard_map.99), channel_id=1, source_target_pairs={{0,4},{4,0},{8,12},{12,8},{1,5},{5,1},{9,13},{13,9},{2,6},{6,2},{1... | collective-permute-start | bytes 589832 | tf_op jit(solution)/shard_map/ppermute | solution.py:277
  17.8 1.4 %collective-permute-start.7 = (f32[16,1024]{1,0:T(8,128)S(1)}, f32[16,1024]{1,0:T(8,128)S(1)}, u32[]{:S(2)}, u32[]{:S(2)}) collective-permute-start(f32[16,1024]{1,0:T(8,128)S(1)} %get-tuple-element.22), channel_id=1, source_target_pairs={{0,8},{4,12},{8,0},{12,4},{1,9},{5,13},{9,1},{13,5},{2,10},{6,14},... | collective-permute-start | bytes 196616 | tf_op jit(solution)/shard_map/ppermute | solution.py:277
  19.1 1.4 %collective-permute-start.8 = (f32[16,1024]{1,0:T(8,128)S(1)}, f32[16,1024]{1,0:T(8,128)S(1)}, u32[]{:S(2)}, u32[]{:S(2)}) collective-permute-start(f32[16,1024]{1,0:T(8,128)S(1)} %get-tuple-element.23), channel_id=1, source_target_pairs={{0,12},{4,8},{8,4},{12,0},{1,13},{5,9},{9,5},{13,1},{2,14},{6,10},... | collective-permute-start | bytes 196616 | tf_op jit(solution)/shard_map/ppermute | solution.py:277
  20.6 3.8 %collective-permute-done.7.refs_2_ = f32[16,1024]{1,0:T(8,128)S(1)} collective-permute-done((f32[16,1024]{1,0:T(8,128)S(1)}, f32[16,1024]{1,0:T(8,128)S(1)}, u32[]{:S(2)}, u32[]{:S(2)}) %collective-permute-start.7) | collective-permute-done | bytes 65568 | tf_op jit(solution)/shard_map/ppermute | solution.py:277
  24.4 2.0 %collective-permute-done.8.refs_3_ = f32[16,1024]{1,0:T(8,128)S(1)} collective-permute-done((f32[16,1024]{1,0:T(8,128)S(1)}, f32[16,1024]{1,0:T(8,128)S(1)}, u32[]{:S(2)}, u32[]{:S(2)}) %collective-permute-start.8) | collective-permute-done | bytes 65568 | tf_op jit(solution)/shard_map/ppermute | solution.py:277
  26.4 0.4 %shard_map.101 = f32[64,128]{1,0:T(8,128)S(1)} custom-call(s32[1,128]{1,0:T(1,128)S(1)} %bitcast.5, f32[16,1024]{1,0:T(8,128)S(1)} %get-tuple-element.20.refs_0_, f32[48,1024]{1,0:T(8,128)S(1)} %collective-permute-done.6.refs_1_, f32[16,1024]{1,0:T(8,128)S(1)} %collective-permute-done.7.refs_2_, f32[16,1024]{1,0:T(8,128)S(1)} %collective-permute-done.8.refs_3_, ...), custom_call_target="tpu_custom_call" | custom-call | flops 50331648 | bytes 524288 | tf_op jit(solution)/shard_map/pallas_call | solution.py:250
  26.9 1.2 %collective-permute-done.9 = f32[64,128]{1,0:T(8,128)S(1)} collective-permute-done((f32[64,128]{1,0:T(8,128)S(1)}, f32[64,128]{1,0:T(8,128)S(1)}, u32[]{:S(2)}, u32[]{:S(2)}) %collective-permute-start.9) | collective-permute-done | bytes 32800 | tf_op jit(solution)/shard_map/ppermute | solution.py:277
  28.1 1.4 %collective-permute-start.10 = (f32[64,128]{1,0:T(8,128)S(1)}, f32[64,128]{1,0:T(8,128)S(1)}, u32[]{:S(2)}, u32[]{:S(2)}) collective-permute-start(f32[64,128]{1,0:T(8,128)S(1)} %add.6), channel_id=1, source_target_pairs={{0,2},{1,3},{2,0},{3,1},{4,6},{5,7},{6,4},{7,5},{8,10},{9,11},{10,... | collective-permute-start | bytes 98312 | tf_op jit(solution)/shard_map/ppermute | solution.py:277
  29.5 0.7 %shard_map.100 = f32[64,1024]{1,0:T(8,128)} custom-call(f32[16,1024]{1,0:T(8,128)S(1)} %get-tuple-element.20.refs_0_, f32[48,1024]{1,0:T(8,128)S(1)} %collective-permute-done.6.refs_1_, f32[16,1024]{1,0:T(8,128)S(1)} %collective-permute-done.7.refs_2_, f32[16,1024]{1,0:T(8,128)S(1)} %collective-permute-done.8.refs_3_), custom_call_target="tpu_custom_call" | custom-call | bytes 524288 | tf_op jit(solution)/shard_map/pallas_call | solution.py:268
  30.3 1.8 %collective-permute-done.10 = f32[64,128]{1,0:T(8,128)S(1)} collective-permute-done((f32[64,128]{1,0:T(8,128)S(1)}, f32[64,128]{1,0:T(8,128)S(1)}, u32[]{:S(2)}, u32[]{:S(2)}) %collective-permute-start.10) | collective-permute-done | bytes 32800 | tf_op jit(solution)/shard_map/ppermute | solution.py:277
  32.1 0.6 %add_multiply_fusion = f32[64,128]{1,0:T(8,128)} fusion(f32[64,128]{1,0:T(8,128)S(1)} %add.6, f32[64,128]{1,0:T(8,128)S(1)} %collective-permute-done.10), kind=kLoop, calls=%fused_computation | loop fusion | flops 16384 | bytes 98304 | tf_op jit(solution)/shard_map/mul | solution.py:334
  (15 shorter events, 0.1 us)
Async XLA Ops:
  0.6 7.5 %copy-start.1 = (bf16[3584,64]{0,1:T(8,128)(2,1)S(1)}, bf16[3584,64]{0,1:T(8,128)(2,1)}, u32[]{:S(2)}) copy-start(bf16[3584,64]{0,1:T(8,128)(2,1)} %param.11) | copy-start | bytes 1376260
  0.6 7.5 %copy-start = (bf16[512,3584]{1,0:T(8,128)(2,1)S(1)}, bf16[512,3584]{1,0:T(8,128)(2,1)}, u32[]{:S(2)}) copy-start(bf16[512,3584]{1,0:T(8,128)(2,1)} %grad_ref.1) | copy-start | bytes 11010052
  0.7 13.1 %collective-permute-start.2 = (f32[32,1024]{1,0:T(8,128)}, f32[32,1024]{1,0:T(8,128)S(1)}, u32[]{:S(2)}, u32[]{:S(2)}) collective-permute-start(f32[32,1024]{1,0:T(8,128)} %refs_4_.1), channel_id=1, source_target_pairs={{0,8},{4,12},{8,0},{12,4},{1,9},{5,13},{9,1},{13,5},{2,10},{6,14},... | collective-permute-start | bytes 393224 | tf_op jit(solution)/shard_map/ppermute | solution.py:277
  4.8 5.2 %copy-start.2 = (f32[32,1024]{1,0:T(8,128)S(1)}, f32[32,1024]{1,0:T(8,128)}, u32[]{:S(2)}) copy-start(f32[32,1024]{1,0:T(8,128)} %refs_4_.1) | copy-start | bytes 393220
  6.6 19.9 %copy-start.3 = (s32[128]{0:T(128)S(1)}, s32[128]{0:T(128)}, u32[]{:S(2)}) copy-start(s32[128]{0:T(128)} %param.15) | copy-start | bytes 1540
  6.6 7.1 %collective-permute-start = (f32[64,512]{1,0:T(8,128)S(1)}, f32[64,512]{1,0:T(8,128)S(1)}, u32[]{:S(2)}, u32[]{:S(2)}) collective-permute-start(f32[64,512]{1,0:T(8,128)S(1)} %get-tuple-element.14.refs_0_), channel_id=1, source_target_pairs={{0,2},{1,3},{2,0},{3,1},{4,6},{5,7},{6,4},{7,5},{8,10},{9,11},{10,... | collective-permute-start | bytes 393224 | tf_op jit(solution)/shard_map/ppermute | solution.py:277
  9.4 4.3 %collective-permute-start.1 = (f32[32,512]{1,0:T(8,128)S(1)}, f32[32,512]{1,0:T(8,128)S(1)}, u32[]{:S(2)}, u32[]{:S(2)}) collective-permute-start(f32[32,512]{1,0:T(8,128)S(1)} %get-tuple-element.15), channel_id=1, source_target_pairs={{0,2},{1,3},{2,0},{3,1},{4,6},{5,7},{6,4},{7,5},{8,10},{9,11},{10,... | collective-permute-start | bytes 196616 | tf_op jit(solution)/shard_map/ppermute | solution.py:277
  10.0 5.0 %collective-permute-start.5 = (f32[32,1024]{1,0:T(8,128)S(1)}, f32[32,1024]{1,0:T(8,128)S(1)}, u32[]{:S(2)}, u32[]{:S(2)}) collective-permute-start(f32[32,1024]{1,0:T(8,128)S(1)} %copy-done.2), channel_id=1, source_target_pairs={{0,4},{4,0},{8,12},{12,8},{1,5},{5,1},{9,13},{13,9},{2,6},{6,2},{1... | collective-permute-start | bytes 393224 | tf_op jit(solution)/shard_map/ppermute | solution.py:277
  13.7 1.3 %collective-permute-start.3 = (f32[40,512]{1,0:T(8,128)S(1)}, f32[40,512]{1,0:T(8,128)S(1)}, u32[]{:S(2)}, u32[]{:S(2)}) collective-permute-start(f32[40,512]{1,0:T(8,128)S(1)} %get-tuple-element.18.refs_0_), channel_id=1, source_target_pairs={{0,1},{1,0},{2,3},{3,2},{4,5},{5,4},{6,7},{7,6},{8,9},{9,8},{10,11... | collective-permute-start | bytes 245768 | tf_op jit(solution)/shard_map/ppermute | solution.py:277
  13.8 1.4 %collective-permute-start.4 = (f32[40,512]{1,0:T(8,128)S(1)}, f32[40,512]{1,0:T(8,128)S(1)}, u32[]{:S(2)}, u32[]{:S(2)}) collective-permute-start(f32[40,512]{1,0:T(8,128)S(1)} %get-tuple-element.19.refs_1_), channel_id=1, source_target_pairs={{0,1},{1,0},{2,3},{3,2},{4,5},{5,4},{6,7},{7,6},{8,9},{9,8},{10,11... | collective-permute-start | bytes 245768 | tf_op jit(solution)/shard_map/ppermute | solution.py:277
  16.1 10.3 %collective-permute-start.6 = (f32[48,1024]{1,0:T(8,128)S(1)}, f32[48,1024]{1,0:T(8,128)S(1)}, u32[]{:S(2)}, u32[]{:S(2)}) collective-permute-start(f32[48,1024]{1,0:T(8,128)S(1)} %shard_map.99), channel_id=1, source_target_pairs={{0,4},{4,0},{8,12},{12,8},{1,5},{5,1},{9,13},{13,9},{2,6},{6,2},{1... | collective-permute-start | bytes 589832 | tf_op jit(solution)/shard_map/ppermute | solution.py:277
  17.8 6.6 %collective-permute-start.7 = (f32[16,1024]{1,0:T(8,128)S(1)}, f32[16,1024]{1,0:T(8,128)S(1)}, u32[]{:S(2)}, u32[]{:S(2)}) collective-permute-start(f32[16,1024]{1,0:T(8,128)S(1)} %get-tuple-element.22), channel_id=1, source_target_pairs={{0,8},{4,12},{8,0},{12,4},{1,9},{5,13},{9,1},{13,5},{2,10},{6,14},... | collective-permute-start | bytes 196616 | tf_op jit(solution)/shard_map/ppermute | solution.py:277
  19.1 7.3 %collective-permute-start.8 = (f32[16,1024]{1,0:T(8,128)S(1)}, f32[16,1024]{1,0:T(8,128)S(1)}, u32[]{:S(2)}, u32[]{:S(2)}) collective-permute-start(f32[16,1024]{1,0:T(8,128)S(1)} %get-tuple-element.23), channel_id=1, source_target_pairs={{0,12},{4,8},{8,4},{12,0},{1,13},{5,9},{9,5},{13,1},{2,14},{6,10},... | collective-permute-start | bytes 196616 | tf_op jit(solution)/shard_map/ppermute | solution.py:277
  26.9 1.3 %collective-permute-start.9 = (f32[64,128]{1,0:T(8,128)S(1)}, f32[64,128]{1,0:T(8,128)S(1)}, u32[]{:S(2)}, u32[]{:S(2)}) collective-permute-start(f32[64,128]{1,0:T(8,128)S(1)} %shard_map.101), channel_id=1, source_target_pairs={{0,1},{1,0},{2,3},{3,2},{4,5},{5,4},{6,7},{7,6},{8,9},{9,8},{10,11... | collective-permute-start | bytes 98312 | tf_op jit(solution)/shard_map/ppermute | solution.py:277
  28.1 3.9 %collective-permute-start.10 = (f32[64,128]{1,0:T(8,128)S(1)}, f32[64,128]{1,0:T(8,128)S(1)}, u32[]{:S(2)}, u32[]{:S(2)}) collective-permute-start(f32[64,128]{1,0:T(8,128)S(1)} %add.6), channel_id=1, source_target_pairs={{0,2},{1,3},{2,0},{3,1},{4,6},{5,7},{6,4},{7,5},{8,10},{9,11},{10,... | collective-permute-start | bytes 98312 | tf_op jit(solution)/shard_map/ppermute | solution.py:277

commit v8 on v7

--- a/solution.py
+++ b/solution.py
@@ -12,6 +12,7 @@
 MIB = 1024 * 1024
 NT = (((1,), (1,)), ((), ()))
 MOST_DIRECT = 8
+LATE_FLOPS = 16 * 10**8
 
 
 def params(mib):
@@ -62,7 +63,7 @@
 
 
 def x_kernel(
-    owners, relative, cap, act_hbm, in_hbm, len_hbm, own_hbm, x_ref, mask_ref,
+    owners, relative, cap, act_hbm, in_hbm, len_hbm, own_hbm, keep_ref, send_ref, mask_ref,
     act, proj_in, lens, owner, sems,
 ):
     pairs = [(in_hbm, proj_in), (act_hbm, act), (len_hbm, lens), (own_hbm, owner)]
@@ -72,7 +73,11 @@
     mask_ref[...] = slot_mask(owners, relative, cap, lens[...], owner[...], *mask_ref.shape)
     in_copy.wait()
     act_copy.wait()
-    x_ref[...] = mm(proj_in[...], act[...], NT)
+    full = mm(proj_in[...], act[...], NT)
+    half = full.shape[0] // 2
+    odd = lax.rem(lax.axis_index("tensor"), 2) == 1
+    keep_ref[...] = jnp.where(odd, full[half:], full[:half])
+    send_ref[...] = jnp.where(odd, full[:half], full[half:])
 
 
 def project_x(act, in_t, lengths, owner_row, owners, cap, relative):
@@ -82,9 +87,10 @@
     return pl.pallas_call(
         functools.partial(x_kernel, owners, relative, cap),
         in_specs=[hbm] * 4,
-        out_specs=[vmem] * 2,
+        out_specs=[vmem] * 3,
         out_shape=[
-            jax.ShapeDtypeStruct((rank, tokens), F32),
+            jax.ShapeDtypeStruct((rank // 2, tokens), F32),
+            jax.ShapeDtypeStruct((rank // 2, tokens), F32),
             jax.ShapeDtypeStruct((owners * cap, tokens), F32),
         ],
         scratch_shapes=[
@@ -107,11 +113,12 @@
 def g_kernel(width, grad_ref, proj_ref, keep_ref, send_ref, full):
     full[...] = mm(proj_ref[...], grad_ref[...], NT)
     me = lax.axis_index("tensor")
-    count = full.shape[0] // width
-    for apart in range(count):
-        block = pl.ds(pl.multiple_of((me ^ apart) * width, width), width)
-        ref, spot = (keep_ref, apart) if apart < count // 2 else (send_ref, apart - count // 2)
-        ref[spot * width : (spot + 1) * width, :] = full[block, :]
+    spot = 0
+    for apart in range(full.shape[0] // width - 2, -1, -2):
+        for ref, who in ((keep_ref, me ^ apart), (send_ref, me ^ (apart ^ 1))):
+            block = pl.ds(pl.multiple_of(who * width, width), width)
+            ref[spot : spot + width, :] = full[block, :]
+        spot += width
 
 
 def project_g(grad, out_t, width):
@@ -130,43 +137,36 @@
     return jnp.concatenate([r[...] for r in refs], axis=0)
 
 
-def fold_kernel(rank, owned, came, keep_ref, *refs):
-    first_ref, second_ref, kept_ref = refs[-3:]
-    got = stack(refs[owned : owned + came])
-    total = keep_ref[...] + got[rank:]
-    kept = kept_ref.shape[0]
-    kept_ref[...] = total[:kept]
-    x = stack(refs[:owned])[:rank] + got[:rank]
-    sent = jnp.concatenate([x, total[kept:]], axis=0)
-    cut = first_ref.shape[0]
-    first_ref[...] = sent[:cut]
-    second_ref[...] = sent[cut:]
-
-
-def fold(rank, keep, own, gots, pieces):
-    tokens = keep.shape[1]
-    kept = keep.shape[0] // 2
-    cut = (rank + kept) // 16 * 8
-    *sent, keep = pl.pallas_call(
-        functools.partial(fold_kernel, rank, len(own), len(gots)),
-        in_specs=[pl.BlockSpec(memory_space=pltpu.VMEM)] * (1 + len(own) + len(gots))
-        + [pl.BlockSpec(memory_space=pl.ANY)] * len(pieces),
-        out_shape=[
-            jax.ShapeDtypeStruct((rows, tokens), F32) for rows in (cut, rank + kept - cut, kept)
-        ],
+def sum_kernel(cuts, *refs):
+    count = len(cuts)
+    outs = list(refs[2 * count :])
+    for i, cut in enumerate(cuts):
+        total = refs[i][...] + refs[count + i][...]
+        if cut:
+            outs.pop(0)[...] = total[:cut]
+        outs.pop(0)[...] = total[cut:]
+
+
+def add(owns, gots, cuts):
+    shapes = []
+    for own, cut in zip(owns, cuts):
+        rows, tokens = own.shape
+        shapes += [jax.ShapeDtypeStruct((n, tokens), F32) for n in (cut, rows - cut) if n]
+    return pl.pallas_call(
+        functools.partial(sum_kernel, tuple(cuts)),
+        out_shape=shapes,
         compiler_params=params(16),
         cost_estimate=cost(0, 0),
-    )(keep, *own, *gots, *pieces)
-    return keep, sent
-
-
-def outer_kernel(owners, sent, g_ref, mask_ref, *refs):
-    blocks = refs[-owners:]
+    )(*owns, *gots)
+
+
+def outer_kernel(x_ref, x_other_ref, g_ref, mask_ref, *blocks):
     width = g_ref.shape[0]
-    own, got = stack(refs[:sent]), stack(refs[sent : 2 * sent])
-    rank = got.shape[0] - width
-    x_full = own[:rank] + got[:rank]
-    g_full = g_ref[...] + got[rank:]
+    rank = 2 * x_ref.shape[0]
+    odd = lax.rem(lax.axis_index("tensor"), 2) == 1
+    own, other = x_ref[...], x_other_ref[...]
+    x_full = jnp.concatenate([jnp.where(odd, other, own), jnp.where(odd, own, other)], axis=0)
+    g_full = g_ref[...]
     x_both = jnp.concatenate(halves(x_full), axis=0)
     g_high = g_full.astype(BF16).astype(F32)
     g_low = g_full - g_high
@@ -186,19 +186,32 @@
             block[:, i * rank : (i + step) * rank] = columns[k * cap : (k + 1) * cap, :]
 
 
-def outer(sent, gots, g, mask, owners, pieces):
+def outer(x_half, x_other, g, mask, owners):
     slots, tokens = mask.shape
-    width = g.shape[0]
-    rank = sum(p.shape[0] for p in sent) - width
+    width, rank = g.shape[0], 2 * x_half.shape[0]
     cap = slots // owners
     return pl.pallas_call(
-        functools.partial(outer_kernel, owners, len(sent)),
-        in_specs=[pl.BlockSpec(memory_space=pltpu.VMEM)] * (2 + 2 * len(sent))
-        + [pl.BlockSpec(memory_space=pl.ANY)] * len(pieces),
+        outer_kernel,
         out_shape=[jax.ShapeDtypeStruct((cap, width * rank), F32)] * owners,
         compiler_params=params(24),
-        cost_estimate=cost(8 * slots * width * tokens * rank, 4 * slots * width * rank),
-    )(g, mask, *sent, *gots, *pieces)
+        cost_estimate=cost(14 * slots * width * tokens * rank, 0),
+    )(x_half, x_other, g, mask)
+
+
+def pass_kernel(*refs):
+    del refs
+
+
+def pass_on(arrays, flops):
+    anywhere = pl.BlockSpec(memory_space=pl.ANY)
+    return pl.pallas_call(
+        pass_kernel,
+        in_specs=[anywhere] * len(arrays),
+        out_specs=[anywhere] * len(arrays),
+        out_shape=[jax.ShapeDtypeStruct(a.shape, a.dtype) for a in arrays],
+        input_output_aliases={i: i for i in range(len(arrays))},
+        cost_estimate=cost(flops, 0),
+    )(*arrays)
 
 
 def join_kernel(*refs):
@@ -303,24 +316,27 @@
         mate = swap(query_grads, "dp", 1)
     else:
         pieces, gaps = [lax.all_gather(query_grads, "dp", axis=0, tiled=True)], [0]
-        mate = pieces[0]
-
-    x, mask = project_x(
+
+    x_keep, x_send, mask = project_x(
         activations, proj_in.T, doc_lengths, doc_owner.T, data_size, cap, direct
     )
+    x_got = swap(x_send, "tensor", 1)
+    g_keep, g_send = project_g(out_grads, proj_out.T, width)
+    (x_half,) = add([x_keep], [x_got], [0])
     bit = tensor_size // 2
-    x_got = swap(x, "tensor", bit)
-    keep, send = project_g(out_grads, proj_out.T, width)
-    own, gots = [x], [x_got, swap(send, "tensor", bit)]
+    parts = add([g_keep], [swap(g_send, "tensor", 1)], [g_keep.shape[0] // 2 if bit > 1 else 0])
     while bit > 1:
+        away, g_mine = parts
+        gots = [swap(x_half, "tensor", bit), swap(away, "tensor", bit)]
         bit //= 2
-        keep, own = fold(rank, keep, own, gots, pieces[1:])
-        gots = [swap(part, "tensor", bit) for part in own]
-    blocks = outer(own, gots, keep, mask, data_size, [mate])
+        x_half, *parts = add([x_half, g_mine], gots, [0, g_mine.shape[0] // 2 if bit > 1 else 0])
+    x_other = swap(x_half, "tensor", 1)
+    blocks = outer(x_half, x_other, parts[0], mask, data_size)
     if direct:
+        far = [swap(blocks[k], "dp", k) for k in range(data_size - 1, 1, -1)]
         near = swap(join(blocks[1], pieces[1:]), "dp", 1)
-        far = [swap(blocks[k], "dp", k) for k in range(2, data_size)]
-        rows = [blocks[0], near, *far]
+        mate, *far = pass_on([mate, *far], LATE_FLOPS)
+        rows = [blocks[0], near, *far[::-1]]
         pieces, gaps = [*pieces, mate], [*gaps, 1, *(g ^ 1 for g in gaps[1:])]
         store = place(rows)
     else:

time: 32.8 us -> 35.7 us (1.088)
  local copies, waits for them, and re-layouts: 0.02 us -> 3.35 us
  waiting for transfers between devices: 11.9 us -> 11.1 us
    unnamed x8 -> x20, local copies, waits for them, and re-layouts: 0.02 us -> 3.35 us
    ppermute x11 -> x12, waiting for transfers between devices: 11.9 us -> 11.1 us  [swap(): lax.ppermute(x, axis, [(i, i ^ gap) for i in range(lax.axis_size(axis))])]
    ppermute x11 -> x12, starting transfers between devices: 14.3 us -> 14.4 us  [swap(): lax.ppermute(x, axis, [(i, i ^ gap) for i in range(lax.axis_size(axis))])]
    pallas_call x2 -> x5, Pallas kernels: 0.87 us -> 0.87 us  [the longest x1 0.84 us: outer(): pl.pallas_call(outer_kernel, out_shape=[jax.ShapeDtypeStruct((cap, width...]
  transfers between devices with their start and end apart: 11 -> 12, of which waited for: 8 -> 8; matrix products, arithmetic and copies ran while one was open for 0% -> 0% of each run, Pallas kernels for 12% -> 8%
where the time goes in v8:
time: 35.7 us; the launch traced here: 35.4 us
  starting transfers between devices  14.4 us (40%)
  waiting for transfers between devices  11.1 us (31%)
  Pallas kernels  5.19 us (15%)
  local copies, waits for them, and re-layouts  3.35 us (9%)
  between operations  0.74 us (2%)
  other arithmetic  0.63 us (2%)
    ppermute x12, starting transfers between devices, swap(): lax.ppermute(x, axis, [(i, i ^ gap) for i in range(lax.axis_size(axis))])  14.4 us
    ppermute x12, waiting for transfers between devices, swap(): lax.ppermute(x, axis, [(i, i ^ gap) for i in range(lax.axis_size(axis))])  11.1 us
    unnamed x20, local copies, waits for them, and re-layouts  3.35 us
    pallas_call x1, Pallas kernels, project_x(): pl.pallas_call(functools.partial(x_kernel, owners, relative, cap), in_spe...  1.92 us
    pallas_call x1, Pallas kernels, project_g(): pl.pallas_call(functools.partial(g_kernel, width), out_shape=[part, part]...  1.23 us
    pallas_call x1, Pallas kernels, outer(): pl.pallas_call(outer_kernel, out_shape=[jax.ShapeDtypeStruct((cap, width...  0.84 us
    pallas_call x1, Pallas kernels, place(): pl.pallas_call(place_kernel, out_shape=jax.ShapeDtypeStruct((slots, feats...  0.73 us
  transfers between devices with their start and end apart: 12, of which 8 were waited for; matrix products, arithmetic and copies ran while one was open for 0% of the time, Pallas kernels for 8%

profile of v8, /device:TPU:0, one launch (start us, length us, event | category | flops | bytes accessed | tf_op | source)
XLA Modules:
  0.0 35.4 jit_solution(17291716884440331740)
XLA Ops:
  0.7 1.9 %shard_map.95 = (f32[32,512]{1,0:T(8,128)S(1)}, f32[32,512]{1,0:T(8,128)S(1)}, f32[64,512]{1,0:T(8,128)S(1)}) custom-call(bf16[512,1024]{1,0:T(8,128)(2,1)} %act_hbm.1, bf16[64,1024]{1,0:T(8,128)(2,1)} %bitcast.6, s32[1,32]{1,0:T(1,128)} %len_hbm.1, s32[1,32]{1,0:T(1,128)} %bitcast.7), custom_call_target="tpu_custom_call" | custom-call | flops 1500000000 | tf_op jit(solution)/shard_map/pallas_call | solution.py:87
  2.6 0.5 %collective-permute-start = (f32[32,512]{1,0:T(8,128)S(1)}, f32[32,512]{1,0:T(8,128)S(1)}, u32[]{:S(2)}, u32[]{:S(2)}) collective-permute-start(f32[32,512]{1,0:T(8,128)S(1)} %get-tuple-element.19), channel_id=1, source_target_pairs={{0,1},{1,0},{2,3},{3,2},{4,5},{5,4},{6,7},{7,6},{8,9},{9,8},{10,11... | collective-permute-start | bytes 196616 | tf_op jit(solution)/shard_map/ppermute | solution.py:290
  3.2 1.2 %shard_map.97 = (f32[32,512]{1,0:T(8,128)S(1)}, f32[32,512]{1,0:T(8,128)S(1)}) custom-call(bf16[512,3584]{1,0:T(8,128)(2,1)S(1)} %copy-done, bf16[64,3584]{1,0:T(8,128)(2,1)S(1)} %bitcast.4), custom_call_target="tpu_custom_call" | custom-call | tf_op jit(solution)/shard_map/pallas_call | solution.py:127
  4.5 0.5 %collective-permute-start.1 = (f32[32,512]{1,0:T(8,128)S(1)}, f32[32,512]{1,0:T(8,128)S(1)}, u32[]{:S(2)}, u32[]{:S(2)}) collective-permute-start(f32[32,512]{1,0:T(8,128)S(1)} %get-tuple-element.21), channel_id=1, source_target_pairs={{0,1},{1,0},{2,3},{3,2},{4,5},{5,4},{6,7},{7,6},{8,9},{9,8},{10,11... | collective-permute-start | bytes 196616 | tf_op jit(solution)/shard_map/ppermute | solution.py:290
  5.0 2.6 %collective-permute-start.2 = (f32[32,512]{1,0:T(8,128)S(1)}, f32[32,512]{1,0:T(8,128)S(1)}, u32[]{:S(2)}, u32[]{:S(2)}) collective-permute-start(f32[32,512]{1,0:T(8,128)S(1)} %shard_map.96.refs_0_), channel_id=1, source_target_pairs={{0,2},{1,3},{2,0},{3,1},{4,6},{5,7},{6,4},{7,5},{8,10},{9,11},{10,... | collective-permute-start | bytes 196616 | tf_op jit(solution)/shard_map/ppermute | solution.py:290
  7.6 1.2 %collective-permute-start.3 = (f32[16,512]{1,0:T(8,128)S(1)}, f32[16,512]{1,0:T(8,128)S(1)}, u32[]{:S(2)}, u32[]{:S(2)}) collective-permute-start(f32[16,512]{1,0:T(8,128)S(1)} %get-tuple-element.23), channel_id=1, source_target_pairs={{0,2},{1,3},{2,0},{3,1},{4,6},{5,7},{6,4},{7,5},{8,10},{9,11},{10,... | collective-permute-start | bytes 98312 | tf_op jit(solution)/shard_map/ppermute | solution.py:290
  8.8 2.6 %collective-permute-start.5 = (f32[32,1024]{1,0:T(8,128)S(1)}, f32[32,1024]{1,0:T(8,128)S(1)}, u32[]{:S(2)}, u32[]{:S(2)}) collective-permute-start(f32[32,1024]{1,0:T(8,128)S(1)} %copy-done.6), channel_id=1, source_target_pairs={{0,8},{4,12},{8,0},{12,4},{1,9},{5,13},{9,1},{13,5},{2,10},{6,14},... | collective-permute-start | bytes 393224 | tf_op jit(solution)/shard_map/ppermute | solution.py:290
  11.7 1.6 %collective-permute-start.7 = (f32[32,1024]{1,0:T(8,128)S(1)}, f32[32,1024]{1,0:T(8,128)S(1)}, u32[]{:S(2)}, u32[]{:S(2)}) collective-permute-start(f32[32,1024]{1,0:T(8,128)S(1)} %copy-done.6), channel_id=1, source_target_pairs={{0,4},{4,0},{8,12},{12,8},{1,5},{5,1},{9,13},{13,9},{2,6},{6,2},{1... | collective-permute-start | bytes 393224 | tf_op jit(solution)/shard_map/ppermute | solution.py:290
  13.3 0.8 %shard_map.100 = (f32[16,1024]{1,0:T(8,128)S(1)}, f32[16,1024]{1,0:T(8,128)S(1)}, f32[16,1024]{1,0:T(8,128)S(1)}, f32[16,1024]{1,0:T(8,128)S(1)}) custom-call(f32[32,512]{1,0:T(8,128)S(1)} %get-tuple-element.24.x_ref, f32[32,512]{1,0:T(8,128)S(1)} %collective-permute-done.4.x_other_ref, f32[16,512]{1,0:T(8,128)S(1)} %get-tuple-element.25.g_ref, ...), custom_call_target="tpu_custom_call" | custom-call | flops 469762048 | tf_op jit(solution)/shard_map/pallas_call | solution.py:193
  14.2 3.3 %collective-permute-start.8 = (f32[16,1024]{1,0:T(8,128)S(1)}, f32[16,1024]{1,0:T(8,128)S(1)}, u32[]{:S(2)}, u32[]{:S(2)}) collective-permute-start(f32[16,1024]{1,0:T(8,128)S(1)} %get-tuple-element.29), channel_id=1, source_target_pairs={{0,12},{4,8},{8,4},{12,0},{1,13},{5,9},{9,5},{13,1},{2,14},{6,10},... | collective-permute-start | bytes 196616 | tf_op jit(solution)/shard_map/ppermute | solution.py:290
  17.9 0.8 %collective-permute-start.6 = (f32[48,1024]{1,0:T(8,128)S(1)}, f32[48,1024]{1,0:T(8,128)S(1)}, u32[]{:S(2)}, u32[]{:S(2)}) collective-permute-start(f32[48,1024]{1,0:T(8,128)S(1)} %shard_map.101), channel_id=1, source_target_pairs={{0,4},{4,0},{8,12},{12,8},{1,5},{5,1},{9,13},{13,9},{2,6},{6,2},{1... | collective-permute-start | bytes 589832 | tf_op jit(solution)/shard_map/ppermute | solution.py:290
  18.7 0.7 %collective-permute-done.7.refs_0_ = f32[32,1024]{1,0:T(8,128)S(1)} collective-permute-done((f32[32,1024]{1,0:T(8,128)S(1)}, f32[32,1024]{1,0:T(8,128)S(1)}, u32[]{:S(2)}, u32[]{:S(2)}) %collective-permute-start.7) | collective-permute-done | bytes 131104 | tf_op jit(solution)/shard_map/ppermute | solution.py:290
  19.4 2.2 %collective-permute-done.8.refs_1_ = f32[16,1024]{1,0:T(8,128)S(1)} collective-permute-done((f32[16,1024]{1,0:T(8,128)S(1)}, f32[16,1024]{1,0:T(8,128)S(1)}, u32[]{:S(2)}, u32[]{:S(2)}) %collective-permute-start.8) | collective-permute-done | bytes 65568 | tf_op jit(solution)/shard_map/ppermute | solution.py:290
  21.5 2.4 %collective-permute-done.9.refs_2_ = f32[16,1024]{1,0:T(8,128)S(1)} collective-permute-done((f32[16,1024]{1,0:T(8,128)S(1)}, f32[16,1024]{1,0:T(8,128)S(1)}, u32[]{:S(2)}, u32[]{:S(2)}) %collective-permute-start.9) | collective-permute-done | bytes 65568 | tf_op jit(solution)/shard_map/ppermute | solution.py:290
  23.9 0.6 %copy-done.4 = f32[16,1024]{1,0:T(8,128)} copy-done((f32[16,1024]{1,0:T(8,128)}, f32[16,1024]{1,0:T(8,128)S(1)}, u32[]{:S(2)}) %copy-start.4) | copy-done | bytes 65560
  24.6 2.0 %collective-permute-done.6.refs_1_ = f32[48,1024]{1,0:T(8,128)S(1)} collective-permute-done((f32[48,1024]{1,0:T(8,128)S(1)}, f32[48,1024]{1,0:T(8,128)S(1)}, u32[]{:S(2)}, u32[]{:S(2)}) %collective-permute-start.6) | collective-permute-done | bytes 196640 | tf_op jit(solution)/shard_map/ppermute | solution.py:290
  26.6 0.8 %copy-done.3 = f32[16,1024]{1,0:T(8,128)S(1)} copy-done((f32[16,1024]{1,0:T(8,128)S(1)}, f32[16,1024]{1,0:T(8,128)}, u32[]{:S(2)}) %copy-start.3) | copy-done | bytes 65560
  27.4 0.8 %copy-done.5 = f32[16,1024]{1,0:T(8,128)S(1)} copy-done((f32[16,1024]{1,0:T(8,128)S(1)}, f32[16,1024]{1,0:T(8,128)}, u32[]{:S(2)}) %copy-start.5) | copy-done | bytes 65560
  28.3 0.9 %copy-done.8 = f32[32,1024]{1,0:T(8,128)S(1)} copy-done((f32[32,1024]{1,0:T(8,128)S(1)}, f32[32,1024]{1,0:T(8,128)}, u32[]{:S(2)}) %copy-start.8) | copy-done | bytes 131096
  29.7 1.2 %collective-permute-done.10 = f32[64,128]{1,0:T(8,128)S(1)} collective-permute-done((f32[64,128]{1,0:T(8,128)S(1)}, f32[64,128]{1,0:T(8,128)S(1)}, u32[]{:S(2)}, u32[]{:S(2)}) %collective-permute-start.10) | collective-permute-done | bytes 32800 | tf_op jit(solution)/shard_map/ppermute | solution.py:290
  30.9 1.2 %collective-permute-start.11 = (f32[64,128]{1,0:T(8,128)S(1)}, f32[64,128]{1,0:T(8,128)S(1)}, u32[]{:S(2)}, u32[]{:S(2)}) collective-permute-start(f32[64,128]{1,0:T(8,128)S(1)} %add.6), channel_id=1, source_target_pairs={{0,2},{1,3},{2,0},{3,1},{4,6},{5,7},{6,4},{7,5},{8,10},{9,11},{10,... | collective-permute-start | bytes 98312 | tf_op jit(solution)/shard_map/ppermute | solution.py:290
  32.1 0.7 %shard_map.103 = f32[64,1024]{1,0:T(8,128)} custom-call(f32[16,1024]{1,0:T(8,128)S(1)} %get-tuple-element.27.refs_0_, f32[48,1024]{1,0:T(8,128)S(1)} %collective-permute-done.6.refs_1_, f32[16,1024]{1,0:T(8,128)S(1)} %copy-done.5, f32[16,1024]{1,0:T(8,128)S(1)} %copy-done.3), custom_call_target="tpu_custom_call" | custom-call | bytes 524288 | tf_op jit(solution)/shard_map/pallas_call | solution.py:281
  32.8 2.0 %collective-permute-done.11 = f32[64,128]{1,0:T(8,128)S(1)} collective-permute-done((f32[64,128]{1,0:T(8,128)S(1)}, f32[64,128]{1,0:T(8,128)S(1)}, u32[]{:S(2)}, u32[]{:S(2)}) %collective-permute-start.11) | collective-permute-done | bytes 32800 | tf_op jit(solution)/shard_map/ppermute | solution.py:290
  34.8 0.6 %add_multiply_fusion = f32[64,128]{1,0:T(8,128)} fusion(f32[64,128]{1,0:T(8,128)S(1)} %add.6, f32[64,128]{1,0:T(8,128)S(1)} %collective-permute-done.11), kind=kLoop, calls=%fused_computation | loop fusion | flops 16384 | bytes 98304 | tf_op jit(solution)/shard_map/mul | solution.py:350
  (32 shorter events, 1.4 us)
Async XLA Ops:
  0.6 2.5 %copy-start.1 = (bf16[3584,64]{0,1:T(8,128)(2,1)S(1)}, bf16[3584,64]{0,1:T(8,128)(2,1)}, u32[]{:S(2)}) copy-start(bf16[3584,64]{0,1:T(8,128)(2,1)} %param.11) | copy-start | bytes 1376260
  0.6 2.6 %copy-start = (bf16[512,3584]{1,0:T(8,128)(2,1)S(1)}, bf16[512,3584]{1,0:T(8,128)(2,1)}, u32[]{:S(2)}) copy-start(bf16[512,3584]{1,0:T(8,128)(2,1)} %grad_ref.1) | copy-start | bytes 11010052
  0.7 8.2 %copy-start.6 = (f32[32,1024]{1,0:T(8,128)S(1)}, f32[32,1024]{1,0:T(8,128)}, u32[]{:S(2)}) copy-start(f32[32,1024]{1,0:T(8,128)} %refs_4_.1) | copy-start | bytes 393220
  2.6 2.4 %collective-permute-start = (f32[32,512]{1,0:T(8,128)S(1)}, f32[32,512]{1,0:T(8,128)S(1)}, u32[]{:S(2)}, u32[]{:S(2)}) collective-permute-start(f32[32,512]{1,0:T(8,128)S(1)} %get-tuple-element.19), channel_id=1, source_target_pairs={{0,1},{1,0},{2,3},{3,2},{4,5},{5,4},{6,7},{7,6},{8,9},{9,8},{10,11... | collective-permute-start | bytes 196616 | tf_op jit(solution)/shard_map/ppermute | solution.py:290
  4.5 3.1 %collective-permute-start.1 = (f32[32,512]{1,0:T(8,128)S(1)}, f32[32,512]{1,0:T(8,128)S(1)}, u32[]{:S(2)}, u32[]{:S(2)}) collective-permute-start(f32[32,512]{1,0:T(8,128)S(1)} %get-tuple-element.21), channel_id=1, source_target_pairs={{0,1},{1,0},{2,3},{3,2},{4,5},{5,4},{6,7},{7,6},{8,9},{9,8},{10,11... | collective-permute-start | bytes 196616 | tf_op jit(solution)/shard_map/ppermute | solution.py:290
  5.0 6.6 %collective-permute-start.2 = (f32[32,512]{1,0:T(8,128)S(1)}, f32[32,512]{1,0:T(8,128)S(1)}, u32[]{:S(2)}, u32[]{:S(2)}) collective-permute-start(f32[32,512]{1,0:T(8,128)S(1)} %shard_map.96.refs_0_), channel_id=1, source_target_pairs={{0,2},{1,3},{2,0},{3,1},{4,6},{5,7},{6,4},{7,5},{8,10},{9,11},{10,... | collective-permute-start | bytes 196616 | tf_op jit(solution)/shard_map/ppermute | solution.py:290
  7.6 4.0 %collective-permute-start.3 = (f32[16,512]{1,0:T(8,128)S(1)}, f32[16,512]{1,0:T(8,128)S(1)}, u32[]{:S(2)}, u32[]{:S(2)}) collective-permute-start(f32[16,512]{1,0:T(8,128)S(1)} %get-tuple-element.23), channel_id=1, source_target_pairs={{0,2},{1,3},{2,0},{3,1},{4,6},{5,7},{6,4},{7,5},{8,10},{9,11},{10,... | collective-permute-start | bytes 98312 | tf_op jit(solution)/shard_map/ppermute | solution.py:290
  8.8 9.1 %collective-permute-start.5 = (f32[32,1024]{1,0:T(8,128)S(1)}, f32[32,1024]{1,0:T(8,128)S(1)}, u32[]{:S(2)}, u32[]{:S(2)}) collective-permute-start(f32[32,1024]{1,0:T(8,128)S(1)} %copy-done.6), channel_id=1, source_target_pairs={{0,8},{4,12},{8,0},{12,4},{1,9},{5,13},{9,1},{13,5},{2,10},{6,14},... | collective-permute-start | bytes 393224 | tf_op jit(solution)/shard_map/ppermute | solution.py:290
  11.6 1.7 %collective-permute-start.4 = (f32[32,512]{1,0:T(8,128)S(1)}, f32[32,512]{1,0:T(8,128)S(1)}, u32[]{:S(2)}, u32[]{:S(2)}) collective-permute-start(f32[32,512]{1,0:T(8,128)S(1)} %get-tuple-element.24.x_ref), channel_id=1, source_target_pairs={{0,1},{1,0},{2,3},{3,2},{4,5},{5,4},{6,7},{7,6},{8,9},{9,8},{10,11... | collective-permute-start | bytes 196616 | tf_op jit(solution)/shard_map/ppermute | solution.py:290
  11.7 7.7 %collective-permute-start.7 = (f32[32,1024]{1,0:T(8,128)S(1)}, f32[32,1024]{1,0:T(8,128)S(1)}, u32[]{:S(2)}, u32[]{:S(2)}) collective-permute-start(f32[32,1024]{1,0:T(8,128)S(1)} %copy-done.6), channel_id=1, source_target_pairs={{0,4},{4,0},{8,12},{12,8},{1,5},{5,1},{9,13},{13,9},{2,6},{6,2},{1... | collective-permute-start | bytes 393224 | tf_op jit(solution)/shard_map/ppermute | solution.py:290
  13.3 13.3 %copy-start.9 = (s32[128]{0:T(128)S(1)}, s32[128]{0:T(128)}, u32[]{:S(2)}) copy-start(s32[128]{0:T(128)} %param.15) | copy-start | bytes 1540
  14.2 7.4 %collective-permute-start.8 = (f32[16,1024]{1,0:T(8,128)S(1)}, f32[16,1024]{1,0:T(8,128)S(1)}, u32[]{:S(2)}, u32[]{:S(2)}) collective-permute-start(f32[16,1024]{1,0:T(8,128)S(1)} %get-tuple-element.29), channel_id=1, source_target_pairs={{0,12},{4,8},{8,4},{12,0},{1,13},{5,9},{9,5},{13,1},{2,14},{6,10},... | collective-permute-start | bytes 196616 | tf_op jit(solution)/shard_map/ppermute | solution.py:290
  17.4 6.5 %collective-permute-start.9 = (f32[16,1024]{1,0:T(8,128)S(1)}, f32[16,1024]{1,0:T(8,128)S(1)}, u32[]{:S(2)}, u32[]{:S(2)}) collective-permute-start(f32[16,1024]{1,0:T(8,128)S(1)} %get-tuple-element.30), channel_id=1, source_target_pairs={{0,8},{4,12},{8,0},{12,4},{1,9},{5,13},{9,1},{13,5},{2,10},{6,14},... | collective-permute-start | bytes 196616 | tf_op jit(solution)/shard_map/ppermute | solution.py:290
  17.9 8.7 %collective-permute-start.6 = (f32[48,1024]{1,0:T(8,128)S(1)}, f32[48,1024]{1,0:T(8,128)S(1)}, u32[]{:S(2)}, u32[]{:S(2)}) collective-permute-start(f32[48,1024]{1,0:T(8,128)S(1)} %shard_map.101), channel_id=1, source_target_pairs={{0,4},{4,0},{8,12},{12,8},{1,5},{5,1},{9,13},{13,9},{2,6},{6,2},{1... | collective-permute-start | bytes 589832 | tf_op jit(solution)/shard_map/ppermute | solution.py:290
  19.4 4.6 %copy-start.7 = (f32[32,1024]{1,0:T(8,128)}, f32[32,1024]{1,0:T(8,128)S(1)}, u32[]{:S(2)}) copy-start(f32[32,1024]{1,0:T(8,128)S(1)} %collective-permute-done.7.refs_0_) | copy-start | bytes 393220
  21.5 2.4 %copy-start.2 = (f32[16,1024]{1,0:T(8,128)}, f32[16,1024]{1,0:T(8,128)S(1)}, u32[]{:S(2)}) copy-start(f32[16,1024]{1,0:T(8,128)S(1)} %collective-permute-done.8.refs_1_) | copy-start | bytes 196612
  23.9 0.6 %copy-start.4 = (f32[16,1024]{1,0:T(8,128)}, f32[16,1024]{1,0:T(8,128)S(1)}, u32[]{:S(2)}) copy-start(f32[16,1024]{1,0:T(8,128)S(1)} %collective-permute-done.9.refs_2_) | copy-start | bytes 196612
  26.6 0.8 %copy-start.3 = (f32[16,1024]{1,0:T(8,128)S(1)}, f32[16,1024]{1,0:T(8,128)}, u32[]{:S(2)}) copy-start(f32[16,1024]{1,0:T(8,128)} %get-tuple-element.32.refs_3_) | copy-start | bytes 196612
  27.4 0.8 %copy-start.5 = (f32[16,1024]{1,0:T(8,128)S(1)}, f32[16,1024]{1,0:T(8,128)}, u32[]{:S(2)}) copy-start(f32[16,1024]{1,0:T(8,128)} %get-tuple-element.31.refs_2_) | copy-start | bytes 196612
  28.3 0.9 %copy-start.8 = (f32[32,1024]{1,0:T(8,128)S(1)}, f32[32,1024]{1,0:T(8,128)}, u32[]{:S(2)}) copy-start(f32[32,1024]{1,0:T(8,128)} %get-tuple-element.33.refs_6_) | copy-start | bytes 393220
  29.6 1.3 %collective-permute-start.10 = (f32[64,128]{1,0:T(8,128)S(1)}, f32[64,128]{1,0:T(8,128)S(1)}, u32[]{:S(2)}, u32[]{:S(2)}) collective-permute-start(f32[64,128]{1,0:T(8,128)S(1)} %shard_map.104), channel_id=1, source_target_pairs={{0,1},{1,0},{2,3},{3,2},{4,5},{5,4},{6,7},{7,6},{8,9},{9,8},{10,11... | collective-permute-start | bytes 98312 | tf_op jit(solution)/shard_map/ppermute | solution.py:290
  30.9 3.9 %collective-permute-start.11 = (f32[64,128]{1,0:T(8,128)S(1)}, f32[64,128]{1,0:T(8,128)S(1)}, u32[]{:S(2)}, u32[]{:S(2)}) collective-permute-start(f32[64,128]{1,0:T(8,128)S(1)} %add.6), channel_id=1, source_target_pairs={{0,2},{1,3},{2,0},{3,1},{4,6},{5,7},{6,4},{7,5},{8,10},{9,11},{10,... | collective-permute-start | bytes 98312 | tf_op jit(solution)/shard_map/ppermute | solution.py:290

commit v9 on v8

--- a/solution.py
+++ b/solution.py
@@ -12,7 +12,8 @@
 MIB = 1024 * 1024
 NT = (((1,), (1,)), ((), ()))
 MOST_DIRECT = 8
-LATE_FLOPS = 16 * 10**8
+EARLY_FLOPS = 3 * 10**8
+LATE_FLOPS = 13 * 10**8
 
 
 def params(mib):
@@ -137,9 +138,9 @@
     return jnp.concatenate([r[...] for r in refs], axis=0)
 
 
-def sum_kernel(cuts, *refs):
+def sum_kernel(cuts, tokens, *refs):
     count = len(cuts)
-    outs = list(refs[2 * count :])
+    outs = list(refs[2 * count + tokens :])
     for i, cut in enumerate(cuts):
         total = refs[i][...] + refs[count + i][...]
         if cut:
@@ -147,17 +148,20 @@
         outs.pop(0)[...] = total[cut:]
 
 
-def add(owns, gots, cuts):
+def add(owns, gots, cuts, tokens=()):
     shapes = []
     for own, cut in zip(owns, cuts):
-        rows, tokens = own.shape
-        shapes += [jax.ShapeDtypeStruct((n, tokens), F32) for n in (cut, rows - cut) if n]
-    return pl.pallas_call(
-        functools.partial(sum_kernel, tuple(cuts)),
+        rows, width = own.shape
+        shapes += [jax.ShapeDtypeStruct((n, width), F32) for n in (cut, rows - cut) if n]
+    vmem = pl.BlockSpec(memory_space=pltpu.VMEM)
+    anywhere = pl.BlockSpec(memory_space=pl.ANY)
+    return pl.pallas_call(
+        functools.partial(sum_kernel, tuple(cuts), len(tokens)),
+        in_specs=[vmem] * (2 * len(cuts)) + [anywhere] * len(tokens),
         out_shape=shapes,
         compiler_params=params(16),
         cost_estimate=cost(0, 0),
-    )(*owns, *gots)
+    )(*owns, *gots, *tokens)
 
 
 def outer_kernel(x_ref, x_other_ref, g_ref, mask_ref, *blocks):
@@ -198,18 +202,15 @@
     )(x_half, x_other, g, mask)
 
 
-def pass_kernel(*refs):
-    del refs
-
-
-def pass_on(arrays, flops):
-    anywhere = pl.BlockSpec(memory_space=pl.ANY)
-    return pl.pallas_call(
-        pass_kernel,
-        in_specs=[anywhere] * len(arrays),
-        out_specs=[anywhere] * len(arrays),
-        out_shape=[jax.ShapeDtypeStruct(a.shape, a.dtype) for a in arrays],
-        input_output_aliases={i: i for i in range(len(arrays))},
+def token_kernel(*refs):
+    refs[-1][...] = jnp.zeros_like(refs[-1])
+
+
+def token(arrays, flops):
+    return pl.pallas_call(
+        token_kernel,
+        in_specs=[pl.BlockSpec(memory_space=pl.ANY)] * len(arrays),
+        out_shape=jax.ShapeDtypeStruct((8, 128), F32),
         cost_estimate=cost(flops, 0),
     )(*arrays)
 
@@ -229,7 +230,7 @@
 
 
 def score_kernel(count, early, size, gaps, relative, ids_ref, *refs):
-    rows, pieces, scores_ref = refs[:count], refs[count:-1], refs[-1]
+    rows, pieces, scores_ref = refs[:count], refs[count : count + early], refs[-1]
     queries = ids_ref.shape[1]
     me = lax.axis_index("dp")
     cap = rows[0].shape[0]
@@ -255,17 +256,19 @@
         scores_ref[spot, :] = total[k * cap : (k + 1) * cap, :]
 
 
-def score(ids_row, rows, pieces, gaps, relative):
+def score(ids_row, rows, pieces, gaps, relative, tokens):
     slots = rows[0].shape[0] * len(rows)
     queries = ids_row.shape[1]
     size, feats = pieces[0].shape
     flops = 6 * slots * size * len(gaps) * feats
     return pl.pallas_call(
         functools.partial(score_kernel, len(rows), len(pieces), size, gaps, relative),
+        in_specs=[pl.BlockSpec(memory_space=pltpu.VMEM)] * (1 + len(rows) + len(pieces))
+        + [pl.BlockSpec(memory_space=pl.ANY)] * len(tokens),
         out_shape=jax.ShapeDtypeStruct((slots, queries), F32),
         compiler_params=params(24),
         cost_estimate=cost(flops, 4 * size * len(gaps) * feats),
-    )(ids_row, *rows, *pieces)
+    )(ids_row, *rows, *pieces, *tokens)
 
 
 def place_kernel(*refs):
@@ -329,20 +332,22 @@
         away, g_mine = parts
         gots = [swap(x_half, "tensor", bit), swap(away, "tensor", bit)]
         bit //= 2
-        x_half, *parts = add([x_half, g_mine], gots, [0, g_mine.shape[0] // 2 if bit > 1 else 0])
+        early = [token(pieces[1:], EARLY_FLOPS)] if direct and bit == 1 else []
+        cut = g_mine.shape[0] // 2 if bit > 1 else 0
+        x_half, *parts = add([x_half, g_mine], gots, [0, cut], early)
     x_other = swap(x_half, "tensor", 1)
     blocks = outer(x_half, x_other, parts[0], mask, data_size)
     if direct:
         far = [swap(blocks[k], "dp", k) for k in range(data_size - 1, 1, -1)]
         near = swap(join(blocks[1], pieces[1:]), "dp", 1)
-        mate, *far = pass_on([mate, *far], LATE_FLOPS)
+        late = [token([mate, *far], LATE_FLOPS)]
         rows = [blocks[0], near, *far[::-1]]
         pieces, gaps = [*pieces, mate], [*gaps, 1, *(g ^ 1 for g in gaps[1:])]
         store = place(rows)
     else:
         rows = [lax.all_to_all(jnp.stack(blocks), "dp", 0, 0, tiled=True).reshape(-1, width * rank)]
-        store = rows[0]
-    scores = score(query_ids[None, :], rows, pieces, gaps, direct)
+        store, late = rows[0], []
+    scores = score(query_ids[None, :], rows, pieces, gaps, direct, late)
     bit = 1
     while bit < tensor_size:
         scores = scores + swap(scores, "tensor", bit)

time: 35.7 us -> 39.7 us (1.11)
  local copies, waits for them, and re-layouts: 3.35 us -> 6.15 us
  Pallas kernels: 5.19 us -> 6.25 us
  starting transfers between devices: 14.4 us -> 14.9 us
  waiting for transfers between devices: 11.1 us -> 10.6 us
    unnamed x20 -> x30, local copies, waits for them, and re-layouts: 3.35 us -> 6.15 us
    pallas_call x4 -> x5, Pallas kernels: 0.03 us -> 1.22 us  [the longest x2 1.19 us: token(): pl.pallas_call(token_kernel, in_specs=[pl.BlockSpec(memory_space=pl.ANY)]...]
    ppermute x12, waiting for transfers between devices: 11.1 us -> 10.6 us  [swap(): lax.ppermute(x, axis, [(i, i ^ gap) for i in range(lax.axis_size(axis))])]
    ppermute x12, starting transfers between devices: 14.4 us -> 14.9 us  [swap(): lax.ppermute(x, axis, [(i, i ^ gap) for i in range(lax.axis_size(axis))])]
  transfers between devices with their start and end apart: 12 -> 12, of which waited for: 8 -> 6; matrix products, arithmetic and copies ran while one was open for 0% -> 0% of each run, Pallas kernels for 8% -> 15%
where the time goes in v9:
time: 39.7 us; the launch traced here: 39.3 us
  starting transfers between devices  14.9 us (38%)
  waiting for transfers between devices  10.6 us (27%)
  Pallas kernels  6.25 us (16%)
  local copies, waits for them, and re-layouts  6.15 us (15%)
  between operations  0.79 us (2%)
  other arithmetic  0.63 us (2%)
    ppermute x12, starting transfers between devices, swap(): lax.ppermute(x, axis, [(i, i ^ gap) for i in range(lax.axis_size(axis))])  14.9 us
    ppermute x12, waiting for transfers between devices, swap(): lax.ppermute(x, axis, [(i, i ^ gap) for i in range(lax.axis_size(axis))])  10.6 us
    unnamed x30, local copies, waits for them, and re-layouts  6.15 us
    pallas_call x1, Pallas kernels, project_x(): pl.pallas_call(functools.partial(x_kernel, owners, relative, cap), in_spe...  1.78 us
    pallas_call x1, Pallas kernels, project_g(): pl.pallas_call(functools.partial(g_kernel, width), out_shape=[part, part]...  1.23 us
    pallas_call x2, Pallas kernels, token(): pl.pallas_call(token_kernel, in_specs=[pl.BlockSpec(memory_space=pl.ANY)]...  1.19 us
    pallas_call x1, Pallas kernels, outer(): pl.pallas_call(outer_kernel, out_shape=[jax.ShapeDtypeStruct((cap, width...  0.85 us
  transfers between devices with their start and end apart: 12, of which 6 were waited for; matrix products, arithmetic and copies ran while one was open for 0% of the time, Pallas kernels for 15%

profile of v9, /device:TPU:0, one launch (start us, length us, event | category | flops | bytes accessed | tf_op | source)
XLA Modules:
  0.0 39.3 jit_solution(12870259917288464437)
XLA Ops:
  0.7 4.1 %collective-permute-start.4 = (f32[32,1024]{1,0:T(8,128)}, f32[32,1024]{1,0:T(8,128)S(1)}, u32[]{:S(2)}, u32[]{:S(2)}) collective-permute-start(f32[32,1024]{1,0:T(8,128)} %refs_4_.1), channel_id=1, source_target_pairs={{0,8},{4,12},{8,0},{12,4},{1,9},{5,13},{9,1},{13,5},{2,10},{6,14},... | collective-permute-start | bytes 393224 | tf_op jit(solution)/shard_map/ppermute | solution.py:293
  4.8 1.8 %shard_map.95 = (f32[32,512]{1,0:T(8,128)S(1)}, f32[32,512]{1,0:T(8,128)S(1)}, f32[64,512]{1,0:T(8,128)S(1)}) custom-call(bf16[512,1024]{1,0:T(8,128)(2,1)} %act_hbm.1, bf16[64,1024]{1,0:T(8,128)(2,1)} %bitcast.6, s32[1,32]{1,0:T(1,128)} %len_hbm.1, s32[1,32]{1,0:T(1,128)} %bitcast.7), custom_call_target="tpu_custom_call" | custom-call | flops 1500000000 | tf_op jit(solution)/shard_map/pallas_call | solution.py:88
  6.7 1.2 %shard_map.97 = (f32[32,512]{1,0:T(8,128)S(1)}, f32[32,512]{1,0:T(8,128)S(1)}) custom-call(bf16[512,3584]{1,0:T(8,128)(2,1)S(1)} %copy-done, bf16[64,3584]{1,0:T(8,128)(2,1)S(1)} %bitcast.4), custom_call_target="tpu_custom_call" | custom-call | tf_op jit(solution)/shard_map/pallas_call | solution.py:128
  8.5 1.6 %collective-permute-start.2 = (f32[32,512]{1,0:T(8,128)S(1)}, f32[32,512]{1,0:T(8,128)S(1)}, u32[]{:S(2)}, u32[]{:S(2)}) collective-permute-start(f32[32,512]{1,0:T(8,128)S(1)} %shard_map.96.refs_0_), channel_id=1, source_target_pairs={{0,2},{1,3},{2,0},{3,1},{4,6},{5,7},{6,4},{7,5},{8,10},{9,11},{10,... | collective-permute-start | bytes 196616 | tf_op jit(solution)/shard_map/ppermute | solution.py:293
  10.0 0.9 %collective-permute-start.3 = (f32[16,512]{1,0:T(8,128)S(1)}, f32[16,512]{1,0:T(8,128)S(1)}, u32[]{:S(2)}, u32[]{:S(2)}) collective-permute-start(f32[16,512]{1,0:T(8,128)S(1)} %get-tuple-element.20), channel_id=1, source_target_pairs={{0,2},{1,3},{2,0},{3,1},{4,6},{5,7},{6,4},{7,5},{8,10},{9,11},{10,... | collective-permute-start | bytes 98312 | tf_op jit(solution)/shard_map/ppermute | solution.py:293
  11.3 0.7 %copy-done.1 = f32[32,1024]{1,0:T(8,128)} copy-done((f32[32,1024]{1,0:T(8,128)}, f32[32,1024]{1,0:T(8,128)S(1)}, u32[]{:S(2)}) %copy-start.1) | copy-done | bytes 131096
  12.5 1.5 %collective-permute-done.3.refs_3_ = f32[16,512]{1,0:T(8,128)S(1)} collective-permute-done((f32[16,512]{1,0:T(8,128)S(1)}, f32[16,512]{1,0:T(8,128)S(1)}, u32[]{:S(2)}, u32[]{:S(2)}) %collective-permute-start.3) | collective-permute-done | bytes 32800 | tf_op jit(solution)/shard_map/ppermute | solution.py:293
  14.0 0.7 %copy-done.13 = f32[8,128]{1,0:T(8,128)S(1)} copy-done((f32[8,128]{1,0:T(8,128)S(1)}, f32[8,128]{1,0:T(8,128)}, u32[]{:S(2)}) %copy-start.13) | copy-done | bytes 4120
  14.8 1.6 %collective-permute-start.9 = (f32[32,1024]{1,0:T(8,128)S(1)}, f32[32,1024]{1,0:T(8,128)S(1)}, u32[]{:S(2)}, u32[]{:S(2)}) collective-permute-start(f32[32,1024]{1,0:T(8,128)S(1)} %copy-done.9), channel_id=1, source_target_pairs={{0,4},{4,0},{8,12},{12,8},{1,5},{5,1},{9,13},{13,9},{2,6},{6,2},{1... | collective-permute-start | bytes 393224 | tf_op jit(solution)/shard_map/ppermute | solution.py:293
  16.5 0.8 %shard_map.101 = (f32[16,1024]{1,0:T(8,128)S(1)}, f32[16,1024]{1,0:T(8,128)S(1)}, f32[16,1024]{1,0:T(8,128)S(1)}, f32[16,1024]{1,0:T(8,128)S(1)}) custom-call(f32[32,512]{1,0:T(8,128)S(1)} %get-tuple-element.21.x_ref, f32[32,512]{1,0:T(8,128)S(1)} %collective-permute-done.5.x_other_ref, f32[16,512]{1,0:T(8,128)S(1)} %get-tuple-element.22.g_ref, ...), custom_call_target="tpu_custom_call" | custom-call | flops 469762048 | tf_op jit(solution)/shard_map/pallas_call | solution.py:197
  17.3 0.9 %copy-done.2 = f32[32,1024]{1,0:T(8,128)S(1)} copy-done((f32[32,1024]{1,0:T(8,128)S(1)}, f32[32,1024]{1,0:T(8,128)}, u32[]{:S(2)}) %copy-start.2) | copy-done | bytes 131096
  18.2 1.2 %collective-permute-start.6 = (f32[48,1024]{1,0:T(8,128)S(1)}, f32[48,1024]{1,0:T(8,128)S(1)}, u32[]{:S(2)}, u32[]{:S(2)}) collective-permute-start(f32[48,1024]{1,0:T(8,128)S(1)} %shard_map.102), channel_id=1, source_target_pairs={{0,4},{4,0},{8,12},{12,8},{1,5},{5,1},{9,13},{13,9},{2,6},{6,2},{1... | collective-permute-start | bytes 589832 | tf_op jit(solution)/shard_map/ppermute | solution.py:293
  19.5 1.1 %collective-permute-start.7 = (f32[16,1024]{1,0:T(8,128)S(1)}, f32[16,1024]{1,0:T(8,128)S(1)}, u32[]{:S(2)}, u32[]{:S(2)}) collective-permute-start(f32[16,1024]{1,0:T(8,128)S(1)} %get-tuple-element.26), channel_id=1, source_target_pairs={{0,8},{4,12},{8,0},{12,4},{1,9},{5,13},{9,1},{13,5},{2,10},{6,14},... | collective-permute-start | bytes 196616 | tf_op jit(solution)/shard_map/ppermute | solution.py:293
  20.5 2.2 %collective-permute-start.8 = (f32[16,1024]{1,0:T(8,128)S(1)}, f32[16,1024]{1,0:T(8,128)S(1)}, u32[]{:S(2)}, u32[]{:S(2)}) collective-permute-start(f32[16,1024]{1,0:T(8,128)S(1)} %get-tuple-element.27), channel_id=1, source_target_pairs={{0,12},{4,8},{8,4},{12,0},{1,13},{5,9},{9,5},{13,1},{2,14},{6,10},... | collective-permute-start | bytes 196616 | tf_op jit(solution)/shard_map/ppermute | solution.py:293
  22.7 3.4 %collective-permute-done.7.refs_2_ = f32[16,1024]{1,0:T(8,128)S(1)} collective-permute-done((f32[16,1024]{1,0:T(8,128)S(1)}, f32[16,1024]{1,0:T(8,128)S(1)}, u32[]{:S(2)}, u32[]{:S(2)}) %collective-permute-start.7) | collective-permute-done | bytes 65568 | tf_op jit(solution)/shard_map/ppermute | solution.py:293
  26.1 2.5 %collective-permute-done.8.refs_3_.refs_1_ = f32[16,1024]{1,0:T(8,128)S(1)} collective-permute-done((f32[16,1024]{1,0:T(8,128)S(1)}, f32[16,1024]{1,0:T(8,128)S(1)}, u32[]{:S(2)}, u32[]{:S(2)}) %collective-permute-start.8) | collective-permute-done | bytes 65568 | tf_op jit(solution)/shard_map/ppermute | solution.py:293
  29.8 0.8 %copy-done.6 = f32[16,1024]{1,0:T(8,128)S(1)} copy-done((f32[16,1024]{1,0:T(8,128)S(1)}, f32[16,1024]{1,0:T(8,128)}, u32[]{:S(2)}) %copy-start.6) | copy-done | bytes 65560
  30.6 0.8 %copy-done.8 = f32[16,1024]{1,0:T(8,128)S(1)} copy-done((f32[16,1024]{1,0:T(8,128)S(1)}, f32[16,1024]{1,0:T(8,128)}, u32[]{:S(2)}) %copy-start.8) | copy-done | bytes 65560
  31.5 0.9 %copy-done.11 = f32[32,1024]{1,0:T(8,128)S(1)} copy-done((f32[32,1024]{1,0:T(8,128)S(1)}, f32[32,1024]{1,0:T(8,128)}, u32[]{:S(2)}) %copy-start.11) | copy-done | bytes 131096
  32.4 0.7 %copy-done.12 = f32[8,128]{1,0:T(8,128)S(1)} copy-done((f32[8,128]{1,0:T(8,128)S(1)}, f32[8,128]{1,0:T(8,128)}, u32[]{:S(2)}) %copy-start.12) | copy-done | bytes 4120
  33.6 1.2 %collective-permute-done.10 = f32[64,128]{1,0:T(8,128)S(1)} collective-permute-done((f32[64,128]{1,0:T(8,128)S(1)}, f32[64,128]{1,0:T(8,128)S(1)}, u32[]{:S(2)}, u32[]{:S(2)}) %collective-permute-start.10) | collective-permute-done | bytes 32800 | tf_op jit(solution)/shard_map/ppermute | solution.py:293
  34.8 1.5 %collective-permute-start.11 = (f32[64,128]{1,0:T(8,128)S(1)}, f32[64,128]{1,0:T(8,128)S(1)}, u32[]{:S(2)}, u32[]{:S(2)}) collective-permute-start(f32[64,128]{1,0:T(8,128)S(1)} %add.6), channel_id=1, source_target_pairs={{0,2},{1,3},{2,0},{3,1},{4,6},{5,7},{6,4},{7,5},{8,10},{9,11},{10,... | collective-permute-start | bytes 98312 | tf_op jit(solution)/shard_map/ppermute | solution.py:293
  36.3 0.7 %shard_map.103 = f32[64,1024]{1,0:T(8,128)} custom-call(f32[16,1024]{1,0:T(8,128)S(1)} %get-tuple-element.24.refs_0_, f32[48,1024]{1,0:T(8,128)S(1)} %collective-permute-done.6.refs_1_, f32[16,1024]{1,0:T(8,128)S(1)} %copy-done.6, f32[16,1024]{1,0:T(8,128)S(1)} %copy-done.8), custom_call_target="tpu_custom_call" | custom-call | bytes 524288 | tf_op jit(solution)/shard_map/pallas_call | solution.py:284
  37.0 1.7 %collective-permute-done.11 = f32[64,128]{1,0:T(8,128)S(1)} collective-permute-done((f32[64,128]{1,0:T(8,128)S(1)}, f32[64,128]{1,0:T(8,128)S(1)}, u32[]{:S(2)}, u32[]{:S(2)}) %collective-permute-start.11) | collective-permute-done | bytes 32800 | tf_op jit(solution)/shard_map/ppermute | solution.py:293
  (43 shorter events, 4.1 us)
Async XLA Ops:
  0.6 6.0 %copy-start.4 = (bf16[3584,64]{0,1:T(8,128)(2,1)S(1)}, bf16[3584,64]{0,1:T(8,128)(2,1)}, u32[]{:S(2)}) copy-start(bf16[3584,64]{0,1:T(8,128)(2,1)} %param.11) | copy-start | bytes 1376260
  0.6 6.0 %copy-start = (bf16[512,3584]{1,0:T(8,128)(2,1)S(1)}, bf16[512,3584]{1,0:T(8,128)(2,1)}, u32[]{:S(2)}) copy-start(bf16[512,3584]{1,0:T(8,128)(2,1)} %grad_ref.1) | copy-start | bytes 11010052
  0.7 10.6 %collective-permute-start.4 = (f32[32,1024]{1,0:T(8,128)}, f32[32,1024]{1,0:T(8,128)S(1)}, u32[]{:S(2)}, u32[]{:S(2)}) collective-permute-start(f32[32,1024]{1,0:T(8,128)} %refs_4_.1), channel_id=1, source_target_pairs={{0,8},{4,12},{8,0},{12,4},{1,9},{5,13},{9,1},{13,5},{2,10},{6,14},... | collective-permute-start | bytes 393224 | tf_op jit(solution)/shard_map/ppermute | solution.py:293
  6.5 8.3 %copy-start.9 = (f32[32,1024]{1,0:T(8,128)S(1)}, f32[32,1024]{1,0:T(8,128)}, u32[]{:S(2)}) copy-start(f32[32,1024]{1,0:T(8,128)} %refs_4_.1) | copy-start | bytes 393220
  6.6 1.9 %collective-permute-start = (f32[32,512]{1,0:T(8,128)S(1)}, f32[32,512]{1,0:T(8,128)S(1)}, u32[]{:S(2)}, u32[]{:S(2)}) collective-permute-start(f32[32,512]{1,0:T(8,128)S(1)} %get-tuple-element.16), channel_id=1, source_target_pairs={{0,1},{1,0},{2,3},{3,2},{4,5},{5,4},{6,7},{7,6},{8,9},{9,8},{10,11... | collective-permute-start | bytes 196616 | tf_op jit(solution)/shard_map/ppermute | solution.py:293
  7.9 2.1 %collective-permute-start.1 = (f32[32,512]{1,0:T(8,128)S(1)}, f32[32,512]{1,0:T(8,128)S(1)}, u32[]{:S(2)}, u32[]{:S(2)}) collective-permute-start(f32[32,512]{1,0:T(8,128)S(1)} %get-tuple-element.18), channel_id=1, source_target_pairs={{0,1},{1,0},{2,3},{3,2},{4,5},{5,4},{6,7},{7,6},{8,9},{9,8},{10,11... | collective-permute-start | bytes 196616 | tf_op jit(solution)/shard_map/ppermute | solution.py:293
  8.5 5.6 %collective-permute-start.2 = (f32[32,512]{1,0:T(8,128)S(1)}, f32[32,512]{1,0:T(8,128)S(1)}, u32[]{:S(2)}, u32[]{:S(2)}) collective-permute-start(f32[32,512]{1,0:T(8,128)S(1)} %shard_map.96.refs_0_), channel_id=1, source_target_pairs={{0,2},{1,3},{2,0},{3,1},{4,6},{5,7},{6,4},{7,5},{8,10},{9,11},{10,... | collective-permute-start | bytes 196616 | tf_op jit(solution)/shard_map/ppermute | solution.py:293
  10.0 4.0 %collective-permute-start.3 = (f32[16,512]{1,0:T(8,128)S(1)}, f32[16,512]{1,0:T(8,128)S(1)}, u32[]{:S(2)}, u32[]{:S(2)}) collective-permute-start(f32[16,512]{1,0:T(8,128)S(1)} %get-tuple-element.20), channel_id=1, source_target_pairs={{0,2},{1,3},{2,0},{3,1},{4,6},{5,7},{6,4},{7,5},{8,10},{9,11},{10,... | collective-permute-start | bytes 98312 | tf_op jit(solution)/shard_map/ppermute | solution.py:293
  11.9 17.9 %copy-start.14 = (s32[128]{0:T(128)S(1)}, s32[128]{0:T(128)}, u32[]{:S(2)}) copy-start(s32[128]{0:T(128)} %param.15) | copy-start | bytes 1540
  12.5 17.3 %copy-start.3 = (f32[32,1024]{1,0:T(8,128)S(1)}, f32[32,1024]{1,0:T(8,128)}, u32[]{:S(2)}) copy-start(f32[32,1024]{1,0:T(8,128)} %copy-done.1) | copy-start | bytes 393220
  14.0 0.7 %copy-start.13 = (f32[8,128]{1,0:T(8,128)S(1)}, f32[8,128]{1,0:T(8,128)}, u32[]{:S(2)}) copy-start(f32[8,128]{1,0:T(8,128)} %shard_map.99.refs_4_) | copy-start | bytes 12292
  14.7 1.7 %collective-permute-start.5 = (f32[32,512]{1,0:T(8,128)S(1)}, f32[32,512]{1,0:T(8,128)S(1)}, u32[]{:S(2)}, u32[]{:S(2)}) collective-permute-start(f32[32,512]{1,0:T(8,128)S(1)} %get-tuple-element.21.x_ref), channel_id=1, source_target_pairs={{0,1},{1,0},{2,3},{3,2},{4,5},{5,4},{6,7},{7,6},{8,9},{9,8},{10,11... | collective-permute-start | bytes 196616 | tf_op jit(solution)/shard_map/ppermute | solution.py:293
  14.8 7.9 %collective-permute-start.9 = (f32[32,1024]{1,0:T(8,128)S(1)}, f32[32,1024]{1,0:T(8,128)S(1)}, u32[]{:S(2)}, u32[]{:S(2)}) collective-permute-start(f32[32,1024]{1,0:T(8,128)S(1)} %copy-done.9), channel_id=1, source_target_pairs={{0,4},{4,0},{8,12},{12,8},{1,5},{5,1},{9,13},{13,9},{2,6},{6,2},{1... | collective-permute-start | bytes 393224 | tf_op jit(solution)/shard_map/ppermute | solution.py:293
  17.3 0.9 %copy-start.2 = (f32[32,1024]{1,0:T(8,128)S(1)}, f32[32,1024]{1,0:T(8,128)}, u32[]{:S(2)}) copy-start(f32[32,1024]{1,0:T(8,128)} %copy-done.1) | copy-start | bytes 393220
  18.2 11.6 %collective-permute-start.6 = (f32[48,1024]{1,0:T(8,128)S(1)}, f32[48,1024]{1,0:T(8,128)S(1)}, u32[]{:S(2)}, u32[]{:S(2)}) collective-permute-start(f32[48,1024]{1,0:T(8,128)S(1)} %shard_map.102), channel_id=1, source_target_pairs={{0,4},{4,0},{8,12},{12,8},{1,5},{5,1},{9,13},{13,9},{2,6},{6,2},{1... | collective-permute-start | bytes 589832 | tf_op jit(solution)/shard_map/ppermute | solution.py:293
  19.5 6.7 %collective-permute-start.7 = (f32[16,1024]{1,0:T(8,128)S(1)}, f32[16,1024]{1,0:T(8,128)S(1)}, u32[]{:S(2)}, u32[]{:S(2)}) collective-permute-start(f32[16,1024]{1,0:T(8,128)S(1)} %get-tuple-element.26), channel_id=1, source_target_pairs={{0,8},{4,12},{8,0},{12,4},{1,9},{5,13},{9,1},{13,5},{2,10},{6,14},... | collective-permute-start | bytes 196616 | tf_op jit(solution)/shard_map/ppermute | solution.py:293
  20.5 8.0 %collective-permute-start.8 = (f32[16,1024]{1,0:T(8,128)S(1)}, f32[16,1024]{1,0:T(8,128)S(1)}, u32[]{:S(2)}, u32[]{:S(2)}) collective-permute-start(f32[16,1024]{1,0:T(8,128)S(1)} %get-tuple-element.27), channel_id=1, source_target_pairs={{0,12},{4,8},{8,4},{12,0},{1,13},{5,9},{9,5},{13,1},{2,14},{6,10},... | collective-permute-start | bytes 196616 | tf_op jit(solution)/shard_map/ppermute | solution.py:293
  22.7 5.9 %copy-start.10 = (f32[32,1024]{1,0:T(8,128)}, f32[32,1024]{1,0:T(8,128)S(1)}, u32[]{:S(2)}) copy-start(f32[32,1024]{1,0:T(8,128)S(1)} %collective-permute-done.9.refs_0_.refs_6_) | copy-start | bytes 393220
  26.1 2.5 %copy-start.5 = (f32[16,1024]{1,0:T(8,128)}, f32[16,1024]{1,0:T(8,128)S(1)}, u32[]{:S(2)}) copy-start(f32[16,1024]{1,0:T(8,128)S(1)} %collective-permute-done.7.refs_2_) | copy-start | bytes 196612
  29.8 0.8 %copy-start.6 = (f32[16,1024]{1,0:T(8,128)S(1)}, f32[16,1024]{1,0:T(8,128)}, u32[]{:S(2)}) copy-start(f32[16,1024]{1,0:T(8,128)} %copy-done.5) | copy-start | bytes 196612
  30.6 0.8 %copy-start.8 = (f32[16,1024]{1,0:T(8,128)S(1)}, f32[16,1024]{1,0:T(8,128)}, u32[]{:S(2)}) copy-start(f32[16,1024]{1,0:T(8,128)} %copy-done.7) | copy-start | bytes 196612
  31.5 0.9 %copy-start.11 = (f32[32,1024]{1,0:T(8,128)S(1)}, f32[32,1024]{1,0:T(8,128)}, u32[]{:S(2)}) copy-start(f32[32,1024]{1,0:T(8,128)} %copy-done.10) | copy-start | bytes 393220
  33.5 1.3 %collective-permute-start.10 = (f32[64,128]{1,0:T(8,128)S(1)}, f32[64,128]{1,0:T(8,128)S(1)}, u32[]{:S(2)}, u32[]{:S(2)}) collective-permute-start(f32[64,128]{1,0:T(8,128)S(1)} %shard_map.105), channel_id=1, source_target_pairs={{0,1},{1,0},{2,3},{3,2},{4,5},{5,4},{6,7},{7,6},{8,9},{9,8},{10,11... | collective-permute-start | bytes 98312 | tf_op jit(solution)/shard_map/ppermute | solution.py:293
  34.8 3.9 %collective-permute-start.11 = (f32[64,128]{1,0:T(8,128)S(1)}, f32[64,128]{1,0:T(8,128)S(1)}, u32[]{:S(2)}, u32[]{:S(2)}) collective-permute-start(f32[64,128]{1,0:T(8,128)S(1)} %add.6), channel_id=1, source_target_pairs={{0,2},{1,3},{2,0},{3,1},{4,6},{5,7},{6,4},{7,5},{8,10},{9,11},{10,... | collective-permute-start | bytes 98312 | tf_op jit(solution)/shard_map/ppermute | solution.py:293
  (3 other events, 2.0 us)

commit v10 on v7

--- a/solution.py
+++ b/solution.py
@@ -12,6 +12,8 @@
 MIB = 1024 * 1024
 NT = (((1,), (1,)), ((), ()))
 MOST_DIRECT = 8
+EARLY_FLOPS = 3 * 10**8
+LATE_FLOPS = 2 * 10**8
 
 
 def params(mib):
@@ -186,47 +188,57 @@
             block[:, i * rank : (i + step) * rank] = columns[k * cap : (k + 1) * cap, :]
 
 
-def outer(sent, gots, g, mask, owners, pieces):
+def outer(sent, gots, g, mask, owners):
     slots, tokens = mask.shape
     width = g.shape[0]
     rank = sum(p.shape[0] for p in sent) - width
     cap = slots // owners
     return pl.pallas_call(
         functools.partial(outer_kernel, owners, len(sent)),
-        in_specs=[pl.BlockSpec(memory_space=pltpu.VMEM)] * (2 + 2 * len(sent))
-        + [pl.BlockSpec(memory_space=pl.ANY)] * len(pieces),
         out_shape=[jax.ShapeDtypeStruct((cap, width * rank), F32)] * owners,
         compiler_params=params(24),
         cost_estimate=cost(8 * slots * width * tokens * rank, 4 * slots * width * rank),
-    )(g, mask, *sent, *gots, *pieces)
-
-
-def join_kernel(*refs):
-    refs[-1][...] = stack(refs[:-1])
-
-
-def join(block, pieces):
-    rows = block.shape[0] + sum(p.shape[0] for p in pieces)
-    return pl.pallas_call(
-        join_kernel,
-        out_shape=jax.ShapeDtypeStruct((rows, block.shape[1]), F32),
-        compiler_params=params(16),
+    )(g, mask, *sent, *gots)
+
+
+def token_kernel(*refs):
+    refs[-1][...] = jnp.zeros_like(refs[-1])
+
+
+def token(arrays, flops):
+    return pl.pallas_call(
+        token_kernel,
+        in_specs=[pl.BlockSpec(memory_space=pl.ANY)] * len(arrays),
+        out_shape=jax.ShapeDtypeStruct((8, 128), F32),
+        compiler_params=params(4),
+        cost_estimate=cost(flops, 0),
+    )(*arrays)
+
+
+def after_kernel(block_ref, piece, out_ref):
+    out_ref[...] = block_ref[...]
+
+
+def after(block, piece):
+    return pl.pallas_call(
+        after_kernel,
+        in_specs=[pl.BlockSpec(memory_space=pltpu.VMEM), pl.BlockSpec(memory_space=pl.ANY)],
+        out_shape=jax.ShapeDtypeStruct(block.shape, F32),
+        compiler_params=params(4),
         cost_estimate=cost(0, 0),
-    )(block, *pieces)
-
-
-def score_kernel(count, early, size, gaps, relative, ids_ref, *refs):
-    rows, pieces, scores_ref = refs[:count], refs[count:-1], refs[-1]
+    )(block, piece)
+
+
+def score_kernel(count, gaps, relative, ids_ref, *refs):
+    rows, pieces, scores_ref = refs[:count], refs[count : count + len(gaps)], refs[-1]
     queries = ids_ref.shape[1]
     me = lax.axis_index("dp")
     cap = rows[0].shape[0]
-    high, low = halves(jnp.concatenate([r[:cap, :] for r in rows], axis=0))
+    high, low = halves(stack(rows))
     slots = high.shape[0]
     both = jnp.concatenate([high, low], axis=0)
-    parts = [piece[...] for piece in pieces]
-    parts += [rows[1][cap + i * size : cap + (i + 1) * size, :] for i in range(len(gaps) - early)]
-    held = parts[0].shape[0]
-    pool = jnp.concatenate(parts, axis=0)
+    held = pieces[0].shape[0]
+    pool = stack(pieces)
     products = mm(both, jnp.concatenate(halves(pool), axis=0), NT)
     split = pool.shape[0]
     part = products[:slots, :split] + products[:slots, split:] + products[slots:, :split]
@@ -242,17 +254,19 @@
         scores_ref[spot, :] = total[k * cap : (k + 1) * cap, :]
 
 
-def score(ids_row, rows, pieces, gaps, relative):
+def score(ids_row, rows, pieces, gaps, relative, tokens):
     slots = rows[0].shape[0] * len(rows)
     queries = ids_row.shape[1]
     size, feats = pieces[0].shape
     flops = 6 * slots * size * len(gaps) * feats
     return pl.pallas_call(
-        functools.partial(score_kernel, len(rows), len(pieces), size, gaps, relative),
+        functools.partial(score_kernel, len(rows), gaps, relative),
+        in_specs=[pl.BlockSpec(memory_space=pltpu.VMEM)] * (1 + len(rows) + len(pieces))
+        + [pl.BlockSpec(memory_space=pl.ANY)] * len(tokens),
         out_shape=jax.ShapeDtypeStruct((slots, queries), F32),
         compiler_params=params(24),
         cost_estimate=cost(flops, 4 * size * len(gaps) * feats),
-    )(ids_row, *rows, *pieces)
+    )(ids_row, *rows, *pieces, *tokens)
 
 
 def place_kernel(*refs):
@@ -260,7 +274,7 @@
     me = lax.axis_index("dp")
     cap = rows[0].shape[0]
     for k, row in enumerate(rows):
-        store_ref[pl.ds(pl.multiple_of((me ^ k) * cap, cap), cap), :] = row[:cap, :]
+        store_ref[pl.ds(pl.multiple_of((me ^ k) * cap, cap), cap), :] = row[...]
 
 
 def place(rows):
@@ -301,9 +315,9 @@
     if direct:
         pieces, gaps = gather_pieces(query_grads)
         mate = swap(query_grads, "dp", 1)
+        passed = [swap(piece, "dp", 1) for piece in pieces[1:]]
     else:
         pieces, gaps = [lax.all_gather(query_grads, "dp", axis=0, tiled=True)], [0]
-        mate = pieces[0]
 
     x, mask = project_x(
         activations, proj_in.T, doc_lengths, doc_owner.T, data_size, cap, direct
@@ -311,22 +325,23 @@
     bit = tensor_size // 2
     x_got = swap(x, "tensor", bit)
     keep, send = project_g(out_grads, proj_out.T, width)
+    early = [token(pieces[1:], EARLY_FLOPS)] if direct else []
     own, gots = [x], [x_got, swap(send, "tensor", bit)]
     while bit > 1:
         bit //= 2
-        keep, own = fold(rank, keep, own, gots, pieces[1:])
+        keep, own = fold(rank, keep, own, gots, early)
         gots = [swap(part, "tensor", bit) for part in own]
-    blocks = outer(own, gots, keep, mask, data_size, [mate])
+    blocks = outer(own, gots, keep, mask, data_size)
     if direct:
-        near = swap(join(blocks[1], pieces[1:]), "dp", 1)
-        far = [swap(blocks[k], "dp", k) for k in range(2, data_size)]
-        rows = [blocks[0], near, *far]
-        pieces, gaps = [*pieces, mate], [*gaps, 1, *(g ^ 1 for g in gaps[1:])]
+        far = [swap(blocks[k], "dp", k) for k in range(data_size - 1, 1, -1)]
+        rows = [blocks[0], swap(after(blocks[1], mate), "dp", 1), *far[::-1]]
+        late = [token(far, LATE_FLOPS)]
+        pieces, gaps = [*pieces, mate, *passed], [*gaps, *(g ^ 1 for g in gaps)]
         store = place(rows)
     else:
         rows = [lax.all_to_all(jnp.stack(blocks), "dp", 0, 0, tiled=True).reshape(-1, width * rank)]
-        store = rows[0]
-    scores = score(query_ids[None, :], rows, pieces, gaps, direct)
+        store, late = rows[0], []
+    scores = score(query_ids[None, :], rows, pieces, gaps, direct, late)
     bit = 1
     while bit < tensor_size:
         scores = scores + swap(scores, "tensor", bit)

time: 32.8 us -> 32.2 us (0.982)
  waiting for transfers between devices: 11.9 us -> 11.1 us
    ppermute x11 -> x12, waiting for transfers between devices: 11.9 us -> 11.1 us  [swap(): lax.ppermute(x, axis, [(i, i ^ gap) for i in range(lax.axis_size(axis))])]
    ppermute x11 -> x12, starting transfers between devices: 14.3 us -> 14.5 us  [swap(): lax.ppermute(x, axis, [(i, i ^ gap) for i in range(lax.axis_size(axis))])]
    pallas_call x3 -> x5, Pallas kernels: 1.3 us -> 1.3 us  [the longest x1 0.85 us: outer(): pl.pallas_call(functools.partial(outer_kernel, owners, len(sent)), out_sh...]
  transfers between devices with their start and end apart: 11 -> 12, of which waited for: 8 -> 5; matrix products, arithmetic and copies ran while one was open for 0% -> 0% of each run, Pallas kernels for 12% -> 15%
where the time goes in v10:
time: 32.2 us; the launch traced here: 32 us
  starting transfers between devices  14.5 us (45%)
  waiting for transfers between devices  11.1 us (34%)
  Pallas kernels  5.09 us (16%)
  between operations  0.71 us (2%)
  other arithmetic  0.63 us (2%)
    ppermute x12, starting transfers between devices, swap(): lax.ppermute(x, axis, [(i, i ^ gap) for i in range(lax.axis_size(axis))])  14.5 us
    ppermute x12, waiting for transfers between devices, swap(): lax.ppermute(x, axis, [(i, i ^ gap) for i in range(lax.axis_size(axis))])  11.1 us
    pallas_call x1, Pallas kernels, project_x(): pl.pallas_call(functools.partial(x_kernel, owners, relative, cap), in_spe...  1.81 us
    pallas_call x1, Pallas kernels, project_g(): pl.pallas_call(functools.partial(g_kernel, width), out_shape=[part, part]...  1.23 us
    pallas_call x1, Pallas kernels, outer(): pl.pallas_call(functools.partial(outer_kernel, owners, len(sent)), out_sh...  0.85 us
    pallas_call x1, Pallas kernels, place(): pl.pallas_call(place_kernel, out_shape=jax.ShapeDtypeStruct((slots, feats...  0.73 us
  transfers between devices with their start and end apart: 12, of which 5 were waited for; matrix products, arithmetic and copies ran while one was open for 0% of the time, Pallas kernels for 15%

profile of v10, /device:TPU:0, one launch (start us, length us, event | category | flops | bytes accessed | tf_op | source)
XLA Modules:
  0.0 32.0 jit_solution(16116550222787175168)
XLA Ops:
  0.7 4.1 %collective-permute-start.2 = (f32[32,1024]{1,0:T(8,128)}, f32[32,1024]{1,0:T(8,128)S(1)}, u32[]{:S(2)}, u32[]{:S(2)}) collective-permute-start(f32[32,1024]{1,0:T(8,128)} %refs_4_.1), channel_id=1, source_target_pairs={{0,8},{4,12},{8,0},{12,4},{1,9},{5,13},{9,1},{13,5},{2,10},{6,14},... | collective-permute-start | bytes 393224 | tf_op jit(solution)/shard_map/ppermute | solution.py:291
  4.8 1.8 %shard_map.96 = (f32[64,512]{1,0:T(8,128)S(1)}, f32[64,512]{1,0:T(8,128)S(1)}) custom-call(bf16[512,1024]{1,0:T(8,128)(2,1)} %act_hbm.1, bf16[64,1024]{1,0:T(8,128)(2,1)} %bitcast.6, s32[1,32]{1,0:T(1,128)} %len_hbm.1, s32[1,32]{1,0:T(1,128)} %bitcast.7), custom_call_target="tpu_custom_call" | custom-call | flops 1500000000 | tf_op jit(solution)/shard_map/pallas_call | solution.py:84
  6.6 1.6 %collective-permute-start = (f32[64,512]{1,0:T(8,128)S(1)}, f32[64,512]{1,0:T(8,128)S(1)}, u32[]{:S(2)}, u32[]{:S(2)}) collective-permute-start(f32[64,512]{1,0:T(8,128)S(1)} %get-tuple-element.14.refs_0_), channel_id=1, source_target_pairs={{0,2},{1,3},{2,0},{3,1},{4,6},{5,7},{6,4},{7,5},{8,10},{9,11},{10,... | collective-permute-start | bytes 393224 | tf_op jit(solution)/shard_map/ppermute | solution.py:291
  8.1 1.2 %shard_map.95 = (f32[32,512]{1,0:T(8,128)S(1)}, f32[32,512]{1,0:T(8,128)S(1)}) custom-call(bf16[512,3584]{1,0:T(8,128)(2,1)S(1)} %copy-done, bf16[64,3584]{1,0:T(8,128)(2,1)S(1)} %bitcast.4), custom_call_target="tpu_custom_call" | custom-call | tf_op jit(solution)/shard_map/pallas_call | solution.py:122
  9.4 0.6 %collective-permute-start.1 = (f32[32,512]{1,0:T(8,128)S(1)}, f32[32,512]{1,0:T(8,128)S(1)}, u32[]{:S(2)}, u32[]{:S(2)}) collective-permute-start(f32[32,512]{1,0:T(8,128)S(1)} %get-tuple-element.15), channel_id=1, source_target_pairs={{0,2},{1,3},{2,0},{3,1},{4,6},{5,7},{6,4},{7,5},{8,10},{9,11},{10,... | collective-permute-start | bytes 196616 | tf_op jit(solution)/shard_map/ppermute | solution.py:291
  10.0 1.6 %collective-permute-start.5 = (f32[32,1024]{1,0:T(8,128)S(1)}, f32[32,1024]{1,0:T(8,128)S(1)}, u32[]{:S(2)}, u32[]{:S(2)}) collective-permute-start(f32[32,1024]{1,0:T(8,128)S(1)} %copy-done.2), channel_id=1, source_target_pairs={{0,4},{4,0},{8,12},{12,8},{1,5},{5,1},{9,13},{13,9},{2,6},{6,2},{1... | collective-permute-start | bytes 393224 | tf_op jit(solution)/shard_map/ppermute | solution.py:291
  11.6 2.2 %collective-permute-done.1.refs_2_ = f32[32,512]{1,0:T(8,128)S(1)} collective-permute-done((f32[32,512]{1,0:T(8,128)S(1)}, f32[32,512]{1,0:T(8,128)S(1)}, u32[]{:S(2)}, u32[]{:S(2)}) %collective-permute-start.1) | collective-permute-done | bytes 65568 | tf_op jit(solution)/shard_map/ppermute | solution.py:291
  13.7 0.1 collective-permute-start.3
  13.8 0.5 %collective-permute-start.4 = (f32[40,512]{1,0:T(8,128)S(1)}, f32[40,512]{1,0:T(8,128)S(1)}, u32[]{:S(2)}, u32[]{:S(2)}) collective-permute-start(f32[40,512]{1,0:T(8,128)S(1)} %get-tuple-element.19.refs_1_), channel_id=1, source_target_pairs={{0,1},{1,0},{2,3},{3,2},{4,5},{5,4},{6,7},{7,6},{8,9},{9,8},{10,11... | collective-permute-start | bytes 245768 | tf_op jit(solution)/shard_map/ppermute | solution.py:291
  14.3 1.6 %collective-permute-start.9 = (f32[32,1024]{1,0:T(8,128)S(1)}, f32[32,1024]{1,0:T(8,128)S(1)}, u32[]{:S(2)}, u32[]{:S(2)}) collective-permute-start(f32[32,1024]{1,0:T(8,128)S(1)} %collective-permute-done.2.refs_0_.refs_5_), channel_id=1, source_target_pairs={{0,4},{4,0},{8,12},{12,8},{1,5},{5,1},{9,13},{13,9},{2,6},{6,2},{1... | collective-permute-start | bytes 393224 | tf_op jit(solution)/shard_map/ppermute | solution.py:291
  15.9 0.0 collective-permute-done.3.refs_2_
  15.9 0.8 %shard_map.99 = (f32[16,1024]{1,0:T(8,128)S(1)}, f32[16,1024]{1,0:T(8,128)S(1)}, f32[16,1024]{1,0:T(8,128)S(1)}, f32[16,1024]{1,0:T(8,128)S(1)}) custom-call(f32[16,512]{1,0:T(8,128)S(1)} %get-tuple-element.16.g_ref, f32[64,512]{1,0:T(8,128)S(1)} %get-tuple-element.17.mask_ref, f32[40,512]{1,0:T(8,128)S(1)} %get-tuple-element.18.refs_0_, ...), custom_call_target="tpu_custom_call" | custom-call | flops 268435456 | bytes 262144 | tf_op jit(solution)/shard_map/pallas_call | solution.py:196
  16.7 0.6 %collective-permute-start.7 = (f32[16,1024]{1,0:T(8,128)S(1)}, f32[16,1024]{1,0:T(8,128)S(1)}, u32[]{:S(2)}, u32[]{:S(2)}) collective-permute-start(f32[16,1024]{1,0:T(8,128)S(1)} %get-tuple-element.22), channel_id=1, source_target_pairs={{0,8},{4,12},{8,0},{12,4},{1,9},{5,13},{9,1},{13,5},{2,10},{6,14},... | collective-permute-start | bytes 196616 | tf_op jit(solution)/shard_map/ppermute | solution.py:291
  17.3 2.8 %collective-permute-start.8 = (f32[16,1024]{1,0:T(8,128)S(1)}, f32[16,1024]{1,0:T(8,128)S(1)}, u32[]{:S(2)}, u32[]{:S(2)}) collective-permute-start(f32[16,1024]{1,0:T(8,128)S(1)} %get-tuple-element.23), channel_id=1, source_target_pairs={{0,12},{4,8},{8,4},{12,0},{1,13},{5,9},{9,5},{13,1},{2,14},{6,10},... | collective-permute-start | bytes 196616 | tf_op jit(solution)/shard_map/ppermute | solution.py:291
  20.1 0.3 collective-permute-start.6
  20.4 4.7 %collective-permute-done.7.refs_2_.refs_1_ = f32[16,1024]{1,0:T(8,128)S(1)} collective-permute-done((f32[16,1024]{1,0:T(8,128)S(1)}, f32[16,1024]{1,0:T(8,128)S(1)}, u32[]{:S(2)}, u32[]{:S(2)}) %collective-permute-start.7) | collective-permute-done | bytes 65568 | tf_op jit(solution)/shard_map/ppermute | solution.py:291
  25.0 0.7 %collective-permute-done.6.refs_1_ = f32[16,1024]{1,0:T(8,128)S(1)} collective-permute-done((f32[16,1024]{1,0:T(8,128)S(1)}, f32[16,1024]{1,0:T(8,128)S(1)}, u32[]{:S(2)}, u32[]{:S(2)}) %collective-permute-start.6) | collective-permute-done | bytes 65568 | tf_op jit(solution)/shard_map/ppermute | solution.py:291
  25.8 0.4 %shard_map.103 = f32[64,128]{1,0:T(8,128)S(1)} custom-call(s32[1,128]{1,0:T(1,128)S(1)} %bitcast.5, f32[16,1024]{1,0:T(8,128)S(1)} %get-tuple-element.20.refs_0_, f32[16,1024]{1,0:T(8,128)S(1)} %collective-permute-done.6.refs_1_, f32[16,1024]{1,0:T(8,128)S(1)} %collective-permute-done.7.refs_2_.refs_1_, ...), custom_call_target="tpu_custom_call" | custom-call | flops 50331648 | bytes 524288 | tf_op jit(solution)/shard_map/pallas_call | solution.py:262
  26.2 0.1 collective-permute-start.10
  26.3 1.2 %collective-permute-done.10 = f32[64,128]{1,0:T(8,128)S(1)} collective-permute-done((f32[64,128]{1,0:T(8,128)S(1)}, f32[64,128]{1,0:T(8,128)S(1)}, u32[]{:S(2)}, u32[]{:S(2)}) %collective-permute-start.10) | collective-permute-done | bytes 32800 | tf_op jit(solution)/shard_map/ppermute | solution.py:291
  27.5 0.8 %collective-permute-start.11 = (f32[64,128]{1,0:T(8,128)S(1)}, f32[64,128]{1,0:T(8,128)S(1)}, u32[]{:S(2)}, u32[]{:S(2)}) collective-permute-start(f32[64,128]{1,0:T(8,128)S(1)} %add.6), channel_id=1, source_target_pairs={{0,2},{1,3},{2,0},{3,1},{4,6},{5,7},{6,4},{7,5},{8,10},{9,11},{10,... | collective-permute-start | bytes 98312 | tf_op jit(solution)/shard_map/ppermute | solution.py:291
  28.3 0.7 %shard_map.101 = f32[64,1024]{1,0:T(8,128)} custom-call(f32[16,1024]{1,0:T(8,128)S(1)} %get-tuple-element.20.refs_0_, f32[16,1024]{1,0:T(8,128)S(1)} %collective-permute-done.6.refs_1_, f32[16,1024]{1,0:T(8,128)S(1)} %collective-permute-done.7.refs_2_.refs_1_, f32[16,1024]{1,0:T(8,128)S(1)} %collective-permute-done.8.refs_3_.refs_0_), custom_call_target="tpu_custom_call" | custom-call | bytes 524288 | tf_op jit(solution)/shard_map/pallas_call | solution.py:282
  29.0 2.4 %collective-permute-done.11 = f32[64,128]{1,0:T(8,128)S(1)} collective-permute-done((f32[64,128]{1,0:T(8,128)S(1)}, f32[64,128]{1,0:T(8,128)S(1)}, u32[]{:S(2)}, u32[]{:S(2)}) %collective-permute-start.11) | collective-permute-done | bytes 32800 | tf_op jit(solution)/shard_map/ppermute | solution.py:291
  31.4 0.6 %add_multiply_fusion = f32[64,128]{1,0:T(8,128)} fusion(f32[64,128]{1,0:T(8,128)S(1)} %add.6, f32[64,128]{1,0:T(8,128)S(1)} %collective-permute-done.11), kind=kLoop, calls=%fused_computation | loop fusion | flops 16384 | bytes 98304 | tf_op jit(solution)/shard_map/mul | solution.py:349
  (19 shorter events, 0.1 us)
Async XLA Ops:
  0.6 7.5 %copy-start.1 = (bf16[3584,64]{0,1:T(8,128)(2,1)S(1)}, bf16[3584,64]{0,1:T(8,128)(2,1)}, u32[]{:S(2)}) copy-start(bf16[3584,64]{0,1:T(8,128)(2,1)} %param.11) | copy-start | bytes 1376260
  0.6 7.5 %copy-start = (bf16[512,3584]{1,0:T(8,128)(2,1)S(1)}, bf16[512,3584]{1,0:T(8,128)(2,1)}, u32[]{:S(2)}) copy-start(bf16[512,3584]{1,0:T(8,128)(2,1)} %grad_ref.1) | copy-start | bytes 11010052
  0.7 10.9 %collective-permute-start.2 = (f32[32,1024]{1,0:T(8,128)}, f32[32,1024]{1,0:T(8,128)S(1)}, u32[]{:S(2)}, u32[]{:S(2)}) collective-permute-start(f32[32,1024]{1,0:T(8,128)} %refs_4_.1), channel_id=1, source_target_pairs={{0,8},{4,12},{8,0},{12,4},{1,9},{5,13},{9,1},{13,5},{2,10},{6,14},... | collective-permute-start | bytes 393224 | tf_op jit(solution)/shard_map/ppermute | solution.py:291
  4.8 5.2 %copy-start.2 = (f32[32,1024]{1,0:T(8,128)S(1)}, f32[32,1024]{1,0:T(8,128)}, u32[]{:S(2)}) copy-start(f32[32,1024]{1,0:T(8,128)} %refs_4_.1) | copy-start | bytes 393220
  6.6 7.1 %collective-permute-start = (f32[64,512]{1,0:T(8,128)S(1)}, f32[64,512]{1,0:T(8,128)S(1)}, u32[]{:S(2)}, u32[]{:S(2)}) collective-permute-start(f32[64,512]{1,0:T(8,128)S(1)} %get-tuple-element.14.refs_0_), channel_id=1, source_target_pairs={{0,2},{1,3},{2,0},{3,1},{4,6},{5,7},{6,4},{7,5},{8,10},{9,11},{10,... | collective-permute-start | bytes 393224 | tf_op jit(solution)/shard_map/ppermute | solution.py:291
  8.1 17.6 %copy-start.3 = (s32[128]{0:T(128)S(1)}, s32[128]{0:T(128)}, u32[]{:S(2)}) copy-start(s32[128]{0:T(128)} %param.15) | copy-start | bytes 1540
  9.4 4.3 %collective-permute-start.1 = (f32[32,512]{1,0:T(8,128)S(1)}, f32[32,512]{1,0:T(8,128)S(1)}, u32[]{:S(2)}, u32[]{:S(2)}) collective-permute-start(f32[32,512]{1,0:T(8,128)S(1)} %get-tuple-element.15), channel_id=1, source_target_pairs={{0,2},{1,3},{2,0},{3,1},{4,6},{5,7},{6,4},{7,5},{8,10},{9,11},{10,... | collective-permute-start | bytes 196616 | tf_op jit(solution)/shard_map/ppermute | solution.py:291
  10.0 10.1 %collective-permute-start.5 = (f32[32,1024]{1,0:T(8,128)S(1)}, f32[32,1024]{1,0:T(8,128)S(1)}, u32[]{:S(2)}, u32[]{:S(2)}) collective-permute-start(f32[32,1024]{1,0:T(8,128)S(1)} %copy-done.2), channel_id=1, source_target_pairs={{0,4},{4,0},{8,12},{12,8},{1,5},{5,1},{9,13},{13,9},{2,6},{6,2},{1... | collective-permute-start | bytes 393224 | tf_op jit(solution)/shard_map/ppermute | solution.py:291
  13.7 2.1 %collective-permute-start.3 = (f32[40,512]{1,0:T(8,128)S(1)}, f32[40,512]{1,0:T(8,128)S(1)}, u32[]{:S(2)}, u32[]{:S(2)}) collective-permute-start(f32[40,512]{1,0:T(8,128)S(1)} %get-tuple-element.18.refs_0_), channel_id=1, source_target_pairs={{0,1},{1,0},{2,3},{3,2},{4,5},{5,4},{6,7},{7,6},{8,9},{9,8},{10,11... | collective-permute-start | bytes 245768 | tf_op jit(solution)/shard_map/ppermute | solution.py:291
  13.8 2.1 %collective-permute-start.4 = (f32[40,512]{1,0:T(8,128)S(1)}, f32[40,512]{1,0:T(8,128)S(1)}, u32[]{:S(2)}, u32[]{:S(2)}) collective-permute-start(f32[40,512]{1,0:T(8,128)S(1)} %get-tuple-element.19.refs_1_), channel_id=1, source_target_pairs={{0,1},{1,0},{2,3},{3,2},{4,5},{5,4},{6,7},{7,6},{8,9},{9,8},{10,11... | collective-permute-start | bytes 245768 | tf_op jit(solution)/shard_map/ppermute | solution.py:291
  14.3 10.7 %collective-permute-start.9 = (f32[32,1024]{1,0:T(8,128)S(1)}, f32[32,1024]{1,0:T(8,128)S(1)}, u32[]{:S(2)}, u32[]{:S(2)}) collective-permute-start(f32[32,1024]{1,0:T(8,128)S(1)} %collective-permute-done.2.refs_0_.refs_5_), channel_id=1, source_target_pairs={{0,4},{4,0},{8,12},{12,8},{1,5},{5,1},{9,13},{13,9},{2,6},{6,2},{1... | collective-permute-start | bytes 393224 | tf_op jit(solution)/shard_map/ppermute | solution.py:291
  16.7 8.3 %collective-permute-start.7 = (f32[16,1024]{1,0:T(8,128)S(1)}, f32[16,1024]{1,0:T(8,128)S(1)}, u32[]{:S(2)}, u32[]{:S(2)}) collective-permute-start(f32[16,1024]{1,0:T(8,128)S(1)} %get-tuple-element.22), channel_id=1, source_target_pairs={{0,8},{4,12},{8,0},{12,4},{1,9},{5,13},{9,1},{13,5},{2,10},{6,14},... | collective-permute-start | bytes 196616 | tf_op jit(solution)/shard_map/ppermute | solution.py:291
  17.3 7.7 %collective-permute-start.8 = (f32[16,1024]{1,0:T(8,128)S(1)}, f32[16,1024]{1,0:T(8,128)S(1)}, u32[]{:S(2)}, u32[]{:S(2)}) collective-permute-start(f32[16,1024]{1,0:T(8,128)S(1)} %get-tuple-element.23), channel_id=1, source_target_pairs={{0,12},{4,8},{8,4},{12,0},{1,13},{5,9},{9,5},{13,1},{2,14},{6,10},... | collective-permute-start | bytes 196616 | tf_op jit(solution)/shard_map/ppermute | solution.py:291
  20.1 5.7 %collective-permute-start.6 = (f32[16,1024]{1,0:T(8,128)S(1)}, f32[16,1024]{1,0:T(8,128)S(1)}, u32[]{:S(2)}, u32[]{:S(2)}) collective-permute-start(f32[16,1024]{1,0:T(8,128)S(1)} %shard_map.100), channel_id=1, source_target_pairs={{0,4},{4,0},{8,12},{12,8},{1,5},{5,1},{9,13},{13,9},{2,6},{6,2},{1... | collective-permute-start | bytes 196616 | tf_op jit(solution)/shard_map/ppermute | solution.py:291
  26.2 1.3 %collective-permute-start.10 = (f32[64,128]{1,0:T(8,128)S(1)}, f32[64,128]{1,0:T(8,128)S(1)}, u32[]{:S(2)}, u32[]{:S(2)}) collective-permute-start(f32[64,128]{1,0:T(8,128)S(1)} %shard_map.103), channel_id=1, source_target_pairs={{0,1},{1,0},{2,3},{3,2},{4,5},{5,4},{6,7},{7,6},{8,9},{9,8},{10,11... | collective-permute-start | bytes 98312 | tf_op jit(solution)/shard_map/ppermute | solution.py:291
  27.5 3.9 %collective-permute-start.11 = (f32[64,128]{1,0:T(8,128)S(1)}, f32[64,128]{1,0:T(8,128)S(1)}, u32[]{:S(2)}, u32[]{:S(2)}) collective-permute-start(f32[64,128]{1,0:T(8,128)S(1)} %add.6), channel_id=1, source_target_pairs={{0,2},{1,3},{2,0},{3,1},{4,6},{5,7},{6,4},{7,5},{8,10},{9,11},{10,... | collective-permute-start | bytes 98312 | tf_op jit(solution)/shard_map/ppermute | solution.py:291

commit v11 on v10

--- a/solution.py
+++ b/solution.py
@@ -12,6 +12,9 @@
 MIB = 1024 * 1024
 NT = (((1,), (1,)), ((), ()))
 MOST_DIRECT = 8
+FIRST_FLOPS = 10 * 10**8
+X_FLOPS = 6 * 10**8
+MASK_FLOPS = 2 * 10**8
 EARLY_FLOPS = 3 * 10**8
 LATE_FLOPS = 2 * 10**8
 
@@ -31,13 +34,6 @@
 
 def mm(a, b, dims=(((1,), (0,)), ((), ()))):
     return lax.dot_general(a, b, dims, preferred_element_type=F32)
-
-
-def copies(pairs, sems):
-    made = [pltpu.make_async_copy(src, dst, sems.at[i]) for i, (src, dst) in enumerate(pairs)]
-    for copy in made:
-        copy.start()
-    return made
 
 
 def slot_mask(owners, relative, cap, lengths, owner, slots, tokens):
@@ -63,47 +59,32 @@
     return jnp.where((token >= first) & (token < last), 1.0, 0.0)
 
 
-def x_kernel(
-    owners, relative, cap, act_hbm, in_hbm, len_hbm, own_hbm, x_ref, mask_ref,
-    act, proj_in, lens, owner, sems,
-):
-    pairs = [(in_hbm, proj_in), (act_hbm, act), (len_hbm, lens), (own_hbm, owner)]
-    in_copy, act_copy, len_copy, own_copy = copies(pairs, sems)
-    len_copy.wait()
-    own_copy.wait()
-    mask_ref[...] = slot_mask(owners, relative, cap, lens[...], owner[...], *mask_ref.shape)
-    in_copy.wait()
-    act_copy.wait()
-    x_ref[...] = mm(proj_in[...], act[...], NT)
-
-
-def project_x(act, in_t, lengths, owner_row, owners, cap, relative):
-    tokens, rank = act.shape[0], in_t.shape[0]
-    hbm = pl.BlockSpec(memory_space=pl.ANY)
-    vmem = pl.BlockSpec(memory_space=pltpu.VMEM)
-    return pl.pallas_call(
-        functools.partial(x_kernel, owners, relative, cap),
-        in_specs=[hbm] * 4,
-        out_specs=[vmem] * 2,
-        out_shape=[
-            jax.ShapeDtypeStruct((rank, tokens), F32),
-            jax.ShapeDtypeStruct((owners * cap, tokens), F32),
-        ],
-        scratch_shapes=[
-            pltpu.VMEM(act.shape, BF16),
-            pltpu.VMEM(in_t.shape, BF16),
-            pltpu.VMEM(lengths.shape, jnp.int32),
-            pltpu.VMEM(owner_row.shape, jnp.int32),
-            pltpu.SemaphoreType.DMA((4,)),
-        ],
-        compiler_params=params(24),
-        cost_estimate=cost(15 * 10**8, 0),
-    )(
-        *(
-            pltpu.with_memory_space_constraint(x, pltpu.HBM)
-            for x in (act, in_t, lengths, owner_row)
-        )
-    )
+def mask_kernel(owners, relative, cap, lengths_ref, owner_ref, mask_ref):
+    mask_ref[...] = slot_mask(owners, relative, cap, lengths_ref[...], owner_ref[...], *mask_ref.shape)
+
+
+def dispatch_mask(lengths, owner_row, owners, cap, tokens, relative):
+    return pl.pallas_call(
+        functools.partial(mask_kernel, owners, relative, cap),
+        out_shape=jax.ShapeDtypeStruct((owners * cap, tokens), F32),
+        compiler_params=params(8),
+        cost_estimate=cost(MASK_FLOPS, 0),
+    )(lengths, owner_row)
+
+
+def x_kernel(act_ref, proj_ref, *refs):
+    refs[-1][...] = mm(proj_ref[...], act_ref[...], NT)
+
+
+def project_x(act, in_t, tokens):
+    return pl.pallas_call(
+        x_kernel,
+        in_specs=[pl.BlockSpec(memory_space=pltpu.VMEM)] * 2
+        + [pl.BlockSpec(memory_space=pl.ANY)] * len(tokens),
+        out_shape=jax.ShapeDtypeStruct((in_t.shape[0], act.shape[0]), F32),
+        compiler_params=params(8),
+        cost_estimate=cost(X_FLOPS, 0),
+    )(act, in_t, *tokens)
 
 
 def g_kernel(width, grad_ref, proj_ref, keep_ref, send_ref, full):
@@ -319,13 +300,12 @@
     else:
         pieces, gaps = [lax.all_gather(query_grads, "dp", axis=0, tiled=True)], [0]
 
-    x, mask = project_x(
-        activations, proj_in.T, doc_lengths, doc_owner.T, data_size, cap, direct
-    )
+    mask = dispatch_mask(doc_lengths, doc_owner.T, data_size, cap, activations.shape[0], direct)
+    x = project_x(activations, proj_in.T, [token([], FIRST_FLOPS)])
     bit = tensor_size // 2
     x_got = swap(x, "tensor", bit)
     keep, send = project_g(out_grads, proj_out.T, width)
-    early = [token(pieces[1:], EARLY_FLOPS)] if direct else []
+    early = [mask] + ([token(pieces[1:], EARLY_FLOPS)] if direct else [])
     own, gots = [x], [x_got, swap(send, "tensor", bit)]
     while bit > 1:
         bit //= 2

time: 32.2 us -> 31 us (0.963)
  Pallas kernels: 5.09 us -> 3.91 us
    pallas_call x1 -> x2, Pallas kernels: 1.81 us -> 0.64 us  [the longest x1 0.44 us: project_x(): pl.pallas_call(x_kernel, in_specs=[pl.BlockSpec(memory_space=pltpu.VMEM)]...]
  transfers between devices with their start and end apart: 12 -> 12, of which waited for: 5 -> 6; matrix products, arithmetic and copies ran while one was open for 0% -> 0% of each run, Pallas kernels for 15% -> 11%
where the time goes in v11:
time: 31 us; the launch traced here: 30.8 us
  starting transfers between devices  14.4 us (46%)
  waiting for transfers between devices  11.1 us (36%)
  Pallas kernels  3.91 us (13%)
  between operations  0.75 us (2%)
  other arithmetic  0.63 us (2%)
    ppermute x12, starting transfers between devices, swap(): lax.ppermute(x, axis, [(i, i ^ gap) for i in range(lax.axis_size(axis))])  14.4 us
    ppermute x12, waiting for transfers between devices, swap(): lax.ppermute(x, axis, [(i, i ^ gap) for i in range(lax.axis_size(axis))])  11.1 us
    pallas_call x1, Pallas kernels, project_g(): pl.pallas_call(functools.partial(g_kernel, width), out_shape=[part, part]...  1.23 us
    pallas_call x1, Pallas kernels, outer(): pl.pallas_call(functools.partial(outer_kernel, owners, len(sent)), out_sh...  0.85 us
    pallas_call x1, Pallas kernels, place(): pl.pallas_call(place_kernel, out_shape=jax.ShapeDtypeStruct((slots, feats...  0.73 us
    mul x1, other arithmetic, local(): return (store, scores * (1.0 / (rank * rank)))  0.62 us
  transfers between devices with their start and end apart: 12, of which 6 were waited for; matrix products, arithmetic and copies ran while one was open for 0% of the time, Pallas kernels for 11%

profile of v11, /device:TPU:0, one launch (start us, length us, event | category | flops | bytes accessed | tf_op | source)
XLA Modules:
  0.0 30.8 jit_solution(809605069771396411)
XLA Ops:
  0.7 4.1 %collective-permute-start.2 = (f32[32,1024]{1,0:T(8,128)}, f32[32,1024]{1,0:T(8,128)S(1)}, u32[]{:S(2)}, u32[]{:S(2)}) collective-permute-start(f32[32,1024]{1,0:T(8,128)} %refs_4_.1), channel_id=1, source_target_pairs={{0,8},{4,12},{8,0},{12,4},{1,9},{5,13},{9,1},{13,5},{2,10},{6,14},... | collective-permute-start | bytes 393224 | tf_op jit(solution)/shard_map/ppermute | solution.py:272
  4.8 0.4 %shard_map.97.refs_0_ = f32[64,512]{1,0:T(8,128)S(1)} custom-call(bf16[512,1024]{1,0:T(8,128)(2,1)S(1)} %copy-done.4, bf16[64,1024]{1,0:T(8,128)(2,1)S(1)} %bitcast.6, f32[8,128]{1,0:T(8,128)S(1)} %shard_map.96.refs_0_), custom_call_target="tpu_custom_call" | custom-call | flops 600000000 | tf_op jit(solution)/shard_map/pallas_call | solution.py:80
  5.2 1.6 %collective-permute-start = (f32[64,512]{1,0:T(8,128)S(1)}, f32[64,512]{1,0:T(8,128)S(1)}, u32[]{:S(2)}, u32[]{:S(2)}) collective-permute-start(f32[64,512]{1,0:T(8,128)S(1)} %shard_map.97.refs_0_), channel_id=1, source_target_pairs={{0,2},{1,3},{2,0},{3,1},{4,6},{5,7},{6,4},{7,5},{8,10},{9,11},{10,... | collective-permute-start | bytes 393224 | tf_op jit(solution)/shard_map/ppermute | solution.py:272
  6.8 1.2 %shard_map.95 = (f32[32,512]{1,0:T(8,128)S(1)}, f32[32,512]{1,0:T(8,128)S(1)}) custom-call(bf16[512,3584]{1,0:T(8,128)(2,1)S(1)} %copy-done, bf16[64,3584]{1,0:T(8,128)(2,1)S(1)} %bitcast.4), custom_call_target="tpu_custom_call" | custom-call | tf_op jit(solution)/shard_map/pallas_call | solution.py:103
  8.0 0.6 %collective-permute-start.1 = (f32[32,512]{1,0:T(8,128)S(1)}, f32[32,512]{1,0:T(8,128)S(1)}, u32[]{:S(2)}, u32[]{:S(2)}) collective-permute-start(f32[32,512]{1,0:T(8,128)S(1)} %get-tuple-element.12), channel_id=1, source_target_pairs={{0,2},{1,3},{2,0},{3,1},{4,6},{5,7},{6,4},{7,5},{8,10},{9,11},{10,... | collective-permute-start | bytes 196616 | tf_op jit(solution)/shard_map/ppermute | solution.py:272
  8.7 1.6 %collective-permute-start.5 = (f32[32,1024]{1,0:T(8,128)S(1)}, f32[32,1024]{1,0:T(8,128)S(1)}, u32[]{:S(2)}, u32[]{:S(2)}) collective-permute-start(f32[32,1024]{1,0:T(8,128)S(1)} %copy-done.2), channel_id=1, source_target_pairs={{0,4},{4,0},{8,12},{12,8},{1,5},{5,1},{9,13},{13,9},{2,6},{6,2},{1... | collective-permute-start | bytes 393224 | tf_op jit(solution)/shard_map/ppermute | solution.py:272
  10.2 0.2 shard_map.98.refs_3_.mask_ref
  10.4 1.0 %collective-permute-done.2.refs_0_.refs_5_ = f32[32,1024]{1,0:T(8,128)S(1)} collective-permute-done((f32[32,1024]{1,0:T(8,128)}, f32[32,1024]{1,0:T(8,128)S(1)}, u32[]{:S(2)}, u32[]{:S(2)}) %collective-permute-start.2) | collective-permute-done | bytes 131104 | tf_op jit(solution)/shard_map/ppermute | solution.py:272
  11.4 1.0 %collective-permute-done.1.refs_2_ = f32[32,512]{1,0:T(8,128)S(1)} collective-permute-done((f32[32,512]{1,0:T(8,128)S(1)}, f32[32,512]{1,0:T(8,128)S(1)}, u32[]{:S(2)}, u32[]{:S(2)}) %collective-permute-start.1) | collective-permute-done | bytes 65568 | tf_op jit(solution)/shard_map/ppermute | solution.py:272
  12.5 0.5 %collective-permute-start.4 = (f32[40,512]{1,0:T(8,128)S(1)}, f32[40,512]{1,0:T(8,128)S(1)}, u32[]{:S(2)}, u32[]{:S(2)}) collective-permute-start(f32[40,512]{1,0:T(8,128)S(1)} %get-tuple-element.15.refs_1_), channel_id=1, source_target_pairs={{0,1},{1,0},{2,3},{3,2},{4,5},{5,4},{6,7},{7,6},{8,9},{9,8},{10,11... | collective-permute-start | bytes 245768 | tf_op jit(solution)/shard_map/ppermute | solution.py:272
  13.0 1.6 %collective-permute-start.9 = (f32[32,1024]{1,0:T(8,128)S(1)}, f32[32,1024]{1,0:T(8,128)S(1)}, u32[]{:S(2)}, u32[]{:S(2)}) collective-permute-start(f32[32,1024]{1,0:T(8,128)S(1)} %collective-permute-done.2.refs_0_.refs_5_), channel_id=1, source_target_pairs={{0,4},{4,0},{8,12},{12,8},{1,5},{5,1},{9,13},{13,9},{2,6},{6,2},{1... | collective-permute-start | bytes 393224 | tf_op jit(solution)/shard_map/ppermute | solution.py:272
  14.6 0.8 %shard_map.101 = (f32[16,1024]{1,0:T(8,128)S(1)}, f32[16,1024]{1,0:T(8,128)S(1)}, f32[16,1024]{1,0:T(8,128)S(1)}, f32[16,1024]{1,0:T(8,128)S(1)}) custom-call(f32[16,512]{1,0:T(8,128)S(1)} %get-tuple-element.13.g_ref, f32[64,512]{1,0:T(8,128)S(1)} %shard_map.98.refs_3_.mask_ref, f32[40,512]{1,0:T(8,128)S(1)} %get-tuple-element.14.refs_0_, ...), custom_call_target="tpu_custom_call" | custom-call | flops 268435456 | bytes 262144 | tf_op jit(solution)/shard_map/pallas_call | solution.py:177
  15.4 1.6 %collective-permute-start.7 = (f32[16,1024]{1,0:T(8,128)S(1)}, f32[16,1024]{1,0:T(8,128)S(1)}, u32[]{:S(2)}, u32[]{:S(2)}) collective-permute-start(f32[16,1024]{1,0:T(8,128)S(1)} %get-tuple-element.18), channel_id=1, source_target_pairs={{0,8},{4,12},{8,0},{12,4},{1,9},{5,13},{9,1},{13,5},{2,10},{6,14},... | collective-permute-start | bytes 196616 | tf_op jit(solution)/shard_map/ppermute | solution.py:272
  17.0 1.7 %collective-permute-start.8 = (f32[16,1024]{1,0:T(8,128)S(1)}, f32[16,1024]{1,0:T(8,128)S(1)}, u32[]{:S(2)}, u32[]{:S(2)}) collective-permute-start(f32[16,1024]{1,0:T(8,128)S(1)} %get-tuple-element.19), channel_id=1, source_target_pairs={{0,12},{4,8},{8,4},{12,0},{1,13},{5,9},{9,5},{13,1},{2,14},{6,10},... | collective-permute-start | bytes 196616 | tf_op jit(solution)/shard_map/ppermute | solution.py:272
  18.8 0.3 collective-permute-start.6
  19.0 4.8 %collective-permute-done.7.refs_2_.refs_1_ = f32[16,1024]{1,0:T(8,128)S(1)} collective-permute-done((f32[16,1024]{1,0:T(8,128)S(1)}, f32[16,1024]{1,0:T(8,128)S(1)}, u32[]{:S(2)}, u32[]{:S(2)}) %collective-permute-start.7) | collective-permute-done | bytes 65568 | tf_op jit(solution)/shard_map/ppermute | solution.py:272
  23.9 0.7 %collective-permute-done.6.refs_1_ = f32[16,1024]{1,0:T(8,128)S(1)} collective-permute-done((f32[16,1024]{1,0:T(8,128)S(1)}, f32[16,1024]{1,0:T(8,128)S(1)}, u32[]{:S(2)}, u32[]{:S(2)}) %collective-permute-start.6) | collective-permute-done | bytes 65568 | tf_op jit(solution)/shard_map/ppermute | solution.py:272
  24.6 0.4 %shard_map.105 = f32[64,128]{1,0:T(8,128)S(1)} custom-call(s32[1,128]{1,0:T(1,128)S(1)} %bitcast.5, f32[16,1024]{1,0:T(8,128)S(1)} %get-tuple-element.16.refs_0_, f32[16,1024]{1,0:T(8,128)S(1)} %collective-permute-done.6.refs_1_, f32[16,1024]{1,0:T(8,128)S(1)} %collective-permute-done.7.refs_2_.refs_1_, ...), custom_call_target="tpu_custom_call" | custom-call | flops 50331648 | bytes 524288 | tf_op jit(solution)/shard_map/pallas_call | solution.py:243
  25.0 0.1 collective-permute-start.10
  25.1 1.2 %collective-permute-done.10 = f32[64,128]{1,0:T(8,128)S(1)} collective-permute-done((f32[64,128]{1,0:T(8,128)S(1)}, f32[64,128]{1,0:T(8,128)S(1)}, u32[]{:S(2)}, u32[]{:S(2)}) %collective-permute-start.10) | collective-permute-done | bytes 32800 | tf_op jit(solution)/shard_map/ppermute | solution.py:272
  26.3 0.7 %collective-permute-start.11 = (f32[64,128]{1,0:T(8,128)S(1)}, f32[64,128]{1,0:T(8,128)S(1)}, u32[]{:S(2)}, u32[]{:S(2)}) collective-permute-start(f32[64,128]{1,0:T(8,128)S(1)} %add.6), channel_id=1, source_target_pairs={{0,2},{1,3},{2,0},{3,1},{4,6},{5,7},{6,4},{7,5},{8,10},{9,11},{10,... | collective-permute-start | bytes 98312 | tf_op jit(solution)/shard_map/ppermute | solution.py:272
  27.0 0.7 %shard_map.103 = f32[64,1024]{1,0:T(8,128)} custom-call(f32[16,1024]{1,0:T(8,128)S(1)} %get-tuple-element.16.refs_0_, f32[16,1024]{1,0:T(8,128)S(1)} %collective-permute-done.6.refs_1_, f32[16,1024]{1,0:T(8,128)S(1)} %collective-permute-done.7.refs_2_.refs_1_, f32[16,1024]{1,0:T(8,128)S(1)} %collective-permute-done.8.refs_3_.refs_0_), custom_call_target="tpu_custom_call" | custom-call | bytes 524288 | tf_op jit(solution)/shard_map/pallas_call | solution.py:263
  27.7 2.5 %collective-permute-done.11 = f32[64,128]{1,0:T(8,128)S(1)} collective-permute-done((f32[64,128]{1,0:T(8,128)S(1)}, f32[64,128]{1,0:T(8,128)S(1)}, u32[]{:S(2)}, u32[]{:S(2)}) %collective-permute-start.11) | collective-permute-done | bytes 32800 | tf_op jit(solution)/shard_map/ppermute | solution.py:272
  30.2 0.6 %add_multiply_fusion = f32[64,128]{1,0:T(8,128)} fusion(f32[64,128]{1,0:T(8,128)S(1)} %add.6, f32[64,128]{1,0:T(8,128)S(1)} %collective-permute-done.11), kind=kLoop, calls=%fused_computation | loop fusion | flops 16384 | bytes 98304 | tf_op jit(solution)/shard_map/mul | solution.py:329
  (29 shorter events, 0.2 us)
Async XLA Ops:
  0.6 4.2 %copy-start.5 = (bf16[1024,64]{0,1:T(8,128)(2,1)S(1)}, bf16[1024,64]{0,1:T(8,128)(2,1)}, u32[]{:S(2)}) copy-start(bf16[1024,64]{0,1:T(8,128)(2,1)} %param.10) | copy-start | bytes 393220
  0.6 4.2 %copy-start.4 = (bf16[512,1024]{1,0:T(8,128)(2,1)S(1)}, bf16[512,1024]{1,0:T(8,128)(2,1)}, u32[]{:S(2)}) copy-start(bf16[512,1024]{1,0:T(8,128)(2,1)} %act_ref.1) | copy-start | bytes 3145732
  0.7 6.2 %copy-start.1 = (bf16[3584,64]{0,1:T(8,128)(2,1)S(1)}, bf16[3584,64]{0,1:T(8,128)(2,1)}, u32[]{:S(2)}) copy-start(bf16[3584,64]{0,1:T(8,128)(2,1)} %param.11) | copy-start | bytes 1376260
  0.7 6.1 %copy-start = (bf16[512,3584]{1,0:T(8,128)(2,1)S(1)}, bf16[512,3584]{1,0:T(8,128)(2,1)}, u32[]{:S(2)}) copy-start(bf16[512,3584]{1,0:T(8,128)(2,1)} %grad_ref.1) | copy-start | bytes 11010052
  0.7 10.7 %collective-permute-start.2 = (f32[32,1024]{1,0:T(8,128)}, f32[32,1024]{1,0:T(8,128)S(1)}, u32[]{:S(2)}, u32[]{:S(2)}) collective-permute-start(f32[32,1024]{1,0:T(8,128)} %refs_4_.1), channel_id=1, source_target_pairs={{0,8},{4,12},{8,0},{12,4},{1,9},{5,13},{9,1},{13,5},{2,10},{6,14},... | collective-permute-start | bytes 393224 | tf_op jit(solution)/shard_map/ppermute | solution.py:272
  4.8 3.9 %copy-start.2 = (f32[32,1024]{1,0:T(8,128)S(1)}, f32[32,1024]{1,0:T(8,128)}, u32[]{:S(2)}) copy-start(f32[32,1024]{1,0:T(8,128)} %refs_4_.1) | copy-start | bytes 393220
  4.8 5.5 %copy-start.6 = (s32[1,32]{1,0:T(1,128)S(1)}, s32[1,32]{1,0:T(1,128)}, u32[]{:S(2)}) copy-start(s32[1,32]{1,0:T(1,128)} %lengths_ref.1) | copy-start | bytes 388
  4.8 5.5 %copy-start.7 = (s32[32,1]{0,1:T(1,128)S(1)}, s32[32,1]{0,1:T(1,128)}, u32[]{:S(2)}) copy-start(s32[32,1]{0,1:T(1,128)} %param.13) | copy-start | bytes 388
  5.2 7.1 %collective-permute-start = (f32[64,512]{1,0:T(8,128)S(1)}, f32[64,512]{1,0:T(8,128)S(1)}, u32[]{:S(2)}, u32[]{:S(2)}) collective-permute-start(f32[64,512]{1,0:T(8,128)S(1)} %shard_map.97.refs_0_), channel_id=1, source_target_pairs={{0,2},{1,3},{2,0},{3,1},{4,6},{5,7},{6,4},{7,5},{8,10},{9,11},{10,... | collective-permute-start | bytes 393224 | tf_op jit(solution)/shard_map/ppermute | solution.py:272
  6.8 17.8 %copy-start.3 = (s32[128]{0:T(128)S(1)}, s32[128]{0:T(128)}, u32[]{:S(2)}) copy-start(s32[128]{0:T(128)} %param.15) | copy-start | bytes 1540
  8.0 4.3 %collective-permute-start.1 = (f32[32,512]{1,0:T(8,128)S(1)}, f32[32,512]{1,0:T(8,128)S(1)}, u32[]{:S(2)}, u32[]{:S(2)}) collective-permute-start(f32[32,512]{1,0:T(8,128)S(1)} %get-tuple-element.12), channel_id=1, source_target_pairs={{0,2},{1,3},{2,0},{3,1},{4,6},{5,7},{6,4},{7,5},{8,10},{9,11},{10,... | collective-permute-start | bytes 196616 | tf_op jit(solution)/shard_map/ppermute | solution.py:272
  8.7 10.1 %collective-permute-start.5 = (f32[32,1024]{1,0:T(8,128)S(1)}, f32[32,1024]{1,0:T(8,128)S(1)}, u32[]{:S(2)}, u32[]{:S(2)}) collective-permute-start(f32[32,1024]{1,0:T(8,128)S(1)} %copy-done.2), channel_id=1, source_target_pairs={{0,4},{4,0},{8,12},{12,8},{1,5},{5,1},{9,13},{13,9},{2,6},{6,2},{1... | collective-permute-start | bytes 393224 | tf_op jit(solution)/shard_map/ppermute | solution.py:272
  12.4 2.2 %collective-permute-start.3 = (f32[40,512]{1,0:T(8,128)S(1)}, f32[40,512]{1,0:T(8,128)S(1)}, u32[]{:S(2)}, u32[]{:S(2)}) collective-permute-start(f32[40,512]{1,0:T(8,128)S(1)} %get-tuple-element.14.refs_0_), channel_id=1, source_target_pairs={{0,1},{1,0},{2,3},{3,2},{4,5},{5,4},{6,7},{7,6},{8,9},{9,8},{10,11... | collective-permute-start | bytes 245768 | tf_op jit(solution)/shard_map/ppermute | solution.py:272
  12.5 2.1 %collective-permute-start.4 = (f32[40,512]{1,0:T(8,128)S(1)}, f32[40,512]{1,0:T(8,128)S(1)}, u32[]{:S(2)}, u32[]{:S(2)}) collective-permute-start(f32[40,512]{1,0:T(8,128)S(1)} %get-tuple-element.15.refs_1_), channel_id=1, source_target_pairs={{0,1},{1,0},{2,3},{3,2},{4,5},{5,4},{6,7},{7,6},{8,9},{9,8},{10,11... | collective-permute-start | bytes 245768 | tf_op jit(solution)/shard_map/ppermute | solution.py:272
  13.0 10.9 %collective-permute-start.9 = (f32[32,1024]{1,0:T(8,128)S(1)}, f32[32,1024]{1,0:T(8,128)S(1)}, u32[]{:S(2)}, u32[]{:S(2)}) collective-permute-start(f32[32,1024]{1,0:T(8,128)S(1)} %collective-permute-done.2.refs_0_.refs_5_), channel_id=1, source_target_pairs={{0,4},{4,0},{8,12},{12,8},{1,5},{5,1},{9,13},{13,9},{2,6},{6,2},{1... | collective-permute-start | bytes 393224 | tf_op jit(solution)/shard_map/ppermute | solution.py:272
  15.4 8.5 %collective-permute-start.7 = (f32[16,1024]{1,0:T(8,128)S(1)}, f32[16,1024]{1,0:T(8,128)S(1)}, u32[]{:S(2)}, u32[]{:S(2)}) collective-permute-start(f32[16,1024]{1,0:T(8,128)S(1)} %get-tuple-element.18), channel_id=1, source_target_pairs={{0,8},{4,12},{8,0},{12,4},{1,9},{5,13},{9,1},{13,5},{2,10},{6,14},... | collective-permute-start | bytes 196616 | tf_op jit(solution)/shard_map/ppermute | solution.py:272
  17.0 6.9 %collective-permute-start.8 = (f32[16,1024]{1,0:T(8,128)S(1)}, f32[16,1024]{1,0:T(8,128)S(1)}, u32[]{:S(2)}, u32[]{:S(2)}) collective-permute-start(f32[16,1024]{1,0:T(8,128)S(1)} %get-tuple-element.19), channel_id=1, source_target_pairs={{0,12},{4,8},{8,4},{12,0},{1,13},{5,9},{9,5},{13,1},{2,14},{6,10},... | collective-permute-start | bytes 196616 | tf_op jit(solution)/shard_map/ppermute | solution.py:272
  18.8 5.8 %collective-permute-start.6 = (f32[16,1024]{1,0:T(8,128)S(1)}, f32[16,1024]{1,0:T(8,128)S(1)}, u32[]{:S(2)}, u32[]{:S(2)}) collective-permute-start(f32[16,1024]{1,0:T(8,128)S(1)} %shard_map.102), channel_id=1, source_target_pairs={{0,4},{4,0},{8,12},{12,8},{1,5},{5,1},{9,13},{13,9},{2,6},{6,2},{1... | collective-permute-start | bytes 196616 | tf_op jit(solution)/shard_map/ppermute | solution.py:272
  25.0 1.3 %collective-permute-start.10 = (f32[64,128]{1,0:T(8,128)S(1)}, f32[64,128]{1,0:T(8,128)S(1)}, u32[]{:S(2)}, u32[]{:S(2)}) collective-permute-start(f32[64,128]{1,0:T(8,128)S(1)} %shard_map.105), channel_id=1, source_target_pairs={{0,1},{1,0},{2,3},{3,2},{4,5},{5,4},{6,7},{7,6},{8,9},{9,8},{10,11... | collective-permute-start | bytes 98312 | tf_op jit(solution)/shard_map/ppermute | solution.py:272
  26.3 3.9 %collective-permute-start.11 = (f32[64,128]{1,0:T(8,128)S(1)}, f32[64,128]{1,0:T(8,128)S(1)}, u32[]{:S(2)}, u32[]{:S(2)}) collective-permute-start(f32[64,128]{1,0:T(8,128)S(1)} %add.6), channel_id=1, source_target_pairs={{0,2},{1,3},{2,0},{3,1},{4,6},{5,7},{6,4},{7,5},{8,10},{9,11},{10,... | collective-permute-start | bytes 98312 | tf_op jit(solution)/shard_map/ppermute | solution.py:272

commit v12 on v11

--- a/solution.py
+++ b/solution.py
@@ -143,7 +143,7 @@
     return keep, sent
 
 
-def outer_kernel(owners, sent, g_ref, mask_ref, *refs):
+def outer_kernel(first, owners, sent, g_ref, mask_ref, *refs):
     blocks = refs[-owners:]
     width = g_ref.shape[0]
     own, got = stack(refs[:sent]), stack(refs[sent : 2 * sent])
@@ -153,13 +153,13 @@
     x_both = jnp.concatenate(halves(x_full), axis=0)
     g_high = g_full.astype(BF16).astype(F32)
     g_low = g_full - g_high
-    mask = mask_ref[...]
     cap = blocks[0].shape[0]
+    slots = owners * cap
+    mask = mask_ref[first * cap : first * cap + slots, :]
 
     def product(i):
         pair = [(mask * g[i : i + 1, :]).astype(BF16) for g in (g_high, g_low)]
         both = mm(jnp.concatenate(pair, axis=0), x_both, NT)
-        slots = mask.shape[0]
         return both[:slots, :rank] + both[:slots, rank:] + both[slots:, :rank]
 
     step = max(1, 128 // rank)
@@ -169,16 +169,14 @@
             block[:, i * rank : (i + step) * rank] = columns[k * cap : (k + 1) * cap, :]
 
 
-def outer(sent, gots, g, mask, owners):
-    slots, tokens = mask.shape
+def outer(sent, gots, g, mask, cap, first, owners):
     width = g.shape[0]
     rank = sum(p.shape[0] for p in sent) - width
-    cap = slots // owners
-    return pl.pallas_call(
-        functools.partial(outer_kernel, owners, len(sent)),
+    return pl.pallas_call(
+        functools.partial(outer_kernel, first, owners, len(sent)),
         out_shape=[jax.ShapeDtypeStruct((cap, width * rank), F32)] * owners,
         compiler_params=params(24),
-        cost_estimate=cost(8 * slots * width * tokens * rank, 4 * slots * width * rank),
+        cost_estimate=cost(8 * owners * cap * width * mask.shape[1] * rank, 0),
     )(g, mask, *sent, *gots)
 
 
@@ -311,14 +309,18 @@
         bit //= 2
         keep, own = fold(rank, keep, own, gots, early)
         gots = [swap(part, "tensor", bit) for part in own]
-    blocks = outer(own, gots, keep, mask, data_size)
     if direct:
-        far = [swap(blocks[k], "dp", k) for k in range(data_size - 1, 1, -1)]
-        rows = [blocks[0], swap(after(blocks[1], mate), "dp", 1), *far[::-1]]
+        split = max(1, data_size // 2)
+        blocks = outer(own, gots, keep, mask, cap, split, data_size - split)
+        far = [swap(blocks[k - split], "dp", k) for k in range(data_size - 1, split - 1, -1)]
+        blocks = outer(own, gots, keep, mask, cap, 0, split)
+        rows = [swap(after(blocks[k], mate), "dp", k) for k in range(1, split)]
+        rows = [blocks[0], *rows, *far[::-1]]
         late = [token(far, LATE_FLOPS)]
         pieces, gaps = [*pieces, mate, *passed], [*gaps, *(g ^ 1 for g in gaps)]
         store = place(rows)
     else:
+        blocks = outer(own, gots, keep, mask, cap, 0, data_size)
         rows = [lax.all_to_all(jnp.stack(blocks), "dp", 0, 0, tiled=True).reshape(-1, width * rank)]
         store, late = rows[0], []
     scores = score(query_ids[None, :], rows, pieces, gaps, direct, late)

time: 31 us -> 31.3 us (level)
  Pallas kernels: 3.91 us -> 4.98 us
  waiting for transfers between devices: 11.1 us -> 10.2 us
    pallas_call x1 -> x2, Pallas kernels: 0.85 us -> 1.91 us  [outer(): pl.pallas_call(functools.partial(outer_kernel, first, owners, len(sent)),...]
    ppermute x12, waiting for transfers between devices: 11.1 us -> 10.2 us  [swap(): lax.ppermute(x, axis, [(i, i ^ gap) for i in range(lax.axis_size(axis))])]
  transfers between devices with their start and end apart: 12 -> 12, of which waited for: 6 -> 6; matrix products, arithmetic and copies ran while one was open for 0% -> 0% of each run, Pallas kernels for 11% -> 15%
where the time goes in v12:
time: 31.3 us; the launch traced here: 31.1 us
  starting transfers between devices  14.5 us (46%)
  waiting for transfers between devices  10.2 us (33%)
  Pallas kernels  4.98 us (16%)
  between operations  0.76 us (2%)
  other arithmetic  0.63 us (2%)
    ppermute x12, starting transfers between devices, swap(): lax.ppermute(x, axis, [(i, i ^ gap) for i in range(lax.axis_size(axis))])  14.5 us
    ppermute x12, waiting for transfers between devices, swap(): lax.ppermute(x, axis, [(i, i ^ gap) for i in range(lax.axis_size(axis))])  10.2 us
    pallas_call x2, Pallas kernels, outer(): pl.pallas_call(functools.partial(outer_kernel, first, owners, len(sent)),...  1.91 us
    pallas_call x1, Pallas kernels, project_g(): pl.pallas_call(functools.partial(g_kernel, width), out_shape=[part, part]...  1.23 us
    pallas_call x1, Pallas kernels, place(): pl.pallas_call(place_kernel, out_shape=jax.ShapeDtypeStruct((slots, feats...  0.73 us
  transfers between devices with their start and end apart: 12, of which 6 were waited for; matrix products, arithmetic and copies ran while one was open for 0% of the time, Pallas kernels for 15%

profile of v12, /device:TPU:0, one launch (start us, length us, event | category | flops | bytes accessed | tf_op | source)
XLA Modules:
  0.0 31.1 jit_solution(11314350345003578364)
XLA Ops:
  0.7 4.1 %collective-permute-start.2 = (f32[32,1024]{1,0:T(8,128)}, f32[32,1024]{1,0:T(8,128)S(1)}, u32[]{:S(2)}, u32[]{:S(2)}) collective-permute-start(f32[32,1024]{1,0:T(8,128)} %refs_4_.1), channel_id=1, source_target_pairs={{0,8},{4,12},{8,0},{12,4},{1,9},{5,13},{9,1},{13,5},{2,10},{6,14},... | collective-permute-start | bytes 393224 | tf_op jit(solution)/shard_map/ppermute | solution.py:270
  4.8 0.4 %shard_map.97.refs_0_ = f32[64,512]{1,0:T(8,128)S(1)} custom-call(bf16[512,1024]{1,0:T(8,128)(2,1)S(1)} %copy-done.4, bf16[64,1024]{1,0:T(8,128)(2,1)S(1)} %bitcast.6, f32[8,128]{1,0:T(8,128)S(1)} %shard_map.96.refs_0_), custom_call_target="tpu_custom_call" | custom-call | flops 600000000 | tf_op jit(solution)/shard_map/pallas_call | solution.py:80
  5.2 1.6 %collective-permute-start = (f32[64,512]{1,0:T(8,128)S(1)}, f32[64,512]{1,0:T(8,128)S(1)}, u32[]{:S(2)}, u32[]{:S(2)}) collective-permute-start(f32[64,512]{1,0:T(8,128)S(1)} %shard_map.97.refs_0_), channel_id=1, source_target_pairs={{0,2},{1,3},{2,0},{3,1},{4,6},{5,7},{6,4},{7,5},{8,10},{9,11},{10,... | collective-permute-start | bytes 393224 | tf_op jit(solution)/shard_map/ppermute | solution.py:270
  6.8 1.2 %shard_map.95 = (f32[32,512]{1,0:T(8,128)S(1)}, f32[32,512]{1,0:T(8,128)S(1)}) custom-call(bf16[512,3584]{1,0:T(8,128)(2,1)S(1)} %copy-done, bf16[64,3584]{1,0:T(8,128)(2,1)S(1)} %bitcast.4), custom_call_target="tpu_custom_call" | custom-call | tf_op jit(solution)/shard_map/pallas_call | solution.py:103
  8.0 0.6 %collective-permute-start.1 = (f32[32,512]{1,0:T(8,128)S(1)}, f32[32,512]{1,0:T(8,128)S(1)}, u32[]{:S(2)}, u32[]{:S(2)}) collective-permute-start(f32[32,512]{1,0:T(8,128)S(1)} %get-tuple-element.12), channel_id=1, source_target_pairs={{0,2},{1,3},{2,0},{3,1},{4,6},{5,7},{6,4},{7,5},{8,10},{9,11},{10,... | collective-permute-start | bytes 196616 | tf_op jit(solution)/shard_map/ppermute | solution.py:270
  8.7 1.6 %collective-permute-start.5 = (f32[32,1024]{1,0:T(8,128)S(1)}, f32[32,1024]{1,0:T(8,128)S(1)}, u32[]{:S(2)}, u32[]{:S(2)}) collective-permute-start(f32[32,1024]{1,0:T(8,128)S(1)} %copy-done.2), channel_id=1, source_target_pairs={{0,4},{4,0},{8,12},{12,8},{1,5},{5,1},{9,13},{13,9},{2,6},{6,2},{1... | collective-permute-start | bytes 393224 | tf_op jit(solution)/shard_map/ppermute | solution.py:270
  10.2 0.2 shard_map.98.refs_3_.mask_ref
  10.4 1.0 %collective-permute-done.2.refs_0_.refs_5_ = f32[32,1024]{1,0:T(8,128)S(1)} collective-permute-done((f32[32,1024]{1,0:T(8,128)}, f32[32,1024]{1,0:T(8,128)S(1)}, u32[]{:S(2)}, u32[]{:S(2)}) %collective-permute-start.2) | collective-permute-done | bytes 131104 | tf_op jit(solution)/shard_map/ppermute | solution.py:270
  11.4 1.0 %collective-permute-done.1.refs_2_ = f32[32,512]{1,0:T(8,128)S(1)} collective-permute-done((f32[32,512]{1,0:T(8,128)S(1)}, f32[32,512]{1,0:T(8,128)S(1)}, u32[]{:S(2)}, u32[]{:S(2)}) %collective-permute-start.1) | collective-permute-done | bytes 65568 | tf_op jit(solution)/shard_map/ppermute | solution.py:270
  12.5 0.5 %collective-permute-start.4 = (f32[40,512]{1,0:T(8,128)S(1)}, f32[40,512]{1,0:T(8,128)S(1)}, u32[]{:S(2)}, u32[]{:S(2)}) collective-permute-start(f32[40,512]{1,0:T(8,128)S(1)} %get-tuple-element.15.refs_1_), channel_id=1, source_target_pairs={{0,1},{1,0},{2,3},{3,2},{4,5},{5,4},{6,7},{7,6},{8,9},{9,8},{10,11... | collective-permute-start | bytes 245768 | tf_op jit(solution)/shard_map/ppermute | solution.py:270
  13.0 1.6 %collective-permute-start.9 = (f32[32,1024]{1,0:T(8,128)S(1)}, f32[32,1024]{1,0:T(8,128)S(1)}, u32[]{:S(2)}, u32[]{:S(2)}) collective-permute-start(f32[32,1024]{1,0:T(8,128)S(1)} %collective-permute-done.2.refs_0_.refs_5_), channel_id=1, source_target_pairs={{0,4},{4,0},{8,12},{12,8},{1,5},{5,1},{9,13},{13,9},{2,6},{6,2},{1... | collective-permute-start | bytes 393224 | tf_op jit(solution)/shard_map/ppermute | solution.py:270
  14.6 1.0 %shard_map.103 = (f32[16,1024]{1,0:T(8,128)S(1)}, f32[16,1024]{1,0:T(8,128)S(1)}) custom-call(f32[16,512]{1,0:T(8,128)S(1)} %get-tuple-element.13.g_ref, f32[64,512]{1,0:T(8,128)S(1)} %shard_map.98.refs_3_.mask_ref, f32[40,512]{1,0:T(8,128)S(1)} %get-tuple-element.14.refs_0_, f32[40,512]{1,0:T(8,128)S(1)} %get-tuple-element.15.refs_1_, ...), custom_call_target="tpu_custom_call" | custom-call | flops 134217728 | tf_op jit(solution)/shard_map/pallas_call | solution.py:175
  15.5 1.6 %collective-permute-start.7 = (f32[16,1024]{1,0:T(8,128)S(1)}, f32[16,1024]{1,0:T(8,128)S(1)}, u32[]{:S(2)}, u32[]{:S(2)}) collective-permute-start(f32[16,1024]{1,0:T(8,128)S(1)} %get-tuple-element.18), channel_id=1, source_target_pairs={{0,8},{4,12},{8,0},{12,4},{1,9},{5,13},{9,1},{13,5},{2,10},{6,14},... | collective-permute-start | bytes 196616 | tf_op jit(solution)/shard_map/ppermute | solution.py:270
  17.1 1.7 %collective-permute-start.8 = (f32[16,1024]{1,0:T(8,128)S(1)}, f32[16,1024]{1,0:T(8,128)S(1)}, u32[]{:S(2)}, u32[]{:S(2)}) collective-permute-start(f32[16,1024]{1,0:T(8,128)S(1)} %get-tuple-element.19), channel_id=1, source_target_pairs={{0,12},{4,8},{8,4},{12,0},{1,13},{5,9},{9,5},{13,1},{2,14},{6,10},... | collective-permute-start | bytes 196616 | tf_op jit(solution)/shard_map/ppermute | solution.py:270
  18.9 1.0 %shard_map.101 = (f32[16,1024]{1,0:T(8,128)S(1)}, f32[16,1024]{1,0:T(8,128)S(1)}) custom-call(f32[16,512]{1,0:T(8,128)S(1)} %get-tuple-element.13.g_ref, f32[64,512]{1,0:T(8,128)S(1)} %shard_map.98.refs_3_.mask_ref, f32[40,512]{1,0:T(8,128)S(1)} %get-tuple-element.14.refs_0_, f32[40,512]{1,0:T(8,128)S(1)} %get-tuple-element.15.refs_1_, ...), custom_call_target="tpu_custom_call" | custom-call | flops 134217728 | tf_op jit(solution)/shard_map/pallas_call | solution.py:175
  19.8 0.3 collective-permute-start.6
  20.1 3.9 %collective-permute-done.7.refs_2_.refs_1_ = f32[16,1024]{1,0:T(8,128)S(1)} collective-permute-done((f32[16,1024]{1,0:T(8,128)S(1)}, f32[16,1024]{1,0:T(8,128)S(1)}, u32[]{:S(2)}, u32[]{:S(2)}) %collective-permute-start.7) | collective-permute-done | bytes 65568 | tf_op jit(solution)/shard_map/ppermute | solution.py:270
  24.0 0.9 %collective-permute-done.6.refs_1_ = f32[16,1024]{1,0:T(8,128)S(1)} collective-permute-done((f32[16,1024]{1,0:T(8,128)S(1)}, f32[16,1024]{1,0:T(8,128)S(1)}, u32[]{:S(2)}, u32[]{:S(2)}) %collective-permute-start.6) | collective-permute-done | bytes 65568 | tf_op jit(solution)/shard_map/ppermute | solution.py:270
  24.9 0.4 %shard_map.106 = f32[64,128]{1,0:T(8,128)S(1)} custom-call(s32[1,128]{1,0:T(1,128)S(1)} %bitcast.5, f32[16,1024]{1,0:T(8,128)S(1)} %get-tuple-element.16.refs_0_, f32[16,1024]{1,0:T(8,128)S(1)} %collective-permute-done.6.refs_1_, f32[16,1024]{1,0:T(8,128)S(1)} %collective-permute-done.7.refs_2_.refs_1_, ...), custom_call_target="tpu_custom_call" | custom-call | flops 50331648 | bytes 524288 | tf_op jit(solution)/shard_map/pallas_call | solution.py:241
  25.4 1.2 %collective-permute-done.10 = f32[64,128]{1,0:T(8,128)S(1)} collective-permute-done((f32[64,128]{1,0:T(8,128)S(1)}, f32[64,128]{1,0:T(8,128)S(1)}, u32[]{:S(2)}, u32[]{:S(2)}) %collective-permute-start.10) | collective-permute-done | bytes 32800 | tf_op jit(solution)/shard_map/ppermute | solution.py:270
  26.6 0.9 %collective-permute-start.11 = (f32[64,128]{1,0:T(8,128)S(1)}, f32[64,128]{1,0:T(8,128)S(1)}, u32[]{:S(2)}, u32[]{:S(2)}) collective-permute-start(f32[64,128]{1,0:T(8,128)S(1)} %add.6), channel_id=1, source_target_pairs={{0,2},{1,3},{2,0},{3,1},{4,6},{5,7},{6,4},{7,5},{8,10},{9,11},{10,... | collective-permute-start | bytes 98312 | tf_op jit(solution)/shard_map/ppermute | solution.py:270
  27.5 0.7 %shard_map.104 = f32[64,1024]{1,0:T(8,128)} custom-call(f32[16,1024]{1,0:T(8,128)S(1)} %get-tuple-element.16.refs_0_, f32[16,1024]{1,0:T(8,128)S(1)} %collective-permute-done.6.refs_1_, f32[16,1024]{1,0:T(8,128)S(1)} %collective-permute-done.7.refs_2_.refs_1_, f32[16,1024]{1,0:T(8,128)S(1)} %collective-permute-done.8.refs_3_.refs_0_), custom_call_target="tpu_custom_call" | custom-call | bytes 524288 | tf_op jit(solution)/shard_map/pallas_call | solution.py:261
  28.2 2.3 %collective-permute-done.11 = f32[64,128]{1,0:T(8,128)S(1)} collective-permute-done((f32[64,128]{1,0:T(8,128)S(1)}, f32[64,128]{1,0:T(8,128)S(1)}, u32[]{:S(2)}, u32[]{:S(2)}) %collective-permute-start.11) | collective-permute-done | bytes 32800 | tf_op jit(solution)/shard_map/ppermute | solution.py:270
  30.5 0.6 %add_multiply_fusion = f32[64,128]{1,0:T(8,128)} fusion(f32[64,128]{1,0:T(8,128)S(1)} %add.6, f32[64,128]{1,0:T(8,128)S(1)} %collective-permute-done.11), kind=kLoop, calls=%fused_computation | loop fusion | flops 16384 | bytes 98304 | tf_op jit(solution)/shard_map/mul | solution.py:331
  (30 shorter events, 0.2 us)
Async XLA Ops:
  0.6 4.2 %copy-start.5 = (bf16[1024,64]{0,1:T(8,128)(2,1)S(1)}, bf16[1024,64]{0,1:T(8,128)(2,1)}, u32[]{:S(2)}) copy-start(bf16[1024,64]{0,1:T(8,128)(2,1)} %param.10) | copy-start | bytes 393220
  0.6 4.2 %copy-start.4 = (bf16[512,1024]{1,0:T(8,128)(2,1)S(1)}, bf16[512,1024]{1,0:T(8,128)(2,1)}, u32[]{:S(2)}) copy-start(bf16[512,1024]{1,0:T(8,128)(2,1)} %act_ref.1) | copy-start | bytes 3145732
  0.7 6.2 %copy-start.1 = (bf16[3584,64]{0,1:T(8,128)(2,1)S(1)}, bf16[3584,64]{0,1:T(8,128)(2,1)}, u32[]{:S(2)}) copy-start(bf16[3584,64]{0,1:T(8,128)(2,1)} %param.11) | copy-start | bytes 1376260
  0.7 6.1 %copy-start = (bf16[512,3584]{1,0:T(8,128)(2,1)S(1)}, bf16[512,3584]{1,0:T(8,128)(2,1)}, u32[]{:S(2)}) copy-start(bf16[512,3584]{1,0:T(8,128)(2,1)} %grad_ref.1) | copy-start | bytes 11010052
  0.7 10.7 %collective-permute-start.2 = (f32[32,1024]{1,0:T(8,128)}, f32[32,1024]{1,0:T(8,128)S(1)}, u32[]{:S(2)}, u32[]{:S(2)}) collective-permute-start(f32[32,1024]{1,0:T(8,128)} %refs_4_.1), channel_id=1, source_target_pairs={{0,8},{4,12},{8,0},{12,4},{1,9},{5,13},{9,1},{13,5},{2,10},{6,14},... | collective-permute-start | bytes 393224 | tf_op jit(solution)/shard_map/ppermute | solution.py:270
  4.8 3.9 %copy-start.2 = (f32[32,1024]{1,0:T(8,128)S(1)}, f32[32,1024]{1,0:T(8,128)}, u32[]{:S(2)}) copy-start(f32[32,1024]{1,0:T(8,128)} %refs_4_.1) | copy-start | bytes 393220
  4.8 5.5 %copy-start.6 = (s32[1,32]{1,0:T(1,128)S(1)}, s32[1,32]{1,0:T(1,128)}, u32[]{:S(2)}) copy-start(s32[1,32]{1,0:T(1,128)} %lengths_ref.1) | copy-start | bytes 388
  4.8 5.5 %copy-start.7 = (s32[32,1]{0,1:T(1,128)S(1)}, s32[32,1]{0,1:T(1,128)}, u32[]{:S(2)}) copy-start(s32[32,1]{0,1:T(1,128)} %param.13) | copy-start | bytes 388
  5.2 7.1 %collective-permute-start = (f32[64,512]{1,0:T(8,128)S(1)}, f32[64,512]{1,0:T(8,128)S(1)}, u32[]{:S(2)}, u32[]{:S(2)}) collective-permute-start(f32[64,512]{1,0:T(8,128)S(1)} %shard_map.97.refs_0_), channel_id=1, source_target_pairs={{0,2},{1,3},{2,0},{3,1},{4,6},{5,7},{6,4},{7,5},{8,10},{9,11},{10,... | collective-permute-start | bytes 393224 | tf_op jit(solution)/shard_map/ppermute | solution.py:270
  6.8 18.1 %copy-start.3 = (s32[128]{0:T(128)S(1)}, s32[128]{0:T(128)}, u32[]{:S(2)}) copy-start(s32[128]{0:T(128)} %param.15) | copy-start | bytes 1540
  8.0 4.3 %collective-permute-start.1 = (f32[32,512]{1,0:T(8,128)S(1)}, f32[32,512]{1,0:T(8,128)S(1)}, u32[]{:S(2)}, u32[]{:S(2)}) collective-permute-start(f32[32,512]{1,0:T(8,128)S(1)} %get-tuple-element.12), channel_id=1, source_target_pairs={{0,2},{1,3},{2,0},{3,1},{4,6},{5,7},{6,4},{7,5},{8,10},{9,11},{10,... | collective-permute-start | bytes 196616 | tf_op jit(solution)/shard_map/ppermute | solution.py:270
  8.7 11.2 %collective-permute-start.5 = (f32[32,1024]{1,0:T(8,128)S(1)}, f32[32,1024]{1,0:T(8,128)S(1)}, u32[]{:S(2)}, u32[]{:S(2)}) collective-permute-start(f32[32,1024]{1,0:T(8,128)S(1)} %copy-done.2), channel_id=1, source_target_pairs={{0,4},{4,0},{8,12},{12,8},{1,5},{5,1},{9,13},{13,9},{2,6},{6,2},{1... | collective-permute-start | bytes 393224 | tf_op jit(solution)/shard_map/ppermute | solution.py:270
  12.4 2.2 %collective-permute-start.3 = (f32[40,512]{1,0:T(8,128)S(1)}, f32[40,512]{1,0:T(8,128)S(1)}, u32[]{:S(2)}, u32[]{:S(2)}) collective-permute-start(f32[40,512]{1,0:T(8,128)S(1)} %get-tuple-element.14.refs_0_), channel_id=1, source_target_pairs={{0,1},{1,0},{2,3},{3,2},{4,5},{5,4},{6,7},{7,6},{8,9},{9,8},{10,11... | collective-permute-start | bytes 245768 | tf_op jit(solution)/shard_map/ppermute | solution.py:270
  12.5 2.1 %collective-permute-start.4 = (f32[40,512]{1,0:T(8,128)S(1)}, f32[40,512]{1,0:T(8,128)S(1)}, u32[]{:S(2)}, u32[]{:S(2)}) collective-permute-start(f32[40,512]{1,0:T(8,128)S(1)} %get-tuple-element.15.refs_1_), channel_id=1, source_target_pairs={{0,1},{1,0},{2,3},{3,2},{4,5},{5,4},{6,7},{7,6},{8,9},{9,8},{10,11... | collective-permute-start | bytes 245768 | tf_op jit(solution)/shard_map/ppermute | solution.py:270
  13.0 11.0 %collective-permute-start.9 = (f32[32,1024]{1,0:T(8,128)S(1)}, f32[32,1024]{1,0:T(8,128)S(1)}, u32[]{:S(2)}, u32[]{:S(2)}) collective-permute-start(f32[32,1024]{1,0:T(8,128)S(1)} %collective-permute-done.2.refs_0_.refs_5_), channel_id=1, source_target_pairs={{0,4},{4,0},{8,12},{12,8},{1,5},{5,1},{9,13},{13,9},{2,6},{6,2},{1... | collective-permute-start | bytes 393224 | tf_op jit(solution)/shard_map/ppermute | solution.py:270
  15.5 8.4 %collective-permute-start.7 = (f32[16,1024]{1,0:T(8,128)S(1)}, f32[16,1024]{1,0:T(8,128)S(1)}, u32[]{:S(2)}, u32[]{:S(2)}) collective-permute-start(f32[16,1024]{1,0:T(8,128)S(1)} %get-tuple-element.18), channel_id=1, source_target_pairs={{0,8},{4,12},{8,0},{12,4},{1,9},{5,13},{9,1},{13,5},{2,10},{6,14},... | collective-permute-start | bytes 196616 | tf_op jit(solution)/shard_map/ppermute | solution.py:270
  17.1 6.9 %collective-permute-start.8 = (f32[16,1024]{1,0:T(8,128)S(1)}, f32[16,1024]{1,0:T(8,128)S(1)}, u32[]{:S(2)}, u32[]{:S(2)}) collective-permute-start(f32[16,1024]{1,0:T(8,128)S(1)} %get-tuple-element.19), channel_id=1, source_target_pairs={{0,12},{4,8},{8,4},{12,0},{1,13},{5,9},{9,5},{13,1},{2,14},{6,10},... | collective-permute-start | bytes 196616 | tf_op jit(solution)/shard_map/ppermute | solution.py:270
  19.8 5.1 %collective-permute-start.6 = (f32[16,1024]{1,0:T(8,128)S(1)}, f32[16,1024]{1,0:T(8,128)S(1)}, u32[]{:S(2)}, u32[]{:S(2)}) collective-permute-start(f32[16,1024]{1,0:T(8,128)S(1)} %shard_map.102), channel_id=1, source_target_pairs={{0,4},{4,0},{8,12},{12,8},{1,5},{5,1},{9,13},{13,9},{2,6},{6,2},{1... | collective-permute-start | bytes 196616 | tf_op jit(solution)/shard_map/ppermute | solution.py:270
  25.3 1.3 %collective-permute-start.10 = (f32[64,128]{1,0:T(8,128)S(1)}, f32[64,128]{1,0:T(8,128)S(1)}, u32[]{:S(2)}, u32[]{:S(2)}) collective-permute-start(f32[64,128]{1,0:T(8,128)S(1)} %shard_map.106), channel_id=1, source_target_pairs={{0,1},{1,0},{2,3},{3,2},{4,5},{5,4},{6,7},{7,6},{8,9},{9,8},{10,11... | collective-permute-start | bytes 98312 | tf_op jit(solution)/shard_map/ppermute | solution.py:270
  26.6 3.9 %collective-permute-start.11 = (f32[64,128]{1,0:T(8,128)S(1)}, f32[64,128]{1,0:T(8,128)S(1)}, u32[]{:S(2)}, u32[]{:S(2)}) collective-permute-start(f32[64,128]{1,0:T(8,128)S(1)} %add.6), channel_id=1, source_target_pairs={{0,2},{1,3},{2,0},{3,1},{4,6},{5,7},{6,4},{7,5},{8,10},{9,11},{10,... | collective-permute-start | bytes 98312 | tf_op jit(solution)/shard_map/ppermute | solution.py:270

commit v13 on v11

--- a/solution.py
+++ b/solution.py
@@ -12,6 +12,7 @@
 MIB = 1024 * 1024
 NT = (((1,), (1,)), ((), ()))
 MOST_DIRECT = 8
+GROUP = 4
 FIRST_FLOPS = 10 * 10**8
 X_FLOPS = 6 * 10**8
 MASK_FLOPS = 2 * 10**8
@@ -72,8 +73,14 @@
     )(lengths, owner_row)
 
 
+def put_projection(out_ref, proj_ref, act_ref):
+    half = act_ref.shape[0] // 2
+    out_ref[:, :half] = mm(proj_ref[...], act_ref[:half, :], NT)
+    out_ref[:, half:] = mm(act_ref[half:, :], proj_ref[...], NT).T
+
+
 def x_kernel(act_ref, proj_ref, *refs):
-    refs[-1][...] = mm(proj_ref[...], act_ref[...], NT)
+    put_projection(refs[-1], proj_ref, act_ref)
 
 
 def project_x(act, in_t, tokens):
@@ -88,7 +95,7 @@
 
 
 def g_kernel(width, grad_ref, proj_ref, keep_ref, send_ref, full):
-    full[...] = mm(proj_ref[...], grad_ref[...], NT)
+    put_projection(full, proj_ref, grad_ref)
     me = lax.axis_index("tensor")
     count = full.shape[0] // width
     for apart in range(count):
@@ -156,17 +163,19 @@
     mask = mask_ref[...]
     cap = blocks[0].shape[0]
 
-    def product(i):
-        pair = [(mask * g[i : i + 1, :]).astype(BF16) for g in (g_high, g_low)]
-        both = mm(jnp.concatenate(pair, axis=0), x_both, NT)
-        slots = mask.shape[0]
-        return both[:slots, :rank] + both[:slots, rank:] + both[slots:, :rank]
-
-    step = max(1, 128 // rank)
-    for i in range(0, width, step):
-        columns = jnp.concatenate([product(i + j) for j in range(step)], axis=1)
+    slots = mask.shape[0]
+    group = min(width, GROUP)
+    for i in range(0, width, group):
+        rows = [mask * g[j : j + 1, :] for j in range(i, i + group) for g in (g_high, g_low)]
+        both = mm(jnp.concatenate([r.astype(BF16) for r in rows], axis=0), x_both, NT)
+        columns = []
+        for j in range(group):
+            high = both[2 * j * slots : (2 * j + 1) * slots]
+            low = both[(2 * j + 1) * slots : (2 * j + 2) * slots]
+            columns.append(high[:, :rank] + high[:, rank:] + low[:, :rank])
+        out = jnp.concatenate(columns, axis=1)
         for k, block in enumerate(blocks):
-            block[:, i * rank : (i + step) * rank] = columns[k * cap : (k + 1) * cap, :]
+            block[:, i * rank : (i + group) * rank] = out[k * cap : (k + 1) * cap, :]
 
 
 def outer(sent, gots, g, mask, owners):

time: 31 us -> 30.9 us (level)
  no operation moved by 1% of the time
where the time goes in v13:
time: 30.9 us; the launch traced here: 30.8 us
  starting transfers between devices  14.4 us (47%)
  waiting for transfers between devices  11.1 us (36%)
  Pallas kernels  3.86 us (12%)
  between operations  0.75 us (2%)
  other arithmetic  0.63 us (2%)
    ppermute x12, starting transfers between devices, swap(): lax.ppermute(x, axis, [(i, i ^ gap) for i in range(lax.axis_size(axis))])  14.4 us
    ppermute x12, waiting for transfers between devices, swap(): lax.ppermute(x, axis, [(i, i ^ gap) for i in range(lax.axis_size(axis))])  11.1 us
    pallas_call x1, Pallas kernels, project_g(): pl.pallas_call(functools.partial(g_kernel, width), out_shape=[part, part]...  1.16 us
    pallas_call x1, Pallas kernels, outer(): pl.pallas_call(functools.partial(outer_kernel, owners, len(sent)), out_sh...  0.85 us
    pallas_call x1, Pallas kernels, place(): pl.pallas_call(place_kernel, out_shape=jax.ShapeDtypeStruct((slots, feats...  0.73 us
    mul x1, other arithmetic, local(): return (store, scores * (1.0 / (rank * rank)))  0.62 us
  transfers between devices with their start and end apart: 12, of which 6 were waited for; matrix products, arithmetic and copies ran while one was open for 0% of the time, Pallas kernels for 11%

profile of v13, /device:TPU:0, one launch (start us, length us, event | category | flops | bytes accessed | tf_op | source)
XLA Modules:
  0.0 30.8 jit_solution(5544908762402723730)
XLA Ops:
  0.7 4.1 %collective-permute-start.2 = (f32[32,1024]{1,0:T(8,128)}, f32[32,1024]{1,0:T(8,128)S(1)}, u32[]{:S(2)}, u32[]{:S(2)}) collective-permute-start(f32[32,1024]{1,0:T(8,128)} %refs_4_.1), channel_id=1, source_target_pairs={{0,8},{4,12},{8,0},{12,4},{1,9},{5,13},{9,1},{13,5},{2,10},{6,14},... | collective-permute-start | bytes 393224 | tf_op jit(solution)/shard_map/ppermute | solution.py:281
  4.8 0.5 %shard_map.97.refs_0_ = f32[64,512]{1,0:T(8,128)S(1)} custom-call(bf16[512,1024]{1,0:T(8,128)(2,1)S(1)} %copy-done.4, bf16[64,1024]{1,0:T(8,128)(2,1)S(1)} %bitcast.6, f32[8,128]{1,0:T(8,128)S(1)} %shard_map.96.refs_0_), custom_call_target="tpu_custom_call" | custom-call | flops 600000000 | tf_op jit(solution)/shard_map/pallas_call | solution.py:87
  5.3 1.5 %collective-permute-start = (f32[64,512]{1,0:T(8,128)S(1)}, f32[64,512]{1,0:T(8,128)S(1)}, u32[]{:S(2)}, u32[]{:S(2)}) collective-permute-start(f32[64,512]{1,0:T(8,128)S(1)} %shard_map.97.refs_0_), channel_id=1, source_target_pairs={{0,2},{1,3},{2,0},{3,1},{4,6},{5,7},{6,4},{7,5},{8,10},{9,11},{10,... | collective-permute-start | bytes 393224 | tf_op jit(solution)/shard_map/ppermute | solution.py:281
  6.8 1.2 %shard_map.95 = (f32[32,512]{1,0:T(8,128)S(1)}, f32[32,512]{1,0:T(8,128)S(1)}) custom-call(bf16[512,3584]{1,0:T(8,128)(2,1)S(1)} %copy-done, bf16[64,3584]{1,0:T(8,128)(2,1)S(1)} %bitcast.4), custom_call_target="tpu_custom_call" | custom-call | tf_op jit(solution)/shard_map/pallas_call | solution.py:110
  8.0 0.6 %collective-permute-start.1 = (f32[32,512]{1,0:T(8,128)S(1)}, f32[32,512]{1,0:T(8,128)S(1)}, u32[]{:S(2)}, u32[]{:S(2)}) collective-permute-start(f32[32,512]{1,0:T(8,128)S(1)} %get-tuple-element.12), channel_id=1, source_target_pairs={{0,2},{1,3},{2,0},{3,1},{4,6},{5,7},{6,4},{7,5},{8,10},{9,11},{10,... | collective-permute-start | bytes 196616 | tf_op jit(solution)/shard_map/ppermute | solution.py:281
  8.6 1.6 %collective-permute-start.5 = (f32[32,1024]{1,0:T(8,128)S(1)}, f32[32,1024]{1,0:T(8,128)S(1)}, u32[]{:S(2)}, u32[]{:S(2)}) collective-permute-start(f32[32,1024]{1,0:T(8,128)S(1)} %copy-done.2), channel_id=1, source_target_pairs={{0,4},{4,0},{8,12},{12,8},{1,5},{5,1},{9,13},{13,9},{2,6},{6,2},{1... | collective-permute-start | bytes 393224 | tf_op jit(solution)/shard_map/ppermute | solution.py:281
  10.2 0.2 shard_map.98.refs_3_.mask_ref
  10.4 1.0 %collective-permute-done.2.refs_0_.refs_5_ = f32[32,1024]{1,0:T(8,128)S(1)} collective-permute-done((f32[32,1024]{1,0:T(8,128)}, f32[32,1024]{1,0:T(8,128)S(1)}, u32[]{:S(2)}, u32[]{:S(2)}) %collective-permute-start.2) | collective-permute-done | bytes 131104 | tf_op jit(solution)/shard_map/ppermute | solution.py:281
  11.4 0.9 %collective-permute-done.1.refs_2_ = f32[32,512]{1,0:T(8,128)S(1)} collective-permute-done((f32[32,512]{1,0:T(8,128)S(1)}, f32[32,512]{1,0:T(8,128)S(1)}, u32[]{:S(2)}, u32[]{:S(2)}) %collective-permute-start.1) | collective-permute-done | bytes 65568 | tf_op jit(solution)/shard_map/ppermute | solution.py:281
  12.3 0.1 collective-permute-start.3
  12.4 0.5 %collective-permute-start.4 = (f32[40,512]{1,0:T(8,128)S(1)}, f32[40,512]{1,0:T(8,128)S(1)}, u32[]{:S(2)}, u32[]{:S(2)}) collective-permute-start(f32[40,512]{1,0:T(8,128)S(1)} %get-tuple-element.15.refs_1_), channel_id=1, source_target_pairs={{0,1},{1,0},{2,3},{3,2},{4,5},{5,4},{6,7},{7,6},{8,9},{9,8},{10,11... | collective-permute-start | bytes 245768 | tf_op jit(solution)/shard_map/ppermute | solution.py:281
  12.9 1.6 %collective-permute-start.9 = (f32[32,1024]{1,0:T(8,128)S(1)}, f32[32,1024]{1,0:T(8,128)S(1)}, u32[]{:S(2)}, u32[]{:S(2)}) collective-permute-start(f32[32,1024]{1,0:T(8,128)S(1)} %collective-permute-done.2.refs_0_.refs_5_), channel_id=1, source_target_pairs={{0,4},{4,0},{8,12},{12,8},{1,5},{5,1},{9,13},{13,9},{2,6},{6,2},{1... | collective-permute-start | bytes 393224 | tf_op jit(solution)/shard_map/ppermute | solution.py:281
  14.5 0.8 %shard_map.101 = (f32[16,1024]{1,0:T(8,128)S(1)}, f32[16,1024]{1,0:T(8,128)S(1)}, f32[16,1024]{1,0:T(8,128)S(1)}, f32[16,1024]{1,0:T(8,128)S(1)}) custom-call(f32[16,512]{1,0:T(8,128)S(1)} %get-tuple-element.13.g_ref, f32[64,512]{1,0:T(8,128)S(1)} %shard_map.98.refs_3_.mask_ref, f32[40,512]{1,0:T(8,128)S(1)} %get-tuple-element.14.refs_0_, ...), custom_call_target="tpu_custom_call" | custom-call | flops 268435456 | bytes 262144 | tf_op jit(solution)/shard_map/pallas_call | solution.py:186
  15.4 1.7 %collective-permute-start.7 = (f32[16,1024]{1,0:T(8,128)S(1)}, f32[16,1024]{1,0:T(8,128)S(1)}, u32[]{:S(2)}, u32[]{:S(2)}) collective-permute-start(f32[16,1024]{1,0:T(8,128)S(1)} %get-tuple-element.18), channel_id=1, source_target_pairs={{0,8},{4,12},{8,0},{12,4},{1,9},{5,13},{9,1},{13,5},{2,10},{6,14},... | collective-permute-start | bytes 196616 | tf_op jit(solution)/shard_map/ppermute | solution.py:281
  17.0 1.7 %collective-permute-start.8 = (f32[16,1024]{1,0:T(8,128)S(1)}, f32[16,1024]{1,0:T(8,128)S(1)}, u32[]{:S(2)}, u32[]{:S(2)}) collective-permute-start(f32[16,1024]{1,0:T(8,128)S(1)} %get-tuple-element.19), channel_id=1, source_target_pairs={{0,12},{4,8},{8,4},{12,0},{1,13},{5,9},{9,5},{13,1},{2,14},{6,10},... | collective-permute-start | bytes 196616 | tf_op jit(solution)/shard_map/ppermute | solution.py:281
  18.7 0.3 collective-permute-start.6
  19.0 4.8 %collective-permute-done.7.refs_2_.refs_1_ = f32[16,1024]{1,0:T(8,128)S(1)} collective-permute-done((f32[16,1024]{1,0:T(8,128)S(1)}, f32[16,1024]{1,0:T(8,128)S(1)}, u32[]{:S(2)}, u32[]{:S(2)}) %collective-permute-start.7) | collective-permute-done | bytes 65568 | tf_op jit(solution)/shard_map/ppermute | solution.py:281
  23.8 0.7 %collective-permute-done.6.refs_1_ = f32[16,1024]{1,0:T(8,128)S(1)} collective-permute-done((f32[16,1024]{1,0:T(8,128)S(1)}, f32[16,1024]{1,0:T(8,128)S(1)}, u32[]{:S(2)}, u32[]{:S(2)}) %collective-permute-start.6) | collective-permute-done | bytes 65568 | tf_op jit(solution)/shard_map/ppermute | solution.py:281
  24.5 0.4 %shard_map.105 = f32[64,128]{1,0:T(8,128)S(1)} custom-call(s32[1,128]{1,0:T(1,128)S(1)} %bitcast.5, f32[16,1024]{1,0:T(8,128)S(1)} %get-tuple-element.16.refs_0_, f32[16,1024]{1,0:T(8,128)S(1)} %collective-permute-done.6.refs_1_, f32[16,1024]{1,0:T(8,128)S(1)} %collective-permute-done.7.refs_2_.refs_1_, ...), custom_call_target="tpu_custom_call" | custom-call | flops 50331648 | bytes 524288 | tf_op jit(solution)/shard_map/pallas_call | solution.py:252
  25.1 1.2 %collective-permute-done.10 = f32[64,128]{1,0:T(8,128)S(1)} collective-permute-done((f32[64,128]{1,0:T(8,128)S(1)}, f32[64,128]{1,0:T(8,128)S(1)}, u32[]{:S(2)}, u32[]{:S(2)}) %collective-permute-start.10) | collective-permute-done | bytes 32800 | tf_op jit(solution)/shard_map/ppermute | solution.py:281
  26.3 0.8 %collective-permute-start.11 = (f32[64,128]{1,0:T(8,128)S(1)}, f32[64,128]{1,0:T(8,128)S(1)}, u32[]{:S(2)}, u32[]{:S(2)}) collective-permute-start(f32[64,128]{1,0:T(8,128)S(1)} %add.6), channel_id=1, source_target_pairs={{0,2},{1,3},{2,0},{3,1},{4,6},{5,7},{6,4},{7,5},{8,10},{9,11},{10,... | collective-permute-start | bytes 98312 | tf_op jit(solution)/shard_map/ppermute | solution.py:281
  27.0 0.7 %shard_map.103 = f32[64,1024]{1,0:T(8,128)} custom-call(f32[16,1024]{1,0:T(8,128)S(1)} %get-tuple-element.16.refs_0_, f32[16,1024]{1,0:T(8,128)S(1)} %collective-permute-done.6.refs_1_, f32[16,1024]{1,0:T(8,128)S(1)} %collective-permute-done.7.refs_2_.refs_1_, f32[16,1024]{1,0:T(8,128)S(1)} %collective-permute-done.8.refs_3_.refs_0_), custom_call_target="tpu_custom_call" | custom-call | bytes 524288 | tf_op jit(solution)/shard_map/pallas_call | solution.py:272
  27.8 2.4 %collective-permute-done.11 = f32[64,128]{1,0:T(8,128)S(1)} collective-permute-done((f32[64,128]{1,0:T(8,128)S(1)}, f32[64,128]{1,0:T(8,128)S(1)}, u32[]{:S(2)}, u32[]{:S(2)}) %collective-permute-start.11) | collective-permute-done | bytes 32800 | tf_op jit(solution)/shard_map/ppermute | solution.py:281
  30.2 0.6 %add_multiply_fusion = f32[64,128]{1,0:T(8,128)} fusion(f32[64,128]{1,0:T(8,128)S(1)} %add.6, f32[64,128]{1,0:T(8,128)S(1)} %collective-permute-done.11), kind=kLoop, calls=%fused_computation | loop fusion | flops 16384 | bytes 98304 | tf_op jit(solution)/shard_map/mul | solution.py:338
  (29 shorter events, 0.2 us)
Async XLA Ops:
  0.6 4.2 %copy-start.5 = (bf16[1024,64]{0,1:T(8,128)(2,1)S(1)}, bf16[1024,64]{0,1:T(8,128)(2,1)}, u32[]{:S(2)}) copy-start(bf16[1024,64]{0,1:T(8,128)(2,1)} %param.10) | copy-start | bytes 393220
  0.6 4.2 %copy-start.4 = (bf16[512,1024]{1,0:T(8,128)(2,1)S(1)}, bf16[512,1024]{1,0:T(8,128)(2,1)}, u32[]{:S(2)}) copy-start(bf16[512,1024]{1,0:T(8,128)(2,1)} %act_ref.1) | copy-start | bytes 3145732
  0.7 6.2 %copy-start.1 = (bf16[3584,64]{0,1:T(8,128)(2,1)S(1)}, bf16[3584,64]{0,1:T(8,128)(2,1)}, u32[]{:S(2)}) copy-start(bf16[3584,64]{0,1:T(8,128)(2,1)} %param.11) | copy-start | bytes 1376260
  0.7 6.2 %copy-start = (bf16[512,3584]{1,0:T(8,128)(2,1)S(1)}, bf16[512,3584]{1,0:T(8,128)(2,1)}, u32[]{:S(2)}) copy-start(bf16[512,3584]{1,0:T(8,128)(2,1)} %grad_ref.1) | copy-start | bytes 11010052
  0.7 10.7 %collective-permute-start.2 = (f32[32,1024]{1,0:T(8,128)}, f32[32,1024]{1,0:T(8,128)S(1)}, u32[]{:S(2)}, u32[]{:S(2)}) collective-permute-start(f32[32,1024]{1,0:T(8,128)} %refs_4_.1), channel_id=1, source_target_pairs={{0,8},{4,12},{8,0},{12,4},{1,9},{5,13},{9,1},{13,5},{2,10},{6,14},... | collective-permute-start | bytes 393224 | tf_op jit(solution)/shard_map/ppermute | solution.py:281
  4.8 3.8 %copy-start.2 = (f32[32,1024]{1,0:T(8,128)S(1)}, f32[32,1024]{1,0:T(8,128)}, u32[]{:S(2)}) copy-start(f32[32,1024]{1,0:T(8,128)} %refs_4_.1) | copy-start | bytes 393220
  4.8 5.4 %copy-start.6 = (s32[1,32]{1,0:T(1,128)S(1)}, s32[1,32]{1,0:T(1,128)}, u32[]{:S(2)}) copy-start(s32[1,32]{1,0:T(1,128)} %lengths_ref.1) | copy-start | bytes 388
  4.8 5.4 %copy-start.7 = (s32[32,1]{0,1:T(1,128)S(1)}, s32[32,1]{0,1:T(1,128)}, u32[]{:S(2)}) copy-start(s32[32,1]{0,1:T(1,128)} %param.13) | copy-start | bytes 388
  5.3 7.1 %collective-permute-start = (f32[64,512]{1,0:T(8,128)S(1)}, f32[64,512]{1,0:T(8,128)S(1)}, u32[]{:S(2)}, u32[]{:S(2)}) collective-permute-start(f32[64,512]{1,0:T(8,128)S(1)} %shard_map.97.refs_0_), channel_id=1, source_target_pairs={{0,2},{1,3},{2,0},{3,1},{4,6},{5,7},{6,4},{7,5},{8,10},{9,11},{10,... | collective-permute-start | bytes 393224 | tf_op jit(solution)/shard_map/ppermute | solution.py:281
  6.8 17.7 %copy-start.3 = (s32[128]{0:T(128)S(1)}, s32[128]{0:T(128)}, u32[]{:S(2)}) copy-start(s32[128]{0:T(128)} %param.15) | copy-start | bytes 1540
  8.0 4.3 %collective-permute-start.1 = (f32[32,512]{1,0:T(8,128)S(1)}, f32[32,512]{1,0:T(8,128)S(1)}, u32[]{:S(2)}, u32[]{:S(2)}) collective-permute-start(f32[32,512]{1,0:T(8,128)S(1)} %get-tuple-element.12), channel_id=1, source_target_pairs={{0,2},{1,3},{2,0},{3,1},{4,6},{5,7},{6,4},{7,5},{8,10},{9,11},{10,... | collective-permute-start | bytes 196616 | tf_op jit(solution)/shard_map/ppermute | solution.py:281
  8.6 10.1 %collective-permute-start.5 = (f32[32,1024]{1,0:T(8,128)S(1)}, f32[32,1024]{1,0:T(8,128)S(1)}, u32[]{:S(2)}, u32[]{:S(2)}) collective-permute-start(f32[32,1024]{1,0:T(8,128)S(1)} %copy-done.2), channel_id=1, source_target_pairs={{0,4},{4,0},{8,12},{12,8},{1,5},{5,1},{9,13},{13,9},{2,6},{6,2},{1... | collective-permute-start | bytes 393224 | tf_op jit(solution)/shard_map/ppermute | solution.py:281
  12.3 2.2 %collective-permute-start.3 = (f32[40,512]{1,0:T(8,128)S(1)}, f32[40,512]{1,0:T(8,128)S(1)}, u32[]{:S(2)}, u32[]{:S(2)}) collective-permute-start(f32[40,512]{1,0:T(8,128)S(1)} %get-tuple-element.14.refs_0_), channel_id=1, source_target_pairs={{0,1},{1,0},{2,3},{3,2},{4,5},{5,4},{6,7},{7,6},{8,9},{9,8},{10,11... | collective-permute-start | bytes 245768 | tf_op jit(solution)/shard_map/ppermute | solution.py:281
  12.4 2.1 %collective-permute-start.4 = (f32[40,512]{1,0:T(8,128)S(1)}, f32[40,512]{1,0:T(8,128)S(1)}, u32[]{:S(2)}, u32[]{:S(2)}) collective-permute-start(f32[40,512]{1,0:T(8,128)S(1)} %get-tuple-element.15.refs_1_), channel_id=1, source_target_pairs={{0,1},{1,0},{2,3},{3,2},{4,5},{5,4},{6,7},{7,6},{8,9},{9,8},{10,11... | collective-permute-start | bytes 245768 | tf_op jit(solution)/shard_map/ppermute | solution.py:281
  12.9 10.9 %collective-permute-start.9 = (f32[32,1024]{1,0:T(8,128)S(1)}, f32[32,1024]{1,0:T(8,128)S(1)}, u32[]{:S(2)}, u32[]{:S(2)}) collective-permute-start(f32[32,1024]{1,0:T(8,128)S(1)} %collective-permute-done.2.refs_0_.refs_5_), channel_id=1, source_target_pairs={{0,4},{4,0},{8,12},{12,8},{1,5},{5,1},{9,13},{13,9},{2,6},{6,2},{1... | collective-permute-start | bytes 393224 | tf_op jit(solution)/shard_map/ppermute | solution.py:281
  15.4 8.5 %collective-permute-start.7 = (f32[16,1024]{1,0:T(8,128)S(1)}, f32[16,1024]{1,0:T(8,128)S(1)}, u32[]{:S(2)}, u32[]{:S(2)}) collective-permute-start(f32[16,1024]{1,0:T(8,128)S(1)} %get-tuple-element.18), channel_id=1, source_target_pairs={{0,8},{4,12},{8,0},{12,4},{1,9},{5,13},{9,1},{13,5},{2,10},{6,14},... | collective-permute-start | bytes 196616 | tf_op jit(solution)/shard_map/ppermute | solution.py:281
  17.0 6.8 %collective-permute-start.8 = (f32[16,1024]{1,0:T(8,128)S(1)}, f32[16,1024]{1,0:T(8,128)S(1)}, u32[]{:S(2)}, u32[]{:S(2)}) collective-permute-start(f32[16,1024]{1,0:T(8,128)S(1)} %get-tuple-element.19), channel_id=1, source_target_pairs={{0,12},{4,8},{8,4},{12,0},{1,13},{5,9},{9,5},{13,1},{2,14},{6,10},... | collective-permute-start | bytes 196616 | tf_op jit(solution)/shard_map/ppermute | solution.py:281
  18.7 5.8 %collective-permute-start.6 = (f32[16,1024]{1,0:T(8,128)S(1)}, f32[16,1024]{1,0:T(8,128)S(1)}, u32[]{:S(2)}, u32[]{:S(2)}) collective-permute-start(f32[16,1024]{1,0:T(8,128)S(1)} %shard_map.102), channel_id=1, source_target_pairs={{0,4},{4,0},{8,12},{12,8},{1,5},{5,1},{9,13},{13,9},{2,6},{6,2},{1... | collective-permute-start | bytes 196616 | tf_op jit(solution)/shard_map/ppermute | solution.py:281
  25.0 1.3 %collective-permute-start.10 = (f32[64,128]{1,0:T(8,128)S(1)}, f32[64,128]{1,0:T(8,128)S(1)}, u32[]{:S(2)}, u32[]{:S(2)}) collective-permute-start(f32[64,128]{1,0:T(8,128)S(1)} %shard_map.105), channel_id=1, source_target_pairs={{0,1},{1,0},{2,3},{3,2},{4,5},{5,4},{6,7},{7,6},{8,9},{9,8},{10,11... | collective-permute-start | bytes 98312 | tf_op jit(solution)/shard_map/ppermute | solution.py:281
  26.3 3.9 %collective-permute-start.11 = (f32[64,128]{1,0:T(8,128)S(1)}, f32[64,128]{1,0:T(8,128)S(1)}, u32[]{:S(2)}, u32[]{:S(2)}) collective-permute-start(f32[64,128]{1,0:T(8,128)S(1)} %add.6), channel_id=1, source_target_pairs={{0,2},{1,3},{2,0},{3,1},{4,6},{5,7},{6,4},{7,5},{8,10},{9,11},{10,... | collective-permute-start | bytes 98312 | tf_op jit(solution)/shard_map/ppermute | solution.py:281

commit v14 on v13

--- a/solution.py
+++ b/solution.py
@@ -17,7 +17,7 @@
 X_FLOPS = 6 * 10**8
 MASK_FLOPS = 2 * 10**8
 EARLY_FLOPS = 3 * 10**8
-LATE_FLOPS = 2 * 10**8
+LATE_FLOPS = 10**8
 
 
 def params(mib):
@@ -42,7 +42,7 @@
     row = lax.broadcasted_iota(jnp.int32, (docs, docs), 0)
     col = lax.broadcasted_iota(jnp.int32, (docs, docs), 1)
     len_row = lengths.astype(F32)
-    place_row = owner ^ lax.axis_index("dp") if relative else owner
+    place_row = lax.rem(owner - lax.axis_index("dp") + 2 * owners - 1, owners) if relative else owner
     own_row = place_row.astype(F32)
 
     def column(values):
@@ -240,7 +240,8 @@
     picked = mm(jnp.concatenate([top, rest, last], axis=0), hot)
     total = picked[:slots] + picked[slots : 2 * slots] + picked[2 * slots :]
     for k in range(count):
-        spot = pl.ds(pl.multiple_of((me ^ k) * cap, cap), cap) if relative else pl.ds(k * cap, cap)
+        source = lax.rem(me - k + count, count) if relative else k
+        spot = pl.ds(pl.multiple_of(source * cap, cap), cap)
         scores_ref[spot, :] = total[k * cap : (k + 1) * cap, :]
 
 
@@ -264,7 +265,8 @@
     me = lax.axis_index("dp")
     cap = rows[0].shape[0]
     for k, row in enumerate(rows):
-        store_ref[pl.ds(pl.multiple_of((me ^ k) * cap, cap), cap), :] = row[...]
+        source = lax.rem(me - k + len(rows), len(rows))
+        store_ref[pl.ds(pl.multiple_of(source * cap, cap), cap), :] = row[...]
 
 
 def place(rows):
@@ -279,6 +281,11 @@
 
 def swap(x, axis, gap):
     return lax.ppermute(x, axis, [(i, i ^ gap) for i in range(lax.axis_size(axis))])
+
+
+def shift(x, axis, by):
+    size = lax.axis_size(axis)
+    return lax.ppermute(x, axis, [(i, (i + by) % size) for i in range(size)])
 
 
 def gather_pieces(piece):
@@ -322,9 +329,12 @@
         gots = [swap(part, "tensor", bit) for part in own]
     blocks = outer(own, gots, keep, mask, data_size)
     if direct:
-        far = [swap(blocks[k], "dp", k) for k in range(data_size - 1, 1, -1)]
-        rows = [blocks[0], swap(after(blocks[1], mate), "dp", 1), *far[::-1]]
-        late = [token(far, LATE_FLOPS)]
+        *sent, kept = blocks
+        sent[-1] = after(sent[-1], mate)
+        rows = [kept] + [shift(block, "dp", k) for k, block in enumerate(sent, 1)]
+        late = []
+        for row in rows[1:-1]:
+            late = [token([row, *late], LATE_FLOPS)]
         pieces, gaps = [*pieces, mate, *passed], [*gaps, *(g ^ 1 for g in gaps)]
         store = place(rows)
     else:

time: 30.9 us -> 30.3 us (0.981)
  waiting for transfers between devices: 11.1 us -> 9.02 us
  starting transfers between devices: 14.4 us -> 15.9 us
    ppermute x12 -> x9, waiting for transfers between devices: 11.1 us -> 5.14 us  [swap(): lax.ppermute(x, axis, [(i, i ^ gap) for i in range(lax.axis_size(axis))])]
    ppermute x0 -> x3, starting transfers between devices: none -> 4.65 us  [shift(): return lax.ppermute(x, axis, [(i, (i + by) % size) for i in range(size)])]
    ppermute x0 -> x3, waiting for transfers between devices: none -> 3.88 us  [shift(): return lax.ppermute(x, axis, [(i, (i + by) % size) for i in range(size)])]
    ppermute x12 -> x9, starting transfers between devices: 14.4 us -> 11.2 us  [swap(): lax.ppermute(x, axis, [(i, i ^ gap) for i in range(lax.axis_size(axis))])]
where the time goes in v14:
time: 30.3 us; the launch traced here: 30.2 us
  starting transfers between devices  15.9 us (52%)
  waiting for transfers between devices  9.02 us (30%)
  Pallas kernels  3.87 us (13%)
  between operations  0.76 us (3%)
  other arithmetic  0.63 us (2%)
    ppermute x9, starting transfers between devices, swap(): lax.ppermute(x, axis, [(i, i ^ gap) for i in range(lax.axis_size(axis))])  11.2 us
    ppermute x9, waiting for transfers between devices, swap(): lax.ppermute(x, axis, [(i, i ^ gap) for i in range(lax.axis_size(axis))])  5.14 us
    ppermute x3, starting transfers between devices, shift(): return lax.ppermute(x, axis, [(i, (i + by) % size) for i in range(size)])  4.65 us
    ppermute x3, waiting for transfers between devices, shift(): return lax.ppermute(x, axis, [(i, (i + by) % size) for i in range(size)])  3.88 us
    pallas_call x1, Pallas kernels, project_g(): pl.pallas_call(functools.partial(g_kernel, width), out_shape=[part, part]...  1.16 us
    pallas_call x1, Pallas kernels, outer(): pl.pallas_call(functools.partial(outer_kernel, owners, len(sent)), out_sh...  0.84 us
    pallas_call x1, Pallas kernels, place(): pl.pallas_call(place_kernel, out_shape=jax.ShapeDtypeStruct((slots, feats...  0.72 us
    mul x1, other arithmetic, local(): return (store, scores * (1.0 / (rank * rank)))  0.62 us
  transfers between devices with their start and end apart: 12, of which 6 were waited for; matrix products, arithmetic and copies ran while one was open for 0% of the time, Pallas kernels for 11%

profile of v14, /device:TPU:0, one launch (start us, length us, event | category | flops | bytes accessed | tf_op | source)
XLA Modules:
  0.0 30.2 jit_solution(18119051021301539052)
XLA Ops:
  0.7 4.1 %collective-permute-start.2 = (f32[32,1024]{1,0:T(8,128)}, f32[32,1024]{1,0:T(8,128)S(1)}, u32[]{:S(2)}, u32[]{:S(2)}) collective-permute-start(f32[32,1024]{1,0:T(8,128)} %refs_4_.1), channel_id=1, source_target_pairs={{0,8},{4,12},{8,0},{12,4},{1,9},{5,13},{9,1},{13,5},{2,10},{6,14},... | collective-permute-start | bytes 393224 | tf_op jit(solution)/shard_map/ppermute | solution.py:283
  4.8 0.5 %shard_map.97.refs_0_ = f32[64,512]{1,0:T(8,128)S(1)} custom-call(bf16[512,1024]{1,0:T(8,128)(2,1)S(1)} %copy-done.4, bf16[64,1024]{1,0:T(8,128)(2,1)S(1)} %bitcast.6, f32[8,128]{1,0:T(8,128)S(1)} %shard_map.96.refs_0_), custom_call_target="tpu_custom_call" | custom-call | flops 600000000 | tf_op jit(solution)/shard_map/pallas_call | solution.py:87
  5.3 1.5 %collective-permute-start = (f32[64,512]{1,0:T(8,128)S(1)}, f32[64,512]{1,0:T(8,128)S(1)}, u32[]{:S(2)}, u32[]{:S(2)}) collective-permute-start(f32[64,512]{1,0:T(8,128)S(1)} %shard_map.97.refs_0_), channel_id=1, source_target_pairs={{0,2},{1,3},{2,0},{3,1},{4,6},{5,7},{6,4},{7,5},{8,10},{9,11},{10,... | collective-permute-start | bytes 393224 | tf_op jit(solution)/shard_map/ppermute | solution.py:283
  6.8 1.2 %shard_map.95 = (f32[32,512]{1,0:T(8,128)S(1)}, f32[32,512]{1,0:T(8,128)S(1)}) custom-call(bf16[512,3584]{1,0:T(8,128)(2,1)S(1)} %copy-done, bf16[64,3584]{1,0:T(8,128)(2,1)S(1)} %bitcast.4), custom_call_target="tpu_custom_call" | custom-call | tf_op jit(solution)/shard_map/pallas_call | solution.py:110
  8.0 0.6 %collective-permute-start.1 = (f32[32,512]{1,0:T(8,128)S(1)}, f32[32,512]{1,0:T(8,128)S(1)}, u32[]{:S(2)}, u32[]{:S(2)}) collective-permute-start(f32[32,512]{1,0:T(8,128)S(1)} %get-tuple-element.12), channel_id=1, source_target_pairs={{0,2},{1,3},{2,0},{3,1},{4,6},{5,7},{6,4},{7,5},{8,10},{9,11},{10,... | collective-permute-start | bytes 196616 | tf_op jit(solution)/shard_map/ppermute | solution.py:283
  8.6 1.6 %collective-permute-start.7 = (f32[32,1024]{1,0:T(8,128)S(1)}, f32[32,1024]{1,0:T(8,128)S(1)}, u32[]{:S(2)}, u32[]{:S(2)}) collective-permute-start(f32[32,1024]{1,0:T(8,128)S(1)} %copy-done.2), channel_id=1, source_target_pairs={{0,4},{4,0},{8,12},{12,8},{1,5},{5,1},{9,13},{13,9},{2,6},{6,2},{1... | collective-permute-start | bytes 393224 | tf_op jit(solution)/shard_map/ppermute | solution.py:283
  10.2 0.2 shard_map.98.refs_3_.mask_ref
  10.4 1.0 %collective-permute-done.2.refs_0_.refs_5_ = f32[32,1024]{1,0:T(8,128)S(1)} collective-permute-done((f32[32,1024]{1,0:T(8,128)}, f32[32,1024]{1,0:T(8,128)S(1)}, u32[]{:S(2)}, u32[]{:S(2)}) %collective-permute-start.2) | collective-permute-done | bytes 131104 | tf_op jit(solution)/shard_map/ppermute | solution.py:283
  11.4 0.9 %collective-permute-done.1.refs_2_ = f32[32,512]{1,0:T(8,128)S(1)} collective-permute-done((f32[32,512]{1,0:T(8,128)S(1)}, f32[32,512]{1,0:T(8,128)S(1)}, u32[]{:S(2)}, u32[]{:S(2)}) %collective-permute-start.1) | collective-permute-done | bytes 65568 | tf_op jit(solution)/shard_map/ppermute | solution.py:283
  12.4 0.5 %collective-permute-start.4 = (f32[40,512]{1,0:T(8,128)S(1)}, f32[40,512]{1,0:T(8,128)S(1)}, u32[]{:S(2)}, u32[]{:S(2)}) collective-permute-start(f32[40,512]{1,0:T(8,128)S(1)} %get-tuple-element.15.refs_1_), channel_id=1, source_target_pairs={{0,1},{1,0},{2,3},{3,2},{4,5},{5,4},{6,7},{7,6},{8,9},{9,8},{10,11... | collective-permute-start | bytes 245768 | tf_op jit(solution)/shard_map/ppermute | solution.py:283
  12.9 1.6 %collective-permute-start.9 = (f32[32,1024]{1,0:T(8,128)S(1)}, f32[32,1024]{1,0:T(8,128)S(1)}, u32[]{:S(2)}, u32[]{:S(2)}) collective-permute-start(f32[32,1024]{1,0:T(8,128)S(1)} %collective-permute-done.2.refs_0_.refs_5_), channel_id=1, source_target_pairs={{0,4},{4,0},{8,12},{12,8},{1,5},{5,1},{9,13},{13,9},{2,6},{6,2},{1... | collective-permute-start | bytes 393224 | tf_op jit(solution)/shard_map/ppermute | solution.py:283
  14.5 0.8 %shard_map.101 = (f32[16,1024]{1,0:T(8,128)S(1)}, f32[16,1024]{1,0:T(8,128)S(1)}, f32[16,1024]{1,0:T(8,128)S(1)}, f32[16,1024]{1,0:T(8,128)S(1)}) custom-call(f32[16,512]{1,0:T(8,128)S(1)} %get-tuple-element.13.g_ref, f32[64,512]{1,0:T(8,128)S(1)} %shard_map.98.refs_3_.mask_ref, f32[40,512]{1,0:T(8,128)S(1)} %get-tuple-element.14.refs_0_, ...), custom_call_target="tpu_custom_call" | custom-call | flops 268435456 | bytes 262144 | tf_op jit(solution)/shard_map/pallas_call | solution.py:186
  15.4 1.0 %collective-permute-start.5 = (f32[16,1024]{1,0:T(8,128)S(1)}, f32[16,1024]{1,0:T(8,128)S(1)}, u32[]{:S(2)}, u32[]{:S(2)}) collective-permute-start(f32[16,1024]{1,0:T(8,128)S(1)} %get-tuple-element.17), channel_id=1, source_target_pairs={{0,4},{4,8},{8,12},{12,0},{1,5},{5,9},{9,13},{13,1},{2,6},{6,10},{... | collective-permute-start | bytes 196616 | tf_op jit(solution)/shard_map/ppermute | solution.py:288
  16.3 1.6 %collective-permute-start.6 = (f32[16,1024]{1,0:T(8,128)S(1)}, f32[16,1024]{1,0:T(8,128)S(1)}, u32[]{:S(2)}, u32[]{:S(2)}) collective-permute-start(f32[16,1024]{1,0:T(8,128)S(1)} %get-tuple-element.18), channel_id=1, source_target_pairs={{0,8},{4,12},{8,0},{12,4},{1,9},{5,13},{9,1},{13,5},{2,10},{6,14},... | collective-permute-start | bytes 196616 | tf_op jit(solution)/shard_map/ppermute | solution.py:288
  18.0 2.0 %collective-permute-start.8 = (f32[16,1024]{1,0:T(8,128)S(1)}, f32[16,1024]{1,0:T(8,128)S(1)}, u32[]{:S(2)}, u32[]{:S(2)}) collective-permute-start(f32[16,1024]{1,0:T(8,128)S(1)} %shard_map.102), channel_id=1, source_target_pairs={{0,12},{4,0},{8,4},{12,8},{1,13},{5,1},{9,5},{13,9},{2,14},{6,2},{... | collective-permute-start | bytes 196616 | tf_op jit(solution)/shard_map/ppermute | solution.py:288
  20.0 2.3 %collective-permute-done.5.refs_1_.refs_0_ = f32[16,1024]{1,0:T(8,128)S(1)} collective-permute-done((f32[16,1024]{1,0:T(8,128)S(1)}, f32[16,1024]{1,0:T(8,128)S(1)}, u32[]{:S(2)}, u32[]{:S(2)}) %collective-permute-start.5) | collective-permute-done | bytes 65568 | tf_op jit(solution)/shard_map/ppermute | solution.py:288
  22.3 1.6 %collective-permute-done.6.refs_2_.refs_0_ = f32[16,1024]{1,0:T(8,128)S(1)} collective-permute-done((f32[16,1024]{1,0:T(8,128)S(1)}, f32[16,1024]{1,0:T(8,128)S(1)}, u32[]{:S(2)}, u32[]{:S(2)}) %collective-permute-start.6) | collective-permute-done | bytes 65568 | tf_op jit(solution)/shard_map/ppermute | solution.py:288
  23.9 0.4 %shard_map.106 = f32[64,128]{1,0:T(8,128)S(1)} custom-call(s32[1,128]{1,0:T(1,128)S(1)} %bitcast.5, f32[16,1024]{1,0:T(8,128)S(1)} %get-tuple-element.16.refs_0_, f32[16,1024]{1,0:T(8,128)S(1)} %collective-permute-done.5.refs_1_.refs_0_, f32[16,1024]{1,0:T(8,128)S(1)} %collective-permute-done.6.refs_2_.refs_0_, ...), custom_call_target="tpu_custom_call" | custom-call | flops 50331648 | bytes 524288 | tf_op jit(solution)/shard_map/pallas_call | solution.py:253
  24.4 0.1 collective-permute-start.10
  24.4 1.2 %collective-permute-done.10 = f32[64,128]{1,0:T(8,128)S(1)} collective-permute-done((f32[64,128]{1,0:T(8,128)S(1)}, f32[64,128]{1,0:T(8,128)S(1)}, u32[]{:S(2)}, u32[]{:S(2)}) %collective-permute-start.10) | collective-permute-done | bytes 32800 | tf_op jit(solution)/shard_map/ppermute | solution.py:283
  25.6 1.2 %collective-permute-start.11 = (f32[64,128]{1,0:T(8,128)S(1)}, f32[64,128]{1,0:T(8,128)S(1)}, u32[]{:S(2)}, u32[]{:S(2)}) collective-permute-start(f32[64,128]{1,0:T(8,128)S(1)} %add.6), channel_id=1, source_target_pairs={{0,2},{1,3},{2,0},{3,1},{4,6},{5,7},{6,4},{7,5},{8,10},{9,11},{10,... | collective-permute-start | bytes 98312 | tf_op jit(solution)/shard_map/ppermute | solution.py:283
  26.8 0.7 %shard_map.103 = f32[64,1024]{1,0:T(8,128)} custom-call(f32[16,1024]{1,0:T(8,128)S(1)} %get-tuple-element.16.refs_0_, f32[16,1024]{1,0:T(8,128)S(1)} %collective-permute-done.5.refs_1_.refs_0_, f32[16,1024]{1,0:T(8,128)S(1)} %collective-permute-done.6.refs_2_.refs_0_, f32[16,1024]{1,0:T(8,128)S(1)} %collective-permute-done.8.refs_3_), custom_call_target="tpu_custom_call" | custom-call | bytes 524288 | tf_op jit(solution)/shard_map/pallas_call | solution.py:274
  27.6 2.0 %collective-permute-done.11 = f32[64,128]{1,0:T(8,128)S(1)} collective-permute-done((f32[64,128]{1,0:T(8,128)S(1)}, f32[64,128]{1,0:T(8,128)S(1)}, u32[]{:S(2)}, u32[]{:S(2)}) %collective-permute-start.11) | collective-permute-done | bytes 32800 | tf_op jit(solution)/shard_map/ppermute | solution.py:283
  29.6 0.6 %add_multiply_fusion = f32[64,128]{1,0:T(8,128)} fusion(f32[64,128]{1,0:T(8,128)S(1)} %add.6, f32[64,128]{1,0:T(8,128)S(1)} %collective-permute-done.11), kind=kLoop, calls=%fused_computation | loop fusion | flops 16384 | bytes 98304 | tf_op jit(solution)/shard_map/mul | solution.py:348
  (30 shorter events, 0.2 us)
Async XLA Ops:
  0.6 4.2 %copy-start.5 = (bf16[1024,64]{0,1:T(8,128)(2,1)S(1)}, bf16[1024,64]{0,1:T(8,128)(2,1)}, u32[]{:S(2)}) copy-start(bf16[1024,64]{0,1:T(8,128)(2,1)} %param.10) | copy-start | bytes 393220
  0.6 4.2 %copy-start.4 = (bf16[512,1024]{1,0:T(8,128)(2,1)S(1)}, bf16[512,1024]{1,0:T(8,128)(2,1)}, u32[]{:S(2)}) copy-start(bf16[512,1024]{1,0:T(8,128)(2,1)} %act_ref.1) | copy-start | bytes 3145732
  0.7 6.2 %copy-start.1 = (bf16[3584,64]{0,1:T(8,128)(2,1)S(1)}, bf16[3584,64]{0,1:T(8,128)(2,1)}, u32[]{:S(2)}) copy-start(bf16[3584,64]{0,1:T(8,128)(2,1)} %param.11) | copy-start | bytes 1376260
  0.7 6.2 %copy-start = (bf16[512,3584]{1,0:T(8,128)(2,1)S(1)}, bf16[512,3584]{1,0:T(8,128)(2,1)}, u32[]{:S(2)}) copy-start(bf16[512,3584]{1,0:T(8,128)(2,1)} %grad_ref.1) | copy-start | bytes 11010052
  0.7 10.7 %collective-permute-start.2 = (f32[32,1024]{1,0:T(8,128)}, f32[32,1024]{1,0:T(8,128)S(1)}, u32[]{:S(2)}, u32[]{:S(2)}) collective-permute-start(f32[32,1024]{1,0:T(8,128)} %refs_4_.1), channel_id=1, source_target_pairs={{0,8},{4,12},{8,0},{12,4},{1,9},{5,13},{9,1},{13,5},{2,10},{6,14},... | collective-permute-start | bytes 393224 | tf_op jit(solution)/shard_map/ppermute | solution.py:283
  4.8 3.8 %copy-start.2 = (f32[32,1024]{1,0:T(8,128)S(1)}, f32[32,1024]{1,0:T(8,128)}, u32[]{:S(2)}) copy-start(f32[32,1024]{1,0:T(8,128)} %refs_4_.1) | copy-start | bytes 393220
  4.8 5.4 %copy-start.6 = (s32[1,32]{1,0:T(1,128)S(1)}, s32[1,32]{1,0:T(1,128)}, u32[]{:S(2)}) copy-start(s32[1,32]{1,0:T(1,128)} %lengths_ref.1) | copy-start | bytes 388
  4.8 5.4 %copy-start.7 = (s32[32,1]{0,1:T(1,128)S(1)}, s32[32,1]{0,1:T(1,128)}, u32[]{:S(2)}) copy-start(s32[32,1]{0,1:T(1,128)} %param.13) | copy-start | bytes 388
  5.3 7.1 %collective-permute-start = (f32[64,512]{1,0:T(8,128)S(1)}, f32[64,512]{1,0:T(8,128)S(1)}, u32[]{:S(2)}, u32[]{:S(2)}) collective-permute-start(f32[64,512]{1,0:T(8,128)S(1)} %shard_map.97.refs_0_), channel_id=1, source_target_pairs={{0,2},{1,3},{2,0},{3,1},{4,6},{5,7},{6,4},{7,5},{8,10},{9,11},{10,... | collective-permute-start | bytes 393224 | tf_op jit(solution)/shard_map/ppermute | solution.py:283
  6.8 17.1 %copy-start.3 = (s32[128]{0:T(128)S(1)}, s32[128]{0:T(128)}, u32[]{:S(2)}) copy-start(s32[128]{0:T(128)} %param.15) | copy-start | bytes 1540
  8.0 4.3 %collective-permute-start.1 = (f32[32,512]{1,0:T(8,128)S(1)}, f32[32,512]{1,0:T(8,128)S(1)}, u32[]{:S(2)}, u32[]{:S(2)}) collective-permute-start(f32[32,512]{1,0:T(8,128)S(1)} %get-tuple-element.12), channel_id=1, source_target_pairs={{0,2},{1,3},{2,0},{3,1},{4,6},{5,7},{6,4},{7,5},{8,10},{9,11},{10,... | collective-permute-start | bytes 196616 | tf_op jit(solution)/shard_map/ppermute | solution.py:283
  8.6 9.4 %collective-permute-start.7 = (f32[32,1024]{1,0:T(8,128)S(1)}, f32[32,1024]{1,0:T(8,128)S(1)}, u32[]{:S(2)}, u32[]{:S(2)}) collective-permute-start(f32[32,1024]{1,0:T(8,128)S(1)} %copy-done.2), channel_id=1, source_target_pairs={{0,4},{4,0},{8,12},{12,8},{1,5},{5,1},{9,13},{13,9},{2,6},{6,2},{1... | collective-permute-start | bytes 393224 | tf_op jit(solution)/shard_map/ppermute | solution.py:283
  12.3 2.2 %collective-permute-start.3 = (f32[40,512]{1,0:T(8,128)S(1)}, f32[40,512]{1,0:T(8,128)S(1)}, u32[]{:S(2)}, u32[]{:S(2)}) collective-permute-start(f32[40,512]{1,0:T(8,128)S(1)} %get-tuple-element.14.refs_0_), channel_id=1, source_target_pairs={{0,1},{1,0},{2,3},{3,2},{4,5},{5,4},{6,7},{7,6},{8,9},{9,8},{10,11... | collective-permute-start | bytes 245768 | tf_op jit(solution)/shard_map/ppermute | solution.py:283
  12.4 2.1 %collective-permute-start.4 = (f32[40,512]{1,0:T(8,128)S(1)}, f32[40,512]{1,0:T(8,128)S(1)}, u32[]{:S(2)}, u32[]{:S(2)}) collective-permute-start(f32[40,512]{1,0:T(8,128)S(1)} %get-tuple-element.15.refs_1_), channel_id=1, source_target_pairs={{0,1},{1,0},{2,3},{3,2},{4,5},{5,4},{6,7},{7,6},{8,9},{9,8},{10,11... | collective-permute-start | bytes 245768 | tf_op jit(solution)/shard_map/ppermute | solution.py:283
  12.9 11.0 %collective-permute-start.9 = (f32[32,1024]{1,0:T(8,128)S(1)}, f32[32,1024]{1,0:T(8,128)S(1)}, u32[]{:S(2)}, u32[]{:S(2)}) collective-permute-start(f32[32,1024]{1,0:T(8,128)S(1)} %collective-permute-done.2.refs_0_.refs_5_), channel_id=1, source_target_pairs={{0,4},{4,0},{8,12},{12,8},{1,5},{5,1},{9,13},{13,9},{2,6},{6,2},{1... | collective-permute-start | bytes 393224 | tf_op jit(solution)/shard_map/ppermute | solution.py:283
  15.4 6.9 %collective-permute-start.5 = (f32[16,1024]{1,0:T(8,128)S(1)}, f32[16,1024]{1,0:T(8,128)S(1)}, u32[]{:S(2)}, u32[]{:S(2)}) collective-permute-start(f32[16,1024]{1,0:T(8,128)S(1)} %get-tuple-element.17), channel_id=1, source_target_pairs={{0,4},{4,8},{8,12},{12,0},{1,5},{5,9},{9,13},{13,1},{2,6},{6,10},{... | collective-permute-start | bytes 196616 | tf_op jit(solution)/shard_map/ppermute | solution.py:288
  16.3 7.6 %collective-permute-start.6 = (f32[16,1024]{1,0:T(8,128)S(1)}, f32[16,1024]{1,0:T(8,128)S(1)}, u32[]{:S(2)}, u32[]{:S(2)}) collective-permute-start(f32[16,1024]{1,0:T(8,128)S(1)} %get-tuple-element.18), channel_id=1, source_target_pairs={{0,8},{4,12},{8,0},{12,4},{1,9},{5,13},{9,1},{13,5},{2,10},{6,14},... | collective-permute-start | bytes 196616 | tf_op jit(solution)/shard_map/ppermute | solution.py:288
  18.0 5.9 %collective-permute-start.8 = (f32[16,1024]{1,0:T(8,128)S(1)}, f32[16,1024]{1,0:T(8,128)S(1)}, u32[]{:S(2)}, u32[]{:S(2)}) collective-permute-start(f32[16,1024]{1,0:T(8,128)S(1)} %shard_map.102), channel_id=1, source_target_pairs={{0,12},{4,0},{8,4},{12,8},{1,13},{5,1},{9,5},{13,9},{2,14},{6,2},{... | collective-permute-start | bytes 196616 | tf_op jit(solution)/shard_map/ppermute | solution.py:288
  24.4 1.3 %collective-permute-start.10 = (f32[64,128]{1,0:T(8,128)S(1)}, f32[64,128]{1,0:T(8,128)S(1)}, u32[]{:S(2)}, u32[]{:S(2)}) collective-permute-start(f32[64,128]{1,0:T(8,128)S(1)} %shard_map.106), channel_id=1, source_target_pairs={{0,1},{1,0},{2,3},{3,2},{4,5},{5,4},{6,7},{7,6},{8,9},{9,8},{10,11... | collective-permute-start | bytes 98312 | tf_op jit(solution)/shard_map/ppermute | solution.py:283
  25.6 3.9 %collective-permute-start.11 = (f32[64,128]{1,0:T(8,128)S(1)}, f32[64,128]{1,0:T(8,128)S(1)}, u32[]{:S(2)}, u32[]{:S(2)}) collective-permute-start(f32[64,128]{1,0:T(8,128)S(1)} %add.6), channel_id=1, source_target_pairs={{0,2},{1,3},{2,0},{3,1},{4,6},{5,7},{6,4},{7,5},{8,10},{9,11},{10,... | collective-permute-start | bytes 98312 | tf_op jit(solution)/shard_map/ppermute | solution.py:283

commit v15 on v14

--- a/solution.py
+++ b/solution.py
@@ -205,18 +205,19 @@
     )(*arrays)
 
 
-def after_kernel(block_ref, piece, out_ref):
-    out_ref[...] = block_ref[...]
-
-
-def after(block, piece):
+def after_kernel(block_ref, *refs):
+    refs[-1][...] = block_ref[...]
+
+
+def after(block, pieces):
     return pl.pallas_call(
         after_kernel,
-        in_specs=[pl.BlockSpec(memory_space=pltpu.VMEM), pl.BlockSpec(memory_space=pl.ANY)],
+        in_specs=[pl.BlockSpec(memory_space=pltpu.VMEM)]
+        + [pl.BlockSpec(memory_space=pl.ANY)] * len(pieces),
         out_shape=jax.ShapeDtypeStruct(block.shape, F32),
         compiler_params=params(4),
         cost_estimate=cost(0, 0),
-    )(block, piece)
+    )(block, *pieces)
 
 
 def score_kernel(count, gaps, relative, ids_ref, *refs):
@@ -330,7 +331,7 @@
     blocks = outer(own, gots, keep, mask, data_size)
     if direct:
         *sent, kept = blocks
-        sent[-1] = after(sent[-1], mate)
+        sent[-1] = after(sent[-1], [mate, *passed])
         rows = [kept] + [shift(block, "dp", k) for k, block in enumerate(sent, 1)]
         late = []
         for row in rows[1:-1]:

time: 30.3 us -> 30.2 us (level)
  waiting for transfers between devices: 9.02 us -> 8.01 us
  starting transfers between devices: 15.9 us -> 16.8 us
    ppermute x3, starting transfers between devices: 4.65 us -> 6.23 us  [shift(): return lax.ppermute(x, axis, [(i, (i + by) % size) for i in range(size)])]
    ppermute x3, waiting for transfers between devices: 3.88 us -> 2.85 us  [shift(): return lax.ppermute(x, axis, [(i, (i + by) % size) for i in range(size)])]
    ppermute x9, starting transfers between devices: 11.2 us -> 10.6 us  [swap(): lax.ppermute(x, axis, [(i, i ^ gap) for i in range(lax.axis_size(axis))])]
  transfers between devices with their start and end apart: 12 -> 12, of which waited for: 6 -> 8; matrix products, arithmetic and copies ran while one was open for 0% -> 0% of each run, Pallas kernels for 11% -> 11%
where the time goes in v15:
time: 30.2 us; the launch traced here: 30.1 us
  starting transfers between devices  16.8 us (56%)
  waiting for transfers between devices  8.01 us (27%)
  Pallas kernels  3.87 us (13%)
  between operations  0.76 us (3%)
  other arithmetic  0.63 us (2%)
    ppermute x9, starting transfers between devices, swap(): lax.ppermute(x, axis, [(i, i ^ gap) for i in range(lax.axis_size(axis))])  10.6 us
    ppermute x3, starting transfers between devices, shift(): return lax.ppermute(x, axis, [(i, (i + by) % size) for i in range(size)])  6.23 us
    ppermute x9, waiting for transfers between devices, swap(): lax.ppermute(x, axis, [(i, i ^ gap) for i in range(lax.axis_size(axis))])  5.16 us
    ppermute x3, waiting for transfers between devices, shift(): return lax.ppermute(x, axis, [(i, (i + by) % size) for i in range(size)])  2.85 us
    pallas_call x1, Pallas kernels, project_g(): pl.pallas_call(functools.partial(g_kernel, width), out_shape=[part, part]...  1.16 us
    pallas_call x1, Pallas kernels, outer(): pl.pallas_call(functools.partial(outer_kernel, owners, len(sent)), out_sh...  0.84 us
    pallas_call x1, Pallas kernels, place(): pl.pallas_call(place_kernel, out_shape=jax.ShapeDtypeStruct((slots, feats...  0.72 us
    mul x1, other arithmetic, local(): return (store, scores * (1.0 / (rank * rank)))  0.62 us
  transfers between devices with their start and end apart: 12, of which 8 were waited for; matrix products, arithmetic and copies ran while one was open for 0% of the time, Pallas kernels for 11%

profile of v15, /device:TPU:0, one launch (start us, length us, event | category | flops | bytes accessed | tf_op | source)
XLA Modules:
  0.0 30.1 jit_solution(5598029394304759027)
XLA Ops:
  0.7 4.1 %collective-permute-start.2 = (f32[32,1024]{1,0:T(8,128)}, f32[32,1024]{1,0:T(8,128)S(1)}, u32[]{:S(2)}, u32[]{:S(2)}) collective-permute-start(f32[32,1024]{1,0:T(8,128)} %refs_4_.1), channel_id=1, source_target_pairs={{0,8},{4,12},{8,0},{12,4},{1,9},{5,13},{9,1},{13,5},{2,10},{6,14},... | collective-permute-start | bytes 393224 | tf_op jit(solution)/shard_map/ppermute | solution.py:284
  4.8 0.5 %shard_map.97.refs_0_ = f32[64,512]{1,0:T(8,128)S(1)} custom-call(bf16[512,1024]{1,0:T(8,128)(2,1)S(1)} %copy-done.4, bf16[64,1024]{1,0:T(8,128)(2,1)S(1)} %bitcast.6, f32[8,128]{1,0:T(8,128)S(1)} %shard_map.96.refs_0_), custom_call_target="tpu_custom_call" | custom-call | flops 600000000 | tf_op jit(solution)/shard_map/pallas_call | solution.py:87
  5.3 1.5 %collective-permute-start = (f32[64,512]{1,0:T(8,128)S(1)}, f32[64,512]{1,0:T(8,128)S(1)}, u32[]{:S(2)}, u32[]{:S(2)}) collective-permute-start(f32[64,512]{1,0:T(8,128)S(1)} %shard_map.97.refs_0_), channel_id=1, source_target_pairs={{0,2},{1,3},{2,0},{3,1},{4,6},{5,7},{6,4},{7,5},{8,10},{9,11},{10,... | collective-permute-start | bytes 393224 | tf_op jit(solution)/shard_map/ppermute | solution.py:284
  6.8 1.2 %shard_map.95 = (f32[32,512]{1,0:T(8,128)S(1)}, f32[32,512]{1,0:T(8,128)S(1)}) custom-call(bf16[512,3584]{1,0:T(8,128)(2,1)S(1)} %copy-done, bf16[64,3584]{1,0:T(8,128)(2,1)S(1)} %bitcast.4), custom_call_target="tpu_custom_call" | custom-call | tf_op jit(solution)/shard_map/pallas_call | solution.py:110
  8.0 0.6 %collective-permute-start.1 = (f32[32,512]{1,0:T(8,128)S(1)}, f32[32,512]{1,0:T(8,128)S(1)}, u32[]{:S(2)}, u32[]{:S(2)}) collective-permute-start(f32[32,512]{1,0:T(8,128)S(1)} %get-tuple-element.12), channel_id=1, source_target_pairs={{0,2},{1,3},{2,0},{3,1},{4,6},{5,7},{6,4},{7,5},{8,10},{9,11},{10,... | collective-permute-start | bytes 196616 | tf_op jit(solution)/shard_map/ppermute | solution.py:284
  8.6 1.6 %collective-permute-start.7 = (f32[32,1024]{1,0:T(8,128)S(1)}, f32[32,1024]{1,0:T(8,128)S(1)}, u32[]{:S(2)}, u32[]{:S(2)}) collective-permute-start(f32[32,1024]{1,0:T(8,128)S(1)} %copy-done.2), channel_id=1, source_target_pairs={{0,4},{4,0},{8,12},{12,8},{1,5},{5,1},{9,13},{13,9},{2,6},{6,2},{1... | collective-permute-start | bytes 393224 | tf_op jit(solution)/shard_map/ppermute | solution.py:284
  10.2 0.2 shard_map.98.refs_3_.mask_ref
  10.4 1.0 %collective-permute-done.2.refs_0_.refs_5_ = f32[32,1024]{1,0:T(8,128)S(1)} collective-permute-done((f32[32,1024]{1,0:T(8,128)}, f32[32,1024]{1,0:T(8,128)S(1)}, u32[]{:S(2)}, u32[]{:S(2)}) %collective-permute-start.2) | collective-permute-done | bytes 131104 | tf_op jit(solution)/shard_map/ppermute | solution.py:284
  11.4 0.7 %collective-permute-start.8 = (f32[32,1024]{1,0:T(8,128)S(1)}, f32[32,1024]{1,0:T(8,128)S(1)}, u32[]{:S(2)}, u32[]{:S(2)}) collective-permute-start(f32[32,1024]{1,0:T(8,128)S(1)} %collective-permute-done.2.refs_0_.refs_5_), channel_id=1, source_target_pairs={{0,4},{4,0},{8,12},{12,8},{1,5},{5,1},{9,13},{13,9},{2,6},{6,2},{1... | collective-permute-start | bytes 393224 | tf_op jit(solution)/shard_map/ppermute | solution.py:284
  12.1 0.2 collective-permute-done.1.refs_2_
  12.4 0.5 %collective-permute-start.4 = (f32[40,512]{1,0:T(8,128)S(1)}, f32[40,512]{1,0:T(8,128)S(1)}, u32[]{:S(2)}, u32[]{:S(2)}) collective-permute-start(f32[40,512]{1,0:T(8,128)S(1)} %get-tuple-element.15.refs_1_), channel_id=1, source_target_pairs={{0,1},{1,0},{2,3},{3,2},{4,5},{5,4},{6,7},{7,6},{8,9},{9,8},{10,11... | collective-permute-start | bytes 245768 | tf_op jit(solution)/shard_map/ppermute | solution.py:284
  12.9 0.8 %collective-permute-done.3.refs_2_ = f32[40,512]{1,0:T(8,128)S(1)} collective-permute-done((f32[40,512]{1,0:T(8,128)S(1)}, f32[40,512]{1,0:T(8,128)S(1)}, u32[]{:S(2)}, u32[]{:S(2)}) %collective-permute-start.3) | collective-permute-done | bytes 81952 | tf_op jit(solution)/shard_map/ppermute | solution.py:284
  13.7 0.2 collective-permute-done.4.refs_3_
  13.8 0.8 %shard_map.101 = (f32[16,1024]{1,0:T(8,128)S(1)}, f32[16,1024]{1,0:T(8,128)S(1)}, f32[16,1024]{1,0:T(8,128)S(1)}, f32[16,1024]{1,0:T(8,128)S(1)}) custom-call(f32[16,512]{1,0:T(8,128)S(1)} %get-tuple-element.13.g_ref, f32[64,512]{1,0:T(8,128)S(1)} %shard_map.98.refs_3_.mask_ref, f32[40,512]{1,0:T(8,128)S(1)} %get-tuple-element.14.refs_0_, ...), custom_call_target="tpu_custom_call" | custom-call | flops 268435456 | bytes 262144 | tf_op jit(solution)/shard_map/pallas_call | solution.py:186
  14.7 1.6 %collective-permute-start.5 = (f32[16,1024]{1,0:T(8,128)S(1)}, f32[16,1024]{1,0:T(8,128)S(1)}, u32[]{:S(2)}, u32[]{:S(2)}) collective-permute-start(f32[16,1024]{1,0:T(8,128)S(1)} %get-tuple-element.17), channel_id=1, source_target_pairs={{0,4},{4,8},{8,12},{12,0},{1,5},{5,9},{9,13},{13,1},{2,6},{6,10},{... | collective-permute-start | bytes 196616 | tf_op jit(solution)/shard_map/ppermute | solution.py:289
  16.3 1.7 %collective-permute-start.6 = (f32[16,1024]{1,0:T(8,128)S(1)}, f32[16,1024]{1,0:T(8,128)S(1)}, u32[]{:S(2)}, u32[]{:S(2)}) collective-permute-start(f32[16,1024]{1,0:T(8,128)S(1)} %get-tuple-element.18), channel_id=1, source_target_pairs={{0,8},{4,12},{8,0},{12,4},{1,9},{5,13},{9,1},{13,5},{2,10},{6,14},... | collective-permute-start | bytes 196616 | tf_op jit(solution)/shard_map/ppermute | solution.py:289
  18.0 2.9 %collective-permute-start.9 = (f32[16,1024]{1,0:T(8,128)S(1)}, f32[16,1024]{1,0:T(8,128)S(1)}, u32[]{:S(2)}, u32[]{:S(2)}) collective-permute-start(f32[16,1024]{1,0:T(8,128)S(1)} %shard_map.102), channel_id=1, source_target_pairs={{0,12},{4,0},{8,4},{12,8},{1,13},{5,1},{9,5},{13,9},{2,14},{6,2},{... | collective-permute-start | bytes 196616 | tf_op jit(solution)/shard_map/ppermute | solution.py:289
  21.0 2.8 %collective-permute-done.6.refs_2_.refs_0_ = f32[16,1024]{1,0:T(8,128)S(1)} collective-permute-done((f32[16,1024]{1,0:T(8,128)S(1)}, f32[16,1024]{1,0:T(8,128)S(1)}, u32[]{:S(2)}, u32[]{:S(2)}) %collective-permute-start.6) | collective-permute-done | bytes 65568 | tf_op jit(solution)/shard_map/ppermute | solution.py:289
  23.8 0.4 %shard_map.106 = f32[64,128]{1,0:T(8,128)S(1)} custom-call(s32[1,128]{1,0:T(1,128)S(1)} %bitcast.5, f32[16,1024]{1,0:T(8,128)S(1)} %get-tuple-element.16.refs_0_, f32[16,1024]{1,0:T(8,128)S(1)} %collective-permute-done.5.refs_1_.refs_0_, f32[16,1024]{1,0:T(8,128)S(1)} %collective-permute-done.6.refs_2_.refs_0_, ...), custom_call_target="tpu_custom_call" | custom-call | flops 50331648 | bytes 524288 | tf_op jit(solution)/shard_map/pallas_call | solution.py:254
  24.3 1.2 %collective-permute-done.10 = f32[64,128]{1,0:T(8,128)S(1)} collective-permute-done((f32[64,128]{1,0:T(8,128)S(1)}, f32[64,128]{1,0:T(8,128)S(1)}, u32[]{:S(2)}, u32[]{:S(2)}) %collective-permute-start.10) | collective-permute-done | bytes 32800 | tf_op jit(solution)/shard_map/ppermute | solution.py:284
  25.5 1.3 %collective-permute-start.11 = (f32[64,128]{1,0:T(8,128)S(1)}, f32[64,128]{1,0:T(8,128)S(1)}, u32[]{:S(2)}, u32[]{:S(2)}) collective-permute-start(f32[64,128]{1,0:T(8,128)S(1)} %add.6), channel_id=1, source_target_pairs={{0,2},{1,3},{2,0},{3,1},{4,6},{5,7},{6,4},{7,5},{8,10},{9,11},{10,... | collective-permute-start | bytes 98312 | tf_op jit(solution)/shard_map/ppermute | solution.py:284
  26.9 0.7 %shard_map.103 = f32[64,1024]{1,0:T(8,128)} custom-call(f32[16,1024]{1,0:T(8,128)S(1)} %get-tuple-element.16.refs_0_, f32[16,1024]{1,0:T(8,128)S(1)} %collective-permute-done.5.refs_1_.refs_0_, f32[16,1024]{1,0:T(8,128)S(1)} %collective-permute-done.6.refs_2_.refs_0_, f32[16,1024]{1,0:T(8,128)S(1)} %collective-permute-done.9.refs_3_), custom_call_target="tpu_custom_call" | custom-call | bytes 524288 | tf_op jit(solution)/shard_map/pallas_call | solution.py:275
  27.6 1.8 %collective-permute-done.11 = f32[64,128]{1,0:T(8,128)S(1)} collective-permute-done((f32[64,128]{1,0:T(8,128)S(1)}, f32[64,128]{1,0:T(8,128)S(1)}, u32[]{:S(2)}, u32[]{:S(2)}) %collective-permute-start.11) | collective-permute-done | bytes 32800 | tf_op jit(solution)/shard_map/ppermute | solution.py:284
  29.4 0.6 %add_multiply_fusion = f32[64,128]{1,0:T(8,128)} fusion(f32[64,128]{1,0:T(8,128)S(1)} %add.6, f32[64,128]{1,0:T(8,128)S(1)} %collective-permute-done.11), kind=kLoop, calls=%fused_computation | loop fusion | flops 16384 | bytes 98304 | tf_op jit(solution)/shard_map/mul | solution.py:349
  (30 shorter events, 0.3 us)
Async XLA Ops:
  0.6 4.2 %copy-start.5 = (bf16[1024,64]{0,1:T(8,128)(2,1)S(1)}, bf16[1024,64]{0,1:T(8,128)(2,1)}, u32[]{:S(2)}) copy-start(bf16[1024,64]{0,1:T(8,128)(2,1)} %param.10) | copy-start | bytes 393220
  0.6 4.2 %copy-start.4 = (bf16[512,1024]{1,0:T(8,128)(2,1)S(1)}, bf16[512,1024]{1,0:T(8,128)(2,1)}, u32[]{:S(2)}) copy-start(bf16[512,1024]{1,0:T(8,128)(2,1)} %act_ref.1) | copy-start | bytes 3145732
  0.7 6.2 %copy-start.1 = (bf16[3584,64]{0,1:T(8,128)(2,1)S(1)}, bf16[3584,64]{0,1:T(8,128)(2,1)}, u32[]{:S(2)}) copy-start(bf16[3584,64]{0,1:T(8,128)(2,1)} %param.11) | copy-start | bytes 1376260
  0.7 6.2 %copy-start = (bf16[512,3584]{1,0:T(8,128)(2,1)S(1)}, bf16[512,3584]{1,0:T(8,128)(2,1)}, u32[]{:S(2)}) copy-start(bf16[512,3584]{1,0:T(8,128)(2,1)} %grad_ref.1) | copy-start | bytes 11010052
  0.7 10.7 %collective-permute-start.2 = (f32[32,1024]{1,0:T(8,128)}, f32[32,1024]{1,0:T(8,128)S(1)}, u32[]{:S(2)}, u32[]{:S(2)}) collective-permute-start(f32[32,1024]{1,0:T(8,128)} %refs_4_.1), channel_id=1, source_target_pairs={{0,8},{4,12},{8,0},{12,4},{1,9},{5,13},{9,1},{13,5},{2,10},{6,14},... | collective-permute-start | bytes 393224 | tf_op jit(solution)/shard_map/ppermute | solution.py:284
  4.8 3.8 %copy-start.2 = (f32[32,1024]{1,0:T(8,128)S(1)}, f32[32,1024]{1,0:T(8,128)}, u32[]{:S(2)}) copy-start(f32[32,1024]{1,0:T(8,128)} %refs_4_.1) | copy-start | bytes 393220
  4.8 5.4 %copy-start.6 = (s32[1,32]{1,0:T(1,128)S(1)}, s32[1,32]{1,0:T(1,128)}, u32[]{:S(2)}) copy-start(s32[1,32]{1,0:T(1,128)} %lengths_ref.1) | copy-start | bytes 388
  4.8 5.4 %copy-start.7 = (s32[32,1]{0,1:T(1,128)S(1)}, s32[32,1]{0,1:T(1,128)}, u32[]{:S(2)}) copy-start(s32[32,1]{0,1:T(1,128)} %param.13) | copy-start | bytes 388
  5.3 7.1 %collective-permute-start = (f32[64,512]{1,0:T(8,128)S(1)}, f32[64,512]{1,0:T(8,128)S(1)}, u32[]{:S(2)}, u32[]{:S(2)}) collective-permute-start(f32[64,512]{1,0:T(8,128)S(1)} %shard_map.97.refs_0_), channel_id=1, source_target_pairs={{0,2},{1,3},{2,0},{3,1},{4,6},{5,7},{6,4},{7,5},{8,10},{9,11},{10,... | collective-permute-start | bytes 393224 | tf_op jit(solution)/shard_map/ppermute | solution.py:284
  6.8 17.0 %copy-start.3 = (s32[128]{0:T(128)S(1)}, s32[128]{0:T(128)}, u32[]{:S(2)}) copy-start(s32[128]{0:T(128)} %param.15) | copy-start | bytes 1540
  8.0 4.3 %collective-permute-start.1 = (f32[32,512]{1,0:T(8,128)S(1)}, f32[32,512]{1,0:T(8,128)S(1)}, u32[]{:S(2)}, u32[]{:S(2)}) collective-permute-start(f32[32,512]{1,0:T(8,128)S(1)} %get-tuple-element.12), channel_id=1, source_target_pairs={{0,2},{1,3},{2,0},{3,1},{4,6},{5,7},{6,4},{7,5},{8,10},{9,11},{10,... | collective-permute-start | bytes 196616 | tf_op jit(solution)/shard_map/ppermute | solution.py:284
  8.6 9.4 %collective-permute-start.7 = (f32[32,1024]{1,0:T(8,128)S(1)}, f32[32,1024]{1,0:T(8,128)S(1)}, u32[]{:S(2)}, u32[]{:S(2)}) collective-permute-start(f32[32,1024]{1,0:T(8,128)S(1)} %copy-done.2), channel_id=1, source_target_pairs={{0,4},{4,0},{8,12},{12,8},{1,5},{5,1},{9,13},{13,9},{2,6},{6,2},{1... | collective-permute-start | bytes 393224 | tf_op jit(solution)/shard_map/ppermute | solution.py:284
  11.4 6.6 %collective-permute-start.8 = (f32[32,1024]{1,0:T(8,128)S(1)}, f32[32,1024]{1,0:T(8,128)S(1)}, u32[]{:S(2)}, u32[]{:S(2)}) collective-permute-start(f32[32,1024]{1,0:T(8,128)S(1)} %collective-permute-done.2.refs_0_.refs_5_), channel_id=1, source_target_pairs={{0,4},{4,0},{8,12},{12,8},{1,5},{5,1},{9,13},{13,9},{2,6},{6,2},{1... | collective-permute-start | bytes 393224 | tf_op jit(solution)/shard_map/ppermute | solution.py:284
  12.3 1.3 %collective-permute-start.3 = (f32[40,512]{1,0:T(8,128)S(1)}, f32[40,512]{1,0:T(8,128)S(1)}, u32[]{:S(2)}, u32[]{:S(2)}) collective-permute-start(f32[40,512]{1,0:T(8,128)S(1)} %get-tuple-element.14.refs_0_), channel_id=1, source_target_pairs={{0,1},{1,0},{2,3},{3,2},{4,5},{5,4},{6,7},{7,6},{8,9},{9,8},{10,11... | collective-permute-start | bytes 245768 | tf_op jit(solution)/shard_map/ppermute | solution.py:284
  12.4 1.4 %collective-permute-start.4 = (f32[40,512]{1,0:T(8,128)S(1)}, f32[40,512]{1,0:T(8,128)S(1)}, u32[]{:S(2)}, u32[]{:S(2)}) collective-permute-start(f32[40,512]{1,0:T(8,128)S(1)} %get-tuple-element.15.refs_1_), channel_id=1, source_target_pairs={{0,1},{1,0},{2,3},{3,2},{4,5},{5,4},{6,7},{7,6},{8,9},{9,8},{10,11... | collective-permute-start | bytes 245768 | tf_op jit(solution)/shard_map/ppermute | solution.py:284
  14.7 6.3 %collective-permute-start.5 = (f32[16,1024]{1,0:T(8,128)S(1)}, f32[16,1024]{1,0:T(8,128)S(1)}, u32[]{:S(2)}, u32[]{:S(2)}) collective-permute-start(f32[16,1024]{1,0:T(8,128)S(1)} %get-tuple-element.17), channel_id=1, source_target_pairs={{0,4},{4,8},{8,12},{12,0},{1,5},{5,9},{9,13},{13,1},{2,6},{6,10},{... | collective-permute-start | bytes 196616 | tf_op jit(solution)/shard_map/ppermute | solution.py:289
  16.3 7.5 %collective-permute-start.6 = (f32[16,1024]{1,0:T(8,128)S(1)}, f32[16,1024]{1,0:T(8,128)S(1)}, u32[]{:S(2)}, u32[]{:S(2)}) collective-permute-start(f32[16,1024]{1,0:T(8,128)S(1)} %get-tuple-element.18), channel_id=1, source_target_pairs={{0,8},{4,12},{8,0},{12,4},{1,9},{5,13},{9,1},{13,5},{2,10},{6,14},... | collective-permute-start | bytes 196616 | tf_op jit(solution)/shard_map/ppermute | solution.py:289
  18.0 5.8 %collective-permute-start.9 = (f32[16,1024]{1,0:T(8,128)S(1)}, f32[16,1024]{1,0:T(8,128)S(1)}, u32[]{:S(2)}, u32[]{:S(2)}) collective-permute-start(f32[16,1024]{1,0:T(8,128)S(1)} %shard_map.102), channel_id=1, source_target_pairs={{0,12},{4,0},{8,4},{12,8},{1,13},{5,1},{9,5},{13,9},{2,14},{6,2},{... | collective-permute-start | bytes 196616 | tf_op jit(solution)/shard_map/ppermute | solution.py:289
  24.2 1.3 %collective-permute-start.10 = (f32[64,128]{1,0:T(8,128)S(1)}, f32[64,128]{1,0:T(8,128)S(1)}, u32[]{:S(2)}, u32[]{:S(2)}) collective-permute-start(f32[64,128]{1,0:T(8,128)S(1)} %shard_map.106), channel_id=1, source_target_pairs={{0,1},{1,0},{2,3},{3,2},{4,5},{5,4},{6,7},{7,6},{8,9},{9,8},{10,11... | collective-permute-start | bytes 98312 | tf_op jit(solution)/shard_map/ppermute | solution.py:284
  25.5 3.9 %collective-permute-start.11 = (f32[64,128]{1,0:T(8,128)S(1)}, f32[64,128]{1,0:T(8,128)S(1)}, u32[]{:S(2)}, u32[]{:S(2)}) collective-permute-start(f32[64,128]{1,0:T(8,128)S(1)} %add.6), channel_id=1, source_target_pairs={{0,2},{1,3},{2,0},{3,1},{4,6},{5,7},{6,4},{7,5},{8,10},{9,11},{10,... | collective-permute-start | bytes 98312 | tf_op jit(solution)/shard_map/ppermute | solution.py:284

commit v16 on v15

--- a/solution.py
+++ b/solution.py
@@ -17,6 +17,7 @@
 X_FLOPS = 6 * 10**8
 MASK_FLOPS = 2 * 10**8
 EARLY_FLOPS = 3 * 10**8
+AFTER_FLOPS = 6 * 10**8
 LATE_FLOPS = 10**8
 
 
@@ -205,27 +206,32 @@
     )(*arrays)
 
 
-def after_kernel(block_ref, *refs):
-    refs[-1][...] = block_ref[...]
-
-
-def after(block, pieces):
-    return pl.pallas_call(
-        after_kernel,
-        in_specs=[pl.BlockSpec(memory_space=pltpu.VMEM)]
+def after_kernel(count, *refs):
+    for block_ref, out_ref in zip(refs[:count], refs[-count:]):
+        out_ref[...] = block_ref[...]
+
+
+def after(blocks, pieces):
+    count = len(blocks)
+    return pl.pallas_call(
+        functools.partial(after_kernel, count),
+        in_specs=[pl.BlockSpec(memory_space=pltpu.VMEM)] * count
         + [pl.BlockSpec(memory_space=pl.ANY)] * len(pieces),
-        out_shape=jax.ShapeDtypeStruct(block.shape, F32),
+        out_shape=[jax.ShapeDtypeStruct(block.shape, F32) for block in blocks],
         compiler_params=params(4),
-        cost_estimate=cost(0, 0),
-    )(block, *pieces)
-
-
-def score_kernel(count, gaps, relative, ids_ref, *refs):
-    rows, pieces, scores_ref = refs[:count], refs[count : count + len(gaps)], refs[-1]
+        cost_estimate=cost(AFTER_FLOPS, 0),
+    )(*blocks, *pieces)
+
+
+def score_kernel(arrivals, gaps, relative, ids_ref, *refs):
+    scores_ref = refs[-1]
+    rows = arrived(arrivals, refs)
+    pieces = refs[sum(arrivals) : sum(arrivals) + len(gaps)]
+    count = len(rows)
     queries = ids_ref.shape[1]
     me = lax.axis_index("dp")
     cap = rows[0].shape[0]
-    high, low = halves(stack(rows))
+    high, low = halves(jnp.concatenate(rows, axis=0))
     slots = high.shape[0]
     both = jnp.concatenate([high, low], axis=0)
     held = pieces[0].shape[0]
@@ -246,47 +252,61 @@
         scores_ref[spot, :] = total[k * cap : (k + 1) * cap, :]
 
 
+def arrived(arrivals, refs):
+    rows, at = [], 0
+    for count in arrivals:
+        row = refs[at][...]
+        for ref in refs[at + 1 : at + count]:
+            row = row + ref[...]
+        rows.append(row)
+        at += count
+    return rows
+
+
 def score(ids_row, rows, pieces, gaps, relative, tokens):
-    slots = rows[0].shape[0] * len(rows)
+    slots = rows[0][0].shape[0] * len(rows)
     queries = ids_row.shape[1]
     size, feats = pieces[0].shape
     flops = 6 * slots * size * len(gaps) * feats
-    return pl.pallas_call(
-        functools.partial(score_kernel, len(rows), gaps, relative),
-        in_specs=[pl.BlockSpec(memory_space=pltpu.VMEM)] * (1 + len(rows) + len(pieces))
+    arrivals = tuple(len(row) for row in rows)
+    arrays = [array for row in rows for array in row]
+    return pl.pallas_call(
+        functools.partial(score_kernel, arrivals, gaps, relative),
+        in_specs=[pl.BlockSpec(memory_space=pltpu.VMEM)] * (1 + len(arrays) + len(pieces))
         + [pl.BlockSpec(memory_space=pl.ANY)] * len(tokens),
         out_shape=jax.ShapeDtypeStruct((slots, queries), F32),
         compiler_params=params(24),
         cost_estimate=cost(flops, 4 * size * len(gaps) * feats),
-    )(ids_row, *rows, *pieces, *tokens)
-
-
-def place_kernel(*refs):
-    rows, store_ref = refs[:-1], refs[-1]
+    )(ids_row, *arrays, *pieces, *tokens)
+
+
+def place_kernel(arrivals, *refs):
+    store_ref = refs[-1]
     me = lax.axis_index("dp")
-    cap = rows[0].shape[0]
-    for k, row in enumerate(rows):
-        source = lax.rem(me - k + len(rows), len(rows))
-        store_ref[pl.ds(pl.multiple_of(source * cap, cap), cap), :] = row[...]
+    for k, row in enumerate(arrived(arrivals, refs)):
+        cap, count = row.shape[0], len(arrivals)
+        source = lax.rem(me - k + count, count)
+        store_ref[pl.ds(pl.multiple_of(source * cap, cap), cap), :] = row
 
 
 def place(rows):
-    slots, feats = rows[0].shape[0] * len(rows), rows[0].shape[1]
-    return pl.pallas_call(
-        place_kernel,
+    slots, feats = rows[0][0].shape[0] * len(rows), rows[0][0].shape[1]
+    arrivals = tuple(len(row) for row in rows)
+    return pl.pallas_call(
+        functools.partial(place_kernel, arrivals),
         out_shape=jax.ShapeDtypeStruct((slots, feats), F32),
         compiler_params=params(16),
         cost_estimate=cost(0, 8 * slots * feats),
-    )(*rows)
+    )(*(array for row in rows for array in row))
 
 
 def swap(x, axis, gap):
     return lax.ppermute(x, axis, [(i, i ^ gap) for i in range(lax.axis_size(axis))])
 
 
-def shift(x, axis, by):
+def shift(x, axis, by, first):
     size = lax.axis_size(axis)
-    return lax.ppermute(x, axis, [(i, (i + by) % size) for i in range(size)])
+    return lax.ppermute(x, axis, [(i, (i + by) % size) for i in range(size) if (i == 0) == first])
 
 
 def gather_pieces(piece):
@@ -331,16 +351,17 @@
     blocks = outer(own, gots, keep, mask, data_size)
     if direct:
         *sent, kept = blocks
-        sent[-1] = after(sent[-1], [mate, *passed])
-        rows = [kept] + [shift(block, "dp", k) for k, block in enumerate(sent, 1)]
-        late = []
-        for row in rows[1:-1]:
-            late = [token([row, *late], LATE_FLOPS)]
+        most = [shift(block, "dp", k, False) for k, block in enumerate(sent, 1)]
+        held = after(sent, [mate, *passed])
+        rest = [shift(block, "dp", k, True) for k, block in enumerate(held, 1)]
+        rows = [(kept,), *zip(most, rest)]
+        late = [token(most, LATE_FLOPS)]
         pieces, gaps = [*pieces, mate, *passed], [*gaps, *(g ^ 1 for g in gaps)]
         store = place(rows)
     else:
         rows = [lax.all_to_all(jnp.stack(blocks), "dp", 0, 0, tiled=True).reshape(-1, width * rank)]
         store, late = rows[0], []
+        rows = [(store,)]
     scores = score(query_ids[None, :], rows, pieces, gaps, direct, late)
     bit = 1
     while bit < tensor_size:

time: 30.2 us -> 38.6 us (1.28)
  starting transfers between devices: 16.8 us -> 26 us
  waiting for transfers between devices: 8.01 us -> 7.01 us
    ppermute x3 -> x6, starting transfers between devices: 6.23 us -> 15.4 us  [shift(): lax.ppermute(x, axis, [(i, (i + by) % size) for i in range(size) if (i ==...]
    ppermute x3 -> x6, waiting for transfers between devices: 2.85 us -> 1.85 us  [shift(): lax.ppermute(x, axis, [(i, (i + by) % size) for i in range(size) if (i ==...]
  transfers between devices with their start and end apart: 12 -> 15, of which waited for: 8 -> 8; matrix products, arithmetic and copies ran while one was open for 0% -> 0% of each run, Pallas kernels for 11% -> 9%
where the time goes in v16:
time: 38.6 us; the launch traced here: 38.4 us
  starting transfers between devices  26 us (67%)
  waiting for transfers between devices  7.01 us (18%)
  Pallas kernels  3.89 us (10%)
  between operations  0.86 us (2%)
  other arithmetic  0.63 us (2%)
    ppermute x6, starting transfers between devices, shift(): lax.ppermute(x, axis, [(i, (i + by) % size) for i in range(size) if (i ==...  15.4 us
    ppermute x9, starting transfers between devices, swap(): lax.ppermute(x, axis, [(i, i ^ gap) for i in range(lax.axis_size(axis))])  10.5 us
    ppermute x9, waiting for transfers between devices, swap(): lax.ppermute(x, axis, [(i, i ^ gap) for i in range(lax.axis_size(axis))])  5.16 us
    ppermute x6, waiting for transfers between devices, shift(): lax.ppermute(x, axis, [(i, (i + by) % size) for i in range(size) if (i ==...  1.85 us
    pallas_call x1, Pallas kernels, project_g(): pl.pallas_call(functools.partial(g_kernel, width), out_shape=[part, part]...  1.16 us
    pallas_call x1, Pallas kernels, outer(): pl.pallas_call(functools.partial(outer_kernel, owners, len(sent)), out_sh...  0.84 us
  transfers between devices with their start and end apart: 15, of which 8 were waited for; matrix products, arithmetic and copies ran while one was open for 0% of the time, Pallas kernels for 9%

profile of v16, /device:TPU:0, one launch (start us, length us, event | category | flops | bytes accessed | tf_op | source)
XLA Modules:
  0.0 38.4 jit_solution(14473774535390928804)
XLA Ops:
  0.7 4.1 %collective-permute-start.2 = (f32[32,1024]{1,0:T(8,128)}, f32[32,1024]{1,0:T(8,128)S(1)}, u32[]{:S(2)}, u32[]{:S(2)}) collective-permute-start(f32[32,1024]{1,0:T(8,128)} %refs_7_.1), channel_id=1, source_target_pairs={{0,8},{4,12},{8,0},{12,4},{1,9},{5,13},{9,1},{13,5},{2,10},{6,14},... | collective-permute-start | bytes 393224 | tf_op jit(solution)/shard_map/ppermute | solution.py:304
  4.8 0.5 %shard_map.97.refs_0_ = f32[64,512]{1,0:T(8,128)S(1)} custom-call(bf16[512,1024]{1,0:T(8,128)(2,1)S(1)} %copy-done.4, bf16[64,1024]{1,0:T(8,128)(2,1)S(1)} %bitcast.6, f32[8,128]{1,0:T(8,128)S(1)} %shard_map.96.refs_0_), custom_call_target="tpu_custom_call" | custom-call | flops 600000000 | tf_op jit(solution)/shard_map/pallas_call | solution.py:88
  5.3 1.5 %collective-permute-start = (f32[64,512]{1,0:T(8,128)S(1)}, f32[64,512]{1,0:T(8,128)S(1)}, u32[]{:S(2)}, u32[]{:S(2)}) collective-permute-start(f32[64,512]{1,0:T(8,128)S(1)} %shard_map.97.refs_0_), channel_id=1, source_target_pairs={{0,2},{1,3},{2,0},{3,1},{4,6},{5,7},{6,4},{7,5},{8,10},{9,11},{10,... | collective-permute-start | bytes 393224 | tf_op jit(solution)/shard_map/ppermute | solution.py:304
  6.8 1.2 %shard_map.95 = (f32[32,512]{1,0:T(8,128)S(1)}, f32[32,512]{1,0:T(8,128)S(1)}) custom-call(bf16[512,3584]{1,0:T(8,128)(2,1)S(1)} %copy-done, bf16[64,3584]{1,0:T(8,128)(2,1)S(1)} %bitcast.4), custom_call_target="tpu_custom_call" | custom-call | tf_op jit(solution)/shard_map/pallas_call | solution.py:111
  8.0 0.6 %collective-permute-start.1 = (f32[32,512]{1,0:T(8,128)S(1)}, f32[32,512]{1,0:T(8,128)S(1)}, u32[]{:S(2)}, u32[]{:S(2)}) collective-permute-start(f32[32,512]{1,0:T(8,128)S(1)} %get-tuple-element.15), channel_id=1, source_target_pairs={{0,2},{1,3},{2,0},{3,1},{4,6},{5,7},{6,4},{7,5},{8,10},{9,11},{10,... | collective-permute-start | bytes 196616 | tf_op jit(solution)/shard_map/ppermute | solution.py:304
  8.6 1.6 %collective-permute-start.6 = (f32[32,1024]{1,0:T(8,128)S(1)}, f32[32,1024]{1,0:T(8,128)S(1)}, u32[]{:S(2)}, u32[]{:S(2)}) collective-permute-start(f32[32,1024]{1,0:T(8,128)S(1)} %copy-done.2), channel_id=1, source_target_pairs={{0,4},{4,0},{8,12},{12,8},{1,5},{5,1},{9,13},{13,9},{2,6},{6,2},{1... | collective-permute-start | bytes 393224 | tf_op jit(solution)/shard_map/ppermute | solution.py:304
  10.4 1.0 %collective-permute-done.2.refs_0_.refs_8_ = f32[32,1024]{1,0:T(8,128)S(1)} collective-permute-done((f32[32,1024]{1,0:T(8,128)}, f32[32,1024]{1,0:T(8,128)S(1)}, u32[]{:S(2)}, u32[]{:S(2)}) %collective-permute-start.2) | collective-permute-done | bytes 131104 | tf_op jit(solution)/shard_map/ppermute | solution.py:304
  11.4 0.7 %collective-permute-start.7 = (f32[32,1024]{1,0:T(8,128)S(1)}, f32[32,1024]{1,0:T(8,128)S(1)}, u32[]{:S(2)}, u32[]{:S(2)}) collective-permute-start(f32[32,1024]{1,0:T(8,128)S(1)} %collective-permute-done.2.refs_0_.refs_8_), channel_id=1, source_target_pairs={{0,4},{4,0},{8,12},{12,8},{1,5},{5,1},{9,13},{13,9},{2,6},{6,2},{1... | collective-permute-start | bytes 393224 | tf_op jit(solution)/shard_map/ppermute | solution.py:304
  12.4 0.5 %collective-permute-start.4 = (f32[40,512]{1,0:T(8,128)S(1)}, f32[40,512]{1,0:T(8,128)S(1)}, u32[]{:S(2)}, u32[]{:S(2)}) collective-permute-start(f32[40,512]{1,0:T(8,128)S(1)} %get-tuple-element.18.refs_1_), channel_id=1, source_target_pairs={{0,1},{1,0},{2,3},{3,2},{4,5},{5,4},{6,7},{7,6},{8,9},{9,8},{10,11... | collective-permute-start | bytes 245768 | tf_op jit(solution)/shard_map/ppermute | solution.py:304
  12.9 0.8 %collective-permute-done.3.refs_2_ = f32[40,512]{1,0:T(8,128)S(1)} collective-permute-done((f32[40,512]{1,0:T(8,128)S(1)}, f32[40,512]{1,0:T(8,128)S(1)}, u32[]{:S(2)}, u32[]{:S(2)}) %collective-permute-start.3) | collective-permute-done | bytes 81952 | tf_op jit(solution)/shard_map/ppermute | solution.py:304
  13.9 0.8 %shard_map.101 = (f32[16,1024]{1,0:T(8,128)S(1)}, f32[16,1024]{1,0:T(8,128)S(1)}, f32[16,1024]{1,0:T(8,128)S(1)}, f32[16,1024]{1,0:T(8,128)S(1)}) custom-call(f32[16,512]{1,0:T(8,128)S(1)} %get-tuple-element.16.g_ref, f32[64,512]{1,0:T(8,128)S(1)} %shard_map.98.refs_3_.mask_ref, f32[40,512]{1,0:T(8,128)S(1)} %get-tuple-element.17.refs_0_, ...), custom_call_target="tpu_custom_call" | custom-call | flops 268435456 | bytes 262144 | tf_op jit(solution)/shard_map/pallas_call | solution.py:187
  14.7 1.3 %collective-permute-start.5 = (f32[16,1024]{1,0:T(8,128)S(1)}, f32[16,1024]{1,0:T(8,128)S(1)}, u32[]{:S(2)}, u32[]{:S(2)}) collective-permute-start(f32[16,1024]{1,0:T(8,128)S(1)} %get-tuple-element.20.refs_0_), channel_id=1, source_target_pairs={{4,8},{8,12},{12,0},{5,9},{9,13},{13,1},{6,10},{10,14},{14,2},{7,1... | collective-permute-start | bytes 196616 | tf_op jit(solution)/shard_map/ppermute | solution.py:309
  16.0 1.3 %collective-permute-start.9 = (f32[16,1024]{1,0:T(8,128)S(1)}, f32[16,1024]{1,0:T(8,128)S(1)}, u32[]{:S(2)}, u32[]{:S(2)}) collective-permute-start(f32[16,1024]{1,0:T(8,128)S(1)} %get-tuple-element.21.refs_1_), channel_id=1, source_target_pairs={{4,12},{8,0},{12,4},{5,13},{9,1},{13,5},{6,14},{10,2},{14,6},{7,15... | collective-permute-start | bytes 196616 | tf_op jit(solution)/shard_map/ppermute | solution.py:309
  17.3 1.3 %collective-permute-start.11 = (f32[16,1024]{1,0:T(8,128)S(1)}, f32[16,1024]{1,0:T(8,128)S(1)}, u32[]{:S(2)}, u32[]{:S(2)}) collective-permute-start(f32[16,1024]{1,0:T(8,128)S(1)} %get-tuple-element.22.refs_2_), channel_id=1, source_target_pairs={{4,0},{8,4},{12,8},{5,1},{9,5},{13,9},{6,2},{10,6},{14,10},{7,3},{... | collective-permute-start | bytes 196616 | tf_op jit(solution)/shard_map/ppermute | solution.py:309
  18.6 8.2 %collective-permute-start.8 = (f32[16,1024]{1,0:T(8,128)S(1)}, f32[16,1024]{1,0:T(8,128)S(1)}, u32[]{:S(2)}, u32[]{:S(2)}) collective-permute-start(f32[16,1024]{1,0:T(8,128)S(1)} %get-tuple-element.23), channel_id=1, source_target_pairs={{0,4},{1,5},{2,6},{3,7},{16,20},{17,21},{18,22},{19,23}} | collective-permute-start | bytes 196616 | tf_op jit(solution)/shard_map/ppermute | solution.py:309
  26.8 2.1 %collective-permute-start.10 = (f32[16,1024]{1,0:T(8,128)S(1)}, f32[16,1024]{1,0:T(8,128)S(1)}, u32[]{:S(2)}, u32[]{:S(2)}) collective-permute-start(f32[16,1024]{1,0:T(8,128)S(1)} %get-tuple-element.24), channel_id=1, source_target_pairs={{0,8},{1,9},{2,10},{3,11},{16,24},{17,25},{18,26},{19,27}} | collective-permute-start | bytes 196616 | tf_op jit(solution)/shard_map/ppermute | solution.py:309
  28.9 1.3 %collective-permute-start.12 = (f32[16,1024]{1,0:T(8,128)S(1)}, f32[16,1024]{1,0:T(8,128)S(1)}, u32[]{:S(2)}, u32[]{:S(2)}) collective-permute-start(f32[16,1024]{1,0:T(8,128)S(1)} %get-tuple-element.25), channel_id=1, source_target_pairs={{0,12},{1,13},{2,14},{3,15},{16,28},{17,29},{18,30},{19,31}} | collective-permute-start | bytes 196616 | tf_op jit(solution)/shard_map/ppermute | solution.py:309
  30.3 1.0 %collective-permute-done.10.refs_4_ = f32[16,1024]{1,0:T(8,128)S(1)} collective-permute-done((f32[16,1024]{1,0:T(8,128)S(1)}, f32[16,1024]{1,0:T(8,128)S(1)}, u32[]{:S(2)}, u32[]{:S(2)}) %collective-permute-start.10) | collective-permute-done | bytes 65568 | tf_op jit(solution)/shard_map/ppermute | solution.py:309
  31.3 0.9 %collective-permute-done.12.refs_6_ = f32[16,1024]{1,0:T(8,128)S(1)} collective-permute-done((f32[16,1024]{1,0:T(8,128)S(1)}, f32[16,1024]{1,0:T(8,128)S(1)}, u32[]{:S(2)}, u32[]{:S(2)}) %collective-permute-start.12) | collective-permute-done | bytes 65568 | tf_op jit(solution)/shard_map/ppermute | solution.py:309
  32.7 1.2 %collective-permute-done.13 = f32[64,128]{1,0:T(8,128)S(1)} collective-permute-done((f32[64,128]{1,0:T(8,128)S(1)}, f32[64,128]{1,0:T(8,128)S(1)}, u32[]{:S(2)}, u32[]{:S(2)}) %collective-permute-start.13) | collective-permute-done | bytes 32800 | tf_op jit(solution)/shard_map/ppermute | solution.py:304
  33.9 1.3 %collective-permute-start.14 = (f32[64,128]{1,0:T(8,128)S(1)}, f32[64,128]{1,0:T(8,128)S(1)}, u32[]{:S(2)}, u32[]{:S(2)}) collective-permute-start(f32[64,128]{1,0:T(8,128)S(1)} %add.6), channel_id=1, source_target_pairs={{0,2},{1,3},{2,0},{3,1},{4,6},{5,7},{6,4},{7,5},{8,10},{9,11},{10,... | collective-permute-start | bytes 98312 | tf_op jit(solution)/shard_map/ppermute | solution.py:304
  35.2 0.7 %shard_map.103 = f32[64,1024]{1,0:T(8,128)} custom-call(f32[16,1024]{1,0:T(8,128)S(1)} %get-tuple-element.19.refs_0_, f32[16,1024]{1,0:T(8,128)S(1)} %collective-permute-done.5.refs_1_.refs_0_, f32[16,1024]{1,0:T(8,128)S(1)} %collective-permute-done.8.refs_2_, f32[16,1024]{1,0:T(8,128)S(1)} %collective-permute-done.9.refs_3_.refs_1_, ...), custom_call_target="tpu_custom_call" | custom-call | bytes 524288 | tf_op jit(solution)/shard_map/pallas_call | solution.py:295
  35.9 1.8 %collective-permute-done.14 = f32[64,128]{1,0:T(8,128)S(1)} collective-permute-done((f32[64,128]{1,0:T(8,128)S(1)}, f32[64,128]{1,0:T(8,128)S(1)}, u32[]{:S(2)}, u32[]{:S(2)}) %collective-permute-start.14) | collective-permute-done | bytes 32800 | tf_op jit(solution)/shard_map/ppermute | solution.py:304
  37.8 0.6 %add_multiply_fusion = f32[64,128]{1,0:T(8,128)} fusion(f32[64,128]{1,0:T(8,128)S(1)} %add.6, f32[64,128]{1,0:T(8,128)S(1)} %collective-permute-done.14), kind=kLoop, calls=%fused_computation | loop fusion | flops 16384 | bytes 98304 | tf_op jit(solution)/shard_map/mul | solution.py:370
  (35 shorter events, 1.2 us)
Async XLA Ops:
  0.6 4.2 %copy-start.5 = (bf16[1024,64]{0,1:T(8,128)(2,1)S(1)}, bf16[1024,64]{0,1:T(8,128)(2,1)}, u32[]{:S(2)}) copy-start(bf16[1024,64]{0,1:T(8,128)(2,1)} %param.10) | copy-start | bytes 393220
  0.6 4.2 %copy-start.4 = (bf16[512,1024]{1,0:T(8,128)(2,1)S(1)}, bf16[512,1024]{1,0:T(8,128)(2,1)}, u32[]{:S(2)}) copy-start(bf16[512,1024]{1,0:T(8,128)(2,1)} %act_ref.1) | copy-start | bytes 3145732
  0.7 6.2 %copy-start.1 = (bf16[3584,64]{0,1:T(8,128)(2,1)S(1)}, bf16[3584,64]{0,1:T(8,128)(2,1)}, u32[]{:S(2)}) copy-start(bf16[3584,64]{0,1:T(8,128)(2,1)} %param.11) | copy-start | bytes 1376260
  0.7 6.2 %copy-start = (bf16[512,3584]{1,0:T(8,128)(2,1)S(1)}, bf16[512,3584]{1,0:T(8,128)(2,1)}, u32[]{:S(2)}) copy-start(bf16[512,3584]{1,0:T(8,128)(2,1)} %grad_ref.1) | copy-start | bytes 11010052
  0.7 10.7 %collective-permute-start.2 = (f32[32,1024]{1,0:T(8,128)}, f32[32,1024]{1,0:T(8,128)S(1)}, u32[]{:S(2)}, u32[]{:S(2)}) collective-permute-start(f32[32,1024]{1,0:T(8,128)} %refs_7_.1), channel_id=1, source_target_pairs={{0,8},{4,12},{8,0},{12,4},{1,9},{5,13},{9,1},{13,5},{2,10},{6,14},... | collective-permute-start | bytes 393224 | tf_op jit(solution)/shard_map/ppermute | solution.py:304
  4.8 3.8 %copy-start.2 = (f32[32,1024]{1,0:T(8,128)S(1)}, f32[32,1024]{1,0:T(8,128)}, u32[]{:S(2)}) copy-start(f32[32,1024]{1,0:T(8,128)} %refs_7_.1) | copy-start | bytes 393220
  4.8 5.4 %copy-start.6 = (s32[1,32]{1,0:T(1,128)S(1)}, s32[1,32]{1,0:T(1,128)}, u32[]{:S(2)}) copy-start(s32[1,32]{1,0:T(1,128)} %lengths_ref.1) | copy-start | bytes 388
  4.8 5.4 %copy-start.7 = (s32[32,1]{0,1:T(1,128)S(1)}, s32[32,1]{0,1:T(1,128)}, u32[]{:S(2)}) copy-start(s32[32,1]{0,1:T(1,128)} %param.13) | copy-start | bytes 388
  5.3 7.1 %collective-permute-start = (f32[64,512]{1,0:T(8,128)S(1)}, f32[64,512]{1,0:T(8,128)S(1)}, u32[]{:S(2)}, u32[]{:S(2)}) collective-permute-start(f32[64,512]{1,0:T(8,128)S(1)} %shard_map.97.refs_0_), channel_id=1, source_target_pairs={{0,2},{1,3},{2,0},{3,1},{4,6},{5,7},{6,4},{7,5},{8,10},{9,11},{10,... | collective-permute-start | bytes 393224 | tf_op jit(solution)/shard_map/ppermute | solution.py:304
  8.0 24.2 %copy-start.3 = (s32[128]{0:T(128)S(1)}, s32[128]{0:T(128)}, u32[]{:S(2)}) copy-start(s32[128]{0:T(128)} %param.15) | copy-start | bytes 1540
  8.0 4.3 %collective-permute-start.1 = (f32[32,512]{1,0:T(8,128)S(1)}, f32[32,512]{1,0:T(8,128)S(1)}, u32[]{:S(2)}, u32[]{:S(2)}) collective-permute-start(f32[32,512]{1,0:T(8,128)S(1)} %get-tuple-element.15), channel_id=1, source_target_pairs={{0,2},{1,3},{2,0},{3,1},{4,6},{5,7},{6,4},{7,5},{8,10},{9,11},{10,... | collective-permute-start | bytes 196616 | tf_op jit(solution)/shard_map/ppermute | solution.py:304
  8.6 10.0 %collective-permute-start.6 = (f32[32,1024]{1,0:T(8,128)S(1)}, f32[32,1024]{1,0:T(8,128)S(1)}, u32[]{:S(2)}, u32[]{:S(2)}) collective-permute-start(f32[32,1024]{1,0:T(8,128)S(1)} %copy-done.2), channel_id=1, source_target_pairs={{0,4},{4,0},{8,12},{12,8},{1,5},{5,1},{9,13},{13,9},{2,6},{6,2},{1... | collective-permute-start | bytes 393224 | tf_op jit(solution)/shard_map/ppermute | solution.py:304
  11.4 7.2 %collective-permute-start.7 = (f32[32,1024]{1,0:T(8,128)S(1)}, f32[32,1024]{1,0:T(8,128)S(1)}, u32[]{:S(2)}, u32[]{:S(2)}) collective-permute-start(f32[32,1024]{1,0:T(8,128)S(1)} %collective-permute-done.2.refs_0_.refs_8_), channel_id=1, source_target_pairs={{0,4},{4,0},{8,12},{12,8},{1,5},{5,1},{9,13},{13,9},{2,6},{6,2},{1... | collective-permute-start | bytes 393224 | tf_op jit(solution)/shard_map/ppermute | solution.py:304
  12.4 1.3 %collective-permute-start.3 = (f32[40,512]{1,0:T(8,128)S(1)}, f32[40,512]{1,0:T(8,128)S(1)}, u32[]{:S(2)}, u32[]{:S(2)}) collective-permute-start(f32[40,512]{1,0:T(8,128)S(1)} %get-tuple-element.17.refs_0_), channel_id=1, source_target_pairs={{0,1},{1,0},{2,3},{3,2},{4,5},{5,4},{6,7},{7,6},{8,9},{9,8},{10,11... | collective-permute-start | bytes 245768 | tf_op jit(solution)/shard_map/ppermute | solution.py:304
  12.4 1.4 %collective-permute-start.4 = (f32[40,512]{1,0:T(8,128)S(1)}, f32[40,512]{1,0:T(8,128)S(1)}, u32[]{:S(2)}, u32[]{:S(2)}) collective-permute-start(f32[40,512]{1,0:T(8,128)S(1)} %get-tuple-element.18.refs_1_), channel_id=1, source_target_pairs={{0,1},{1,0},{2,3},{3,2},{4,5},{5,4},{6,7},{7,6},{8,9},{9,8},{10,11... | collective-permute-start | bytes 245768 | tf_op jit(solution)/shard_map/ppermute | solution.py:304
  14.7 14.2 %collective-permute-start.5 = (f32[16,1024]{1,0:T(8,128)S(1)}, f32[16,1024]{1,0:T(8,128)S(1)}, u32[]{:S(2)}, u32[]{:S(2)}) collective-permute-start(f32[16,1024]{1,0:T(8,128)S(1)} %get-tuple-element.20.refs_0_), channel_id=1, source_target_pairs={{4,8},{8,12},{12,0},{5,9},{9,13},{13,1},{6,10},{10,14},{14,2},{7,1... | collective-permute-start | bytes 196616 | tf_op jit(solution)/shard_map/ppermute | solution.py:309
  16.0 14.2 %collective-permute-start.9 = (f32[16,1024]{1,0:T(8,128)S(1)}, f32[16,1024]{1,0:T(8,128)S(1)}, u32[]{:S(2)}, u32[]{:S(2)}) collective-permute-start(f32[16,1024]{1,0:T(8,128)S(1)} %get-tuple-element.21.refs_1_), channel_id=1, source_target_pairs={{4,12},{8,0},{12,4},{5,13},{9,1},{13,5},{6,14},{10,2},{14,6},{7,15... | collective-permute-start | bytes 196616 | tf_op jit(solution)/shard_map/ppermute | solution.py:309
  17.3 13.0 %collective-permute-start.11 = (f32[16,1024]{1,0:T(8,128)S(1)}, f32[16,1024]{1,0:T(8,128)S(1)}, u32[]{:S(2)}, u32[]{:S(2)}) collective-permute-start(f32[16,1024]{1,0:T(8,128)S(1)} %get-tuple-element.22.refs_2_), channel_id=1, source_target_pairs={{4,0},{8,4},{12,8},{5,1},{9,5},{13,9},{6,2},{10,6},{14,10},{7,3},{... | collective-permute-start | bytes 196616 | tf_op jit(solution)/shard_map/ppermute | solution.py:309
  18.6 11.6 %collective-permute-start.8 = (f32[16,1024]{1,0:T(8,128)S(1)}, f32[16,1024]{1,0:T(8,128)S(1)}, u32[]{:S(2)}, u32[]{:S(2)}) collective-permute-start(f32[16,1024]{1,0:T(8,128)S(1)} %get-tuple-element.23), channel_id=1, source_target_pairs={{0,4},{1,5},{2,6},{3,7},{16,20},{17,21},{18,22},{19,23}} | collective-permute-start | bytes 196616 | tf_op jit(solution)/shard_map/ppermute | solution.py:309
  26.8 4.4 %collective-permute-start.10 = (f32[16,1024]{1,0:T(8,128)S(1)}, f32[16,1024]{1,0:T(8,128)S(1)}, u32[]{:S(2)}, u32[]{:S(2)}) collective-permute-start(f32[16,1024]{1,0:T(8,128)S(1)} %get-tuple-element.24), channel_id=1, source_target_pairs={{0,8},{1,9},{2,10},{3,11},{16,24},{17,25},{18,26},{19,27}} | collective-permute-start | bytes 196616 | tf_op jit(solution)/shard_map/ppermute | solution.py:309
  28.9 3.2 %collective-permute-start.12 = (f32[16,1024]{1,0:T(8,128)S(1)}, f32[16,1024]{1,0:T(8,128)S(1)}, u32[]{:S(2)}, u32[]{:S(2)}) collective-permute-start(f32[16,1024]{1,0:T(8,128)S(1)} %get-tuple-element.25), channel_id=1, source_target_pairs={{0,12},{1,13},{2,14},{3,15},{16,28},{17,29},{18,30},{19,31}} | collective-permute-start | bytes 196616 | tf_op jit(solution)/shard_map/ppermute | solution.py:309
  32.6 1.3 %collective-permute-start.13 = (f32[64,128]{1,0:T(8,128)S(1)}, f32[64,128]{1,0:T(8,128)S(1)}, u32[]{:S(2)}, u32[]{:S(2)}) collective-permute-start(f32[64,128]{1,0:T(8,128)S(1)} %shard_map.105), channel_id=1, source_target_pairs={{0,1},{1,0},{2,3},{3,2},{4,5},{5,4},{6,7},{7,6},{8,9},{9,8},{10,11... | collective-permute-start | bytes 98312 | tf_op jit(solution)/shard_map/ppermute | solution.py:304
  33.9 3.9 %collective-permute-start.14 = (f32[64,128]{1,0:T(8,128)S(1)}, f32[64,128]{1,0:T(8,128)S(1)}, u32[]{:S(2)}, u32[]{:S(2)}) collective-permute-start(f32[64,128]{1,0:T(8,128)S(1)} %add.6), channel_id=1, source_target_pairs={{0,2},{1,3},{2,0},{3,1},{4,6},{5,7},{6,4},{7,5},{8,10},{9,11},{10,... | collective-permute-start | bytes 98312 | tf_op jit(solution)/shard_map/ppermute | solution.py:304

commit v17 on v15

--- a/solution.py
+++ b/solution.py
@@ -12,12 +12,14 @@
 MIB = 1024 * 1024
 NT = (((1,), (1,)), ((), ()))
 MOST_DIRECT = 8
-GROUP = 4
+GROUP = 8
+ROWS = 16
 FIRST_FLOPS = 10 * 10**8
 X_FLOPS = 6 * 10**8
 MASK_FLOPS = 2 * 10**8
 EARLY_FLOPS = 3 * 10**8
 LATE_FLOPS = 10**8
+SCORE_FLOPS = 0
 
 
 def params(mib):
@@ -57,7 +59,7 @@
     first = jnp.sum(jnp.where(hot, ends - len_row, 0.0), axis=1, keepdims=True)
     last = jnp.sum(jnp.where(hot, ends, 0.0), axis=1, keepdims=True)
     token = lax.broadcasted_iota(jnp.int32, (slots, tokens), 1).astype(F32)
-    return jnp.where((token >= first) & (token < last), 1.0, 0.0)
+    return jnp.where((token >= first) & (token < last), 1.0, 0.0).astype(BF16)
 
 
 def mask_kernel(owners, relative, cap, lengths_ref, owner_ref, mask_ref):
@@ -67,7 +69,7 @@
 def dispatch_mask(lengths, owner_row, owners, cap, tokens, relative):
     return pl.pallas_call(
         functools.partial(mask_kernel, owners, relative, cap),
-        out_shape=jax.ShapeDtypeStruct((owners * cap, tokens), F32),
+        out_shape=jax.ShapeDtypeStruct((owners * cap, tokens), BF16),
         compiler_params=params(8),
         cost_estimate=cost(MASK_FLOPS, 0),
     )(lengths, owner_row)
@@ -150,7 +152,7 @@
     return keep, sent
 
 
-def outer_kernel(owners, sent, g_ref, mask_ref, *refs):
+def outer_kernel(first, owners, sent, g_ref, mask_ref, *refs):
     blocks = refs[-owners:]
     width = g_ref.shape[0]
     own, got = stack(refs[:sent]), stack(refs[sent : 2 * sent])
@@ -160,14 +162,19 @@
     x_both = jnp.concatenate(halves(x_full), axis=0)
     g_high = g_full.astype(BF16).astype(F32)
     g_low = g_full - g_high
-    mask = mask_ref[...]
     cap = blocks[0].shape[0]
-
-    slots = mask.shape[0]
+    slots = owners * cap
+    mask = mask_ref[first * cap : first * cap + slots, :]
+    tokens = mask.shape[1]
+
+    def masked(row):
+        wide = jnp.broadcast_to(row, (ROWS, tokens)).astype(BF16)
+        return [mask[i : i + ROWS] * wide for i in range(0, slots, ROWS)]
+
     group = min(width, GROUP)
     for i in range(0, width, group):
-        rows = [mask * g[j : j + 1, :] for j in range(i, i + group) for g in (g_high, g_low)]
-        both = mm(jnp.concatenate([r.astype(BF16) for r in rows], axis=0), x_both, NT)
+        rows = [m for j in range(i, i + group) for g in (g_high, g_low) for m in masked(g[j : j + 1])]
+        both = mm(jnp.concatenate(rows, axis=0), x_both, NT)
         columns = []
         for j in range(group):
             high = both[2 * j * slots : (2 * j + 1) * slots]
@@ -178,16 +185,14 @@
             block[:, i * rank : (i + group) * rank] = out[k * cap : (k + 1) * cap, :]
 
 
-def outer(sent, gots, g, mask, owners):
-    slots, tokens = mask.shape
+def outer(sent, gots, g, mask, cap, first, owners):
     width = g.shape[0]
     rank = sum(p.shape[0] for p in sent) - width
-    cap = slots // owners
-    return pl.pallas_call(
-        functools.partial(outer_kernel, owners, len(sent)),
+    return pl.pallas_call(
+        functools.partial(outer_kernel, first, owners, len(sent)),
         out_shape=[jax.ShapeDtypeStruct((cap, width * rank), F32)] * owners,
         compiler_params=params(24),
-        cost_estimate=cost(8 * slots * width * tokens * rank, 4 * slots * width * rank),
+        cost_estimate=cost(8 * owners * cap * width * mask.shape[1] * rank, 0),
     )(g, mask, *sent, *gots)
 
 
@@ -220,45 +225,74 @@
     )(block, *pieces)
 
 
-def score_kernel(count, gaps, relative, ids_ref, *refs):
-    rows, pieces, scores_ref = refs[:count], refs[count : count + len(gaps)], refs[-1]
-    queries = ids_ref.shape[1]
+def pool_kernel(*refs):
+    refs[-1][...] = jnp.concatenate(halves(stack(refs[:-1])), axis=0)
+
+
+def pool_halves(pieces):
+    rows, feats = sum(piece.shape[0] for piece in pieces), pieces[0].shape[1]
+    return pl.pallas_call(
+        pool_kernel,
+        out_shape=jax.ShapeDtypeStruct((2 * rows, feats), BF16),
+        compiler_params=params(16),
+        cost_estimate=cost(0, 0),
+    )(*pieces)
+
+
+def scores_of(rows, ids, pool, gaps):
     me = lax.axis_index("dp")
-    cap = rows[0].shape[0]
-    high, low = halves(stack(rows))
-    slots = high.shape[0]
-    both = jnp.concatenate([high, low], axis=0)
-    held = pieces[0].shape[0]
-    pool = stack(pieces)
-    products = mm(both, jnp.concatenate(halves(pool), axis=0), NT)
-    split = pool.shape[0]
+    high, low = halves(rows)
+    slots, split, queries = rows.shape[0], pool.shape[0] // 2, ids.shape[1]
+    products = mm(jnp.concatenate([high, low], axis=0), pool, NT)
     part = products[:slots, :split] + products[:slots, split:] + products[slots:, :split]
+    held = split // len(gaps)
     row = lax.broadcasted_iota(jnp.int32, (held, queries), 0)
     places = [row + ((me ^ gap) * held if len(gaps) > 1 else 0) for gap in gaps]
-    hot = (jnp.concatenate(places, axis=0) == ids_ref[...]).astype(F32).astype(BF16)
+    hot = (jnp.concatenate(places, axis=0) == ids).astype(F32).astype(BF16)
     top, rest = halves(part)
     last = (part - top.astype(F32) - rest.astype(F32)).astype(BF16)
     picked = mm(jnp.concatenate([top, rest, last], axis=0), hot)
-    total = picked[:slots] + picked[slots : 2 * slots] + picked[2 * slots :]
-    for k in range(count):
-        source = lax.rem(me - k + count, count) if relative else k
-        spot = pl.ds(pl.multiple_of(source * cap, cap), cap)
-        scores_ref[spot, :] = total[k * cap : (k + 1) * cap, :]
-
-
-def score(ids_row, rows, pieces, gaps, relative, tokens):
-    slots = rows[0].shape[0] * len(rows)
+    return picked[:slots] + picked[slots : 2 * slots] + picked[2 * slots :]
+
+
+def early_kernel(gaps, ids_ref, pool_ref, *refs):
+    refs[-1][...] = scores_of(stack(refs[:-1]), ids_ref[...], pool_ref[...], gaps)
+
+
+def score_early(ids_row, pool, rows, gaps):
+    slots = sum(row.shape[0] for row in rows)
+    return pl.pallas_call(
+        functools.partial(early_kernel, gaps),
+        out_shape=jax.ShapeDtypeStruct((slots, ids_row.shape[1]), F32),
+        compiler_params=params(16),
+        cost_estimate=cost(SCORE_FLOPS, 0),
+    )(ids_row, pool, *rows)
+
+
+def score_kernel(count, gaps, relative, ids_ref, pool_ref, early_ref, *refs):
+    rows, scores_ref = refs[:count], refs[-1]
+    me = lax.axis_index("dp")
+    cap = rows[0].shape[0]
+    total = scores_of(stack(rows), ids_ref[...], pool_ref[...], gaps)
+    done = early_ref.shape[0] // cap if relative else 0
+    for k in range(done + count):
+        part = early_ref if k < done else total
+        at = (k if k < done else k - done) * cap
+        source = lax.rem(me - k + done + count, done + count) if relative else k
+        scores_ref[pl.ds(pl.multiple_of(source * cap, cap), cap), :] = part[at : at + cap, :]
+
+
+def score(ids_row, pool, early, rows, gaps, relative, tokens):
+    slots = sum(row.shape[0] for row in rows) + (early.shape[0] if relative else 0)
     queries = ids_row.shape[1]
-    size, feats = pieces[0].shape
-    flops = 6 * slots * size * len(gaps) * feats
     return pl.pallas_call(
         functools.partial(score_kernel, len(rows), gaps, relative),
-        in_specs=[pl.BlockSpec(memory_space=pltpu.VMEM)] * (1 + len(rows) + len(pieces))
+        in_specs=[pl.BlockSpec(memory_space=pltpu.VMEM)] * (3 + len(rows))
         + [pl.BlockSpec(memory_space=pl.ANY)] * len(tokens),
         out_shape=jax.ShapeDtypeStruct((slots, queries), F32),
         compiler_params=params(24),
-        cost_estimate=cost(flops, 4 * size * len(gaps) * feats),
-    )(ids_row, *rows, *pieces, *tokens)
+        cost_estimate=cost(0, 0),
+    )(ids_row, pool, early, *rows, *tokens)
 
 
 def place_kernel(*refs):
@@ -328,20 +362,25 @@
         bit //= 2
         keep, own = fold(rank, keep, own, gots, early)
         gots = [swap(part, "tensor", bit) for part in own]
-    blocks = outer(own, gots, keep, mask, data_size)
+    ids_row = query_ids[None, :]
     if direct:
-        *sent, kept = blocks
+        split = max(1, data_size // 2)
+        soon = outer(own, gots, keep, mask, cap, 0, split)
+        rows = [shift(block, "dp", k) for k, block in enumerate(soon, 1)]
+        *sent, kept = outer(own, gots, keep, mask, cap, split, data_size - split)
         sent[-1] = after(sent[-1], [mate, *passed])
-        rows = [kept] + [shift(block, "dp", k) for k, block in enumerate(sent, 1)]
-        late = []
-        for row in rows[1:-1]:
-            late = [token([row, *late], LATE_FLOPS)]
-        pieces, gaps = [*pieces, mate, *passed], [*gaps, *(g ^ 1 for g in gaps)]
+        rows = [kept, *rows, *(shift(block, "dp", k) for k, block in enumerate(sent, 1 + split))]
         store = place(rows)
+        late = [token(rows[2:-1], LATE_FLOPS)]
+        pool = pool_halves([*pieces, mate, *passed])
+        gaps = [*gaps, *(g ^ 1 for g in gaps)]
+        early = score_early(ids_row, pool, rows[:2], gaps)
+        scores = score(ids_row, pool, early, rows[2:], gaps, True, late)
     else:
-        rows = [lax.all_to_all(jnp.stack(blocks), "dp", 0, 0, tiled=True).reshape(-1, width * rank)]
-        store, late = rows[0], []
-    scores = score(query_ids[None, :], rows, pieces, gaps, direct, late)
+        blocks = outer(own, gots, keep, mask, cap, 0, data_size)
+        store = lax.all_to_all(jnp.stack(blocks), "dp", 0, 0, tiled=True).reshape(-1, width * rank)
+        pool = pool_halves(pieces)
+        scores = score(ids_row, pool, ids_row, [store], gaps, False, [])
     bit = 1
     while bit < tensor_size:
         scores = scores + swap(scores, "tensor", bit)

time: 30.2 us -> 29.8 us (0.987)
  waiting for transfers between devices: 8.01 us -> 6.94 us
  Pallas kernels: 3.87 us -> 4.61 us
    ppermute x3, waiting for transfers between devices: 2.85 us -> 1.75 us  [shift(): return lax.ppermute(x, axis, [(i, (i + by) % size) for i in range(size)])]
    pallas_call x1 -> x4, Pallas kernels: 0.84 us -> 1.63 us  [the longest x2 1.14 us: outer(): pl.pallas_call(functools.partial(outer_kernel, first, owners, len(sent)),...]
  transfers between devices with their start and end apart: 12 -> 12, of which waited for: 8 -> 7; matrix products, arithmetic and copies ran while one was open for 0% -> 0% of each run, Pallas kernels for 11% -> 14%
where the time goes in v17:
time: 29.8 us; the launch traced here: 29.7 us
  starting transfers between devices  16.7 us (56%)
  waiting for transfers between devices  6.94 us (23%)
  Pallas kernels  4.61 us (15%)
  between operations  0.77 us (3%)
  other arithmetic  0.63 us (2%)
    ppermute x9, starting transfers between devices, swap(): lax.ppermute(x, axis, [(i, i ^ gap) for i in range(lax.axis_size(axis))])  10.5 us
    ppermute x3, starting transfers between devices, shift(): return lax.ppermute(x, axis, [(i, (i + by) % size) for i in range(size)])  6.23 us
    ppermute x9, waiting for transfers between devices, swap(): lax.ppermute(x, axis, [(i, i ^ gap) for i in range(lax.axis_size(axis))])  5.18 us
    ppermute x3, waiting for transfers between devices, shift(): return lax.ppermute(x, axis, [(i, (i + by) % size) for i in range(size)])  1.75 us
    pallas_call x1, Pallas kernels, project_g(): pl.pallas_call(functools.partial(g_kernel, width), out_shape=[part, part]...  1.16 us
    pallas_call x2, Pallas kernels, outer(): pl.pallas_call(functools.partial(outer_kernel, first, owners, len(sent)),...  1.14 us
    pallas_call x1, Pallas kernels, place(): pl.pallas_call(place_kernel, out_shape=jax.ShapeDtypeStruct((slots, feats...  0.72 us
    mul x1, other arithmetic, local(): return (store, scores * (1.0 / (rank * rank)))  0.62 us
  transfers between devices with their start and end apart: 12, of which 7 were waited for; matrix products, arithmetic and copies ran while one was open for 0% of the time, Pallas kernels for 14%

profile of v17, /device:TPU:0, one launch (start us, length us, event | category | flops | bytes accessed | tf_op | source)
XLA Modules:
  0.0 29.7 jit_solution(12431505717638515634)
XLA Ops:
  0.7 4.1 %collective-permute-start.2 = (f32[32,1024]{1,0:T(8,128)}, f32[32,1024]{1,0:T(8,128)S(1)}, u32[]{:S(2)}, u32[]{:S(2)}) collective-permute-start(f32[32,1024]{1,0:T(8,128)} %refs_0_.1), channel_id=1, source_target_pairs={{0,8},{4,12},{8,0},{12,4},{1,9},{5,13},{9,1},{13,5},{2,10},{6,14},... | collective-permute-start | bytes 393224 | tf_op jit(solution)/shard_map/ppermute | solution.py:318
  4.8 0.5 %shard_map.97.refs_0_ = f32[64,512]{1,0:T(8,128)S(1)} custom-call(bf16[512,1024]{1,0:T(8,128)(2,1)S(1)} %copy-done.4, bf16[64,1024]{1,0:T(8,128)(2,1)S(1)} %bitcast.7, f32[8,128]{1,0:T(8,128)S(1)} %shard_map.96.refs_0_), custom_call_target="tpu_custom_call" | custom-call | flops 600000000 | tf_op jit(solution)/shard_map/pallas_call | solution.py:89
  5.3 1.5 %collective-permute-start = (f32[64,512]{1,0:T(8,128)S(1)}, f32[64,512]{1,0:T(8,128)S(1)}, u32[]{:S(2)}, u32[]{:S(2)}) collective-permute-start(f32[64,512]{1,0:T(8,128)S(1)} %shard_map.97.refs_0_), channel_id=1, source_target_pairs={{0,2},{1,3},{2,0},{3,1},{4,6},{5,7},{6,4},{7,5},{8,10},{9,11},{10,... | collective-permute-start | bytes 393224 | tf_op jit(solution)/shard_map/ppermute | solution.py:318
  6.8 1.2 %shard_map.95 = (f32[32,512]{1,0:T(8,128)S(1)}, f32[32,512]{1,0:T(8,128)S(1)}) custom-call(bf16[512,3584]{1,0:T(8,128)(2,1)S(1)} %copy-done, bf16[64,3584]{1,0:T(8,128)(2,1)S(1)} %bitcast.4), custom_call_target="tpu_custom_call" | custom-call | tf_op jit(solution)/shard_map/pallas_call | solution.py:112
  8.0 0.6 %collective-permute-start.1 = (f32[32,512]{1,0:T(8,128)S(1)}, f32[32,512]{1,0:T(8,128)S(1)}, u32[]{:S(2)}, u32[]{:S(2)}) collective-permute-start(f32[32,512]{1,0:T(8,128)S(1)} %get-tuple-element.12), channel_id=1, source_target_pairs={{0,2},{1,3},{2,0},{3,1},{4,6},{5,7},{6,4},{7,5},{8,10},{9,11},{10,... | collective-permute-start | bytes 196616 | tf_op jit(solution)/shard_map/ppermute | solution.py:318
  8.6 1.6 %collective-permute-start.7 = (f32[32,1024]{1,0:T(8,128)S(1)}, f32[32,1024]{1,0:T(8,128)S(1)}, u32[]{:S(2)}, u32[]{:S(2)}) collective-permute-start(f32[32,1024]{1,0:T(8,128)S(1)} %copy-done.2), channel_id=1, source_target_pairs={{0,4},{4,0},{8,12},{12,8},{1,5},{5,1},{9,13},{13,9},{2,6},{6,2},{1... | collective-permute-start | bytes 393224 | tf_op jit(solution)/shard_map/ppermute | solution.py:318
  10.2 0.2 shard_map.98.refs_3_.mask_ref
  10.4 1.0 %collective-permute-done.2.refs_0_.refs_1_ = f32[32,1024]{1,0:T(8,128)S(1)} collective-permute-done((f32[32,1024]{1,0:T(8,128)}, f32[32,1024]{1,0:T(8,128)S(1)}, u32[]{:S(2)}, u32[]{:S(2)}) %collective-permute-start.2) | collective-permute-done | bytes 131104 | tf_op jit(solution)/shard_map/ppermute | solution.py:318
  11.4 0.7 %collective-permute-start.8 = (f32[32,1024]{1,0:T(8,128)S(1)}, f32[32,1024]{1,0:T(8,128)S(1)}, u32[]{:S(2)}, u32[]{:S(2)}) collective-permute-start(f32[32,1024]{1,0:T(8,128)S(1)} %collective-permute-done.2.refs_0_.refs_1_), channel_id=1, source_target_pairs={{0,4},{4,0},{8,12},{12,8},{1,5},{5,1},{9,13},{13,9},{2,6},{6,2},{1... | collective-permute-start | bytes 393224 | tf_op jit(solution)/shard_map/ppermute | solution.py:318
  12.4 0.5 %collective-permute-start.4 = (f32[40,512]{1,0:T(8,128)S(1)}, f32[40,512]{1,0:T(8,128)S(1)}, u32[]{:S(2)}, u32[]{:S(2)}) collective-permute-start(f32[40,512]{1,0:T(8,128)S(1)} %get-tuple-element.15.refs_1_), channel_id=1, source_target_pairs={{0,1},{1,0},{2,3},{3,2},{4,5},{5,4},{6,7},{7,6},{8,9},{9,8},{10,11... | collective-permute-start | bytes 245768 | tf_op jit(solution)/shard_map/ppermute | solution.py:318
  12.9 0.8 %collective-permute-done.3.refs_2_ = f32[40,512]{1,0:T(8,128)S(1)} collective-permute-done((f32[40,512]{1,0:T(8,128)S(1)}, f32[40,512]{1,0:T(8,128)S(1)}, u32[]{:S(2)}, u32[]{:S(2)}) %collective-permute-start.3) | collective-permute-done | bytes 81952 | tf_op jit(solution)/shard_map/ppermute | solution.py:318
  13.8 0.6 %shard_map.102 = (f32[16,1024]{1,0:T(8,128)S(1)}, f32[16,1024]{1,0:T(8,128)S(1)}) custom-call(f32[16,512]{1,0:T(8,128)S(1)} %get-tuple-element.13.g_ref, bf16[64,512]{1,0:T(8,128)(2,1)S(1)} %shard_map.98.refs_3_.mask_ref, f32[40,512]{1,0:T(8,128)S(1)} %get-tuple-element.14.refs_0_, f32[40,512]{1,0:T(8,128)S(1)} %get-tuple-element.15.refs_1_, ...), custom_call_target="tpu_custom_call" | custom-call | flops 134217728 | tf_op jit(solution)/shard_map/pallas_call | solution.py:191
  14.4 1.6 %collective-permute-start.5 = (f32[16,1024]{1,0:T(8,128)S(1)}, f32[16,1024]{1,0:T(8,128)S(1)}, u32[]{:S(2)}, u32[]{:S(2)}) collective-permute-start(f32[16,1024]{1,0:T(8,128)S(1)} %get-tuple-element.17), channel_id=1, source_target_pairs={{0,4},{4,8},{8,12},{12,0},{1,5},{5,9},{9,13},{13,1},{2,6},{6,10},{... | collective-permute-start | bytes 196616 | tf_op jit(solution)/shard_map/ppermute | solution.py:323
  16.1 1.7 %collective-permute-start.6 = (f32[16,1024]{1,0:T(8,128)S(1)}, f32[16,1024]{1,0:T(8,128)S(1)}, u32[]{:S(2)}, u32[]{:S(2)}) collective-permute-start(f32[16,1024]{1,0:T(8,128)S(1)} %get-tuple-element.18), channel_id=1, source_target_pairs={{0,8},{4,12},{8,0},{12,4},{1,9},{5,13},{9,1},{13,5},{2,10},{6,14},... | collective-permute-start | bytes 196616 | tf_op jit(solution)/shard_map/ppermute | solution.py:323
  17.7 0.6 %shard_map.101 = (f32[16,1024]{1,0:T(8,128)S(1)}, f32[16,1024]{1,0:T(8,128)S(1)}) custom-call(f32[16,512]{1,0:T(8,128)S(1)} %get-tuple-element.13.g_ref, bf16[64,512]{1,0:T(8,128)(2,1)S(1)} %shard_map.98.refs_3_.mask_ref, f32[40,512]{1,0:T(8,128)S(1)} %get-tuple-element.14.refs_0_, f32[40,512]{1,0:T(8,128)S(1)} %get-tuple-element.15.refs_1_, ...), custom_call_target="tpu_custom_call" | custom-call | flops 134217728 | tf_op jit(solution)/shard_map/pallas_call | solution.py:191
  18.3 2.9 %collective-permute-start.9 = (f32[16,1024]{1,0:T(8,128)S(1)}, f32[16,1024]{1,0:T(8,128)S(1)}, u32[]{:S(2)}, u32[]{:S(2)}) collective-permute-start(f32[16,1024]{1,0:T(8,128)S(1)} %shard_map.103), channel_id=1, source_target_pairs={{0,12},{4,0},{8,4},{12,8},{1,13},{5,1},{9,5},{13,9},{2,14},{6,2},{... | collective-permute-start | bytes 196616 | tf_op jit(solution)/shard_map/ppermute | solution.py:323
  21.4 0.4 %shard_map.106.early_ref = f32[32,128]{1,0:T(8,128)S(1)} custom-call(s32[1,128]{1,0:T(1,128)S(1)} %bitcast.5, bf16[256,1024]{1,0:T(8,128)(2,1)S(1)} %shard_map.105.pool_ref, f32[16,1024]{1,0:T(8,128)S(1)} %get-tuple-element.16.refs_0_, f32[16,1024]{1,0:T(8,128)S(1)} %collective-permute-done.5.refs_1_), custom_call_target="tpu_custom_call" | custom-call | tf_op jit(solution)/shard_map/pallas_call | solution.py:264
  21.8 1.7 %collective-permute-done.6.refs_2_.refs_0_ = f32[16,1024]{1,0:T(8,128)S(1)} collective-permute-done((f32[16,1024]{1,0:T(8,128)S(1)}, f32[16,1024]{1,0:T(8,128)S(1)}, u32[]{:S(2)}, u32[]{:S(2)}) %collective-permute-start.6) | collective-permute-done | bytes 65568 | tf_op jit(solution)/shard_map/ppermute | solution.py:323
  23.5 0.4 %shard_map.108 = f32[64,128]{1,0:T(8,128)S(1)} custom-call(s32[1,128]{1,0:T(1,128)S(1)} %bitcast.6, bf16[256,1024]{1,0:T(8,128)(2,1)S(1)} %shard_map.105.pool_ref, f32[32,128]{1,0:T(8,128)S(1)} %shard_map.106.early_ref, f32[16,1024]{1,0:T(8,128)S(1)} %collective-permute-done.6.refs_2_.refs_0_, f32[16,1024]{1,0:T(8,128)S(1)} %collective-permute-done.9.refs_3_.refs_1_, ...), custom_call_target="tpu_custom_call" | custom-call | tf_op jit(solution)/shard_map/pallas_call | solution.py:288
  23.9 1.2 %collective-permute-done.10 = f32[64,128]{1,0:T(8,128)S(1)} collective-permute-done((f32[64,128]{1,0:T(8,128)S(1)}, f32[64,128]{1,0:T(8,128)S(1)}, u32[]{:S(2)}, u32[]{:S(2)}) %collective-permute-start.10) | collective-permute-done | bytes 32800 | tf_op jit(solution)/shard_map/ppermute | solution.py:318
  25.1 1.3 %collective-permute-start.11 = (f32[64,128]{1,0:T(8,128)S(1)}, f32[64,128]{1,0:T(8,128)S(1)}, u32[]{:S(2)}, u32[]{:S(2)}) collective-permute-start(f32[64,128]{1,0:T(8,128)S(1)} %add.6), channel_id=1, source_target_pairs={{0,2},{1,3},{2,0},{3,1},{4,6},{5,7},{6,4},{7,5},{8,10},{9,11},{10,... | collective-permute-start | bytes 98312 | tf_op jit(solution)/shard_map/ppermute | solution.py:318
  26.5 0.7 %shard_map.104 = f32[64,1024]{1,0:T(8,128)} custom-call(f32[16,1024]{1,0:T(8,128)S(1)} %get-tuple-element.16.refs_0_, f32[16,1024]{1,0:T(8,128)S(1)} %collective-permute-done.5.refs_1_, f32[16,1024]{1,0:T(8,128)S(1)} %collective-permute-done.6.refs_2_.refs_0_, f32[16,1024]{1,0:T(8,128)S(1)} %collective-permute-done.9.refs_3_.refs_1_), custom_call_target="tpu_custom_call" | custom-call | bytes 524288 | tf_op jit(solution)/shard_map/pallas_call | solution.py:309
  27.2 1.8 %collective-permute-done.11 = f32[64,128]{1,0:T(8,128)S(1)} collective-permute-done((f32[64,128]{1,0:T(8,128)S(1)}, f32[64,128]{1,0:T(8,128)S(1)}, u32[]{:S(2)}, u32[]{:S(2)}) %collective-permute-start.11) | collective-permute-done | bytes 32800 | tf_op jit(solution)/shard_map/ppermute | solution.py:318
  29.1 0.6 %add_multiply_fusion = f32[64,128]{1,0:T(8,128)} fusion(f32[64,128]{1,0:T(8,128)S(1)} %add.6, f32[64,128]{1,0:T(8,128)S(1)} %collective-permute-done.11), kind=kLoop, calls=%fused_computation | loop fusion | flops 16384 | bytes 98304 | tf_op jit(solution)/shard_map/mul | solution.py:388
  (32 shorter events, 0.6 us)
Async XLA Ops:
  0.6 4.2 %copy-start.5 = (bf16[1024,64]{0,1:T(8,128)(2,1)S(1)}, bf16[1024,64]{0,1:T(8,128)(2,1)}, u32[]{:S(2)}) copy-start(bf16[1024,64]{0,1:T(8,128)(2,1)} %param.10) | copy-start | bytes 393220
  0.6 4.2 %copy-start.4 = (bf16[512,1024]{1,0:T(8,128)(2,1)S(1)}, bf16[512,1024]{1,0:T(8,128)(2,1)}, u32[]{:S(2)}) copy-start(bf16[512,1024]{1,0:T(8,128)(2,1)} %act_ref.1) | copy-start | bytes 3145732
  0.7 6.2 %copy-start.1 = (bf16[3584,64]{0,1:T(8,128)(2,1)S(1)}, bf16[3584,64]{0,1:T(8,128)(2,1)}, u32[]{:S(2)}) copy-start(bf16[3584,64]{0,1:T(8,128)(2,1)} %param.11) | copy-start | bytes 1376260
  0.7 6.2 %copy-start = (bf16[512,3584]{1,0:T(8,128)(2,1)S(1)}, bf16[512,3584]{1,0:T(8,128)(2,1)}, u32[]{:S(2)}) copy-start(bf16[512,3584]{1,0:T(8,128)(2,1)} %grad_ref.1) | copy-start | bytes 11010052
  0.7 10.7 %collective-permute-start.2 = (f32[32,1024]{1,0:T(8,128)}, f32[32,1024]{1,0:T(8,128)S(1)}, u32[]{:S(2)}, u32[]{:S(2)}) collective-permute-start(f32[32,1024]{1,0:T(8,128)} %refs_0_.1), channel_id=1, source_target_pairs={{0,8},{4,12},{8,0},{12,4},{1,9},{5,13},{9,1},{13,5},{2,10},{6,14},... | collective-permute-start | bytes 393224 | tf_op jit(solution)/shard_map/ppermute | solution.py:318
  4.8 3.8 %copy-start.2 = (f32[32,1024]{1,0:T(8,128)S(1)}, f32[32,1024]{1,0:T(8,128)}, u32[]{:S(2)}) copy-start(f32[32,1024]{1,0:T(8,128)} %refs_0_.1) | copy-start | bytes 393220
  4.8 5.4 %copy-start.6 = (s32[1,32]{1,0:T(1,128)S(1)}, s32[1,32]{1,0:T(1,128)}, u32[]{:S(2)}) copy-start(s32[1,32]{1,0:T(1,128)} %lengths_ref.1) | copy-start | bytes 388
  4.8 5.4 %copy-start.7 = (s32[32,1]{0,1:T(1,128)S(1)}, s32[32,1]{0,1:T(1,128)}, u32[]{:S(2)}) copy-start(s32[32,1]{0,1:T(1,128)} %param.13) | copy-start | bytes 388
  5.3 7.1 %collective-permute-start = (f32[64,512]{1,0:T(8,128)S(1)}, f32[64,512]{1,0:T(8,128)S(1)}, u32[]{:S(2)}, u32[]{:S(2)}) collective-permute-start(f32[64,512]{1,0:T(8,128)S(1)} %shard_map.97.refs_0_), channel_id=1, source_target_pairs={{0,2},{1,3},{2,0},{3,1},{4,6},{5,7},{6,4},{7,5},{8,10},{9,11},{10,... | collective-permute-start | bytes 393224 | tf_op jit(solution)/shard_map/ppermute | solution.py:318
  6.8 14.5 %copy-start.3 = (s32[128]{0:T(128)S(1)}, s32[128]{0:T(128)}, u32[]{:S(2)}) copy-start(s32[128]{0:T(128)} %param.15) | copy-start | bytes 1540
  8.0 4.3 %collective-permute-start.1 = (f32[32,512]{1,0:T(8,128)S(1)}, f32[32,512]{1,0:T(8,128)S(1)}, u32[]{:S(2)}, u32[]{:S(2)}) collective-permute-start(f32[32,512]{1,0:T(8,128)S(1)} %get-tuple-element.12), channel_id=1, source_target_pairs={{0,2},{1,3},{2,0},{3,1},{4,6},{5,7},{6,4},{7,5},{8,10},{9,11},{10,... | collective-permute-start | bytes 196616 | tf_op jit(solution)/shard_map/ppermute | solution.py:318
  8.6 9.7 %collective-permute-start.7 = (f32[32,1024]{1,0:T(8,128)S(1)}, f32[32,1024]{1,0:T(8,128)S(1)}, u32[]{:S(2)}, u32[]{:S(2)}) collective-permute-start(f32[32,1024]{1,0:T(8,128)S(1)} %copy-done.2), channel_id=1, source_target_pairs={{0,4},{4,0},{8,12},{12,8},{1,5},{5,1},{9,13},{13,9},{2,6},{6,2},{1... | collective-permute-start | bytes 393224 | tf_op jit(solution)/shard_map/ppermute | solution.py:318
  11.4 6.9 %collective-permute-start.8 = (f32[32,1024]{1,0:T(8,128)S(1)}, f32[32,1024]{1,0:T(8,128)S(1)}, u32[]{:S(2)}, u32[]{:S(2)}) collective-permute-start(f32[32,1024]{1,0:T(8,128)S(1)} %collective-permute-done.2.refs_0_.refs_1_), channel_id=1, source_target_pairs={{0,4},{4,0},{8,12},{12,8},{1,5},{5,1},{9,13},{13,9},{2,6},{6,2},{1... | collective-permute-start | bytes 393224 | tf_op jit(solution)/shard_map/ppermute | solution.py:318
  12.3 1.3 %collective-permute-start.3 = (f32[40,512]{1,0:T(8,128)S(1)}, f32[40,512]{1,0:T(8,128)S(1)}, u32[]{:S(2)}, u32[]{:S(2)}) collective-permute-start(f32[40,512]{1,0:T(8,128)S(1)} %get-tuple-element.14.refs_0_), channel_id=1, source_target_pairs={{0,1},{1,0},{2,3},{3,2},{4,5},{5,4},{6,7},{7,6},{8,9},{9,8},{10,11... | collective-permute-start | bytes 245768 | tf_op jit(solution)/shard_map/ppermute | solution.py:318
  12.4 1.4 %collective-permute-start.4 = (f32[40,512]{1,0:T(8,128)S(1)}, f32[40,512]{1,0:T(8,128)S(1)}, u32[]{:S(2)}, u32[]{:S(2)}) collective-permute-start(f32[40,512]{1,0:T(8,128)S(1)} %get-tuple-element.15.refs_1_), channel_id=1, source_target_pairs={{0,1},{1,0},{2,3},{3,2},{4,5},{5,4},{6,7},{7,6},{8,9},{9,8},{10,11... | collective-permute-start | bytes 245768 | tf_op jit(solution)/shard_map/ppermute | solution.py:318
  14.4 6.9 %collective-permute-start.5 = (f32[16,1024]{1,0:T(8,128)S(1)}, f32[16,1024]{1,0:T(8,128)S(1)}, u32[]{:S(2)}, u32[]{:S(2)}) collective-permute-start(f32[16,1024]{1,0:T(8,128)S(1)} %get-tuple-element.17), channel_id=1, source_target_pairs={{0,4},{4,8},{8,12},{12,0},{1,5},{5,9},{9,13},{13,1},{2,6},{6,10},{... | collective-permute-start | bytes 196616 | tf_op jit(solution)/shard_map/ppermute | solution.py:323
  16.1 7.5 %collective-permute-start.6 = (f32[16,1024]{1,0:T(8,128)S(1)}, f32[16,1024]{1,0:T(8,128)S(1)}, u32[]{:S(2)}, u32[]{:S(2)}) collective-permute-start(f32[16,1024]{1,0:T(8,128)S(1)} %get-tuple-element.18), channel_id=1, source_target_pairs={{0,8},{4,12},{8,0},{12,4},{1,9},{5,13},{9,1},{13,5},{2,10},{6,14},... | collective-permute-start | bytes 196616 | tf_op jit(solution)/shard_map/ppermute | solution.py:323
  18.3 5.2 %collective-permute-start.9 = (f32[16,1024]{1,0:T(8,128)S(1)}, f32[16,1024]{1,0:T(8,128)S(1)}, u32[]{:S(2)}, u32[]{:S(2)}) collective-permute-start(f32[16,1024]{1,0:T(8,128)S(1)} %shard_map.103), channel_id=1, source_target_pairs={{0,12},{4,0},{8,4},{12,8},{1,13},{5,1},{9,5},{13,9},{2,14},{6,2},{... | collective-permute-start | bytes 196616 | tf_op jit(solution)/shard_map/ppermute | solution.py:323
  23.9 1.2 %collective-permute-start.10 = (f32[64,128]{1,0:T(8,128)S(1)}, f32[64,128]{1,0:T(8,128)S(1)}, u32[]{:S(2)}, u32[]{:S(2)}) collective-permute-start(f32[64,128]{1,0:T(8,128)S(1)} %shard_map.108), channel_id=1, source_target_pairs={{0,1},{1,0},{2,3},{3,2},{4,5},{5,4},{6,7},{7,6},{8,9},{9,8},{10,11... | collective-permute-start | bytes 98312 | tf_op jit(solution)/shard_map/ppermute | solution.py:318
  25.1 3.9 %collective-permute-start.11 = (f32[64,128]{1,0:T(8,128)S(1)}, f32[64,128]{1,0:T(8,128)S(1)}, u32[]{:S(2)}, u32[]{:S(2)}) collective-permute-start(f32[64,128]{1,0:T(8,128)S(1)} %add.6), channel_id=1, source_target_pairs={{0,2},{1,3},{2,0},{3,1},{4,6},{5,7},{6,4},{7,5},{8,10},{9,11},{10,... | collective-permute-start | bytes 98312 | tf_op jit(solution)/shard_map/ppermute | solution.py:318

commit v18 on v17

--- a/solution.py
+++ b/solution.py
@@ -14,6 +14,7 @@
 MOST_DIRECT = 8
 GROUP = 8
 ROWS = 16
+LANES = 128
 FIRST_FLOPS = 10 * 10**8
 X_FLOPS = 6 * 10**8
 MASK_FLOPS = 2 * 10**8
@@ -246,6 +247,11 @@
     products = mm(jnp.concatenate([high, low], axis=0), pool, NT)
     part = products[:slots, :split] + products[:slots, split:] + products[slots:, :split]
     held = split // len(gaps)
+    if split == LANES and queries == LANES and len(gaps) > 1:
+        spot = lax.rem(ids, held)
+        for place, gap in enumerate(gaps):
+            spot = spot + jnp.where(lax.div(ids, held) == (me ^ gap), place * held, 0)
+        return jnp.take_along_axis(part, jnp.broadcast_to(spot, part.shape), axis=1)
     row = lax.broadcasted_iota(jnp.int32, (held, queries), 0)
     places = [row + ((me ^ gap) * held if len(gaps) > 1 else 0) for gap in gaps]
     hot = (jnp.concatenate(places, axis=0) == ids).astype(F32).astype(BF16)

time: 29.8 us -> 29.8 us (level)
  no operation moved by 1% of the time
where the time goes in v18:
time: 29.8 us; the launch traced here: 29.6 us
  starting transfers between devices  16.7 us (56%)
  waiting for transfers between devices  6.98 us (23%)
  Pallas kernels  4.5 us (15%)
  between operations  0.78 us (3%)
  other arithmetic  0.63 us (2%)
    ppermute x9, starting transfers between devices, swap(): lax.ppermute(x, axis, [(i, i ^ gap) for i in range(lax.axis_size(axis))])  10.5 us
    ppermute x3, starting transfers between devices, shift(): return lax.ppermute(x, axis, [(i, (i + by) % size) for i in range(size)])  6.23 us
    ppermute x9, waiting for transfers between devices, swap(): lax.ppermute(x, axis, [(i, i ^ gap) for i in range(lax.axis_size(axis))])  5.17 us
    ppermute x3, waiting for transfers between devices, shift(): return lax.ppermute(x, axis, [(i, (i + by) % size) for i in range(size)])  1.81 us
    pallas_call x1, Pallas kernels, project_g(): pl.pallas_call(functools.partial(g_kernel, width), out_shape=[part, part]...  1.16 us
    pallas_call x2, Pallas kernels, outer(): pl.pallas_call(functools.partial(outer_kernel, first, owners, len(sent)),...  1.14 us
    pallas_call x1, Pallas kernels, place(): pl.pallas_call(place_kernel, out_shape=jax.ShapeDtypeStruct((slots, feats...  0.72 us
    mul x1, other arithmetic, local(): return (store, scores * (1.0 / (rank * rank)))  0.62 us
  transfers between devices with their start and end apart: 12, of which 7 were waited for; matrix products, arithmetic and copies ran while one was open for 0% of the time, Pallas kernels for 14%

profile of v18, /device:TPU:0, one launch (start us, length us, event | category | flops | bytes accessed | tf_op | source)
XLA Modules:
  0.0 29.6 jit_solution(9594371019683382604)
XLA Ops:
  0.7 4.1 %collective-permute-start.2 = (f32[32,1024]{1,0:T(8,128)}, f32[32,1024]{1,0:T(8,128)S(1)}, u32[]{:S(2)}, u32[]{:S(2)}) collective-permute-start(f32[32,1024]{1,0:T(8,128)} %refs_0_.1), channel_id=1, source_target_pairs={{0,8},{4,12},{8,0},{12,4},{1,9},{5,13},{9,1},{13,5},{2,10},{6,14},... | collective-permute-start | bytes 393224 | tf_op jit(solution)/shard_map/ppermute | solution.py:324
  4.8 0.5 %shard_map.97.refs_0_ = f32[64,512]{1,0:T(8,128)S(1)} custom-call(bf16[512,1024]{1,0:T(8,128)(2,1)S(1)} %copy-done.4, bf16[64,1024]{1,0:T(8,128)(2,1)S(1)} %bitcast.7, f32[8,128]{1,0:T(8,128)S(1)} %shard_map.96.refs_0_), custom_call_target="tpu_custom_call" | custom-call | flops 600000000 | tf_op jit(solution)/shard_map/pallas_call | solution.py:90
  5.3 1.5 %collective-permute-start = (f32[64,512]{1,0:T(8,128)S(1)}, f32[64,512]{1,0:T(8,128)S(1)}, u32[]{:S(2)}, u32[]{:S(2)}) collective-permute-start(f32[64,512]{1,0:T(8,128)S(1)} %shard_map.97.refs_0_), channel_id=1, source_target_pairs={{0,2},{1,3},{2,0},{3,1},{4,6},{5,7},{6,4},{7,5},{8,10},{9,11},{10,... | collective-permute-start | bytes 393224 | tf_op jit(solution)/shard_map/ppermute | solution.py:324
  6.8 1.2 %shard_map.95 = (f32[32,512]{1,0:T(8,128)S(1)}, f32[32,512]{1,0:T(8,128)S(1)}) custom-call(bf16[512,3584]{1,0:T(8,128)(2,1)S(1)} %copy-done, bf16[64,3584]{1,0:T(8,128)(2,1)S(1)} %bitcast.4), custom_call_target="tpu_custom_call" | custom-call | tf_op jit(solution)/shard_map/pallas_call | solution.py:113
  8.0 0.6 %collective-permute-start.1 = (f32[32,512]{1,0:T(8,128)S(1)}, f32[32,512]{1,0:T(8,128)S(1)}, u32[]{:S(2)}, u32[]{:S(2)}) collective-permute-start(f32[32,512]{1,0:T(8,128)S(1)} %get-tuple-element.12), channel_id=1, source_target_pairs={{0,2},{1,3},{2,0},{3,1},{4,6},{5,7},{6,4},{7,5},{8,10},{9,11},{10,... | collective-permute-start | bytes 196616 | tf_op jit(solution)/shard_map/ppermute | solution.py:324
  8.6 1.6 %collective-permute-start.7 = (f32[32,1024]{1,0:T(8,128)S(1)}, f32[32,1024]{1,0:T(8,128)S(1)}, u32[]{:S(2)}, u32[]{:S(2)}) collective-permute-start(f32[32,1024]{1,0:T(8,128)S(1)} %copy-done.2), channel_id=1, source_target_pairs={{0,4},{4,0},{8,12},{12,8},{1,5},{5,1},{9,13},{13,9},{2,6},{6,2},{1... | collective-permute-start | bytes 393224 | tf_op jit(solution)/shard_map/ppermute | solution.py:324
  10.2 0.2 shard_map.98.refs_3_.mask_ref
  10.4 1.0 %collective-permute-done.2.refs_0_.refs_1_ = f32[32,1024]{1,0:T(8,128)S(1)} collective-permute-done((f32[32,1024]{1,0:T(8,128)}, f32[32,1024]{1,0:T(8,128)S(1)}, u32[]{:S(2)}, u32[]{:S(2)}) %collective-permute-start.2) | collective-permute-done | bytes 131104 | tf_op jit(solution)/shard_map/ppermute | solution.py:324
  11.4 0.7 %collective-permute-start.8 = (f32[32,1024]{1,0:T(8,128)S(1)}, f32[32,1024]{1,0:T(8,128)S(1)}, u32[]{:S(2)}, u32[]{:S(2)}) collective-permute-start(f32[32,1024]{1,0:T(8,128)S(1)} %collective-permute-done.2.refs_0_.refs_1_), channel_id=1, source_target_pairs={{0,4},{4,0},{8,12},{12,8},{1,5},{5,1},{9,13},{13,9},{2,6},{6,2},{1... | collective-permute-start | bytes 393224 | tf_op jit(solution)/shard_map/ppermute | solution.py:324
  12.4 0.5 %collective-permute-start.4 = (f32[40,512]{1,0:T(8,128)S(1)}, f32[40,512]{1,0:T(8,128)S(1)}, u32[]{:S(2)}, u32[]{:S(2)}) collective-permute-start(f32[40,512]{1,0:T(8,128)S(1)} %get-tuple-element.15.refs_1_), channel_id=1, source_target_pairs={{0,1},{1,0},{2,3},{3,2},{4,5},{5,4},{6,7},{7,6},{8,9},{9,8},{10,11... | collective-permute-start | bytes 245768 | tf_op jit(solution)/shard_map/ppermute | solution.py:324
  12.9 0.8 %collective-permute-done.3.refs_2_ = f32[40,512]{1,0:T(8,128)S(1)} collective-permute-done((f32[40,512]{1,0:T(8,128)S(1)}, f32[40,512]{1,0:T(8,128)S(1)}, u32[]{:S(2)}, u32[]{:S(2)}) %collective-permute-start.3) | collective-permute-done | bytes 81952 | tf_op jit(solution)/shard_map/ppermute | solution.py:324
  13.8 0.6 %shard_map.102 = (f32[16,1024]{1,0:T(8,128)S(1)}, f32[16,1024]{1,0:T(8,128)S(1)}) custom-call(f32[16,512]{1,0:T(8,128)S(1)} %get-tuple-element.13.g_ref, bf16[64,512]{1,0:T(8,128)(2,1)S(1)} %shard_map.98.refs_3_.mask_ref, f32[40,512]{1,0:T(8,128)S(1)} %get-tuple-element.14.refs_0_, f32[40,512]{1,0:T(8,128)S(1)} %get-tuple-element.15.refs_1_, ...), custom_call_target="tpu_custom_call" | custom-call | flops 134217728 | tf_op jit(solution)/shard_map/pallas_call | solution.py:192
  14.4 1.6 %collective-permute-start.5 = (f32[16,1024]{1,0:T(8,128)S(1)}, f32[16,1024]{1,0:T(8,128)S(1)}, u32[]{:S(2)}, u32[]{:S(2)}) collective-permute-start(f32[16,1024]{1,0:T(8,128)S(1)} %get-tuple-element.17), channel_id=1, source_target_pairs={{0,4},{4,8},{8,12},{12,0},{1,5},{5,9},{9,13},{13,1},{2,6},{6,10},{... | collective-permute-start | bytes 196616 | tf_op jit(solution)/shard_map/ppermute | solution.py:329
  16.1 1.7 %collective-permute-start.6 = (f32[16,1024]{1,0:T(8,128)S(1)}, f32[16,1024]{1,0:T(8,128)S(1)}, u32[]{:S(2)}, u32[]{:S(2)}) collective-permute-start(f32[16,1024]{1,0:T(8,128)S(1)} %get-tuple-element.18), channel_id=1, source_target_pairs={{0,8},{4,12},{8,0},{12,4},{1,9},{5,13},{9,1},{13,5},{2,10},{6,14},... | collective-permute-start | bytes 196616 | tf_op jit(solution)/shard_map/ppermute | solution.py:329
  17.7 0.6 %shard_map.101 = (f32[16,1024]{1,0:T(8,128)S(1)}, f32[16,1024]{1,0:T(8,128)S(1)}) custom-call(f32[16,512]{1,0:T(8,128)S(1)} %get-tuple-element.13.g_ref, bf16[64,512]{1,0:T(8,128)(2,1)S(1)} %shard_map.98.refs_3_.mask_ref, f32[40,512]{1,0:T(8,128)S(1)} %get-tuple-element.14.refs_0_, f32[40,512]{1,0:T(8,128)S(1)} %get-tuple-element.15.refs_1_, ...), custom_call_target="tpu_custom_call" | custom-call | flops 134217728 | tf_op jit(solution)/shard_map/pallas_call | solution.py:192
  18.3 2.9 %collective-permute-start.9 = (f32[16,1024]{1,0:T(8,128)S(1)}, f32[16,1024]{1,0:T(8,128)S(1)}, u32[]{:S(2)}, u32[]{:S(2)}) collective-permute-start(f32[16,1024]{1,0:T(8,128)S(1)} %shard_map.103), channel_id=1, source_target_pairs={{0,12},{4,0},{8,4},{12,8},{1,13},{5,1},{9,5},{13,9},{2,14},{6,2},{... | collective-permute-start | bytes 196616 | tf_op jit(solution)/shard_map/ppermute | solution.py:329
  21.4 0.3 %shard_map.106.early_ref = f32[32,128]{1,0:T(8,128)S(1)} custom-call(s32[1,128]{1,0:T(1,128)S(1)} %bitcast.5, bf16[256,1024]{1,0:T(8,128)(2,1)S(1)} %shard_map.105.pool_ref, f32[16,1024]{1,0:T(8,128)S(1)} %get-tuple-element.16.refs_0_, f32[16,1024]{1,0:T(8,128)S(1)} %collective-permute-done.5.refs_1_), custom_call_target="tpu_custom_call" | custom-call | tf_op jit(solution)/shard_map/pallas_call | solution.py:270
  21.7 1.8 %collective-permute-done.6.refs_2_.refs_0_ = f32[16,1024]{1,0:T(8,128)S(1)} collective-permute-done((f32[16,1024]{1,0:T(8,128)S(1)}, f32[16,1024]{1,0:T(8,128)S(1)}, u32[]{:S(2)}, u32[]{:S(2)}) %collective-permute-start.6) | collective-permute-done | bytes 65568 | tf_op jit(solution)/shard_map/ppermute | solution.py:329
  23.5 0.4 %shard_map.108 = f32[64,128]{1,0:T(8,128)S(1)} custom-call(s32[1,128]{1,0:T(1,128)S(1)} %bitcast.6, bf16[256,1024]{1,0:T(8,128)(2,1)S(1)} %shard_map.105.pool_ref, f32[32,128]{1,0:T(8,128)S(1)} %shard_map.106.early_ref, f32[16,1024]{1,0:T(8,128)S(1)} %collective-permute-done.6.refs_2_.refs_0_, f32[16,1024]{1,0:T(8,128)S(1)} %collective-permute-done.9.refs_3_.refs_1_, ...), custom_call_target="tpu_custom_call" | custom-call | tf_op jit(solution)/shard_map/pallas_call | solution.py:294
  23.9 1.2 %collective-permute-done.10 = f32[64,128]{1,0:T(8,128)S(1)} collective-permute-done((f32[64,128]{1,0:T(8,128)S(1)}, f32[64,128]{1,0:T(8,128)S(1)}, u32[]{:S(2)}, u32[]{:S(2)}) %collective-permute-start.10) | collective-permute-done | bytes 32800 | tf_op jit(solution)/shard_map/ppermute | solution.py:324
  25.1 1.3 %collective-permute-start.11 = (f32[64,128]{1,0:T(8,128)S(1)}, f32[64,128]{1,0:T(8,128)S(1)}, u32[]{:S(2)}, u32[]{:S(2)}) collective-permute-start(f32[64,128]{1,0:T(8,128)S(1)} %add.6), channel_id=1, source_target_pairs={{0,2},{1,3},{2,0},{3,1},{4,6},{5,7},{6,4},{7,5},{8,10},{9,11},{10,... | collective-permute-start | bytes 98312 | tf_op jit(solution)/shard_map/ppermute | solution.py:324
  26.4 0.7 %shard_map.104 = f32[64,1024]{1,0:T(8,128)} custom-call(f32[16,1024]{1,0:T(8,128)S(1)} %get-tuple-element.16.refs_0_, f32[16,1024]{1,0:T(8,128)S(1)} %collective-permute-done.5.refs_1_, f32[16,1024]{1,0:T(8,128)S(1)} %collective-permute-done.6.refs_2_.refs_0_, f32[16,1024]{1,0:T(8,128)S(1)} %collective-permute-done.9.refs_3_.refs_1_), custom_call_target="tpu_custom_call" | custom-call | bytes 524288 | tf_op jit(solution)/shard_map/pallas_call | solution.py:315
  27.2 1.8 %collective-permute-done.11 = f32[64,128]{1,0:T(8,128)S(1)} collective-permute-done((f32[64,128]{1,0:T(8,128)S(1)}, f32[64,128]{1,0:T(8,128)S(1)}, u32[]{:S(2)}, u32[]{:S(2)}) %collective-permute-start.11) | collective-permute-done | bytes 32800 | tf_op jit(solution)/shard_map/ppermute | solution.py:324
  29.0 0.6 %add_multiply_fusion = f32[64,128]{1,0:T(8,128)} fusion(f32[64,128]{1,0:T(8,128)S(1)} %add.6, f32[64,128]{1,0:T(8,128)S(1)} %collective-permute-done.11), kind=kLoop, calls=%fused_computation | loop fusion | flops 16384 | bytes 98304 | tf_op jit(solution)/shard_map/mul | solution.py:394
  (32 shorter events, 0.6 us)
Async XLA Ops:
  0.6 4.2 %copy-start.5 = (bf16[1024,64]{0,1:T(8,128)(2,1)S(1)}, bf16[1024,64]{0,1:T(8,128)(2,1)}, u32[]{:S(2)}) copy-start(bf16[1024,64]{0,1:T(8,128)(2,1)} %param.10) | copy-start | bytes 393220
  0.6 4.2 %copy-start.4 = (bf16[512,1024]{1,0:T(8,128)(2,1)S(1)}, bf16[512,1024]{1,0:T(8,128)(2,1)}, u32[]{:S(2)}) copy-start(bf16[512,1024]{1,0:T(8,128)(2,1)} %act_ref.1) | copy-start | bytes 3145732
  0.7 6.2 %copy-start.1 = (bf16[3584,64]{0,1:T(8,128)(2,1)S(1)}, bf16[3584,64]{0,1:T(8,128)(2,1)}, u32[]{:S(2)}) copy-start(bf16[3584,64]{0,1:T(8,128)(2,1)} %param.11) | copy-start | bytes 1376260
  0.7 6.2 %copy-start = (bf16[512,3584]{1,0:T(8,128)(2,1)S(1)}, bf16[512,3584]{1,0:T(8,128)(2,1)}, u32[]{:S(2)}) copy-start(bf16[512,3584]{1,0:T(8,128)(2,1)} %grad_ref.1) | copy-start | bytes 11010052
  0.7 10.7 %collective-permute-start.2 = (f32[32,1024]{1,0:T(8,128)}, f32[32,1024]{1,0:T(8,128)S(1)}, u32[]{:S(2)}, u32[]{:S(2)}) collective-permute-start(f32[32,1024]{1,0:T(8,128)} %refs_0_.1), channel_id=1, source_target_pairs={{0,8},{4,12},{8,0},{12,4},{1,9},{5,13},{9,1},{13,5},{2,10},{6,14},... | collective-permute-start | bytes 393224 | tf_op jit(solution)/shard_map/ppermute | solution.py:324
  4.8 3.8 %copy-start.2 = (f32[32,1024]{1,0:T(8,128)S(1)}, f32[32,1024]{1,0:T(8,128)}, u32[]{:S(2)}) copy-start(f32[32,1024]{1,0:T(8,128)} %refs_0_.1) | copy-start | bytes 393220
  4.8 5.4 %copy-start.6 = (s32[1,32]{1,0:T(1,128)S(1)}, s32[1,32]{1,0:T(1,128)}, u32[]{:S(2)}) copy-start(s32[1,32]{1,0:T(1,128)} %lengths_ref.1) | copy-start | bytes 388
  4.8 5.4 %copy-start.7 = (s32[32,1]{0,1:T(1,128)S(1)}, s32[32,1]{0,1:T(1,128)}, u32[]{:S(2)}) copy-start(s32[32,1]{0,1:T(1,128)} %param.13) | copy-start | bytes 388
  5.3 7.1 %collective-permute-start = (f32[64,512]{1,0:T(8,128)S(1)}, f32[64,512]{1,0:T(8,128)S(1)}, u32[]{:S(2)}, u32[]{:S(2)}) collective-permute-start(f32[64,512]{1,0:T(8,128)S(1)} %shard_map.97.refs_0_), channel_id=1, source_target_pairs={{0,2},{1,3},{2,0},{3,1},{4,6},{5,7},{6,4},{7,5},{8,10},{9,11},{10,... | collective-permute-start | bytes 393224 | tf_op jit(solution)/shard_map/ppermute | solution.py:324
  6.8 14.5 %copy-start.3 = (s32[128]{0:T(128)S(1)}, s32[128]{0:T(128)}, u32[]{:S(2)}) copy-start(s32[128]{0:T(128)} %param.15) | copy-start | bytes 1540
  8.0 4.3 %collective-permute-start.1 = (f32[32,512]{1,0:T(8,128)S(1)}, f32[32,512]{1,0:T(8,128)S(1)}, u32[]{:S(2)}, u32[]{:S(2)}) collective-permute-start(f32[32,512]{1,0:T(8,128)S(1)} %get-tuple-element.12), channel_id=1, source_target_pairs={{0,2},{1,3},{2,0},{3,1},{4,6},{5,7},{6,4},{7,5},{8,10},{9,11},{10,... | collective-permute-start | bytes 196616 | tf_op jit(solution)/shard_map/ppermute | solution.py:324
  8.6 9.7 %collective-permute-start.7 = (f32[32,1024]{1,0:T(8,128)S(1)}, f32[32,1024]{1,0:T(8,128)S(1)}, u32[]{:S(2)}, u32[]{:S(2)}) collective-permute-start(f32[32,1024]{1,0:T(8,128)S(1)} %copy-done.2), channel_id=1, source_target_pairs={{0,4},{4,0},{8,12},{12,8},{1,5},{5,1},{9,13},{13,9},{2,6},{6,2},{1... | collective-permute-start | bytes 393224 | tf_op jit(solution)/shard_map/ppermute | solution.py:324
  11.4 6.9 %collective-permute-start.8 = (f32[32,1024]{1,0:T(8,128)S(1)}, f32[32,1024]{1,0:T(8,128)S(1)}, u32[]{:S(2)}, u32[]{:S(2)}) collective-permute-start(f32[32,1024]{1,0:T(8,128)S(1)} %collective-permute-done.2.refs_0_.refs_1_), channel_id=1, source_target_pairs={{0,4},{4,0},{8,12},{12,8},{1,5},{5,1},{9,13},{13,9},{2,6},{6,2},{1... | collective-permute-start | bytes 393224 | tf_op jit(solution)/shard_map/ppermute | solution.py:324
  12.3 1.3 %collective-permute-start.3 = (f32[40,512]{1,0:T(8,128)S(1)}, f32[40,512]{1,0:T(8,128)S(1)}, u32[]{:S(2)}, u32[]{:S(2)}) collective-permute-start(f32[40,512]{1,0:T(8,128)S(1)} %get-tuple-element.14.refs_0_), channel_id=1, source_target_pairs={{0,1},{1,0},{2,3},{3,2},{4,5},{5,4},{6,7},{7,6},{8,9},{9,8},{10,11... | collective-permute-start | bytes 245768 | tf_op jit(solution)/shard_map/ppermute | solution.py:324
  12.4 1.4 %collective-permute-start.4 = (f32[40,512]{1,0:T(8,128)S(1)}, f32[40,512]{1,0:T(8,128)S(1)}, u32[]{:S(2)}, u32[]{:S(2)}) collective-permute-start(f32[40,512]{1,0:T(8,128)S(1)} %get-tuple-element.15.refs_1_), channel_id=1, source_target_pairs={{0,1},{1,0},{2,3},{3,2},{4,5},{5,4},{6,7},{7,6},{8,9},{9,8},{10,11... | collective-permute-start | bytes 245768 | tf_op jit(solution)/shard_map/ppermute | solution.py:324
  14.4 6.9 %collective-permute-start.5 = (f32[16,1024]{1,0:T(8,128)S(1)}, f32[16,1024]{1,0:T(8,128)S(1)}, u32[]{:S(2)}, u32[]{:S(2)}) collective-permute-start(f32[16,1024]{1,0:T(8,128)S(1)} %get-tuple-element.17), channel_id=1, source_target_pairs={{0,4},{4,8},{8,12},{12,0},{1,5},{5,9},{9,13},{13,1},{2,6},{6,10},{... | collective-permute-start | bytes 196616 | tf_op jit(solution)/shard_map/ppermute | solution.py:329
  16.1 7.5 %collective-permute-start.6 = (f32[16,1024]{1,0:T(8,128)S(1)}, f32[16,1024]{1,0:T(8,128)S(1)}, u32[]{:S(2)}, u32[]{:S(2)}) collective-permute-start(f32[16,1024]{1,0:T(8,128)S(1)} %get-tuple-element.18), channel_id=1, source_target_pairs={{0,8},{4,12},{8,0},{12,4},{1,9},{5,13},{9,1},{13,5},{2,10},{6,14},... | collective-permute-start | bytes 196616 | tf_op jit(solution)/shard_map/ppermute | solution.py:329
  18.3 5.2 %collective-permute-start.9 = (f32[16,1024]{1,0:T(8,128)S(1)}, f32[16,1024]{1,0:T(8,128)S(1)}, u32[]{:S(2)}, u32[]{:S(2)}) collective-permute-start(f32[16,1024]{1,0:T(8,128)S(1)} %shard_map.103), channel_id=1, source_target_pairs={{0,12},{4,0},{8,4},{12,8},{1,13},{5,1},{9,5},{13,9},{2,14},{6,2},{... | collective-permute-start | bytes 196616 | tf_op jit(solution)/shard_map/ppermute | solution.py:329
  23.9 1.2 %collective-permute-start.10 = (f32[64,128]{1,0:T(8,128)S(1)}, f32[64,128]{1,0:T(8,128)S(1)}, u32[]{:S(2)}, u32[]{:S(2)}) collective-permute-start(f32[64,128]{1,0:T(8,128)S(1)} %shard_map.108), channel_id=1, source_target_pairs={{0,1},{1,0},{2,3},{3,2},{4,5},{5,4},{6,7},{7,6},{8,9},{9,8},{10,11... | collective-permute-start | bytes 98312 | tf_op jit(solution)/shard_map/ppermute | solution.py:324
  25.1 3.9 %collective-permute-start.11 = (f32[64,128]{1,0:T(8,128)S(1)}, f32[64,128]{1,0:T(8,128)S(1)}, u32[]{:S(2)}, u32[]{:S(2)}) collective-permute-start(f32[64,128]{1,0:T(8,128)S(1)} %add.6), channel_id=1, source_target_pairs={{0,2},{1,3},{2,0},{3,1},{4,6},{5,7},{6,4},{7,5},{8,10},{9,11},{10,... | collective-permute-start | bytes 98312 | tf_op jit(solution)/shard_map/ppermute | solution.py:324

commit v19 on v18

--- a/solution.py
+++ b/solution.py
@@ -160,7 +160,14 @@
     rank = got.shape[0] - width
     x_full = own[:rank] + got[:rank]
     g_full = g_ref[...] + got[rank:]
-    x_both = jnp.concatenate(halves(x_full), axis=0)
+    x_high, x_low = halves(x_full)
+    x_both = jnp.concatenate(
+        [
+            jnp.concatenate([x_high, x_high], axis=1),
+            jnp.concatenate([x_low, jnp.zeros_like(x_low)], axis=1),
+        ],
+        axis=0,
+    )
     g_high = g_full.astype(BF16).astype(F32)
     g_low = g_full - g_high
     cap = blocks[0].shape[0]
@@ -174,13 +181,15 @@
 
     group = min(width, GROUP)
     for i in range(0, width, group):
-        rows = [m for j in range(i, i + group) for g in (g_high, g_low) for m in masked(g[j : j + 1])]
-        both = mm(jnp.concatenate(rows, axis=0), x_both, NT)
+        rows = [
+            jnp.concatenate([m for j in range(i, i + group) for m in masked(g[j : j + 1])], axis=0)
+            for g in (g_high, g_low)
+        ]
+        both = mm(jnp.concatenate(rows, axis=1), x_both, NT)
         columns = []
         for j in range(group):
-            high = both[2 * j * slots : (2 * j + 1) * slots]
-            low = both[(2 * j + 1) * slots : (2 * j + 2) * slots]
-            columns.append(high[:, :rank] + high[:, rank:] + low[:, :rank])
+            part = both[j * slots : (j + 1) * slots]
+            columns.append(part[:, :rank] + part[:, rank:])
         out = jnp.concatenate(columns, axis=1)
         for k, block in enumerate(blocks):
             block[:, i * rank : (i + group) * rank] = out[k * cap : (k + 1) * cap, :]

time: 29.8 us -> 29.8 us (level)
  no operation moved by 1% of the time
where the time goes in v19:
time: 29.8 us; the launch traced here: 29.6 us
  starting transfers between devices  16.7 us (56%)
  waiting for transfers between devices  6.97 us (23%)
  Pallas kernels  4.51 us (15%)
  between operations  0.78 us (3%)
  other arithmetic  0.63 us (2%)
    ppermute x9, starting transfers between devices, swap(): lax.ppermute(x, axis, [(i, i ^ gap) for i in range(lax.axis_size(axis))])  10.5 us
    ppermute x3, starting transfers between devices, shift(): return lax.ppermute(x, axis, [(i, (i + by) % size) for i in range(size)])  6.23 us
    ppermute x9, waiting for transfers between devices, swap(): lax.ppermute(x, axis, [(i, i ^ gap) for i in range(lax.axis_size(axis))])  5.16 us
    ppermute x3, waiting for transfers between devices, shift(): return lax.ppermute(x, axis, [(i, (i + by) % size) for i in range(size)])  1.8 us
    pallas_call x1, Pallas kernels, project_g(): pl.pallas_call(functools.partial(g_kernel, width), out_shape=[part, part]...  1.16 us
    pallas_call x2, Pallas kernels, outer(): pl.pallas_call(functools.partial(outer_kernel, first, owners, len(sent)),...  1.15 us
    pallas_call x1, Pallas kernels, place(): pl.pallas_call(place_kernel, out_shape=jax.ShapeDtypeStruct((slots, feats...  0.72 us
    mul x1, other arithmetic, local(): return (store, scores * (1.0 / (rank * rank)))  0.62 us
  transfers between devices with their start and end apart: 12, of which 7 were waited for; matrix products, arithmetic and copies ran while one was open for 0% of the time, Pallas kernels for 14%

profile of v19, /device:TPU:0, one launch (start us, length us, event | category | flops | bytes accessed | tf_op | source)
XLA Modules:
  0.0 29.6 jit_solution(15257229313145344740)
XLA Ops:
  0.7 4.1 %collective-permute-start.2 = (f32[32,1024]{1,0:T(8,128)}, f32[32,1024]{1,0:T(8,128)S(1)}, u32[]{:S(2)}, u32[]{:S(2)}) collective-permute-start(f32[32,1024]{1,0:T(8,128)} %refs_0_.1), channel_id=1, source_target_pairs={{0,8},{4,12},{8,0},{12,4},{1,9},{5,13},{9,1},{13,5},{2,10},{6,14},... | collective-permute-start | bytes 393224 | tf_op jit(solution)/shard_map/ppermute | solution.py:333
  4.8 0.5 %shard_map.97.refs_0_ = f32[64,512]{1,0:T(8,128)S(1)} custom-call(bf16[512,1024]{1,0:T(8,128)(2,1)S(1)} %copy-done.4, bf16[64,1024]{1,0:T(8,128)(2,1)S(1)} %bitcast.7, f32[8,128]{1,0:T(8,128)S(1)} %shard_map.96.refs_0_), custom_call_target="tpu_custom_call" | custom-call | flops 600000000 | tf_op jit(solution)/shard_map/pallas_call | solution.py:90
  5.3 1.5 %collective-permute-start = (f32[64,512]{1,0:T(8,128)S(1)}, f32[64,512]{1,0:T(8,128)S(1)}, u32[]{:S(2)}, u32[]{:S(2)}) collective-permute-start(f32[64,512]{1,0:T(8,128)S(1)} %shard_map.97.refs_0_), channel_id=1, source_target_pairs={{0,2},{1,3},{2,0},{3,1},{4,6},{5,7},{6,4},{7,5},{8,10},{9,11},{10,... | collective-permute-start | bytes 393224 | tf_op jit(solution)/shard_map/ppermute | solution.py:333
  6.8 1.2 %shard_map.95 = (f32[32,512]{1,0:T(8,128)S(1)}, f32[32,512]{1,0:T(8,128)S(1)}) custom-call(bf16[512,3584]{1,0:T(8,128)(2,1)S(1)} %copy-done, bf16[64,3584]{1,0:T(8,128)(2,1)S(1)} %bitcast.4), custom_call_target="tpu_custom_call" | custom-call | tf_op jit(solution)/shard_map/pallas_call | solution.py:113
  8.0 0.6 %collective-permute-start.1 = (f32[32,512]{1,0:T(8,128)S(1)}, f32[32,512]{1,0:T(8,128)S(1)}, u32[]{:S(2)}, u32[]{:S(2)}) collective-permute-start(f32[32,512]{1,0:T(8,128)S(1)} %get-tuple-element.12), channel_id=1, source_target_pairs={{0,2},{1,3},{2,0},{3,1},{4,6},{5,7},{6,4},{7,5},{8,10},{9,11},{10,... | collective-permute-start | bytes 196616 | tf_op jit(solution)/shard_map/ppermute | solution.py:333
  8.6 1.6 %collective-permute-start.7 = (f32[32,1024]{1,0:T(8,128)S(1)}, f32[32,1024]{1,0:T(8,128)S(1)}, u32[]{:S(2)}, u32[]{:S(2)}) collective-permute-start(f32[32,1024]{1,0:T(8,128)S(1)} %copy-done.2), channel_id=1, source_target_pairs={{0,4},{4,0},{8,12},{12,8},{1,5},{5,1},{9,13},{13,9},{2,6},{6,2},{1... | collective-permute-start | bytes 393224 | tf_op jit(solution)/shard_map/ppermute | solution.py:333
  10.2 0.2 shard_map.98.refs_3_.mask_ref
  10.4 1.0 %collective-permute-done.2.refs_0_.refs_1_ = f32[32,1024]{1,0:T(8,128)S(1)} collective-permute-done((f32[32,1024]{1,0:T(8,128)}, f32[32,1024]{1,0:T(8,128)S(1)}, u32[]{:S(2)}, u32[]{:S(2)}) %collective-permute-start.2) | collective-permute-done | bytes 131104 | tf_op jit(solution)/shard_map/ppermute | solution.py:333
  11.4 0.7 %collective-permute-start.8 = (f32[32,1024]{1,0:T(8,128)S(1)}, f32[32,1024]{1,0:T(8,128)S(1)}, u32[]{:S(2)}, u32[]{:S(2)}) collective-permute-start(f32[32,1024]{1,0:T(8,128)S(1)} %collective-permute-done.2.refs_0_.refs_1_), channel_id=1, source_target_pairs={{0,4},{4,0},{8,12},{12,8},{1,5},{5,1},{9,13},{13,9},{2,6},{6,2},{1... | collective-permute-start | bytes 393224 | tf_op jit(solution)/shard_map/ppermute | solution.py:333
  12.4 0.5 %collective-permute-start.4 = (f32[40,512]{1,0:T(8,128)S(1)}, f32[40,512]{1,0:T(8,128)S(1)}, u32[]{:S(2)}, u32[]{:S(2)}) collective-permute-start(f32[40,512]{1,0:T(8,128)S(1)} %get-tuple-element.15.refs_1_), channel_id=1, source_target_pairs={{0,1},{1,0},{2,3},{3,2},{4,5},{5,4},{6,7},{7,6},{8,9},{9,8},{10,11... | collective-permute-start | bytes 245768 | tf_op jit(solution)/shard_map/ppermute | solution.py:333
  12.9 0.8 %collective-permute-done.3.refs_2_ = f32[40,512]{1,0:T(8,128)S(1)} collective-permute-done((f32[40,512]{1,0:T(8,128)S(1)}, f32[40,512]{1,0:T(8,128)S(1)}, u32[]{:S(2)}, u32[]{:S(2)}) %collective-permute-start.3) | collective-permute-done | bytes 81952 | tf_op jit(solution)/shard_map/ppermute | solution.py:333
  13.8 0.6 %shard_map.102 = (f32[16,1024]{1,0:T(8,128)S(1)}, f32[16,1024]{1,0:T(8,128)S(1)}) custom-call(f32[16,512]{1,0:T(8,128)S(1)} %get-tuple-element.13.g_ref, bf16[64,512]{1,0:T(8,128)(2,1)S(1)} %shard_map.98.refs_3_.mask_ref, f32[40,512]{1,0:T(8,128)S(1)} %get-tuple-element.14.refs_0_, f32[40,512]{1,0:T(8,128)S(1)} %get-tuple-element.15.refs_1_, ...), custom_call_target="tpu_custom_call" | custom-call | flops 134217728 | tf_op jit(solution)/shard_map/pallas_call | solution.py:201
  14.4 1.6 %collective-permute-start.5 = (f32[16,1024]{1,0:T(8,128)S(1)}, f32[16,1024]{1,0:T(8,128)S(1)}, u32[]{:S(2)}, u32[]{:S(2)}) collective-permute-start(f32[16,1024]{1,0:T(8,128)S(1)} %get-tuple-element.17), channel_id=1, source_target_pairs={{0,4},{4,8},{8,12},{12,0},{1,5},{5,9},{9,13},{13,1},{2,6},{6,10},{... | collective-permute-start | bytes 196616 | tf_op jit(solution)/shard_map/ppermute | solution.py:338
  16.1 1.7 %collective-permute-start.6 = (f32[16,1024]{1,0:T(8,128)S(1)}, f32[16,1024]{1,0:T(8,128)S(1)}, u32[]{:S(2)}, u32[]{:S(2)}) collective-permute-start(f32[16,1024]{1,0:T(8,128)S(1)} %get-tuple-element.18), channel_id=1, source_target_pairs={{0,8},{4,12},{8,0},{12,4},{1,9},{5,13},{9,1},{13,5},{2,10},{6,14},... | collective-permute-start | bytes 196616 | tf_op jit(solution)/shard_map/ppermute | solution.py:338
  17.7 0.6 %shard_map.101 = (f32[16,1024]{1,0:T(8,128)S(1)}, f32[16,1024]{1,0:T(8,128)S(1)}) custom-call(f32[16,512]{1,0:T(8,128)S(1)} %get-tuple-element.13.g_ref, bf16[64,512]{1,0:T(8,128)(2,1)S(1)} %shard_map.98.refs_3_.mask_ref, f32[40,512]{1,0:T(8,128)S(1)} %get-tuple-element.14.refs_0_, f32[40,512]{1,0:T(8,128)S(1)} %get-tuple-element.15.refs_1_, ...), custom_call_target="tpu_custom_call" | custom-call | flops 134217728 | tf_op jit(solution)/shard_map/pallas_call | solution.py:201
  18.4 2.9 %collective-permute-start.9 = (f32[16,1024]{1,0:T(8,128)S(1)}, f32[16,1024]{1,0:T(8,128)S(1)}, u32[]{:S(2)}, u32[]{:S(2)}) collective-permute-start(f32[16,1024]{1,0:T(8,128)S(1)} %shard_map.103), channel_id=1, source_target_pairs={{0,12},{4,0},{8,4},{12,8},{1,13},{5,1},{9,5},{13,9},{2,14},{6,2},{... | collective-permute-start | bytes 196616 | tf_op jit(solution)/shard_map/ppermute | solution.py:338
  21.4 0.3 %shard_map.106.early_ref = f32[32,128]{1,0:T(8,128)S(1)} custom-call(s32[1,128]{1,0:T(1,128)S(1)} %bitcast.5, bf16[256,1024]{1,0:T(8,128)(2,1)S(1)} %shard_map.105.pool_ref, f32[16,1024]{1,0:T(8,128)S(1)} %get-tuple-element.16.refs_0_, f32[16,1024]{1,0:T(8,128)S(1)} %collective-permute-done.5.refs_1_), custom_call_target="tpu_custom_call" | custom-call | tf_op jit(solution)/shard_map/pallas_call | solution.py:279
  21.7 1.8 %collective-permute-done.6.refs_2_.refs_0_ = f32[16,1024]{1,0:T(8,128)S(1)} collective-permute-done((f32[16,1024]{1,0:T(8,128)S(1)}, f32[16,1024]{1,0:T(8,128)S(1)}, u32[]{:S(2)}, u32[]{:S(2)}) %collective-permute-start.6) | collective-permute-done | bytes 65568 | tf_op jit(solution)/shard_map/ppermute | solution.py:338
  23.5 0.3 %shard_map.108 = f32[64,128]{1,0:T(8,128)S(1)} custom-call(s32[1,128]{1,0:T(1,128)S(1)} %bitcast.6, bf16[256,1024]{1,0:T(8,128)(2,1)S(1)} %shard_map.105.pool_ref, f32[32,128]{1,0:T(8,128)S(1)} %shard_map.106.early_ref, f32[16,1024]{1,0:T(8,128)S(1)} %collective-permute-done.6.refs_2_.refs_0_, f32[16,1024]{1,0:T(8,128)S(1)} %collective-permute-done.9.refs_3_.refs_1_, ...), custom_call_target="tpu_custom_call" | custom-call | tf_op jit(solution)/shard_map/pallas_call | solution.py:303
  23.9 1.2 %collective-permute-done.10 = f32[64,128]{1,0:T(8,128)S(1)} collective-permute-done((f32[64,128]{1,0:T(8,128)S(1)}, f32[64,128]{1,0:T(8,128)S(1)}, u32[]{:S(2)}, u32[]{:S(2)}) %collective-permute-start.10) | collective-permute-done | bytes 32800 | tf_op jit(solution)/shard_map/ppermute | solution.py:333
  25.1 1.3 %collective-permute-start.11 = (f32[64,128]{1,0:T(8,128)S(1)}, f32[64,128]{1,0:T(8,128)S(1)}, u32[]{:S(2)}, u32[]{:S(2)}) collective-permute-start(f32[64,128]{1,0:T(8,128)S(1)} %add.6), channel_id=1, source_target_pairs={{0,2},{1,3},{2,0},{3,1},{4,6},{5,7},{6,4},{7,5},{8,10},{9,11},{10,... | collective-permute-start | bytes 98312 | tf_op jit(solution)/shard_map/ppermute | solution.py:333
  26.4 0.7 %shard_map.104 = f32[64,1024]{1,0:T(8,128)} custom-call(f32[16,1024]{1,0:T(8,128)S(1)} %get-tuple-element.16.refs_0_, f32[16,1024]{1,0:T(8,128)S(1)} %collective-permute-done.5.refs_1_, f32[16,1024]{1,0:T(8,128)S(1)} %collective-permute-done.6.refs_2_.refs_0_, f32[16,1024]{1,0:T(8,128)S(1)} %collective-permute-done.9.refs_3_.refs_1_), custom_call_target="tpu_custom_call" | custom-call | bytes 524288 | tf_op jit(solution)/shard_map/pallas_call | solution.py:324
  27.2 1.8 %collective-permute-done.11 = f32[64,128]{1,0:T(8,128)S(1)} collective-permute-done((f32[64,128]{1,0:T(8,128)S(1)}, f32[64,128]{1,0:T(8,128)S(1)}, u32[]{:S(2)}, u32[]{:S(2)}) %collective-permute-start.11) | collective-permute-done | bytes 32800 | tf_op jit(solution)/shard_map/ppermute | solution.py:333
  29.0 0.6 %add_multiply_fusion = f32[64,128]{1,0:T(8,128)} fusion(f32[64,128]{1,0:T(8,128)S(1)} %add.6, f32[64,128]{1,0:T(8,128)S(1)} %collective-permute-done.11), kind=kLoop, calls=%fused_computation | loop fusion | flops 16384 | bytes 98304 | tf_op jit(solution)/shard_map/mul | solution.py:403
  (32 shorter events, 0.6 us)
Async XLA Ops:
  0.6 4.2 %copy-start.5 = (bf16[1024,64]{0,1:T(8,128)(2,1)S(1)}, bf16[1024,64]{0,1:T(8,128)(2,1)}, u32[]{:S(2)}) copy-start(bf16[1024,64]{0,1:T(8,128)(2,1)} %param.10) | copy-start | bytes 393220
  0.6 4.2 %copy-start.4 = (bf16[512,1024]{1,0:T(8,128)(2,1)S(1)}, bf16[512,1024]{1,0:T(8,128)(2,1)}, u32[]{:S(2)}) copy-start(bf16[512,1024]{1,0:T(8,128)(2,1)} %act_ref.1) | copy-start | bytes 3145732
  0.7 6.2 %copy-start.1 = (bf16[3584,64]{0,1:T(8,128)(2,1)S(1)}, bf16[3584,64]{0,1:T(8,128)(2,1)}, u32[]{:S(2)}) copy-start(bf16[3584,64]{0,1:T(8,128)(2,1)} %param.11) | copy-start | bytes 1376260
  0.7 6.2 %copy-start = (bf16[512,3584]{1,0:T(8,128)(2,1)S(1)}, bf16[512,3584]{1,0:T(8,128)(2,1)}, u32[]{:S(2)}) copy-start(bf16[512,3584]{1,0:T(8,128)(2,1)} %grad_ref.1) | copy-start | bytes 11010052
  0.7 10.7 %collective-permute-start.2 = (f32[32,1024]{1,0:T(8,128)}, f32[32,1024]{1,0:T(8,128)S(1)}, u32[]{:S(2)}, u32[]{:S(2)}) collective-permute-start(f32[32,1024]{1,0:T(8,128)} %refs_0_.1), channel_id=1, source_target_pairs={{0,8},{4,12},{8,0},{12,4},{1,9},{5,13},{9,1},{13,5},{2,10},{6,14},... | collective-permute-start | bytes 393224 | tf_op jit(solution)/shard_map/ppermute | solution.py:333
  4.8 3.8 %copy-start.2 = (f32[32,1024]{1,0:T(8,128)S(1)}, f32[32,1024]{1,0:T(8,128)}, u32[]{:S(2)}) copy-start(f32[32,1024]{1,0:T(8,128)} %refs_0_.1) | copy-start | bytes 393220
  4.8 5.4 %copy-start.6 = (s32[1,32]{1,0:T(1,128)S(1)}, s32[1,32]{1,0:T(1,128)}, u32[]{:S(2)}) copy-start(s32[1,32]{1,0:T(1,128)} %lengths_ref.1) | copy-start | bytes 388
  4.8 5.4 %copy-start.7 = (s32[32,1]{0,1:T(1,128)S(1)}, s32[32,1]{0,1:T(1,128)}, u32[]{:S(2)}) copy-start(s32[32,1]{0,1:T(1,128)} %param.13) | copy-start | bytes 388
  5.3 7.1 %collective-permute-start = (f32[64,512]{1,0:T(8,128)S(1)}, f32[64,512]{1,0:T(8,128)S(1)}, u32[]{:S(2)}, u32[]{:S(2)}) collective-permute-start(f32[64,512]{1,0:T(8,128)S(1)} %shard_map.97.refs_0_), channel_id=1, source_target_pairs={{0,2},{1,3},{2,0},{3,1},{4,6},{5,7},{6,4},{7,5},{8,10},{9,11},{10,... | collective-permute-start | bytes 393224 | tf_op jit(solution)/shard_map/ppermute | solution.py:333
  6.8 14.6 %copy-start.3 = (s32[128]{0:T(128)S(1)}, s32[128]{0:T(128)}, u32[]{:S(2)}) copy-start(s32[128]{0:T(128)} %param.15) | copy-start | bytes 1540
  8.0 4.3 %collective-permute-start.1 = (f32[32,512]{1,0:T(8,128)S(1)}, f32[32,512]{1,0:T(8,128)S(1)}, u32[]{:S(2)}, u32[]{:S(2)}) collective-permute-start(f32[32,512]{1,0:T(8,128)S(1)} %get-tuple-element.12), channel_id=1, source_target_pairs={{0,2},{1,3},{2,0},{3,1},{4,6},{5,7},{6,4},{7,5},{8,10},{9,11},{10,... | collective-permute-start | bytes 196616 | tf_op jit(solution)/shard_map/ppermute | solution.py:333
  8.6 9.7 %collective-permute-start.7 = (f32[32,1024]{1,0:T(8,128)S(1)}, f32[32,1024]{1,0:T(8,128)S(1)}, u32[]{:S(2)}, u32[]{:S(2)}) collective-permute-start(f32[32,1024]{1,0:T(8,128)S(1)} %copy-done.2), channel_id=1, source_target_pairs={{0,4},{4,0},{8,12},{12,8},{1,5},{5,1},{9,13},{13,9},{2,6},{6,2},{1... | collective-permute-start | bytes 393224 | tf_op jit(solution)/shard_map/ppermute | solution.py:333
  11.4 6.9 %collective-permute-start.8 = (f32[32,1024]{1,0:T(8,128)S(1)}, f32[32,1024]{1,0:T(8,128)S(1)}, u32[]{:S(2)}, u32[]{:S(2)}) collective-permute-start(f32[32,1024]{1,0:T(8,128)S(1)} %collective-permute-done.2.refs_0_.refs_1_), channel_id=1, source_target_pairs={{0,4},{4,0},{8,12},{12,8},{1,5},{5,1},{9,13},{13,9},{2,6},{6,2},{1... | collective-permute-start | bytes 393224 | tf_op jit(solution)/shard_map/ppermute | solution.py:333
  12.3 1.3 %collective-permute-start.3 = (f32[40,512]{1,0:T(8,128)S(1)}, f32[40,512]{1,0:T(8,128)S(1)}, u32[]{:S(2)}, u32[]{:S(2)}) collective-permute-start(f32[40,512]{1,0:T(8,128)S(1)} %get-tuple-element.14.refs_0_), channel_id=1, source_target_pairs={{0,1},{1,0},{2,3},{3,2},{4,5},{5,4},{6,7},{7,6},{8,9},{9,8},{10,11... | collective-permute-start | bytes 245768 | tf_op jit(solution)/shard_map/ppermute | solution.py:333
  12.4 1.4 %collective-permute-start.4 = (f32[40,512]{1,0:T(8,128)S(1)}, f32[40,512]{1,0:T(8,128)S(1)}, u32[]{:S(2)}, u32[]{:S(2)}) collective-permute-start(f32[40,512]{1,0:T(8,128)S(1)} %get-tuple-element.15.refs_1_), channel_id=1, source_target_pairs={{0,1},{1,0},{2,3},{3,2},{4,5},{5,4},{6,7},{7,6},{8,9},{9,8},{10,11... | collective-permute-start | bytes 245768 | tf_op jit(solution)/shard_map/ppermute | solution.py:333
  14.4 6.9 %collective-permute-start.5 = (f32[16,1024]{1,0:T(8,128)S(1)}, f32[16,1024]{1,0:T(8,128)S(1)}, u32[]{:S(2)}, u32[]{:S(2)}) collective-permute-start(f32[16,1024]{1,0:T(8,128)S(1)} %get-tuple-element.17), channel_id=1, source_target_pairs={{0,4},{4,8},{8,12},{12,0},{1,5},{5,9},{9,13},{13,1},{2,6},{6,10},{... | collective-permute-start | bytes 196616 | tf_op jit(solution)/shard_map/ppermute | solution.py:338
  16.1 7.5 %collective-permute-start.6 = (f32[16,1024]{1,0:T(8,128)S(1)}, f32[16,1024]{1,0:T(8,128)S(1)}, u32[]{:S(2)}, u32[]{:S(2)}) collective-permute-start(f32[16,1024]{1,0:T(8,128)S(1)} %get-tuple-element.18), channel_id=1, source_target_pairs={{0,8},{4,12},{8,0},{12,4},{1,9},{5,13},{9,1},{13,5},{2,10},{6,14},... | collective-permute-start | bytes 196616 | tf_op jit(solution)/shard_map/ppermute | solution.py:338
  18.4 5.2 %collective-permute-start.9 = (f32[16,1024]{1,0:T(8,128)S(1)}, f32[16,1024]{1,0:T(8,128)S(1)}, u32[]{:S(2)}, u32[]{:S(2)}) collective-permute-start(f32[16,1024]{1,0:T(8,128)S(1)} %shard_map.103), channel_id=1, source_target_pairs={{0,12},{4,0},{8,4},{12,8},{1,13},{5,1},{9,5},{13,9},{2,14},{6,2},{... | collective-permute-start | bytes 196616 | tf_op jit(solution)/shard_map/ppermute | solution.py:338
  23.9 1.2 %collective-permute-start.10 = (f32[64,128]{1,0:T(8,128)S(1)}, f32[64,128]{1,0:T(8,128)S(1)}, u32[]{:S(2)}, u32[]{:S(2)}) collective-permute-start(f32[64,128]{1,0:T(8,128)S(1)} %shard_map.108), channel_id=1, source_target_pairs={{0,1},{1,0},{2,3},{3,2},{4,5},{5,4},{6,7},{7,6},{8,9},{9,8},{10,11... | collective-permute-start | bytes 98312 | tf_op jit(solution)/shard_map/ppermute | solution.py:333
  25.1 3.9 %collective-permute-start.11 = (f32[64,128]{1,0:T(8,128)S(1)}, f32[64,128]{1,0:T(8,128)S(1)}, u32[]{:S(2)}, u32[]{:S(2)}) collective-permute-start(f32[64,128]{1,0:T(8,128)S(1)} %add.6), channel_id=1, source_target_pairs={{0,2},{1,3},{2,0},{3,1},{4,6},{5,7},{6,4},{7,5},{8,10},{9,11},{10,... | collective-permute-start | bytes 98312 | tf_op jit(solution)/shard_map/ppermute | solution.py:333

commit v20 on v19

--- a/solution.py
+++ b/solution.py
@@ -12,7 +12,7 @@
 MIB = 1024 * 1024
 NT = (((1,), (1,)), ((), ()))
 MOST_DIRECT = 8
-GROUP = 8
+GROUP = 16
 ROWS = 16
 LANES = 128
 FIRST_FLOPS = 10 * 10**8
@@ -380,7 +380,7 @@
     ids_row = query_ids[None, :]
     if direct:
         split = max(1, data_size // 2)
-        soon = outer(own, gots, keep, mask, cap, 0, split)
+        soon = [outer(own, gots, keep, mask, cap, k, 1)[0] for k in range(split)]
         rows = [shift(block, "dp", k) for k, block in enumerate(soon, 1)]
         *sent, kept = outer(own, gots, keep, mask, cap, split, data_size - split)
         sent[-1] = after(sent[-1], [mate, *passed])

time: 29.8 us -> 29.7 us (level)
  waiting for transfers between devices: 6.97 us -> 6.46 us
    ppermute x3, waiting for transfers between devices: 1.8 us -> 1.45 us  [shift(): return lax.ppermute(x, axis, [(i, (i + by) % size) for i in range(size)])]
    pallas_call x2 -> x3, Pallas kernels: 1.15 us -> 1.43 us  [outer(): pl.pallas_call(functools.partial(outer_kernel, first, owners, len(sent)),...]
  transfers between devices with their start and end apart: 12 -> 12, of which waited for: 7 -> 8; matrix products, arithmetic and copies ran while one was open for 0% -> 0% of each run, Pallas kernels for 14% -> 15%
where the time goes in v20:
time: 29.7 us; the launch traced here: 29.6 us
  starting transfers between devices  16.9 us (57%)
  waiting for transfers between devices  6.46 us (22%)
  Pallas kernels  4.8 us (16%)
  between operations  0.77 us (3%)
  other arithmetic  0.63 us (2%)
    ppermute x9, starting transfers between devices, swap(): lax.ppermute(x, axis, [(i, i ^ gap) for i in range(lax.axis_size(axis))])  10.6 us
    ppermute x3, starting transfers between devices, shift(): return lax.ppermute(x, axis, [(i, (i + by) % size) for i in range(size)])  6.27 us
    ppermute x9, waiting for transfers between devices, swap(): lax.ppermute(x, axis, [(i, i ^ gap) for i in range(lax.axis_size(axis))])  5.01 us
    ppermute x3, waiting for transfers between devices, shift(): return lax.ppermute(x, axis, [(i, (i + by) % size) for i in range(size)])  1.45 us
    pallas_call x3, Pallas kernels, outer(): pl.pallas_call(functools.partial(outer_kernel, first, owners, len(sent)),...  1.43 us
    pallas_call x1, Pallas kernels, project_g(): pl.pallas_call(functools.partial(g_kernel, width), out_shape=[part, part]...  1.16 us
    pallas_call x1, Pallas kernels, place(): pl.pallas_call(place_kernel, out_shape=jax.ShapeDtypeStruct((slots, feats...  0.72 us
    mul x1, other arithmetic, local(): return (store, scores * (1.0 / (rank * rank)))  0.62 us
  transfers between devices with their start and end apart: 12, of which 8 were waited for; matrix products, arithmetic and copies ran while one was open for 0% of the time, Pallas kernels for 15%

profile of v20, /device:TPU:0, one launch (start us, length us, event | category | flops | bytes accessed | tf_op | source)
XLA Modules:
  0.0 29.6 jit_solution(12137251789161591626)
XLA Ops:
  0.7 4.1 %collective-permute-start.2 = (f32[32,1024]{1,0:T(8,128)}, f32[32,1024]{1,0:T(8,128)S(1)}, u32[]{:S(2)}, u32[]{:S(2)}) collective-permute-start(f32[32,1024]{1,0:T(8,128)} %refs_0_.1), channel_id=1, source_target_pairs={{0,8},{4,12},{8,0},{12,4},{1,9},{5,13},{9,1},{13,5},{2,10},{6,14},... | collective-permute-start | bytes 393224 | tf_op jit(solution)/shard_map/ppermute | solution.py:333
  4.8 0.5 %shard_map.97.refs_0_ = f32[64,512]{1,0:T(8,128)S(1)} custom-call(bf16[512,1024]{1,0:T(8,128)(2,1)S(1)} %copy-done.4, bf16[64,1024]{1,0:T(8,128)(2,1)S(1)} %bitcast.7, f32[8,128]{1,0:T(8,128)S(1)} %shard_map.96.refs_0_), custom_call_target="tpu_custom_call" | custom-call | flops 600000000 | tf_op jit(solution)/shard_map/pallas_call | solution.py:90
  5.3 1.5 %collective-permute-start = (f32[64,512]{1,0:T(8,128)S(1)}, f32[64,512]{1,0:T(8,128)S(1)}, u32[]{:S(2)}, u32[]{:S(2)}) collective-permute-start(f32[64,512]{1,0:T(8,128)S(1)} %shard_map.97.refs_0_), channel_id=1, source_target_pairs={{0,2},{1,3},{2,0},{3,1},{4,6},{5,7},{6,4},{7,5},{8,10},{9,11},{10,... | collective-permute-start | bytes 393224 | tf_op jit(solution)/shard_map/ppermute | solution.py:333
  6.8 1.2 %shard_map.95 = (f32[32,512]{1,0:T(8,128)S(1)}, f32[32,512]{1,0:T(8,128)S(1)}) custom-call(bf16[512,3584]{1,0:T(8,128)(2,1)S(1)} %copy-done, bf16[64,3584]{1,0:T(8,128)(2,1)S(1)} %bitcast.4), custom_call_target="tpu_custom_call" | custom-call | tf_op jit(solution)/shard_map/pallas_call | solution.py:113
  8.0 0.6 %collective-permute-start.1 = (f32[32,512]{1,0:T(8,128)S(1)}, f32[32,512]{1,0:T(8,128)S(1)}, u32[]{:S(2)}, u32[]{:S(2)}) collective-permute-start(f32[32,512]{1,0:T(8,128)S(1)} %get-tuple-element.10), channel_id=1, source_target_pairs={{0,2},{1,3},{2,0},{3,1},{4,6},{5,7},{6,4},{7,5},{8,10},{9,11},{10,... | collective-permute-start | bytes 196616 | tf_op jit(solution)/shard_map/ppermute | solution.py:333
  8.6 1.6 %collective-permute-start.7 = (f32[32,1024]{1,0:T(8,128)S(1)}, f32[32,1024]{1,0:T(8,128)S(1)}, u32[]{:S(2)}, u32[]{:S(2)}) collective-permute-start(f32[32,1024]{1,0:T(8,128)S(1)} %copy-done.2), channel_id=1, source_target_pairs={{0,4},{4,0},{8,12},{12,8},{1,5},{5,1},{9,13},{13,9},{2,6},{6,2},{1... | collective-permute-start | bytes 393224 | tf_op jit(solution)/shard_map/ppermute | solution.py:333
  10.4 1.0 %collective-permute-done.2.refs_0_.refs_1_ = f32[32,1024]{1,0:T(8,128)S(1)} collective-permute-done((f32[32,1024]{1,0:T(8,128)}, f32[32,1024]{1,0:T(8,128)S(1)}, u32[]{:S(2)}, u32[]{:S(2)}) %collective-permute-start.2) | collective-permute-done | bytes 131104 | tf_op jit(solution)/shard_map/ppermute | solution.py:333
  11.4 0.7 %collective-permute-start.8 = (f32[32,1024]{1,0:T(8,128)S(1)}, f32[32,1024]{1,0:T(8,128)S(1)}, u32[]{:S(2)}, u32[]{:S(2)}) collective-permute-start(f32[32,1024]{1,0:T(8,128)S(1)} %collective-permute-done.2.refs_0_.refs_1_), channel_id=1, source_target_pairs={{0,4},{4,0},{8,12},{12,8},{1,5},{5,1},{9,13},{13,9},{2,6},{6,2},{1... | collective-permute-start | bytes 393224 | tf_op jit(solution)/shard_map/ppermute | solution.py:333
  12.4 0.5 %collective-permute-start.4 = (f32[40,512]{1,0:T(8,128)S(1)}, f32[40,512]{1,0:T(8,128)S(1)}, u32[]{:S(2)}, u32[]{:S(2)}) collective-permute-start(f32[40,512]{1,0:T(8,128)S(1)} %get-tuple-element.13.refs_1_), channel_id=1, source_target_pairs={{0,1},{1,0},{2,3},{3,2},{4,5},{5,4},{6,7},{7,6},{8,9},{9,8},{10,11... | collective-permute-start | bytes 245768 | tf_op jit(solution)/shard_map/ppermute | solution.py:333
  12.9 0.8 %collective-permute-done.3.refs_2_ = f32[40,512]{1,0:T(8,128)S(1)} collective-permute-done((f32[40,512]{1,0:T(8,128)S(1)}, f32[40,512]{1,0:T(8,128)S(1)}, u32[]{:S(2)}, u32[]{:S(2)}) %collective-permute-start.3) | collective-permute-done | bytes 81952 | tf_op jit(solution)/shard_map/ppermute | solution.py:333
  13.8 0.4 %shard_map.102 = f32[16,1024]{1,0:T(8,128)S(1)} custom-call(f32[16,512]{1,0:T(8,128)S(1)} %get-tuple-element.11.g_ref, bf16[64,512]{1,0:T(8,128)(2,1)S(1)} %shard_map.98.refs_3_.mask_ref, f32[40,512]{1,0:T(8,128)S(1)} %get-tuple-element.12.refs_0_, f32[40,512]{1,0:T(8,128)S(1)} %get-tuple-element.13.refs_1_, f32[40,512]{1,0:T(8,128)S(1)} %collective-permute-done.3.refs_2_, ...), custom_call_target="tpu_custom_call" | custom-call | flops 67108864 | tf_op jit(solution)/shard_map/pallas_call | solution.py:201
  14.3 1.6 %collective-permute-start.5 = (f32[16,1024]{1,0:T(8,128)S(1)}, f32[16,1024]{1,0:T(8,128)S(1)}, u32[]{:S(2)}, u32[]{:S(2)}) collective-permute-start(f32[16,1024]{1,0:T(8,128)S(1)} %shard_map.102), channel_id=1, source_target_pairs={{0,4},{4,8},{8,12},{12,0},{1,5},{5,9},{9,13},{13,1},{2,6},{6,10},{... | collective-permute-start | bytes 196616 | tf_op jit(solution)/shard_map/ppermute | solution.py:338
  15.9 0.4 %shard_map.103 = f32[16,1024]{1,0:T(8,128)S(1)} custom-call(f32[16,512]{1,0:T(8,128)S(1)} %get-tuple-element.11.g_ref, bf16[64,512]{1,0:T(8,128)(2,1)S(1)} %shard_map.98.refs_3_.mask_ref, f32[40,512]{1,0:T(8,128)S(1)} %get-tuple-element.12.refs_0_, f32[40,512]{1,0:T(8,128)S(1)} %get-tuple-element.13.refs_1_, f32[40,512]{1,0:T(8,128)S(1)} %collective-permute-done.3.refs_2_, ...), custom_call_target="tpu_custom_call" | custom-call | flops 67108864 | tf_op jit(solution)/shard_map/pallas_call | solution.py:201
  16.3 1.7 %collective-permute-start.6 = (f32[16,1024]{1,0:T(8,128)S(1)}, f32[16,1024]{1,0:T(8,128)S(1)}, u32[]{:S(2)}, u32[]{:S(2)}) collective-permute-start(f32[16,1024]{1,0:T(8,128)S(1)} %shard_map.103), channel_id=1, source_target_pairs={{0,8},{4,12},{8,0},{12,4},{1,9},{5,13},{9,1},{13,5},{2,10},{6,14},... | collective-permute-start | bytes 196616 | tf_op jit(solution)/shard_map/ppermute | solution.py:338
  18.0 0.6 %shard_map.101 = (f32[16,1024]{1,0:T(8,128)S(1)}, f32[16,1024]{1,0:T(8,128)S(1)}) custom-call(f32[16,512]{1,0:T(8,128)S(1)} %get-tuple-element.11.g_ref, bf16[64,512]{1,0:T(8,128)(2,1)S(1)} %shard_map.98.refs_3_.mask_ref, f32[40,512]{1,0:T(8,128)S(1)} %get-tuple-element.12.refs_0_, f32[40,512]{1,0:T(8,128)S(1)} %get-tuple-element.13.refs_1_, ...), custom_call_target="tpu_custom_call" | custom-call | flops 134217728 | tf_op jit(solution)/shard_map/pallas_call | solution.py:201
  18.6 3.0 %collective-permute-start.9 = (f32[16,1024]{1,0:T(8,128)S(1)}, f32[16,1024]{1,0:T(8,128)S(1)}, u32[]{:S(2)}, u32[]{:S(2)}) collective-permute-start(f32[16,1024]{1,0:T(8,128)S(1)} %shard_map.104), channel_id=1, source_target_pairs={{0,12},{4,0},{8,4},{12,8},{1,13},{5,1},{9,5},{13,9},{2,14},{6,2},{... | collective-permute-start | bytes 196616 | tf_op jit(solution)/shard_map/ppermute | solution.py:338
  21.7 0.3 %shard_map.107.early_ref = f32[32,128]{1,0:T(8,128)S(1)} custom-call(s32[1,128]{1,0:T(1,128)S(1)} %bitcast.5, bf16[256,1024]{1,0:T(8,128)(2,1)S(1)} %shard_map.106.pool_ref, f32[16,1024]{1,0:T(8,128)S(1)} %get-tuple-element.14.refs_0_, f32[16,1024]{1,0:T(8,128)S(1)} %collective-permute-done.5.refs_1_), custom_call_target="tpu_custom_call" | custom-call | tf_op jit(solution)/shard_map/pallas_call | solution.py:279
  22.0 1.1 %collective-permute-done.6.refs_2_.refs_0_ = f32[16,1024]{1,0:T(8,128)S(1)} collective-permute-done((f32[16,1024]{1,0:T(8,128)S(1)}, f32[16,1024]{1,0:T(8,128)S(1)}, u32[]{:S(2)}, u32[]{:S(2)}) %collective-permute-start.6) | collective-permute-done | bytes 65568 | tf_op jit(solution)/shard_map/ppermute | solution.py:338
  23.5 0.3 %shard_map.109 = f32[64,128]{1,0:T(8,128)S(1)} custom-call(s32[1,128]{1,0:T(1,128)S(1)} %bitcast.6, bf16[256,1024]{1,0:T(8,128)(2,1)S(1)} %shard_map.106.pool_ref, f32[32,128]{1,0:T(8,128)S(1)} %shard_map.107.early_ref, f32[16,1024]{1,0:T(8,128)S(1)} %collective-permute-done.6.refs_2_.refs_0_, f32[16,1024]{1,0:T(8,128)S(1)} %collective-permute-done.9.refs_3_.refs_1_, ...), custom_call_target="tpu_custom_call" | custom-call | tf_op jit(solution)/shard_map/pallas_call | solution.py:303
  23.9 1.2 %collective-permute-done.10 = f32[64,128]{1,0:T(8,128)S(1)} collective-permute-done((f32[64,128]{1,0:T(8,128)S(1)}, f32[64,128]{1,0:T(8,128)S(1)}, u32[]{:S(2)}, u32[]{:S(2)}) %collective-permute-start.10) | collective-permute-done | bytes 32800 | tf_op jit(solution)/shard_map/ppermute | solution.py:333
  25.1 1.5 %collective-permute-start.11 = (f32[64,128]{1,0:T(8,128)S(1)}, f32[64,128]{1,0:T(8,128)S(1)}, u32[]{:S(2)}, u32[]{:S(2)}) collective-permute-start(f32[64,128]{1,0:T(8,128)S(1)} %add.6), channel_id=1, source_target_pairs={{0,2},{1,3},{2,0},{3,1},{4,6},{5,7},{6,4},{7,5},{8,10},{9,11},{10,... | collective-permute-start | bytes 98312 | tf_op jit(solution)/shard_map/ppermute | solution.py:333
  26.6 0.7 %shard_map.105 = f32[64,1024]{1,0:T(8,128)} custom-call(f32[16,1024]{1,0:T(8,128)S(1)} %get-tuple-element.14.refs_0_, f32[16,1024]{1,0:T(8,128)S(1)} %collective-permute-done.5.refs_1_, f32[16,1024]{1,0:T(8,128)S(1)} %collective-permute-done.6.refs_2_.refs_0_, f32[16,1024]{1,0:T(8,128)S(1)} %collective-permute-done.9.refs_3_.refs_1_), custom_call_target="tpu_custom_call" | custom-call | bytes 524288 | tf_op jit(solution)/shard_map/pallas_call | solution.py:324
  27.3 1.7 %collective-permute-done.11 = f32[64,128]{1,0:T(8,128)S(1)} collective-permute-done((f32[64,128]{1,0:T(8,128)S(1)}, f32[64,128]{1,0:T(8,128)S(1)}, u32[]{:S(2)}, u32[]{:S(2)}) %collective-permute-start.11) | collective-permute-done | bytes 32800 | tf_op jit(solution)/shard_map/ppermute | solution.py:333
  29.0 0.6 %add_multiply_fusion = f32[64,128]{1,0:T(8,128)} fusion(f32[64,128]{1,0:T(8,128)S(1)} %add.6, f32[64,128]{1,0:T(8,128)S(1)} %collective-permute-done.11), kind=kLoop, calls=%fused_computation | loop fusion | flops 16384 | bytes 98304 | tf_op jit(solution)/shard_map/mul | solution.py:403
  (33 shorter events, 1.1 us)
Async XLA Ops:
  0.6 4.2 %copy-start.5 = (bf16[1024,64]{0,1:T(8,128)(2,1)S(1)}, bf16[1024,64]{0,1:T(8,128)(2,1)}, u32[]{:S(2)}) copy-start(bf16[1024,64]{0,1:T(8,128)(2,1)} %param.10) | copy-start | bytes 393220
  0.6 4.2 %copy-start.4 = (bf16[512,1024]{1,0:T(8,128)(2,1)S(1)}, bf16[512,1024]{1,0:T(8,128)(2,1)}, u32[]{:S(2)}) copy-start(bf16[512,1024]{1,0:T(8,128)(2,1)} %act_ref.1) | copy-start | bytes 3145732
  0.7 6.2 %copy-start.1 = (bf16[3584,64]{0,1:T(8,128)(2,1)S(1)}, bf16[3584,64]{0,1:T(8,128)(2,1)}, u32[]{:S(2)}) copy-start(bf16[3584,64]{0,1:T(8,128)(2,1)} %param.11) | copy-start | bytes 1376260
  0.7 6.2 %copy-start = (bf16[512,3584]{1,0:T(8,128)(2,1)S(1)}, bf16[512,3584]{1,0:T(8,128)(2,1)}, u32[]{:S(2)}) copy-start(bf16[512,3584]{1,0:T(8,128)(2,1)} %grad_ref.1) | copy-start | bytes 11010052
  0.7 10.7 %collective-permute-start.2 = (f32[32,1024]{1,0:T(8,128)}, f32[32,1024]{1,0:T(8,128)S(1)}, u32[]{:S(2)}, u32[]{:S(2)}) collective-permute-start(f32[32,1024]{1,0:T(8,128)} %refs_0_.1), channel_id=1, source_target_pairs={{0,8},{4,12},{8,0},{12,4},{1,9},{5,13},{9,1},{13,5},{2,10},{6,14},... | collective-permute-start | bytes 393224 | tf_op jit(solution)/shard_map/ppermute | solution.py:333
  4.8 3.8 %copy-start.2 = (f32[32,1024]{1,0:T(8,128)S(1)}, f32[32,1024]{1,0:T(8,128)}, u32[]{:S(2)}) copy-start(f32[32,1024]{1,0:T(8,128)} %refs_0_.1) | copy-start | bytes 393220
  4.8 5.4 %copy-start.6 = (s32[1,32]{1,0:T(1,128)S(1)}, s32[1,32]{1,0:T(1,128)}, u32[]{:S(2)}) copy-start(s32[1,32]{1,0:T(1,128)} %lengths_ref.1) | copy-start | bytes 388
  4.8 5.4 %copy-start.7 = (s32[32,1]{0,1:T(1,128)S(1)}, s32[32,1]{0,1:T(1,128)}, u32[]{:S(2)}) copy-start(s32[32,1]{0,1:T(1,128)} %param.13) | copy-start | bytes 388
  5.3 7.1 %collective-permute-start = (f32[64,512]{1,0:T(8,128)S(1)}, f32[64,512]{1,0:T(8,128)S(1)}, u32[]{:S(2)}, u32[]{:S(2)}) collective-permute-start(f32[64,512]{1,0:T(8,128)S(1)} %shard_map.97.refs_0_), channel_id=1, source_target_pairs={{0,2},{1,3},{2,0},{3,1},{4,6},{5,7},{6,4},{7,5},{8,10},{9,11},{10,... | collective-permute-start | bytes 393224 | tf_op jit(solution)/shard_map/ppermute | solution.py:333
  6.8 14.9 %copy-start.3 = (s32[128]{0:T(128)S(1)}, s32[128]{0:T(128)}, u32[]{:S(2)}) copy-start(s32[128]{0:T(128)} %param.15) | copy-start | bytes 1540
  8.0 4.3 %collective-permute-start.1 = (f32[32,512]{1,0:T(8,128)S(1)}, f32[32,512]{1,0:T(8,128)S(1)}, u32[]{:S(2)}, u32[]{:S(2)}) collective-permute-start(f32[32,512]{1,0:T(8,128)S(1)} %get-tuple-element.10), channel_id=1, source_target_pairs={{0,2},{1,3},{2,0},{3,1},{4,6},{5,7},{6,4},{7,5},{8,10},{9,11},{10,... | collective-permute-start | bytes 196616 | tf_op jit(solution)/shard_map/ppermute | solution.py:333
  8.6 10.0 %collective-permute-start.7 = (f32[32,1024]{1,0:T(8,128)S(1)}, f32[32,1024]{1,0:T(8,128)S(1)}, u32[]{:S(2)}, u32[]{:S(2)}) collective-permute-start(f32[32,1024]{1,0:T(8,128)S(1)} %copy-done.2), channel_id=1, source_target_pairs={{0,4},{4,0},{8,12},{12,8},{1,5},{5,1},{9,13},{13,9},{2,6},{6,2},{1... | collective-permute-start | bytes 393224 | tf_op jit(solution)/shard_map/ppermute | solution.py:333
  11.4 7.2 %collective-permute-start.8 = (f32[32,1024]{1,0:T(8,128)S(1)}, f32[32,1024]{1,0:T(8,128)S(1)}, u32[]{:S(2)}, u32[]{:S(2)}) collective-permute-start(f32[32,1024]{1,0:T(8,128)S(1)} %collective-permute-done.2.refs_0_.refs_1_), channel_id=1, source_target_pairs={{0,4},{4,0},{8,12},{12,8},{1,5},{5,1},{9,13},{13,9},{2,6},{6,2},{1... | collective-permute-start | bytes 393224 | tf_op jit(solution)/shard_map/ppermute | solution.py:333
  12.3 1.3 %collective-permute-start.3 = (f32[40,512]{1,0:T(8,128)S(1)}, f32[40,512]{1,0:T(8,128)S(1)}, u32[]{:S(2)}, u32[]{:S(2)}) collective-permute-start(f32[40,512]{1,0:T(8,128)S(1)} %get-tuple-element.12.refs_0_), channel_id=1, source_target_pairs={{0,1},{1,0},{2,3},{3,2},{4,5},{5,4},{6,7},{7,6},{8,9},{9,8},{10,11... | collective-permute-start | bytes 245768 | tf_op jit(solution)/shard_map/ppermute | solution.py:333
  12.4 1.4 %collective-permute-start.4 = (f32[40,512]{1,0:T(8,128)S(1)}, f32[40,512]{1,0:T(8,128)S(1)}, u32[]{:S(2)}, u32[]{:S(2)}) collective-permute-start(f32[40,512]{1,0:T(8,128)S(1)} %get-tuple-element.13.refs_1_), channel_id=1, source_target_pairs={{0,1},{1,0},{2,3},{3,2},{4,5},{5,4},{6,7},{7,6},{8,9},{9,8},{10,11... | collective-permute-start | bytes 245768 | tf_op jit(solution)/shard_map/ppermute | solution.py:333
  14.3 7.4 %collective-permute-start.5 = (f32[16,1024]{1,0:T(8,128)S(1)}, f32[16,1024]{1,0:T(8,128)S(1)}, u32[]{:S(2)}, u32[]{:S(2)}) collective-permute-start(f32[16,1024]{1,0:T(8,128)S(1)} %shard_map.102), channel_id=1, source_target_pairs={{0,4},{4,8},{8,12},{12,0},{1,5},{5,9},{9,13},{13,1},{2,6},{6,10},{... | collective-permute-start | bytes 196616 | tf_op jit(solution)/shard_map/ppermute | solution.py:338
  16.3 6.8 %collective-permute-start.6 = (f32[16,1024]{1,0:T(8,128)S(1)}, f32[16,1024]{1,0:T(8,128)S(1)}, u32[]{:S(2)}, u32[]{:S(2)}) collective-permute-start(f32[16,1024]{1,0:T(8,128)S(1)} %shard_map.103), channel_id=1, source_target_pairs={{0,8},{4,12},{8,0},{12,4},{1,9},{5,13},{9,1},{13,5},{2,10},{6,14},... | collective-permute-start | bytes 196616 | tf_op jit(solution)/shard_map/ppermute | solution.py:338
  18.6 4.9 %collective-permute-start.9 = (f32[16,1024]{1,0:T(8,128)S(1)}, f32[16,1024]{1,0:T(8,128)S(1)}, u32[]{:S(2)}, u32[]{:S(2)}) collective-permute-start(f32[16,1024]{1,0:T(8,128)S(1)} %shard_map.104), channel_id=1, source_target_pairs={{0,12},{4,0},{8,4},{12,8},{1,13},{5,1},{9,5},{13,9},{2,14},{6,2},{... | collective-permute-start | bytes 196616 | tf_op jit(solution)/shard_map/ppermute | solution.py:338
  23.8 1.2 %collective-permute-start.10 = (f32[64,128]{1,0:T(8,128)S(1)}, f32[64,128]{1,0:T(8,128)S(1)}, u32[]{:S(2)}, u32[]{:S(2)}) collective-permute-start(f32[64,128]{1,0:T(8,128)S(1)} %shard_map.109), channel_id=1, source_target_pairs={{0,1},{1,0},{2,3},{3,2},{4,5},{5,4},{6,7},{7,6},{8,9},{9,8},{10,11... | collective-permute-start | bytes 98312 | tf_op jit(solution)/shard_map/ppermute | solution.py:333
  25.1 3.9 %collective-permute-start.11 = (f32[64,128]{1,0:T(8,128)S(1)}, f32[64,128]{1,0:T(8,128)S(1)}, u32[]{:S(2)}, u32[]{:S(2)}) collective-permute-start(f32[64,128]{1,0:T(8,128)S(1)} %add.6), channel_id=1, source_target_pairs={{0,2},{1,3},{2,0},{3,1},{4,6},{5,7},{6,4},{7,5},{8,10},{9,11},{10,... | collective-permute-start | bytes 98312 | tf_op jit(solution)/shard_map/ppermute | solution.py:333

commit v21 on v20

--- a/solution.py
+++ b/solution.py
@@ -379,12 +379,11 @@
         gots = [swap(part, "tensor", bit) for part in own]
     ids_row = query_ids[None, :]
     if direct:
-        split = max(1, data_size // 2)
-        soon = [outer(own, gots, keep, mask, cap, k, 1)[0] for k in range(split)]
-        rows = [shift(block, "dp", k) for k, block in enumerate(soon, 1)]
-        *sent, kept = outer(own, gots, keep, mask, cap, split, data_size - split)
+        spans = [(0, 1), (1, data_size - 1), (data_size - 1, data_size)]
+        calls = [outer(own, gots, keep, mask, cap, i, j - i) for i, j in spans if i < j]
+        *sent, kept = [block for blocks in calls for block in blocks]
         sent[-1] = after(sent[-1], [mate, *passed])
-        rows = [kept, *rows, *(shift(block, "dp", k) for k, block in enumerate(sent, 1 + split))]
+        rows = [kept, *(shift(block, "dp", k) for k, block in enumerate(sent, 1))]
         store = place(rows)
         late = [token(rows[2:-1], LATE_FLOPS)]
         pool = pool_halves([*pieces, mate, *passed])

time: 29.7 us -> 29.8 us (level)
  waiting for transfers between devices: 6.46 us -> 6.95 us
  starting transfers between devices: 16.9 us -> 16.5 us
    ppermute x9, starting transfers between devices: 10.6 us -> 10.2 us  [swap(): lax.ppermute(x, axis, [(i, i ^ gap) for i in range(lax.axis_size(axis))])]
    ppermute x9, waiting for transfers between devices: 5.01 us -> 5.44 us  [swap(): lax.ppermute(x, axis, [(i, i ^ gap) for i in range(lax.axis_size(axis))])]
  transfers between devices with their start and end apart: 12 -> 12, of which waited for: 8 -> 7; matrix products, arithmetic and copies ran while one was open for 0% -> 0% of each run, Pallas kernels for 15% -> 15%
where the time goes in v21:
time: 29.8 us; the launch traced here: 29.7 us
  starting transfers between devices  16.5 us (55%)
  waiting for transfers between devices  6.95 us (23%)
  Pallas kernels  4.8 us (16%)
  between operations  0.77 us (3%)
  other arithmetic  0.63 us (2%)
    ppermute x9, starting transfers between devices, swap(): lax.ppermute(x, axis, [(i, i ^ gap) for i in range(lax.axis_size(axis))])  10.2 us
    ppermute x3, starting transfers between devices, shift(): return lax.ppermute(x, axis, [(i, (i + by) % size) for i in range(size)])  6.28 us
    ppermute x9, waiting for transfers between devices, swap(): lax.ppermute(x, axis, [(i, i ^ gap) for i in range(lax.axis_size(axis))])  5.44 us
    ppermute x3, waiting for transfers between devices, shift(): return lax.ppermute(x, axis, [(i, (i + by) % size) for i in range(size)])  1.51 us
    pallas_call x3, Pallas kernels, outer(): pl.pallas_call(functools.partial(outer_kernel, first, owners, len(sent)),...  1.44 us
    pallas_call x1, Pallas kernels, project_g(): pl.pallas_call(functools.partial(g_kernel, width), out_shape=[part, part]...  1.16 us
    pallas_call x1, Pallas kernels, place(): pl.pallas_call(place_kernel, out_shape=jax.ShapeDtypeStruct((slots, feats...  0.72 us
    mul x1, other arithmetic, local(): return (store, scores * (1.0 / (rank * rank)))  0.62 us
  transfers between devices with their start and end apart: 12, of which 7 were waited for; matrix products, arithmetic and copies ran while one was open for 0% of the time, Pallas kernels for 15%

profile of v21, /device:TPU:0, one launch (start us, length us, event | category | flops | bytes accessed | tf_op | source)
XLA Modules:
  0.0 29.7 jit_solution(4545638884915184755)
XLA Ops:
  0.7 4.1 %collective-permute-start.2 = (f32[32,1024]{1,0:T(8,128)}, f32[32,1024]{1,0:T(8,128)S(1)}, u32[]{:S(2)}, u32[]{:S(2)}) collective-permute-start(f32[32,1024]{1,0:T(8,128)} %refs_0_.1), channel_id=1, source_target_pairs={{0,8},{4,12},{8,0},{12,4},{1,9},{5,13},{9,1},{13,5},{2,10},{6,14},... | collective-permute-start | bytes 393224 | tf_op jit(solution)/shard_map/ppermute | solution.py:333
  4.8 0.5 %shard_map.97.refs_0_ = f32[64,512]{1,0:T(8,128)S(1)} custom-call(bf16[512,1024]{1,0:T(8,128)(2,1)S(1)} %copy-done.4, bf16[64,1024]{1,0:T(8,128)(2,1)S(1)} %bitcast.7, f32[8,128]{1,0:T(8,128)S(1)} %shard_map.96.refs_0_), custom_call_target="tpu_custom_call" | custom-call | flops 600000000 | tf_op jit(solution)/shard_map/pallas_call | solution.py:90
  5.3 1.5 %collective-permute-start = (f32[64,512]{1,0:T(8,128)S(1)}, f32[64,512]{1,0:T(8,128)S(1)}, u32[]{:S(2)}, u32[]{:S(2)}) collective-permute-start(f32[64,512]{1,0:T(8,128)S(1)} %shard_map.97.refs_0_), channel_id=1, source_target_pairs={{0,2},{1,3},{2,0},{3,1},{4,6},{5,7},{6,4},{7,5},{8,10},{9,11},{10,... | collective-permute-start | bytes 393224 | tf_op jit(solution)/shard_map/ppermute | solution.py:333
  6.8 1.2 %shard_map.95 = (f32[32,512]{1,0:T(8,128)S(1)}, f32[32,512]{1,0:T(8,128)S(1)}) custom-call(bf16[512,3584]{1,0:T(8,128)(2,1)S(1)} %copy-done, bf16[64,3584]{1,0:T(8,128)(2,1)S(1)} %bitcast.4), custom_call_target="tpu_custom_call" | custom-call | tf_op jit(solution)/shard_map/pallas_call | solution.py:113
  8.0 0.6 %collective-permute-start.1 = (f32[32,512]{1,0:T(8,128)S(1)}, f32[32,512]{1,0:T(8,128)S(1)}, u32[]{:S(2)}, u32[]{:S(2)}) collective-permute-start(f32[32,512]{1,0:T(8,128)S(1)} %get-tuple-element.10), channel_id=1, source_target_pairs={{0,2},{1,3},{2,0},{3,1},{4,6},{5,7},{6,4},{7,5},{8,10},{9,11},{10,... | collective-permute-start | bytes 196616 | tf_op jit(solution)/shard_map/ppermute | solution.py:333
  8.6 1.6 %collective-permute-start.7 = (f32[32,1024]{1,0:T(8,128)S(1)}, f32[32,1024]{1,0:T(8,128)S(1)}, u32[]{:S(2)}, u32[]{:S(2)}) collective-permute-start(f32[32,1024]{1,0:T(8,128)S(1)} %copy-done.2), channel_id=1, source_target_pairs={{0,4},{4,0},{8,12},{12,8},{1,5},{5,1},{9,13},{13,9},{2,6},{6,2},{1... | collective-permute-start | bytes 393224 | tf_op jit(solution)/shard_map/ppermute | solution.py:333
  10.4 1.0 %collective-permute-done.2.refs_0_.refs_1_ = f32[32,1024]{1,0:T(8,128)S(1)} collective-permute-done((f32[32,1024]{1,0:T(8,128)}, f32[32,1024]{1,0:T(8,128)S(1)}, u32[]{:S(2)}, u32[]{:S(2)}) %collective-permute-start.2) | collective-permute-done | bytes 131104 | tf_op jit(solution)/shard_map/ppermute | solution.py:333
  11.4 0.7 %collective-permute-start.8 = (f32[32,1024]{1,0:T(8,128)S(1)}, f32[32,1024]{1,0:T(8,128)S(1)}, u32[]{:S(2)}, u32[]{:S(2)}) collective-permute-start(f32[32,1024]{1,0:T(8,128)S(1)} %collective-permute-done.2.refs_0_.refs_1_), channel_id=1, source_target_pairs={{0,4},{4,0},{8,12},{12,8},{1,5},{5,1},{9,13},{13,9},{2,6},{6,2},{1... | collective-permute-start | bytes 393224 | tf_op jit(solution)/shard_map/ppermute | solution.py:333
  12.4 0.5 %collective-permute-start.4 = (f32[40,512]{1,0:T(8,128)S(1)}, f32[40,512]{1,0:T(8,128)S(1)}, u32[]{:S(2)}, u32[]{:S(2)}) collective-permute-start(f32[40,512]{1,0:T(8,128)S(1)} %get-tuple-element.13.refs_1_), channel_id=1, source_target_pairs={{0,1},{1,0},{2,3},{3,2},{4,5},{5,4},{6,7},{7,6},{8,9},{9,8},{10,11... | collective-permute-start | bytes 245768 | tf_op jit(solution)/shard_map/ppermute | solution.py:333
  12.9 0.8 %collective-permute-done.3.refs_2_ = f32[40,512]{1,0:T(8,128)S(1)} collective-permute-done((f32[40,512]{1,0:T(8,128)S(1)}, f32[40,512]{1,0:T(8,128)S(1)}, u32[]{:S(2)}, u32[]{:S(2)}) %collective-permute-start.3) | collective-permute-done | bytes 81952 | tf_op jit(solution)/shard_map/ppermute | solution.py:333
  13.8 0.4 %shard_map.102 = f32[16,1024]{1,0:T(8,128)S(1)} custom-call(f32[16,512]{1,0:T(8,128)S(1)} %get-tuple-element.11.g_ref, bf16[64,512]{1,0:T(8,128)(2,1)S(1)} %shard_map.98.refs_3_.mask_ref, f32[40,512]{1,0:T(8,128)S(1)} %get-tuple-element.12.refs_0_, f32[40,512]{1,0:T(8,128)S(1)} %get-tuple-element.13.refs_1_, f32[40,512]{1,0:T(8,128)S(1)} %collective-permute-done.3.refs_2_, ...), custom_call_target="tpu_custom_call" | custom-call | flops 67108864 | tf_op jit(solution)/shard_map/pallas_call | solution.py:201
  14.3 1.6 %collective-permute-start.5 = (f32[16,1024]{1,0:T(8,128)S(1)}, f32[16,1024]{1,0:T(8,128)S(1)}, u32[]{:S(2)}, u32[]{:S(2)}) collective-permute-start(f32[16,1024]{1,0:T(8,128)S(1)} %shard_map.102), channel_id=1, source_target_pairs={{0,4},{4,8},{8,12},{12,0},{1,5},{5,9},{9,13},{13,1},{2,6},{6,10},{... | collective-permute-start | bytes 196616 | tf_op jit(solution)/shard_map/ppermute | solution.py:338
  15.9 0.6 %shard_map.103 = (f32[16,1024]{1,0:T(8,128)S(1)}, f32[16,1024]{1,0:T(8,128)S(1)}) custom-call(f32[16,512]{1,0:T(8,128)S(1)} %get-tuple-element.11.g_ref, bf16[64,512]{1,0:T(8,128)(2,1)S(1)} %shard_map.98.refs_3_.mask_ref, f32[40,512]{1,0:T(8,128)S(1)} %get-tuple-element.12.refs_0_, f32[40,512]{1,0:T(8,128)S(1)} %get-tuple-element.13.refs_1_, ...), custom_call_target="tpu_custom_call" | custom-call | flops 134217728 | tf_op jit(solution)/shard_map/pallas_call | solution.py:201
  16.5 1.7 %collective-permute-start.6 = (f32[16,1024]{1,0:T(8,128)S(1)}, f32[16,1024]{1,0:T(8,128)S(1)}, u32[]{:S(2)}, u32[]{:S(2)}) collective-permute-start(f32[16,1024]{1,0:T(8,128)S(1)} %get-tuple-element.14), channel_id=1, source_target_pairs={{0,8},{4,12},{8,0},{12,4},{1,9},{5,13},{9,1},{13,5},{2,10},{6,14},... | collective-permute-start | bytes 196616 | tf_op jit(solution)/shard_map/ppermute | solution.py:338
  18.2 3.0 %collective-permute-start.9 = (f32[16,1024]{1,0:T(8,128)S(1)}, f32[16,1024]{1,0:T(8,128)S(1)}, u32[]{:S(2)}, u32[]{:S(2)}) collective-permute-start(f32[16,1024]{1,0:T(8,128)S(1)} %shard_map.104), channel_id=1, source_target_pairs={{0,12},{4,0},{8,4},{12,8},{1,13},{5,1},{9,5},{13,9},{2,14},{6,2},{... | collective-permute-start | bytes 196616 | tf_op jit(solution)/shard_map/ppermute | solution.py:338
  21.1 0.4 %shard_map.101.refs_0_ = f32[16,1024]{1,0:T(8,128)S(1)} custom-call(f32[16,512]{1,0:T(8,128)S(1)} %get-tuple-element.11.g_ref, bf16[64,512]{1,0:T(8,128)(2,1)S(1)} %shard_map.98.refs_3_.mask_ref, f32[40,512]{1,0:T(8,128)S(1)} %get-tuple-element.12.refs_0_, f32[40,512]{1,0:T(8,128)S(1)} %get-tuple-element.13.refs_1_, ...), custom_call_target="tpu_custom_call" | custom-call | flops 67108864 | tf_op jit(solution)/shard_map/pallas_call | solution.py:201
  21.7 0.3 %shard_map.107.early_ref = f32[32,128]{1,0:T(8,128)S(1)} custom-call(s32[1,128]{1,0:T(1,128)S(1)} %bitcast.5, bf16[256,1024]{1,0:T(8,128)(2,1)S(1)} %shard_map.106.pool_ref, f32[16,1024]{1,0:T(8,128)S(1)} %shard_map.101.refs_0_, f32[16,1024]{1,0:T(8,128)S(1)} %collective-permute-done.5.refs_1_), custom_call_target="tpu_custom_call" | custom-call | tf_op jit(solution)/shard_map/pallas_call | solution.py:279
  22.0 1.5 %collective-permute-done.6.refs_2_.refs_0_ = f32[16,1024]{1,0:T(8,128)S(1)} collective-permute-done((f32[16,1024]{1,0:T(8,128)S(1)}, f32[16,1024]{1,0:T(8,128)S(1)}, u32[]{:S(2)}, u32[]{:S(2)}) %collective-permute-start.6) | collective-permute-done | bytes 65568 | tf_op jit(solution)/shard_map/ppermute | solution.py:338
  23.6 0.4 %shard_map.109 = f32[64,128]{1,0:T(8,128)S(1)} custom-call(s32[1,128]{1,0:T(1,128)S(1)} %bitcast.6, bf16[256,1024]{1,0:T(8,128)(2,1)S(1)} %shard_map.106.pool_ref, f32[32,128]{1,0:T(8,128)S(1)} %shard_map.107.early_ref, f32[16,1024]{1,0:T(8,128)S(1)} %collective-permute-done.6.refs_2_.refs_0_, f32[16,1024]{1,0:T(8,128)S(1)} %collective-permute-done.9.refs_3_.refs_1_, ...), custom_call_target="tpu_custom_call" | custom-call | tf_op jit(solution)/shard_map/pallas_call | solution.py:303
  23.9 1.2 %collective-permute-done.10 = f32[64,128]{1,0:T(8,128)S(1)} collective-permute-done((f32[64,128]{1,0:T(8,128)S(1)}, f32[64,128]{1,0:T(8,128)S(1)}, u32[]{:S(2)}, u32[]{:S(2)}) %collective-permute-start.10) | collective-permute-done | bytes 32800 | tf_op jit(solution)/shard_map/ppermute | solution.py:333
  25.1 1.1 %collective-permute-start.11 = (f32[64,128]{1,0:T(8,128)S(1)}, f32[64,128]{1,0:T(8,128)S(1)}, u32[]{:S(2)}, u32[]{:S(2)}) collective-permute-start(f32[64,128]{1,0:T(8,128)S(1)} %add.6), channel_id=1, source_target_pairs={{0,2},{1,3},{2,0},{3,1},{4,6},{5,7},{6,4},{7,5},{8,10},{9,11},{10,... | collective-permute-start | bytes 98312 | tf_op jit(solution)/shard_map/ppermute | solution.py:333
  26.2 0.7 %shard_map.105 = f32[64,1024]{1,0:T(8,128)} custom-call(f32[16,1024]{1,0:T(8,128)S(1)} %shard_map.101.refs_0_, f32[16,1024]{1,0:T(8,128)S(1)} %collective-permute-done.5.refs_1_, f32[16,1024]{1,0:T(8,128)S(1)} %collective-permute-done.6.refs_2_.refs_0_, f32[16,1024]{1,0:T(8,128)S(1)} %collective-permute-done.9.refs_3_.refs_1_), custom_call_target="tpu_custom_call" | custom-call | bytes 524288 | tf_op jit(solution)/shard_map/pallas_call | solution.py:324
  26.9 2.1 %collective-permute-done.11 = f32[64,128]{1,0:T(8,128)S(1)} collective-permute-done((f32[64,128]{1,0:T(8,128)S(1)}, f32[64,128]{1,0:T(8,128)S(1)}, u32[]{:S(2)}, u32[]{:S(2)}) %collective-permute-start.11) | collective-permute-done | bytes 32800 | tf_op jit(solution)/shard_map/ppermute | solution.py:333
  29.0 0.6 %add_multiply_fusion = f32[64,128]{1,0:T(8,128)} fusion(f32[64,128]{1,0:T(8,128)S(1)} %add.6, f32[64,128]{1,0:T(8,128)S(1)} %collective-permute-done.11), kind=kLoop, calls=%fused_computation | loop fusion | flops 16384 | bytes 98304 | tf_op jit(solution)/shard_map/mul | solution.py:402
  (33 shorter events, 0.8 us)
Async XLA Ops:
  0.6 4.2 %copy-start.5 = (bf16[1024,64]{0,1:T(8,128)(2,1)S(1)}, bf16[1024,64]{0,1:T(8,128)(2,1)}, u32[]{:S(2)}) copy-start(bf16[1024,64]{0,1:T(8,128)(2,1)} %param.10) | copy-start | bytes 393220
  0.6 4.2 %copy-start.4 = (bf16[512,1024]{1,0:T(8,128)(2,1)S(1)}, bf16[512,1024]{1,0:T(8,128)(2,1)}, u32[]{:S(2)}) copy-start(bf16[512,1024]{1,0:T(8,128)(2,1)} %act_ref.1) | copy-start | bytes 3145732
  0.7 6.2 %copy-start.1 = (bf16[3584,64]{0,1:T(8,128)(2,1)S(1)}, bf16[3584,64]{0,1:T(8,128)(2,1)}, u32[]{:S(2)}) copy-start(bf16[3584,64]{0,1:T(8,128)(2,1)} %param.11) | copy-start | bytes 1376260
  0.7 6.2 %copy-start = (bf16[512,3584]{1,0:T(8,128)(2,1)S(1)}, bf16[512,3584]{1,0:T(8,128)(2,1)}, u32[]{:S(2)}) copy-start(bf16[512,3584]{1,0:T(8,128)(2,1)} %grad_ref.1) | copy-start | bytes 11010052
  0.7 10.7 %collective-permute-start.2 = (f32[32,1024]{1,0:T(8,128)}, f32[32,1024]{1,0:T(8,128)S(1)}, u32[]{:S(2)}, u32[]{:S(2)}) collective-permute-start(f32[32,1024]{1,0:T(8,128)} %refs_0_.1), channel_id=1, source_target_pairs={{0,8},{4,12},{8,0},{12,4},{1,9},{5,13},{9,1},{13,5},{2,10},{6,14},... | collective-permute-start | bytes 393224 | tf_op jit(solution)/shard_map/ppermute | solution.py:333
  4.8 3.8 %copy-start.2 = (f32[32,1024]{1,0:T(8,128)S(1)}, f32[32,1024]{1,0:T(8,128)}, u32[]{:S(2)}) copy-start(f32[32,1024]{1,0:T(8,128)} %refs_0_.1) | copy-start | bytes 393220
  4.8 5.4 %copy-start.6 = (s32[1,32]{1,0:T(1,128)S(1)}, s32[1,32]{1,0:T(1,128)}, u32[]{:S(2)}) copy-start(s32[1,32]{1,0:T(1,128)} %lengths_ref.1) | copy-start | bytes 388
  4.8 5.4 %copy-start.7 = (s32[32,1]{0,1:T(1,128)S(1)}, s32[32,1]{0,1:T(1,128)}, u32[]{:S(2)}) copy-start(s32[32,1]{0,1:T(1,128)} %param.13) | copy-start | bytes 388
  5.3 7.1 %collective-permute-start = (f32[64,512]{1,0:T(8,128)S(1)}, f32[64,512]{1,0:T(8,128)S(1)}, u32[]{:S(2)}, u32[]{:S(2)}) collective-permute-start(f32[64,512]{1,0:T(8,128)S(1)} %shard_map.97.refs_0_), channel_id=1, source_target_pairs={{0,2},{1,3},{2,0},{3,1},{4,6},{5,7},{6,4},{7,5},{8,10},{9,11},{10,... | collective-permute-start | bytes 393224 | tf_op jit(solution)/shard_map/ppermute | solution.py:333
  6.8 14.9 %copy-start.3 = (s32[128]{0:T(128)S(1)}, s32[128]{0:T(128)}, u32[]{:S(2)}) copy-start(s32[128]{0:T(128)} %param.15) | copy-start | bytes 1540
  8.0 4.3 %collective-permute-start.1 = (f32[32,512]{1,0:T(8,128)S(1)}, f32[32,512]{1,0:T(8,128)S(1)}, u32[]{:S(2)}, u32[]{:S(2)}) collective-permute-start(f32[32,512]{1,0:T(8,128)S(1)} %get-tuple-element.10), channel_id=1, source_target_pairs={{0,2},{1,3},{2,0},{3,1},{4,6},{5,7},{6,4},{7,5},{8,10},{9,11},{10,... | collective-permute-start | bytes 196616 | tf_op jit(solution)/shard_map/ppermute | solution.py:333
  8.6 9.6 %collective-permute-start.7 = (f32[32,1024]{1,0:T(8,128)S(1)}, f32[32,1024]{1,0:T(8,128)S(1)}, u32[]{:S(2)}, u32[]{:S(2)}) collective-permute-start(f32[32,1024]{1,0:T(8,128)S(1)} %copy-done.2), channel_id=1, source_target_pairs={{0,4},{4,0},{8,12},{12,8},{1,5},{5,1},{9,13},{13,9},{2,6},{6,2},{1... | collective-permute-start | bytes 393224 | tf_op jit(solution)/shard_map/ppermute | solution.py:333
  11.4 6.8 %collective-permute-start.8 = (f32[32,1024]{1,0:T(8,128)S(1)}, f32[32,1024]{1,0:T(8,128)S(1)}, u32[]{:S(2)}, u32[]{:S(2)}) collective-permute-start(f32[32,1024]{1,0:T(8,128)S(1)} %collective-permute-done.2.refs_0_.refs_1_), channel_id=1, source_target_pairs={{0,4},{4,0},{8,12},{12,8},{1,5},{5,1},{9,13},{13,9},{2,6},{6,2},{1... | collective-permute-start | bytes 393224 | tf_op jit(solution)/shard_map/ppermute | solution.py:333
  12.3 1.3 %collective-permute-start.3 = (f32[40,512]{1,0:T(8,128)S(1)}, f32[40,512]{1,0:T(8,128)S(1)}, u32[]{:S(2)}, u32[]{:S(2)}) collective-permute-start(f32[40,512]{1,0:T(8,128)S(1)} %get-tuple-element.12.refs_0_), channel_id=1, source_target_pairs={{0,1},{1,0},{2,3},{3,2},{4,5},{5,4},{6,7},{7,6},{8,9},{9,8},{10,11... | collective-permute-start | bytes 245768 | tf_op jit(solution)/shard_map/ppermute | solution.py:333
  12.4 1.4 %collective-permute-start.4 = (f32[40,512]{1,0:T(8,128)S(1)}, f32[40,512]{1,0:T(8,128)S(1)}, u32[]{:S(2)}, u32[]{:S(2)}) collective-permute-start(f32[40,512]{1,0:T(8,128)S(1)} %get-tuple-element.13.refs_1_), channel_id=1, source_target_pairs={{0,1},{1,0},{2,3},{3,2},{4,5},{5,4},{6,7},{7,6},{8,9},{9,8},{10,11... | collective-permute-start | bytes 245768 | tf_op jit(solution)/shard_map/ppermute | solution.py:333
  14.3 7.4 %collective-permute-start.5 = (f32[16,1024]{1,0:T(8,128)S(1)}, f32[16,1024]{1,0:T(8,128)S(1)}, u32[]{:S(2)}, u32[]{:S(2)}) collective-permute-start(f32[16,1024]{1,0:T(8,128)S(1)} %shard_map.102), channel_id=1, source_target_pairs={{0,4},{4,8},{8,12},{12,0},{1,5},{5,9},{9,13},{13,1},{2,6},{6,10},{... | collective-permute-start | bytes 196616 | tf_op jit(solution)/shard_map/ppermute | solution.py:338
  16.5 7.1 %collective-permute-start.6 = (f32[16,1024]{1,0:T(8,128)S(1)}, f32[16,1024]{1,0:T(8,128)S(1)}, u32[]{:S(2)}, u32[]{:S(2)}) collective-permute-start(f32[16,1024]{1,0:T(8,128)S(1)} %get-tuple-element.14), channel_id=1, source_target_pairs={{0,8},{4,12},{8,0},{12,4},{1,9},{5,13},{9,1},{13,5},{2,10},{6,14},... | collective-permute-start | bytes 196616 | tf_op jit(solution)/shard_map/ppermute | solution.py:338
  18.2 5.4 %collective-permute-start.9 = (f32[16,1024]{1,0:T(8,128)S(1)}, f32[16,1024]{1,0:T(8,128)S(1)}, u32[]{:S(2)}, u32[]{:S(2)}) collective-permute-start(f32[16,1024]{1,0:T(8,128)S(1)} %shard_map.104), channel_id=1, source_target_pairs={{0,12},{4,0},{8,4},{12,8},{1,13},{5,1},{9,5},{13,9},{2,14},{6,2},{... | collective-permute-start | bytes 196616 | tf_op jit(solution)/shard_map/ppermute | solution.py:338
  23.9 1.2 %collective-permute-start.10 = (f32[64,128]{1,0:T(8,128)S(1)}, f32[64,128]{1,0:T(8,128)S(1)}, u32[]{:S(2)}, u32[]{:S(2)}) collective-permute-start(f32[64,128]{1,0:T(8,128)S(1)} %shard_map.109), channel_id=1, source_target_pairs={{0,1},{1,0},{2,3},{3,2},{4,5},{5,4},{6,7},{7,6},{8,9},{9,8},{10,11... | collective-permute-start | bytes 98312 | tf_op jit(solution)/shard_map/ppermute | solution.py:333
  25.1 3.9 %collective-permute-start.11 = (f32[64,128]{1,0:T(8,128)S(1)}, f32[64,128]{1,0:T(8,128)S(1)}, u32[]{:S(2)}, u32[]{:S(2)}) collective-permute-start(f32[64,128]{1,0:T(8,128)S(1)} %add.6), channel_id=1, source_target_pairs={{0,2},{1,3},{2,0},{3,1},{4,6},{5,7},{6,4},{7,5},{8,10},{9,11},{10,... | collective-permute-start | bytes 98312 | tf_op jit(solution)/shard_map/ppermute | solution.py:333

commit v22 on v18

--- a/solution.py
+++ b/solution.py
@@ -12,7 +12,7 @@
 MIB = 1024 * 1024
 NT = (((1,), (1,)), ((), ()))
 MOST_DIRECT = 8
-GROUP = 8
+GROUP = 16
 ROWS = 16
 LANES = 128
 FIRST_FLOPS = 10 * 10**8
@@ -370,12 +370,10 @@
         gots = [swap(part, "tensor", bit) for part in own]
     ids_row = query_ids[None, :]
     if direct:
-        split = max(1, data_size // 2)
-        soon = outer(own, gots, keep, mask, cap, 0, split)
-        rows = [shift(block, "dp", k) for k, block in enumerate(soon, 1)]
-        *sent, kept = outer(own, gots, keep, mask, cap, split, data_size - split)
+        calls = [outer(own, gots, keep, mask, cap, k, 1) for k in range(data_size)]
+        *sent, kept = [block for blocks in calls for block in blocks]
         sent[-1] = after(sent[-1], [mate, *passed])
-        rows = [kept, *rows, *(shift(block, "dp", k) for k, block in enumerate(sent, 1 + split))]
+        rows = [kept, *(shift(block, "dp", k) for k, block in enumerate(sent, 1))]
         store = place(rows)
         late = [token(rows[2:-1], LATE_FLOPS)]
         pool = pool_halves([*pieces, mate, *passed])

time: 29.8 us -> 29.9 us (level)
  Pallas kernels: 4.5 us -> 5.12 us
    pallas_call x2 -> x4, Pallas kernels: 1.14 us -> 1.75 us  [outer(): pl.pallas_call(functools.partial(outer_kernel, first, owners, len(sent)),...]
    ppermute x3, waiting for transfers between devices: 1.81 us -> 1.35 us  [shift(): return lax.ppermute(x, axis, [(i, (i + by) % size) for i in range(size)])]
  transfers between devices with their start and end apart: 12 -> 12, of which waited for: 7 -> 7; matrix products, arithmetic and copies ran while one was open for 0% -> 0% of each run, Pallas kernels for 14% -> 16%
where the time goes in v22:
time: 29.9 us; the launch traced here: 29.8 us
  starting transfers between devices  16.5 us (55%)
  waiting for transfers between devices  6.73 us (23%)
  Pallas kernels  5.12 us (17%)
  between operations  0.78 us (3%)
  other arithmetic  0.63 us (2%)
    ppermute x9, starting transfers between devices, swap(): lax.ppermute(x, axis, [(i, i ^ gap) for i in range(lax.axis_size(axis))])  10.3 us
    ppermute x3, starting transfers between devices, shift(): return lax.ppermute(x, axis, [(i, (i + by) % size) for i in range(size)])  6.24 us
    ppermute x9, waiting for transfers between devices, swap(): lax.ppermute(x, axis, [(i, i ^ gap) for i in range(lax.axis_size(axis))])  5.37 us
    pallas_call x4, Pallas kernels, outer(): pl.pallas_call(functools.partial(outer_kernel, first, owners, len(sent)),...  1.75 us
    ppermute x3, waiting for transfers between devices, shift(): return lax.ppermute(x, axis, [(i, (i + by) % size) for i in range(size)])  1.35 us
    pallas_call x1, Pallas kernels, project_g(): pl.pallas_call(functools.partial(g_kernel, width), out_shape=[part, part]...  1.16 us
    pallas_call x1, Pallas kernels, place(): pl.pallas_call(place_kernel, out_shape=jax.ShapeDtypeStruct((slots, feats...  0.72 us
    mul x1, other arithmetic, local(): return (store, scores * (1.0 / (rank * rank)))  0.62 us
  transfers between devices with their start and end apart: 12, of which 7 were waited for; matrix products, arithmetic and copies ran while one was open for 0% of the time, Pallas kernels for 16%

profile of v22, /device:TPU:0, one launch (start us, length us, event | category | flops | bytes accessed | tf_op | source)
XLA Modules:
  0.0 29.8 jit_solution(2643155291729689938)
XLA Ops:
  0.7 4.1 %collective-permute-start.2 = (f32[32,1024]{1,0:T(8,128)}, f32[32,1024]{1,0:T(8,128)S(1)}, u32[]{:S(2)}, u32[]{:S(2)}) collective-permute-start(f32[32,1024]{1,0:T(8,128)} %refs_0_.1), channel_id=1, source_target_pairs={{0,8},{4,12},{8,0},{12,4},{1,9},{5,13},{9,1},{13,5},{2,10},{6,14},... | collective-permute-start | bytes 393224 | tf_op jit(solution)/shard_map/ppermute | solution.py:324
  4.8 0.5 %shard_map.97.refs_0_ = f32[64,512]{1,0:T(8,128)S(1)} custom-call(bf16[512,1024]{1,0:T(8,128)(2,1)S(1)} %copy-done.4, bf16[64,1024]{1,0:T(8,128)(2,1)S(1)} %bitcast.7, f32[8,128]{1,0:T(8,128)S(1)} %shard_map.96.refs_0_), custom_call_target="tpu_custom_call" | custom-call | flops 600000000 | tf_op jit(solution)/shard_map/pallas_call | solution.py:90
  5.3 1.5 %collective-permute-start = (f32[64,512]{1,0:T(8,128)S(1)}, f32[64,512]{1,0:T(8,128)S(1)}, u32[]{:S(2)}, u32[]{:S(2)}) collective-permute-start(f32[64,512]{1,0:T(8,128)S(1)} %shard_map.97.refs_0_), channel_id=1, source_target_pairs={{0,2},{1,3},{2,0},{3,1},{4,6},{5,7},{6,4},{7,5},{8,10},{9,11},{10,... | collective-permute-start | bytes 393224 | tf_op jit(solution)/shard_map/ppermute | solution.py:324
  6.8 1.2 %shard_map.95 = (f32[32,512]{1,0:T(8,128)S(1)}, f32[32,512]{1,0:T(8,128)S(1)}) custom-call(bf16[512,3584]{1,0:T(8,128)(2,1)S(1)} %copy-done, bf16[64,3584]{1,0:T(8,128)(2,1)S(1)} %bitcast.4), custom_call_target="tpu_custom_call" | custom-call | tf_op jit(solution)/shard_map/pallas_call | solution.py:113
  8.0 0.6 %collective-permute-start.1 = (f32[32,512]{1,0:T(8,128)S(1)}, f32[32,512]{1,0:T(8,128)S(1)}, u32[]{:S(2)}, u32[]{:S(2)}) collective-permute-start(f32[32,512]{1,0:T(8,128)S(1)} %get-tuple-element.8), channel_id=1, source_target_pairs={{0,2},{1,3},{2,0},{3,1},{4,6},{5,7},{6,4},{7,5},{8,10},{9,11},{10,... | collective-permute-start | bytes 196616 | tf_op jit(solution)/shard_map/ppermute | solution.py:324
  8.6 1.6 %collective-permute-start.7 = (f32[32,1024]{1,0:T(8,128)S(1)}, f32[32,1024]{1,0:T(8,128)S(1)}, u32[]{:S(2)}, u32[]{:S(2)}) collective-permute-start(f32[32,1024]{1,0:T(8,128)S(1)} %copy-done.2), channel_id=1, source_target_pairs={{0,4},{4,0},{8,12},{12,8},{1,5},{5,1},{9,13},{13,9},{2,6},{6,2},{1... | collective-permute-start | bytes 393224 | tf_op jit(solution)/shard_map/ppermute | solution.py:324
  10.4 1.0 %collective-permute-done.2.refs_0_.refs_1_ = f32[32,1024]{1,0:T(8,128)S(1)} collective-permute-done((f32[32,1024]{1,0:T(8,128)}, f32[32,1024]{1,0:T(8,128)S(1)}, u32[]{:S(2)}, u32[]{:S(2)}) %collective-permute-start.2) | collective-permute-done | bytes 131104 | tf_op jit(solution)/shard_map/ppermute | solution.py:324
  11.4 0.7 %collective-permute-start.8 = (f32[32,1024]{1,0:T(8,128)S(1)}, f32[32,1024]{1,0:T(8,128)S(1)}, u32[]{:S(2)}, u32[]{:S(2)}) collective-permute-start(f32[32,1024]{1,0:T(8,128)S(1)} %collective-permute-done.2.refs_0_.refs_1_), channel_id=1, source_target_pairs={{0,4},{4,0},{8,12},{12,8},{1,5},{5,1},{9,13},{13,9},{2,6},{6,2},{1... | collective-permute-start | bytes 393224 | tf_op jit(solution)/shard_map/ppermute | solution.py:324
  12.4 0.5 %collective-permute-start.4 = (f32[40,512]{1,0:T(8,128)S(1)}, f32[40,512]{1,0:T(8,128)S(1)}, u32[]{:S(2)}, u32[]{:S(2)}) collective-permute-start(f32[40,512]{1,0:T(8,128)S(1)} %get-tuple-element.11.refs_1_), channel_id=1, source_target_pairs={{0,1},{1,0},{2,3},{3,2},{4,5},{5,4},{6,7},{7,6},{8,9},{9,8},{10,11... | collective-permute-start | bytes 245768 | tf_op jit(solution)/shard_map/ppermute | solution.py:324
  12.9 0.8 %collective-permute-done.3.refs_2_ = f32[40,512]{1,0:T(8,128)S(1)} collective-permute-done((f32[40,512]{1,0:T(8,128)S(1)}, f32[40,512]{1,0:T(8,128)S(1)}, u32[]{:S(2)}, u32[]{:S(2)}) %collective-permute-start.3) | collective-permute-done | bytes 81952 | tf_op jit(solution)/shard_map/ppermute | solution.py:324
  13.9 0.4 %shard_map.102 = f32[16,1024]{1,0:T(8,128)S(1)} custom-call(f32[16,512]{1,0:T(8,128)S(1)} %get-tuple-element.9.g_ref, bf16[64,512]{1,0:T(8,128)(2,1)S(1)} %shard_map.98.refs_3_.mask_ref, f32[40,512]{1,0:T(8,128)S(1)} %get-tuple-element.10.refs_0_, f32[40,512]{1,0:T(8,128)S(1)} %get-tuple-element.11.refs_1_, f32[40,512]{1,0:T(8,128)S(1)} %collective-permute-done.3.refs_2_, ...), custom_call_target="tpu_custom_call" | custom-call | flops 67108864 | tf_op jit(solution)/shard_map/pallas_call | solution.py:192
  14.3 1.6 %collective-permute-start.5 = (f32[16,1024]{1,0:T(8,128)S(1)}, f32[16,1024]{1,0:T(8,128)S(1)}, u32[]{:S(2)}, u32[]{:S(2)}) collective-permute-start(f32[16,1024]{1,0:T(8,128)S(1)} %shard_map.102), channel_id=1, source_target_pairs={{0,4},{4,8},{8,12},{12,0},{1,5},{5,9},{9,13},{13,1},{2,6},{6,10},{... | collective-permute-start | bytes 196616 | tf_op jit(solution)/shard_map/ppermute | solution.py:329
  15.9 0.4 %shard_map.103 = f32[16,1024]{1,0:T(8,128)S(1)} custom-call(f32[16,512]{1,0:T(8,128)S(1)} %get-tuple-element.9.g_ref, bf16[64,512]{1,0:T(8,128)(2,1)S(1)} %shard_map.98.refs_3_.mask_ref, f32[40,512]{1,0:T(8,128)S(1)} %get-tuple-element.10.refs_0_, f32[40,512]{1,0:T(8,128)S(1)} %get-tuple-element.11.refs_1_, f32[40,512]{1,0:T(8,128)S(1)} %collective-permute-done.3.refs_2_, ...), custom_call_target="tpu_custom_call" | custom-call | flops 67108864 | tf_op jit(solution)/shard_map/pallas_call | solution.py:192
  16.3 1.7 %collective-permute-start.6 = (f32[16,1024]{1,0:T(8,128)S(1)}, f32[16,1024]{1,0:T(8,128)S(1)}, u32[]{:S(2)}, u32[]{:S(2)}) collective-permute-start(f32[16,1024]{1,0:T(8,128)S(1)} %shard_map.103), channel_id=1, source_target_pairs={{0,8},{4,12},{8,0},{12,4},{1,9},{5,13},{9,1},{13,5},{2,10},{6,14},... | collective-permute-start | bytes 196616 | tf_op jit(solution)/shard_map/ppermute | solution.py:329
  18.0 0.4 %shard_map.104.block_ref = f32[16,1024]{1,0:T(8,128)S(1)} custom-call(f32[16,512]{1,0:T(8,128)S(1)} %get-tuple-element.9.g_ref, bf16[64,512]{1,0:T(8,128)(2,1)S(1)} %shard_map.98.refs_3_.mask_ref, f32[40,512]{1,0:T(8,128)S(1)} %get-tuple-element.10.refs_0_, f32[40,512]{1,0:T(8,128)S(1)} %get-tuple-element.11.refs_1_, ...), custom_call_target="tpu_custom_call" | custom-call | flops 67108864 | tf_op jit(solution)/shard_map/pallas_call | solution.py:192
  18.5 3.0 %collective-permute-start.9 = (f32[16,1024]{1,0:T(8,128)S(1)}, f32[16,1024]{1,0:T(8,128)S(1)}, u32[]{:S(2)}, u32[]{:S(2)}) collective-permute-start(f32[16,1024]{1,0:T(8,128)S(1)} %shard_map.105), channel_id=1, source_target_pairs={{0,12},{4,0},{8,4},{12,8},{1,13},{5,1},{9,5},{13,9},{2,14},{6,2},{... | collective-permute-start | bytes 196616 | tf_op jit(solution)/shard_map/ppermute | solution.py:329
  21.4 0.4 %shard_map.101.refs_0_ = f32[16,1024]{1,0:T(8,128)S(1)} custom-call(f32[16,512]{1,0:T(8,128)S(1)} %get-tuple-element.9.g_ref, bf16[64,512]{1,0:T(8,128)(2,1)S(1)} %shard_map.98.refs_3_.mask_ref, f32[40,512]{1,0:T(8,128)S(1)} %get-tuple-element.10.refs_0_, f32[40,512]{1,0:T(8,128)S(1)} %get-tuple-element.11.refs_1_, ...), custom_call_target="tpu_custom_call" | custom-call | flops 67108864 | tf_op jit(solution)/shard_map/pallas_call | solution.py:192
  22.3 1.3 %collective-permute-done.6.refs_2_.refs_0_ = f32[16,1024]{1,0:T(8,128)S(1)} collective-permute-done((f32[16,1024]{1,0:T(8,128)S(1)}, f32[16,1024]{1,0:T(8,128)S(1)}, u32[]{:S(2)}, u32[]{:S(2)}) %collective-permute-start.6) | collective-permute-done | bytes 65568 | tf_op jit(solution)/shard_map/ppermute | solution.py:329
  23.7 0.4 %shard_map.110 = f32[64,128]{1,0:T(8,128)S(1)} custom-call(s32[1,128]{1,0:T(1,128)S(1)} %bitcast.6, bf16[256,1024]{1,0:T(8,128)(2,1)S(1)} %shard_map.107.pool_ref, f32[32,128]{1,0:T(8,128)S(1)} %shard_map.108.early_ref, f32[16,1024]{1,0:T(8,128)S(1)} %collective-permute-done.6.refs_2_.refs_0_, f32[16,1024]{1,0:T(8,128)S(1)} %collective-permute-done.9.refs_3_.refs_1_, ...), custom_call_target="tpu_custom_call" | custom-call | tf_op jit(solution)/shard_map/pallas_call | solution.py:294
  24.0 1.2 %collective-permute-done.10 = f32[64,128]{1,0:T(8,128)S(1)} collective-permute-done((f32[64,128]{1,0:T(8,128)S(1)}, f32[64,128]{1,0:T(8,128)S(1)}, u32[]{:S(2)}, u32[]{:S(2)}) %collective-permute-start.10) | collective-permute-done | bytes 32800 | tf_op jit(solution)/shard_map/ppermute | solution.py:324
  25.3 1.1 %collective-permute-start.11 = (f32[64,128]{1,0:T(8,128)S(1)}, f32[64,128]{1,0:T(8,128)S(1)}, u32[]{:S(2)}, u32[]{:S(2)}) collective-permute-start(f32[64,128]{1,0:T(8,128)S(1)} %add.6), channel_id=1, source_target_pairs={{0,2},{1,3},{2,0},{3,1},{4,6},{5,7},{6,4},{7,5},{8,10},{9,11},{10,... | collective-permute-start | bytes 98312 | tf_op jit(solution)/shard_map/ppermute | solution.py:324
  26.4 0.7 %shard_map.106 = f32[64,1024]{1,0:T(8,128)} custom-call(f32[16,1024]{1,0:T(8,128)S(1)} %shard_map.101.refs_0_, f32[16,1024]{1,0:T(8,128)S(1)} %collective-permute-done.5.refs_1_, f32[16,1024]{1,0:T(8,128)S(1)} %collective-permute-done.6.refs_2_.refs_0_, f32[16,1024]{1,0:T(8,128)S(1)} %collective-permute-done.9.refs_3_.refs_1_), custom_call_target="tpu_custom_call" | custom-call | bytes 524288 | tf_op jit(solution)/shard_map/pallas_call | solution.py:315
  27.1 2.1 %collective-permute-done.11 = f32[64,128]{1,0:T(8,128)S(1)} collective-permute-done((f32[64,128]{1,0:T(8,128)S(1)}, f32[64,128]{1,0:T(8,128)S(1)}, u32[]{:S(2)}, u32[]{:S(2)}) %collective-permute-start.11) | collective-permute-done | bytes 32800 | tf_op jit(solution)/shard_map/ppermute | solution.py:324
  29.2 0.6 %add_multiply_fusion = f32[64,128]{1,0:T(8,128)} fusion(f32[64,128]{1,0:T(8,128)S(1)} %add.6, f32[64,128]{1,0:T(8,128)S(1)} %collective-permute-done.11), kind=kLoop, calls=%fused_computation | loop fusion | flops 16384 | bytes 98304 | tf_op jit(solution)/shard_map/mul | solution.py:392
  (34 shorter events, 1.1 us)
Async XLA Ops:
  0.6 4.2 %copy-start.5 = (bf16[1024,64]{0,1:T(8,128)(2,1)S(1)}, bf16[1024,64]{0,1:T(8,128)(2,1)}, u32[]{:S(2)}) copy-start(bf16[1024,64]{0,1:T(8,128)(2,1)} %param.10) | copy-start | bytes 393220
  0.6 4.2 %copy-start.4 = (bf16[512,1024]{1,0:T(8,128)(2,1)S(1)}, bf16[512,1024]{1,0:T(8,128)(2,1)}, u32[]{:S(2)}) copy-start(bf16[512,1024]{1,0:T(8,128)(2,1)} %act_ref.1) | copy-start | bytes 3145732
  0.7 6.2 %copy-start.1 = (bf16[3584,64]{0,1:T(8,128)(2,1)S(1)}, bf16[3584,64]{0,1:T(8,128)(2,1)}, u32[]{:S(2)}) copy-start(bf16[3584,64]{0,1:T(8,128)(2,1)} %param.11) | copy-start | bytes 1376260
  0.7 6.2 %copy-start = (bf16[512,3584]{1,0:T(8,128)(2,1)S(1)}, bf16[512,3584]{1,0:T(8,128)(2,1)}, u32[]{:S(2)}) copy-start(bf16[512,3584]{1,0:T(8,128)(2,1)} %grad_ref.1) | copy-start | bytes 11010052
  0.7 10.7 %collective-permute-start.2 = (f32[32,1024]{1,0:T(8,128)}, f32[32,1024]{1,0:T(8,128)S(1)}, u32[]{:S(2)}, u32[]{:S(2)}) collective-permute-start(f32[32,1024]{1,0:T(8,128)} %refs_0_.1), channel_id=1, source_target_pairs={{0,8},{4,12},{8,0},{12,4},{1,9},{5,13},{9,1},{13,5},{2,10},{6,14},... | collective-permute-start | bytes 393224 | tf_op jit(solution)/shard_map/ppermute | solution.py:324
  4.8 3.8 %copy-start.2 = (f32[32,1024]{1,0:T(8,128)S(1)}, f32[32,1024]{1,0:T(8,128)}, u32[]{:S(2)}) copy-start(f32[32,1024]{1,0:T(8,128)} %refs_0_.1) | copy-start | bytes 393220
  4.8 5.4 %copy-start.6 = (s32[1,32]{1,0:T(1,128)S(1)}, s32[1,32]{1,0:T(1,128)}, u32[]{:S(2)}) copy-start(s32[1,32]{1,0:T(1,128)} %lengths_ref.1) | copy-start | bytes 388
  4.8 5.4 %copy-start.7 = (s32[32,1]{0,1:T(1,128)S(1)}, s32[32,1]{0,1:T(1,128)}, u32[]{:S(2)}) copy-start(s32[32,1]{0,1:T(1,128)} %param.13) | copy-start | bytes 388
  5.3 7.1 %collective-permute-start = (f32[64,512]{1,0:T(8,128)S(1)}, f32[64,512]{1,0:T(8,128)S(1)}, u32[]{:S(2)}, u32[]{:S(2)}) collective-permute-start(f32[64,512]{1,0:T(8,128)S(1)} %shard_map.97.refs_0_), channel_id=1, source_target_pairs={{0,2},{1,3},{2,0},{3,1},{4,6},{5,7},{6,4},{7,5},{8,10},{9,11},{10,... | collective-permute-start | bytes 393224 | tf_op jit(solution)/shard_map/ppermute | solution.py:324
  8.0 14.0 %copy-start.3 = (s32[128]{0:T(128)S(1)}, s32[128]{0:T(128)}, u32[]{:S(2)}) copy-start(s32[128]{0:T(128)} %param.15) | copy-start | bytes 1540
  8.0 4.3 %collective-permute-start.1 = (f32[32,512]{1,0:T(8,128)S(1)}, f32[32,512]{1,0:T(8,128)S(1)}, u32[]{:S(2)}, u32[]{:S(2)}) collective-permute-start(f32[32,512]{1,0:T(8,128)S(1)} %get-tuple-element.8), channel_id=1, source_target_pairs={{0,2},{1,3},{2,0},{3,1},{4,6},{5,7},{6,4},{7,5},{8,10},{9,11},{10,... | collective-permute-start | bytes 196616 | tf_op jit(solution)/shard_map/ppermute | solution.py:324
  8.6 9.9 %collective-permute-start.7 = (f32[32,1024]{1,0:T(8,128)S(1)}, f32[32,1024]{1,0:T(8,128)S(1)}, u32[]{:S(2)}, u32[]{:S(2)}) collective-permute-start(f32[32,1024]{1,0:T(8,128)S(1)} %copy-done.2), channel_id=1, source_target_pairs={{0,4},{4,0},{8,12},{12,8},{1,5},{5,1},{9,13},{13,9},{2,6},{6,2},{1... | collective-permute-start | bytes 393224 | tf_op jit(solution)/shard_map/ppermute | solution.py:324
  11.4 7.1 %collective-permute-start.8 = (f32[32,1024]{1,0:T(8,128)S(1)}, f32[32,1024]{1,0:T(8,128)S(1)}, u32[]{:S(2)}, u32[]{:S(2)}) collective-permute-start(f32[32,1024]{1,0:T(8,128)S(1)} %collective-permute-done.2.refs_0_.refs_1_), channel_id=1, source_target_pairs={{0,4},{4,0},{8,12},{12,8},{1,5},{5,1},{9,13},{13,9},{2,6},{6,2},{1... | collective-permute-start | bytes 393224 | tf_op jit(solution)/shard_map/ppermute | solution.py:324
  12.4 1.3 %collective-permute-start.3 = (f32[40,512]{1,0:T(8,128)S(1)}, f32[40,512]{1,0:T(8,128)S(1)}, u32[]{:S(2)}, u32[]{:S(2)}) collective-permute-start(f32[40,512]{1,0:T(8,128)S(1)} %get-tuple-element.10.refs_0_), channel_id=1, source_target_pairs={{0,1},{1,0},{2,3},{3,2},{4,5},{5,4},{6,7},{7,6},{8,9},{9,8},{10,11... | collective-permute-start | bytes 245768 | tf_op jit(solution)/shard_map/ppermute | solution.py:324
  12.4 1.4 %collective-permute-start.4 = (f32[40,512]{1,0:T(8,128)S(1)}, f32[40,512]{1,0:T(8,128)S(1)}, u32[]{:S(2)}, u32[]{:S(2)}) collective-permute-start(f32[40,512]{1,0:T(8,128)S(1)} %get-tuple-element.11.refs_1_), channel_id=1, source_target_pairs={{0,1},{1,0},{2,3},{3,2},{4,5},{5,4},{6,7},{7,6},{8,9},{9,8},{10,11... | collective-permute-start | bytes 245768 | tf_op jit(solution)/shard_map/ppermute | solution.py:324
  14.3 7.7 %collective-permute-start.5 = (f32[16,1024]{1,0:T(8,128)S(1)}, f32[16,1024]{1,0:T(8,128)S(1)}, u32[]{:S(2)}, u32[]{:S(2)}) collective-permute-start(f32[16,1024]{1,0:T(8,128)S(1)} %shard_map.102), channel_id=1, source_target_pairs={{0,4},{4,8},{8,12},{12,0},{1,5},{5,9},{9,13},{13,1},{2,6},{6,10},{... | collective-permute-start | bytes 196616 | tf_op jit(solution)/shard_map/ppermute | solution.py:329
  16.3 7.3 %collective-permute-start.6 = (f32[16,1024]{1,0:T(8,128)S(1)}, f32[16,1024]{1,0:T(8,128)S(1)}, u32[]{:S(2)}, u32[]{:S(2)}) collective-permute-start(f32[16,1024]{1,0:T(8,128)S(1)} %shard_map.103), channel_id=1, source_target_pairs={{0,8},{4,12},{8,0},{12,4},{1,9},{5,13},{9,1},{13,5},{2,10},{6,14},... | collective-permute-start | bytes 196616 | tf_op jit(solution)/shard_map/ppermute | solution.py:329
  18.5 5.2 %collective-permute-start.9 = (f32[16,1024]{1,0:T(8,128)S(1)}, f32[16,1024]{1,0:T(8,128)S(1)}, u32[]{:S(2)}, u32[]{:S(2)}) collective-permute-start(f32[16,1024]{1,0:T(8,128)S(1)} %shard_map.105), channel_id=1, source_target_pairs={{0,12},{4,0},{8,4},{12,8},{1,13},{5,1},{9,5},{13,9},{2,14},{6,2},{... | collective-permute-start | bytes 196616 | tf_op jit(solution)/shard_map/ppermute | solution.py:329
  24.0 1.2 %collective-permute-start.10 = (f32[64,128]{1,0:T(8,128)S(1)}, f32[64,128]{1,0:T(8,128)S(1)}, u32[]{:S(2)}, u32[]{:S(2)}) collective-permute-start(f32[64,128]{1,0:T(8,128)S(1)} %shard_map.110), channel_id=1, source_target_pairs={{0,1},{1,0},{2,3},{3,2},{4,5},{5,4},{6,7},{7,6},{8,9},{9,8},{10,11... | collective-permute-start | bytes 98312 | tf_op jit(solution)/shard_map/ppermute | solution.py:324
  25.3 3.9 %collective-permute-start.11 = (f32[64,128]{1,0:T(8,128)S(1)}, f32[64,128]{1,0:T(8,128)S(1)}, u32[]{:S(2)}, u32[]{:S(2)}) collective-permute-start(f32[64,128]{1,0:T(8,128)S(1)} %add.6), channel_id=1, source_target_pairs={{0,2},{1,3},{2,0},{3,1},{4,6},{5,7},{6,4},{7,5},{8,10},{9,11},{10,... | collective-permute-start | bytes 98312 | tf_op jit(solution)/shard_map/ppermute | solution.py:324

commit v23 on v20

--- a/solution.py
+++ b/solution.py
@@ -383,7 +383,7 @@
         soon = [outer(own, gots, keep, mask, cap, k, 1)[0] for k in range(split)]
         rows = [shift(block, "dp", k) for k, block in enumerate(soon, 1)]
         *sent, kept = outer(own, gots, keep, mask, cap, split, data_size - split)
-        sent[-1] = after(sent[-1], [mate, *passed])
+        sent[-1] = after(sent[-1], [mate])
         rows = [kept, *rows, *(shift(block, "dp", k) for k, block in enumerate(sent, 1 + split))]
         store = place(rows)
         late = [token(rows[2:-1], LATE_FLOPS)]

time: 29.7 us -> 30.3 us (1.020)
  waiting for transfers between devices: 6.46 us -> 8.27 us
  starting transfers between devices: 16.9 us -> 15.7 us
    ppermute x3, starting transfers between devices: 6.27 us -> 4.7 us  [shift(): return lax.ppermute(x, axis, [(i, (i + by) % size) for i in range(size)])]
    ppermute x3, waiting for transfers between devices: 1.45 us -> 2.98 us  [shift(): return lax.ppermute(x, axis, [(i, (i + by) % size) for i in range(size)])]
    ppermute x9, starting transfers between devices: 10.6 us -> 11 us  [swap(): lax.ppermute(x, axis, [(i, i ^ gap) for i in range(lax.axis_size(axis))])]
  transfers between devices with their start and end apart: 12 -> 12, of which waited for: 8 -> 7; matrix products, arithmetic and copies ran while one was open for 0% -> 0% of each run, Pallas kernels for 15% -> 15%
where the time goes in v23:
time: 30.3 us; the launch traced here: 30.2 us
  starting transfers between devices  15.7 us (52%)
  waiting for transfers between devices  8.27 us (27%)
  Pallas kernels  4.79 us (16%)
  between operations  0.75 us (2%)
  other arithmetic  0.63 us (2%)
    ppermute x9, starting transfers between devices, swap(): lax.ppermute(x, axis, [(i, i ^ gap) for i in range(lax.axis_size(axis))])  11 us
    ppermute x9, waiting for transfers between devices, swap(): lax.ppermute(x, axis, [(i, i ^ gap) for i in range(lax.axis_size(axis))])  5.29 us
    ppermute x3, starting transfers between devices, shift(): return lax.ppermute(x, axis, [(i, (i + by) % size) for i in range(size)])  4.7 us
    ppermute x3, waiting for transfers between devices, shift(): return lax.ppermute(x, axis, [(i, (i + by) % size) for i in range(size)])  2.98 us
    pallas_call x3, Pallas kernels, outer(): pl.pallas_call(functools.partial(outer_kernel, first, owners, len(sent)),...  1.43 us
    pallas_call x1, Pallas kernels, project_g(): pl.pallas_call(functools.partial(g_kernel, width), out_shape=[part, part]...  1.16 us
    pallas_call x1, Pallas kernels, place(): pl.pallas_call(place_kernel, out_shape=jax.ShapeDtypeStruct((slots, feats...  0.72 us
    mul x1, other arithmetic, local(): return (store, scores * (1.0 / (rank * rank)))  0.62 us
  transfers between devices with their start and end apart: 12, of which 7 were waited for; matrix products, arithmetic and copies ran while one was open for 0% of the time, Pallas kernels for 15%

profile of v23, /device:TPU:0, one launch (start us, length us, event | category | flops | bytes accessed | tf_op | source)
XLA Modules:
  0.0 30.2 jit_solution(15006764183690693580)
XLA Ops:
  0.7 4.1 %collective-permute-start.2 = (f32[32,1024]{1,0:T(8,128)}, f32[32,1024]{1,0:T(8,128)S(1)}, u32[]{:S(2)}, u32[]{:S(2)}) collective-permute-start(f32[32,1024]{1,0:T(8,128)} %refs_0_.1), channel_id=1, source_target_pairs={{0,8},{4,12},{8,0},{12,4},{1,9},{5,13},{9,1},{13,5},{2,10},{6,14},... | collective-permute-start | bytes 393224 | tf_op jit(solution)/shard_map/ppermute | solution.py:333
  4.8 0.5 %shard_map.97.refs_0_ = f32[64,512]{1,0:T(8,128)S(1)} custom-call(bf16[512,1024]{1,0:T(8,128)(2,1)S(1)} %copy-done.4, bf16[64,1024]{1,0:T(8,128)(2,1)S(1)} %bitcast.7, f32[8,128]{1,0:T(8,128)S(1)} %shard_map.96.refs_0_), custom_call_target="tpu_custom_call" | custom-call | flops 600000000 | tf_op jit(solution)/shard_map/pallas_call | solution.py:90
  5.3 1.5 %collective-permute-start = (f32[64,512]{1,0:T(8,128)S(1)}, f32[64,512]{1,0:T(8,128)S(1)}, u32[]{:S(2)}, u32[]{:S(2)}) collective-permute-start(f32[64,512]{1,0:T(8,128)S(1)} %shard_map.97.refs_0_), channel_id=1, source_target_pairs={{0,2},{1,3},{2,0},{3,1},{4,6},{5,7},{6,4},{7,5},{8,10},{9,11},{10,... | collective-permute-start | bytes 393224 | tf_op jit(solution)/shard_map/ppermute | solution.py:333
  6.8 1.2 %shard_map.95 = (f32[32,512]{1,0:T(8,128)S(1)}, f32[32,512]{1,0:T(8,128)S(1)}) custom-call(bf16[512,3584]{1,0:T(8,128)(2,1)S(1)} %copy-done, bf16[64,3584]{1,0:T(8,128)(2,1)S(1)} %bitcast.4), custom_call_target="tpu_custom_call" | custom-call | tf_op jit(solution)/shard_map/pallas_call | solution.py:113
  8.0 0.6 %collective-permute-start.1 = (f32[32,512]{1,0:T(8,128)S(1)}, f32[32,512]{1,0:T(8,128)S(1)}, u32[]{:S(2)}, u32[]{:S(2)}) collective-permute-start(f32[32,512]{1,0:T(8,128)S(1)} %get-tuple-element.10), channel_id=1, source_target_pairs={{0,2},{1,3},{2,0},{3,1},{4,6},{5,7},{6,4},{7,5},{8,10},{9,11},{10,... | collective-permute-start | bytes 196616 | tf_op jit(solution)/shard_map/ppermute | solution.py:333
  8.6 1.6 %collective-permute-start.7 = (f32[32,1024]{1,0:T(8,128)S(1)}, f32[32,1024]{1,0:T(8,128)S(1)}, u32[]{:S(2)}, u32[]{:S(2)}) collective-permute-start(f32[32,1024]{1,0:T(8,128)S(1)} %copy-done.2), channel_id=1, source_target_pairs={{0,4},{4,0},{8,12},{12,8},{1,5},{5,1},{9,13},{13,9},{2,6},{6,2},{1... | collective-permute-start | bytes 393224 | tf_op jit(solution)/shard_map/ppermute | solution.py:333
  10.4 1.0 %collective-permute-done.2.refs_0_.refs_1_ = f32[32,1024]{1,0:T(8,128)S(1)} collective-permute-done((f32[32,1024]{1,0:T(8,128)}, f32[32,1024]{1,0:T(8,128)S(1)}, u32[]{:S(2)}, u32[]{:S(2)}) %collective-permute-start.2) | collective-permute-done | bytes 131104 | tf_op jit(solution)/shard_map/ppermute | solution.py:333
  11.4 0.9 %collective-permute-done.1.refs_2_ = f32[32,512]{1,0:T(8,128)S(1)} collective-permute-done((f32[32,512]{1,0:T(8,128)S(1)}, f32[32,512]{1,0:T(8,128)S(1)}, u32[]{:S(2)}, u32[]{:S(2)}) %collective-permute-start.1) | collective-permute-done | bytes 65568 | tf_op jit(solution)/shard_map/ppermute | solution.py:333
  12.4 0.5 %collective-permute-start.4 = (f32[40,512]{1,0:T(8,128)S(1)}, f32[40,512]{1,0:T(8,128)S(1)}, u32[]{:S(2)}, u32[]{:S(2)}) collective-permute-start(f32[40,512]{1,0:T(8,128)S(1)} %get-tuple-element.13.refs_1_), channel_id=1, source_target_pairs={{0,1},{1,0},{2,3},{3,2},{4,5},{5,4},{6,7},{7,6},{8,9},{9,8},{10,11... | collective-permute-start | bytes 245768 | tf_op jit(solution)/shard_map/ppermute | solution.py:333
  12.9 1.6 %collective-permute-start.9 = (f32[32,1024]{1,0:T(8,128)S(1)}, f32[32,1024]{1,0:T(8,128)S(1)}, u32[]{:S(2)}, u32[]{:S(2)}) collective-permute-start(f32[32,1024]{1,0:T(8,128)S(1)} %collective-permute-done.2.refs_0_.refs_1_), channel_id=1, source_target_pairs={{0,4},{4,0},{8,12},{12,8},{1,5},{5,1},{9,13},{13,9},{2,6},{6,2},{1... | collective-permute-start | bytes 393224 | tf_op jit(solution)/shard_map/ppermute | solution.py:333
  14.5 0.4 %shard_map.102 = f32[16,1024]{1,0:T(8,128)S(1)} custom-call(f32[16,512]{1,0:T(8,128)S(1)} %get-tuple-element.11.g_ref, bf16[64,512]{1,0:T(8,128)(2,1)S(1)} %shard_map.98.refs_3_.mask_ref, f32[40,512]{1,0:T(8,128)S(1)} %get-tuple-element.12.refs_0_, f32[40,512]{1,0:T(8,128)S(1)} %get-tuple-element.13.refs_1_, f32[40,512]{1,0:T(8,128)S(1)} %collective-permute-done.3.refs_2_, ...), custom_call_target="tpu_custom_call" | custom-call | flops 67108864 | tf_op jit(solution)/shard_map/pallas_call | solution.py:201
  14.9 1.0 %collective-permute-start.5 = (f32[16,1024]{1,0:T(8,128)S(1)}, f32[16,1024]{1,0:T(8,128)S(1)}, u32[]{:S(2)}, u32[]{:S(2)}) collective-permute-start(f32[16,1024]{1,0:T(8,128)S(1)} %shard_map.102), channel_id=1, source_target_pairs={{0,4},{4,8},{8,12},{12,0},{1,5},{5,9},{9,13},{13,1},{2,6},{6,10},{... | collective-permute-start | bytes 196616 | tf_op jit(solution)/shard_map/ppermute | solution.py:338
  15.9 0.4 %shard_map.103 = f32[16,1024]{1,0:T(8,128)S(1)} custom-call(f32[16,512]{1,0:T(8,128)S(1)} %get-tuple-element.11.g_ref, bf16[64,512]{1,0:T(8,128)(2,1)S(1)} %shard_map.98.refs_3_.mask_ref, f32[40,512]{1,0:T(8,128)S(1)} %get-tuple-element.12.refs_0_, f32[40,512]{1,0:T(8,128)S(1)} %get-tuple-element.13.refs_1_, f32[40,512]{1,0:T(8,128)S(1)} %collective-permute-done.3.refs_2_, ...), custom_call_target="tpu_custom_call" | custom-call | flops 67108864 | tf_op jit(solution)/shard_map/pallas_call | solution.py:201
  16.3 1.7 %collective-permute-start.6 = (f32[16,1024]{1,0:T(8,128)S(1)}, f32[16,1024]{1,0:T(8,128)S(1)}, u32[]{:S(2)}, u32[]{:S(2)}) collective-permute-start(f32[16,1024]{1,0:T(8,128)S(1)} %shard_map.103), channel_id=1, source_target_pairs={{0,8},{4,12},{8,0},{12,4},{1,9},{5,13},{9,1},{13,5},{2,10},{6,14},... | collective-permute-start | bytes 196616 | tf_op jit(solution)/shard_map/ppermute | solution.py:338
  18.0 0.6 %shard_map.101 = (f32[16,1024]{1,0:T(8,128)S(1)}, f32[16,1024]{1,0:T(8,128)S(1)}) custom-call(f32[16,512]{1,0:T(8,128)S(1)} %get-tuple-element.11.g_ref, bf16[64,512]{1,0:T(8,128)(2,1)S(1)} %shard_map.98.refs_3_.mask_ref, f32[40,512]{1,0:T(8,128)S(1)} %get-tuple-element.12.refs_0_, f32[40,512]{1,0:T(8,128)S(1)} %get-tuple-element.13.refs_1_, ...), custom_call_target="tpu_custom_call" | custom-call | flops 134217728 | tf_op jit(solution)/shard_map/pallas_call | solution.py:201
  18.6 2.1 %collective-permute-start.8 = (f32[16,1024]{1,0:T(8,128)S(1)}, f32[16,1024]{1,0:T(8,128)S(1)}, u32[]{:S(2)}, u32[]{:S(2)}) collective-permute-start(f32[16,1024]{1,0:T(8,128)S(1)} %shard_map.104), channel_id=1, source_target_pairs={{0,12},{4,0},{8,4},{12,8},{1,13},{5,1},{9,5},{13,9},{2,14},{6,2},{... | collective-permute-start | bytes 196616 | tf_op jit(solution)/shard_map/ppermute | solution.py:338
  20.8 0.9 %collective-permute-done.5.refs_1_ = f32[16,1024]{1,0:T(8,128)S(1)} collective-permute-done((f32[16,1024]{1,0:T(8,128)S(1)}, f32[16,1024]{1,0:T(8,128)S(1)}, u32[]{:S(2)}, u32[]{:S(2)}) %collective-permute-start.5) | collective-permute-done | bytes 65568 | tf_op jit(solution)/shard_map/ppermute | solution.py:338
  22.0 1.7 %collective-permute-done.6.refs_2_.refs_0_ = f32[16,1024]{1,0:T(8,128)S(1)} collective-permute-done((f32[16,1024]{1,0:T(8,128)S(1)}, f32[16,1024]{1,0:T(8,128)S(1)}, u32[]{:S(2)}, u32[]{:S(2)}) %collective-permute-start.6) | collective-permute-done | bytes 65568 | tf_op jit(solution)/shard_map/ppermute | solution.py:338
  23.6 0.5 %collective-permute-done.8.refs_3_.refs_1_ = f32[16,1024]{1,0:T(8,128)S(1)} collective-permute-done((f32[16,1024]{1,0:T(8,128)S(1)}, f32[16,1024]{1,0:T(8,128)S(1)}, u32[]{:S(2)}, u32[]{:S(2)}) %collective-permute-start.8) | collective-permute-done | bytes 65568 | tf_op jit(solution)/shard_map/ppermute | solution.py:338
  24.4 1.2 %collective-permute-done.10 = f32[64,128]{1,0:T(8,128)S(1)} collective-permute-done((f32[64,128]{1,0:T(8,128)S(1)}, f32[64,128]{1,0:T(8,128)S(1)}, u32[]{:S(2)}, u32[]{:S(2)}) %collective-permute-start.10) | collective-permute-done | bytes 32800 | tf_op jit(solution)/shard_map/ppermute | solution.py:333
  25.7 1.1 %collective-permute-start.11 = (f32[64,128]{1,0:T(8,128)S(1)}, f32[64,128]{1,0:T(8,128)S(1)}, u32[]{:S(2)}, u32[]{:S(2)}) collective-permute-start(f32[64,128]{1,0:T(8,128)S(1)} %add.6), channel_id=1, source_target_pairs={{0,2},{1,3},{2,0},{3,1},{4,6},{5,7},{6,4},{7,5},{8,10},{9,11},{10,... | collective-permute-start | bytes 98312 | tf_op jit(solution)/shard_map/ppermute | solution.py:333
  26.7 0.7 %shard_map.105 = f32[64,1024]{1,0:T(8,128)} custom-call(f32[16,1024]{1,0:T(8,128)S(1)} %get-tuple-element.14.refs_0_, f32[16,1024]{1,0:T(8,128)S(1)} %collective-permute-done.5.refs_1_, f32[16,1024]{1,0:T(8,128)S(1)} %collective-permute-done.6.refs_2_.refs_0_, f32[16,1024]{1,0:T(8,128)S(1)} %collective-permute-done.8.refs_3_.refs_1_), custom_call_target="tpu_custom_call" | custom-call | bytes 524288 | tf_op jit(solution)/shard_map/pallas_call | solution.py:324
  27.4 2.1 %collective-permute-done.11 = f32[64,128]{1,0:T(8,128)S(1)} collective-permute-done((f32[64,128]{1,0:T(8,128)S(1)}, f32[64,128]{1,0:T(8,128)S(1)}, u32[]{:S(2)}, u32[]{:S(2)}) %collective-permute-start.11) | collective-permute-done | bytes 32800 | tf_op jit(solution)/shard_map/ppermute | solution.py:333
  29.6 0.6 %add_multiply_fusion = f32[64,128]{1,0:T(8,128)} fusion(f32[64,128]{1,0:T(8,128)S(1)} %add.6, f32[64,128]{1,0:T(8,128)S(1)} %collective-permute-done.11), kind=kLoop, calls=%fused_computation | loop fusion | flops 16384 | bytes 98304 | tf_op jit(solution)/shard_map/mul | solution.py:403
  (33 shorter events, 1.1 us)
Async XLA Ops:
  0.6 4.2 %copy-start.5 = (bf16[1024,64]{0,1:T(8,128)(2,1)S(1)}, bf16[1024,64]{0,1:T(8,128)(2,1)}, u32[]{:S(2)}) copy-start(bf16[1024,64]{0,1:T(8,128)(2,1)} %param.10) | copy-start | bytes 393220
  0.6 4.2 %copy-start.4 = (bf16[512,1024]{1,0:T(8,128)(2,1)S(1)}, bf16[512,1024]{1,0:T(8,128)(2,1)}, u32[]{:S(2)}) copy-start(bf16[512,1024]{1,0:T(8,128)(2,1)} %act_ref.1) | copy-start | bytes 3145732
  0.7 6.2 %copy-start.1 = (bf16[3584,64]{0,1:T(8,128)(2,1)S(1)}, bf16[3584,64]{0,1:T(8,128)(2,1)}, u32[]{:S(2)}) copy-start(bf16[3584,64]{0,1:T(8,128)(2,1)} %param.11) | copy-start | bytes 1376260
  0.7 6.2 %copy-start = (bf16[512,3584]{1,0:T(8,128)(2,1)S(1)}, bf16[512,3584]{1,0:T(8,128)(2,1)}, u32[]{:S(2)}) copy-start(bf16[512,3584]{1,0:T(8,128)(2,1)} %grad_ref.1) | copy-start | bytes 11010052
  0.7 10.7 %collective-permute-start.2 = (f32[32,1024]{1,0:T(8,128)}, f32[32,1024]{1,0:T(8,128)S(1)}, u32[]{:S(2)}, u32[]{:S(2)}) collective-permute-start(f32[32,1024]{1,0:T(8,128)} %refs_0_.1), channel_id=1, source_target_pairs={{0,8},{4,12},{8,0},{12,4},{1,9},{5,13},{9,1},{13,5},{2,10},{6,14},... | collective-permute-start | bytes 393224 | tf_op jit(solution)/shard_map/ppermute | solution.py:333
  4.8 3.8 %copy-start.2 = (f32[32,1024]{1,0:T(8,128)S(1)}, f32[32,1024]{1,0:T(8,128)}, u32[]{:S(2)}) copy-start(f32[32,1024]{1,0:T(8,128)} %refs_0_.1) | copy-start | bytes 393220
  4.8 5.4 %copy-start.6 = (s32[1,32]{1,0:T(1,128)S(1)}, s32[1,32]{1,0:T(1,128)}, u32[]{:S(2)}) copy-start(s32[1,32]{1,0:T(1,128)} %lengths_ref.1) | copy-start | bytes 388
  4.8 5.4 %copy-start.7 = (s32[32,1]{0,1:T(1,128)S(1)}, s32[32,1]{0,1:T(1,128)}, u32[]{:S(2)}) copy-start(s32[32,1]{0,1:T(1,128)} %param.13) | copy-start | bytes 388
  5.3 7.1 %collective-permute-start = (f32[64,512]{1,0:T(8,128)S(1)}, f32[64,512]{1,0:T(8,128)S(1)}, u32[]{:S(2)}, u32[]{:S(2)}) collective-permute-start(f32[64,512]{1,0:T(8,128)S(1)} %shard_map.97.refs_0_), channel_id=1, source_target_pairs={{0,2},{1,3},{2,0},{3,1},{4,6},{5,7},{6,4},{7,5},{8,10},{9,11},{10,... | collective-permute-start | bytes 393224 | tf_op jit(solution)/shard_map/ppermute | solution.py:333
  6.8 14.8 %copy-start.3 = (s32[128]{0:T(128)S(1)}, s32[128]{0:T(128)}, u32[]{:S(2)}) copy-start(s32[128]{0:T(128)} %param.15) | copy-start | bytes 1540
  8.0 4.3 %collective-permute-start.1 = (f32[32,512]{1,0:T(8,128)S(1)}, f32[32,512]{1,0:T(8,128)S(1)}, u32[]{:S(2)}, u32[]{:S(2)}) collective-permute-start(f32[32,512]{1,0:T(8,128)S(1)} %get-tuple-element.10), channel_id=1, source_target_pairs={{0,2},{1,3},{2,0},{3,1},{4,6},{5,7},{6,4},{7,5},{8,10},{9,11},{10,... | collective-permute-start | bytes 196616 | tf_op jit(solution)/shard_map/ppermute | solution.py:333
  8.6 10.0 %collective-permute-start.7 = (f32[32,1024]{1,0:T(8,128)S(1)}, f32[32,1024]{1,0:T(8,128)S(1)}, u32[]{:S(2)}, u32[]{:S(2)}) collective-permute-start(f32[32,1024]{1,0:T(8,128)S(1)} %copy-done.2), channel_id=1, source_target_pairs={{0,4},{4,0},{8,12},{12,8},{1,5},{5,1},{9,13},{13,9},{2,6},{6,2},{1... | collective-permute-start | bytes 393224 | tf_op jit(solution)/shard_map/ppermute | solution.py:333
  12.3 2.2 %collective-permute-start.3 = (f32[40,512]{1,0:T(8,128)S(1)}, f32[40,512]{1,0:T(8,128)S(1)}, u32[]{:S(2)}, u32[]{:S(2)}) collective-permute-start(f32[40,512]{1,0:T(8,128)S(1)} %get-tuple-element.12.refs_0_), channel_id=1, source_target_pairs={{0,1},{1,0},{2,3},{3,2},{4,5},{5,4},{6,7},{7,6},{8,9},{9,8},{10,11... | collective-permute-start | bytes 245768 | tf_op jit(solution)/shard_map/ppermute | solution.py:333
  12.4 2.1 %collective-permute-start.4 = (f32[40,512]{1,0:T(8,128)S(1)}, f32[40,512]{1,0:T(8,128)S(1)}, u32[]{:S(2)}, u32[]{:S(2)}) collective-permute-start(f32[40,512]{1,0:T(8,128)S(1)} %get-tuple-element.13.refs_1_), channel_id=1, source_target_pairs={{0,1},{1,0},{2,3},{3,2},{4,5},{5,4},{6,7},{7,6},{8,9},{9,8},{10,11... | collective-permute-start | bytes 245768 | tf_op jit(solution)/shard_map/ppermute | solution.py:333
  12.9 7.7 %collective-permute-start.9 = (f32[32,1024]{1,0:T(8,128)S(1)}, f32[32,1024]{1,0:T(8,128)S(1)}, u32[]{:S(2)}, u32[]{:S(2)}) collective-permute-start(f32[32,1024]{1,0:T(8,128)S(1)} %collective-permute-done.2.refs_0_.refs_1_), channel_id=1, source_target_pairs={{0,4},{4,0},{8,12},{12,8},{1,5},{5,1},{9,13},{13,9},{2,6},{6,2},{1... | collective-permute-start | bytes 393224 | tf_op jit(solution)/shard_map/ppermute | solution.py:333
  14.9 6.7 %collective-permute-start.5 = (f32[16,1024]{1,0:T(8,128)S(1)}, f32[16,1024]{1,0:T(8,128)S(1)}, u32[]{:S(2)}, u32[]{:S(2)}) collective-permute-start(f32[16,1024]{1,0:T(8,128)S(1)} %shard_map.102), channel_id=1, source_target_pairs={{0,4},{4,8},{8,12},{12,0},{1,5},{5,9},{9,13},{13,1},{2,6},{6,10},{... | collective-permute-start | bytes 196616 | tf_op jit(solution)/shard_map/ppermute | solution.py:338
  16.3 7.3 %collective-permute-start.6 = (f32[16,1024]{1,0:T(8,128)S(1)}, f32[16,1024]{1,0:T(8,128)S(1)}, u32[]{:S(2)}, u32[]{:S(2)}) collective-permute-start(f32[16,1024]{1,0:T(8,128)S(1)} %shard_map.103), channel_id=1, source_target_pairs={{0,8},{4,12},{8,0},{12,4},{1,9},{5,13},{9,1},{13,5},{2,10},{6,14},... | collective-permute-start | bytes 196616 | tf_op jit(solution)/shard_map/ppermute | solution.py:338
  18.6 5.5 %collective-permute-start.8 = (f32[16,1024]{1,0:T(8,128)S(1)}, f32[16,1024]{1,0:T(8,128)S(1)}, u32[]{:S(2)}, u32[]{:S(2)}) collective-permute-start(f32[16,1024]{1,0:T(8,128)S(1)} %shard_map.104), channel_id=1, source_target_pairs={{0,12},{4,0},{8,4},{12,8},{1,13},{5,1},{9,5},{13,9},{2,14},{6,2},{... | collective-permute-start | bytes 196616 | tf_op jit(solution)/shard_map/ppermute | solution.py:338
  24.4 1.2 %collective-permute-start.10 = (f32[64,128]{1,0:T(8,128)S(1)}, f32[64,128]{1,0:T(8,128)S(1)}, u32[]{:S(2)}, u32[]{:S(2)}) collective-permute-start(f32[64,128]{1,0:T(8,128)S(1)} %shard_map.109), channel_id=1, source_target_pairs={{0,1},{1,0},{2,3},{3,2},{4,5},{5,4},{6,7},{7,6},{8,9},{9,8},{10,11... | collective-permute-start | bytes 98312 | tf_op jit(solution)/shard_map/ppermute | solution.py:333
  25.7 3.9 %collective-permute-start.11 = (f32[64,128]{1,0:T(8,128)S(1)}, f32[64,128]{1,0:T(8,128)S(1)}, u32[]{:S(2)}, u32[]{:S(2)}) collective-permute-start(f32[64,128]{1,0:T(8,128)S(1)} %add.6), channel_id=1, source_target_pairs={{0,2},{1,3},{2,0},{3,1},{4,6},{5,7},{6,4},{7,5},{8,10},{9,11},{10,... | collective-permute-start | bytes 98312 | tf_op jit(solution)/shard_map/ppermute | solution.py:333

commit v24 on v20

--- a/solution.py
+++ b/solution.py
@@ -12,6 +12,7 @@
 MIB = 1024 * 1024
 NT = (((1,), (1,)), ((), ()))
 MOST_DIRECT = 8
+MOST_AT_ONCE = 4
 GROUP = 16
 ROWS = 16
 LANES = 128
@@ -396,10 +397,17 @@
         store = lax.all_to_all(jnp.stack(blocks), "dp", 0, 0, tiled=True).reshape(-1, width * rank)
         pool = pool_halves(pieces)
         scores = score(ids_row, pool, ids_row, [store], gaps, False, [])
-    bit = 1
-    while bit < tensor_size:
-        scores = scores + swap(scores, "tensor", bit)
-        bit *= 2
+    if tensor_size <= MOST_AT_ONCE:
+        gots = {gap: swap(scores, "tensor", gap) for gap in range(tensor_size - 1, 0, -1)}
+        parts = [scores] + [gots[gap] for gap in range(1, tensor_size)]
+        while len(parts) > 1:
+            parts = [one + two for one, two in zip(parts[::2], parts[1::2])]
+        scores = parts[0]
+    else:
+        bit = 1
+        while bit < tensor_size:
+            scores = scores + swap(scores, "tensor", bit)
+            bit *= 2
     return store, scores * (1.0 / (rank * rank))
 
 

time: 29.7 us -> 28.8 us (0.970)
  waiting for transfers between devices: 6.46 us -> 5.18 us
  starting transfers between devices: 16.9 us -> 17.3 us
    ppermute x9 -> x10, waiting for transfers between devices: 5.01 us -> 3.73 us  [swap(): lax.ppermute(x, axis, [(i, i ^ gap) for i in range(lax.axis_size(axis))])]
    ppermute x9 -> x10, starting transfers between devices: 10.6 us -> 11 us  [swap(): lax.ppermute(x, axis, [(i, i ^ gap) for i in range(lax.axis_size(axis))])]
  transfers between devices with their start and end apart: 12 -> 13, of which waited for: 8 -> 8; matrix products, arithmetic and copies ran while one was open for 0% -> 0% of each run, Pallas kernels for 15% -> 15%
where the time goes in v24:
time: 28.8 us; the launch traced here: 28.7 us
  starting transfers between devices  17.3 us (60%)
  waiting for transfers between devices  5.18 us (18%)
  Pallas kernels  4.8 us (17%)
  between operations  0.77 us (3%)
  other arithmetic  0.63 us (2%)
    ppermute x10, starting transfers between devices, swap(): lax.ppermute(x, axis, [(i, i ^ gap) for i in range(lax.axis_size(axis))])  11 us
    ppermute x3, starting transfers between devices, shift(): return lax.ppermute(x, axis, [(i, (i + by) % size) for i in range(size)])  6.27 us
    ppermute x10, waiting for transfers between devices, swap(): lax.ppermute(x, axis, [(i, i ^ gap) for i in range(lax.axis_size(axis))])  3.73 us
    ppermute x3, waiting for transfers between devices, shift(): return lax.ppermute(x, axis, [(i, (i + by) % size) for i in range(size)])  1.45 us
    pallas_call x3, Pallas kernels, outer(): pl.pallas_call(functools.partial(outer_kernel, first, owners, len(sent)),...  1.43 us
    pallas_call x1, Pallas kernels, project_g(): pl.pallas_call(functools.partial(g_kernel, width), out_shape=[part, part]...  1.16 us
    pallas_call x1, Pallas kernels, place(): pl.pallas_call(place_kernel, out_shape=jax.ShapeDtypeStruct((slots, feats...  0.72 us
    mul x1, other arithmetic, local(): return (store, scores * (1.0 / (rank * rank)))  0.63 us
  transfers between devices with their start and end apart: 13, of which 8 were waited for; matrix products, arithmetic and copies ran while one was open for 0% of the time, Pallas kernels for 15%

profile of v24, /device:TPU:0, one launch (start us, length us, event | category | flops | bytes accessed | tf_op | source)
XLA Modules:
  0.0 28.7 jit_solution(1399134348920427271)
XLA Ops:
  0.7 4.1 %collective-permute-start.2 = (f32[32,1024]{1,0:T(8,128)}, f32[32,1024]{1,0:T(8,128)S(1)}, u32[]{:S(2)}, u32[]{:S(2)}) collective-permute-start(f32[32,1024]{1,0:T(8,128)} %refs_0_.1), channel_id=1, source_target_pairs={{0,8},{4,12},{8,0},{12,4},{1,9},{5,13},{9,1},{13,5},{2,10},{6,14},... | collective-permute-start | bytes 393224 | tf_op jit(solution)/shard_map/ppermute | solution.py:334
  4.8 0.5 %shard_map.97.refs_0_ = f32[64,512]{1,0:T(8,128)S(1)} custom-call(bf16[512,1024]{1,0:T(8,128)(2,1)S(1)} %copy-done.4, bf16[64,1024]{1,0:T(8,128)(2,1)S(1)} %bitcast.7, f32[8,128]{1,0:T(8,128)S(1)} %shard_map.96.refs_0_), custom_call_target="tpu_custom_call" | custom-call | flops 600000000 | tf_op jit(solution)/shard_map/pallas_call | solution.py:91
  5.3 1.5 %collective-permute-start = (f32[64,512]{1,0:T(8,128)S(1)}, f32[64,512]{1,0:T(8,128)S(1)}, u32[]{:S(2)}, u32[]{:S(2)}) collective-permute-start(f32[64,512]{1,0:T(8,128)S(1)} %shard_map.97.refs_0_), channel_id=1, source_target_pairs={{0,2},{1,3},{2,0},{3,1},{4,6},{5,7},{6,4},{7,5},{8,10},{9,11},{10,... | collective-permute-start | bytes 393224 | tf_op jit(solution)/shard_map/ppermute | solution.py:334
  6.8 1.2 %shard_map.95 = (f32[32,512]{1,0:T(8,128)S(1)}, f32[32,512]{1,0:T(8,128)S(1)}) custom-call(bf16[512,3584]{1,0:T(8,128)(2,1)S(1)} %copy-done, bf16[64,3584]{1,0:T(8,128)(2,1)S(1)} %bitcast.4), custom_call_target="tpu_custom_call" | custom-call | tf_op jit(solution)/shard_map/pallas_call | solution.py:114
  8.0 0.6 %collective-permute-start.1 = (f32[32,512]{1,0:T(8,128)S(1)}, f32[32,512]{1,0:T(8,128)S(1)}, u32[]{:S(2)}, u32[]{:S(2)}) collective-permute-start(f32[32,512]{1,0:T(8,128)S(1)} %get-tuple-element.10), channel_id=1, source_target_pairs={{0,2},{1,3},{2,0},{3,1},{4,6},{5,7},{6,4},{7,5},{8,10},{9,11},{10,... | collective-permute-start | bytes 196616 | tf_op jit(solution)/shard_map/ppermute | solution.py:334
  8.6 1.6 %collective-permute-start.7 = (f32[32,1024]{1,0:T(8,128)S(1)}, f32[32,1024]{1,0:T(8,128)S(1)}, u32[]{:S(2)}, u32[]{:S(2)}) collective-permute-start(f32[32,1024]{1,0:T(8,128)S(1)} %copy-done.2), channel_id=1, source_target_pairs={{0,4},{4,0},{8,12},{12,8},{1,5},{5,1},{9,13},{13,9},{2,6},{6,2},{1... | collective-permute-start | bytes 393224 | tf_op jit(solution)/shard_map/ppermute | solution.py:334
  10.4 1.0 %collective-permute-done.2.refs_0_.refs_1_ = f32[32,1024]{1,0:T(8,128)S(1)} collective-permute-done((f32[32,1024]{1,0:T(8,128)}, f32[32,1024]{1,0:T(8,128)S(1)}, u32[]{:S(2)}, u32[]{:S(2)}) %collective-permute-start.2) | collective-permute-done | bytes 131104 | tf_op jit(solution)/shard_map/ppermute | solution.py:334
  11.4 0.7 %collective-permute-start.8 = (f32[32,1024]{1,0:T(8,128)S(1)}, f32[32,1024]{1,0:T(8,128)S(1)}, u32[]{:S(2)}, u32[]{:S(2)}) collective-permute-start(f32[32,1024]{1,0:T(8,128)S(1)} %collective-permute-done.2.refs_0_.refs_1_), channel_id=1, source_target_pairs={{0,4},{4,0},{8,12},{12,8},{1,5},{5,1},{9,13},{13,9},{2,6},{6,2},{1... | collective-permute-start | bytes 393224 | tf_op jit(solution)/shard_map/ppermute | solution.py:334
  12.4 0.5 %collective-permute-start.4 = (f32[40,512]{1,0:T(8,128)S(1)}, f32[40,512]{1,0:T(8,128)S(1)}, u32[]{:S(2)}, u32[]{:S(2)}) collective-permute-start(f32[40,512]{1,0:T(8,128)S(1)} %get-tuple-element.13.refs_1_), channel_id=1, source_target_pairs={{0,1},{1,0},{2,3},{3,2},{4,5},{5,4},{6,7},{7,6},{8,9},{9,8},{10,11... | collective-permute-start | bytes 245768 | tf_op jit(solution)/shard_map/ppermute | solution.py:334
  12.9 0.8 %collective-permute-done.3.refs_2_ = f32[40,512]{1,0:T(8,128)S(1)} collective-permute-done((f32[40,512]{1,0:T(8,128)S(1)}, f32[40,512]{1,0:T(8,128)S(1)}, u32[]{:S(2)}, u32[]{:S(2)}) %collective-permute-start.3) | collective-permute-done | bytes 81952 | tf_op jit(solution)/shard_map/ppermute | solution.py:334
  13.8 0.4 %shard_map.102 = f32[16,1024]{1,0:T(8,128)S(1)} custom-call(f32[16,512]{1,0:T(8,128)S(1)} %get-tuple-element.11.g_ref, bf16[64,512]{1,0:T(8,128)(2,1)S(1)} %shard_map.98.refs_3_.mask_ref, f32[40,512]{1,0:T(8,128)S(1)} %get-tuple-element.12.refs_0_, f32[40,512]{1,0:T(8,128)S(1)} %get-tuple-element.13.refs_1_, f32[40,512]{1,0:T(8,128)S(1)} %collective-permute-done.3.refs_2_, ...), custom_call_target="tpu_custom_call" | custom-call | flops 67108864 | tf_op jit(solution)/shard_map/pallas_call | solution.py:202
  14.3 1.6 %collective-permute-start.5 = (f32[16,1024]{1,0:T(8,128)S(1)}, f32[16,1024]{1,0:T(8,128)S(1)}, u32[]{:S(2)}, u32[]{:S(2)}) collective-permute-start(f32[16,1024]{1,0:T(8,128)S(1)} %shard_map.102), channel_id=1, source_target_pairs={{0,4},{4,8},{8,12},{12,0},{1,5},{5,9},{9,13},{13,1},{2,6},{6,10},{... | collective-permute-start | bytes 196616 | tf_op jit(solution)/shard_map/ppermute | solution.py:339
  15.9 0.4 %shard_map.103 = f32[16,1024]{1,0:T(8,128)S(1)} custom-call(f32[16,512]{1,0:T(8,128)S(1)} %get-tuple-element.11.g_ref, bf16[64,512]{1,0:T(8,128)(2,1)S(1)} %shard_map.98.refs_3_.mask_ref, f32[40,512]{1,0:T(8,128)S(1)} %get-tuple-element.12.refs_0_, f32[40,512]{1,0:T(8,128)S(1)} %get-tuple-element.13.refs_1_, f32[40,512]{1,0:T(8,128)S(1)} %collective-permute-done.3.refs_2_, ...), custom_call_target="tpu_custom_call" | custom-call | flops 67108864 | tf_op jit(solution)/shard_map/pallas_call | solution.py:202
  16.3 1.7 %collective-permute-start.6 = (f32[16,1024]{1,0:T(8,128)S(1)}, f32[16,1024]{1,0:T(8,128)S(1)}, u32[]{:S(2)}, u32[]{:S(2)}) collective-permute-start(f32[16,1024]{1,0:T(8,128)S(1)} %shard_map.103), channel_id=1, source_target_pairs={{0,8},{4,12},{8,0},{12,4},{1,9},{5,13},{9,1},{13,5},{2,10},{6,14},... | collective-permute-start | bytes 196616 | tf_op jit(solution)/shard_map/ppermute | solution.py:339
  18.0 0.6 %shard_map.101 = (f32[16,1024]{1,0:T(8,128)S(1)}, f32[16,1024]{1,0:T(8,128)S(1)}) custom-call(f32[16,512]{1,0:T(8,128)S(1)} %get-tuple-element.11.g_ref, bf16[64,512]{1,0:T(8,128)(2,1)S(1)} %shard_map.98.refs_3_.mask_ref, f32[40,512]{1,0:T(8,128)S(1)} %get-tuple-element.12.refs_0_, f32[40,512]{1,0:T(8,128)S(1)} %get-tuple-element.13.refs_1_, ...), custom_call_target="tpu_custom_call" | custom-call | flops 134217728 | tf_op jit(solution)/shard_map/pallas_call | solution.py:202
  18.6 3.0 %collective-permute-start.9 = (f32[16,1024]{1,0:T(8,128)S(1)}, f32[16,1024]{1,0:T(8,128)S(1)}, u32[]{:S(2)}, u32[]{:S(2)}) collective-permute-start(f32[16,1024]{1,0:T(8,128)S(1)} %shard_map.104), channel_id=1, source_target_pairs={{0,12},{4,0},{8,4},{12,8},{1,13},{5,1},{9,5},{13,9},{2,14},{6,2},{... | collective-permute-start | bytes 196616 | tf_op jit(solution)/shard_map/ppermute | solution.py:339
  21.7 0.3 %shard_map.107.early_ref = f32[32,128]{1,0:T(8,128)S(1)} custom-call(s32[1,128]{1,0:T(1,128)S(1)} %bitcast.5, bf16[256,1024]{1,0:T(8,128)(2,1)S(1)} %shard_map.106.pool_ref, f32[16,1024]{1,0:T(8,128)S(1)} %get-tuple-element.14.refs_0_, f32[16,1024]{1,0:T(8,128)S(1)} %collective-permute-done.5.refs_1_), custom_call_target="tpu_custom_call" | custom-call | tf_op jit(solution)/shard_map/pallas_call | solution.py:280
  22.0 1.1 %collective-permute-done.6.refs_2_.refs_0_ = f32[16,1024]{1,0:T(8,128)S(1)} collective-permute-done((f32[16,1024]{1,0:T(8,128)S(1)}, f32[16,1024]{1,0:T(8,128)S(1)}, u32[]{:S(2)}, u32[]{:S(2)}) %collective-permute-start.6) | collective-permute-done | bytes 65568 | tf_op jit(solution)/shard_map/ppermute | solution.py:339
  23.5 0.3 %shard_map.109 = f32[64,128]{1,0:T(8,128)S(1)} custom-call(s32[1,128]{1,0:T(1,128)S(1)} %bitcast.6, bf16[256,1024]{1,0:T(8,128)(2,1)S(1)} %shard_map.106.pool_ref, f32[32,128]{1,0:T(8,128)S(1)} %shard_map.107.early_ref, f32[16,1024]{1,0:T(8,128)S(1)} %collective-permute-done.6.refs_2_.refs_0_, f32[16,1024]{1,0:T(8,128)S(1)} %collective-permute-done.9.refs_3_.refs_1_, ...), custom_call_target="tpu_custom_call" | custom-call | tf_op jit(solution)/shard_map/pallas_call | solution.py:304
  24.1 1.3 %collective-permute-start.11 = (f32[64,128]{1,0:T(8,128)S(1)}, f32[64,128]{1,0:T(8,128)S(1)}, u32[]{:S(2)}, u32[]{:S(2)}) collective-permute-start(f32[64,128]{1,0:T(8,128)S(1)} %shard_map.109), channel_id=1, source_target_pairs={{0,2},{1,3},{2,0},{3,1},{4,6},{5,7},{6,4},{7,5},{8,10},{9,11},{10,... | collective-permute-start | bytes 98312 | tf_op jit(solution)/shard_map/ppermute | solution.py:334
  25.7 0.7 %shard_map.105 = f32[64,1024]{1,0:T(8,128)} custom-call(f32[16,1024]{1,0:T(8,128)S(1)} %get-tuple-element.14.refs_0_, f32[16,1024]{1,0:T(8,128)S(1)} %collective-permute-done.5.refs_1_, f32[16,1024]{1,0:T(8,128)S(1)} %collective-permute-done.6.refs_2_.refs_0_, f32[16,1024]{1,0:T(8,128)S(1)} %collective-permute-done.9.refs_3_.refs_1_), custom_call_target="tpu_custom_call" | custom-call | bytes 524288 | tf_op jit(solution)/shard_map/pallas_call | solution.py:325
  26.4 1.0 %collective-permute-done.12 = f32[64,128]{1,0:T(8,128)S(1)} collective-permute-done((f32[64,128]{1,0:T(8,128)S(1)}, f32[64,128]{1,0:T(8,128)S(1)}, u32[]{:S(2)}, u32[]{:S(2)}) %collective-permute-start.12) | collective-permute-done | bytes 32800 | tf_op jit(solution)/shard_map/ppermute | solution.py:334
  27.5 0.6 %collective-permute-done.11 = f32[64,128]{1,0:T(8,128)S(1)} collective-permute-done((f32[64,128]{1,0:T(8,128)S(1)}, f32[64,128]{1,0:T(8,128)S(1)}, u32[]{:S(2)}, u32[]{:S(2)}) %collective-permute-start.11) | collective-permute-done | bytes 32800 | tf_op jit(solution)/shard_map/ppermute | solution.py:334
  28.0 0.6 %add_multiply_fusion = f32[64,128]{1,0:T(8,128)} fusion(f32[64,128]{1,0:T(8,128)S(1)} %collective-permute-done.11, f32[64,128]{1,0:T(8,128)S(1)} %collective-permute-done.12, f32[64,128]{1,0:T(8,128)S(1)} %shard_map.109, f32[64,128]{1,0:T(8,128)S(1)} %collective-permute-done.10), kind=kLoop, calls=%fused_computation | loop fusion | flops 32768 | bytes 163840 | tf_op jit(solution)/shard_map/mul | solution.py:411
  (34 shorter events, 1.7 us)
Async XLA Ops:
  0.6 4.2 %copy-start.5 = (bf16[1024,64]{0,1:T(8,128)(2,1)S(1)}, bf16[1024,64]{0,1:T(8,128)(2,1)}, u32[]{:S(2)}) copy-start(bf16[1024,64]{0,1:T(8,128)(2,1)} %param.10) | copy-start | bytes 393220
  0.6 4.2 %copy-start.4 = (bf16[512,1024]{1,0:T(8,128)(2,1)S(1)}, bf16[512,1024]{1,0:T(8,128)(2,1)}, u32[]{:S(2)}) copy-start(bf16[512,1024]{1,0:T(8,128)(2,1)} %act_ref.1) | copy-start | bytes 3145732
  0.7 6.2 %copy-start.1 = (bf16[3584,64]{0,1:T(8,128)(2,1)S(1)}, bf16[3584,64]{0,1:T(8,128)(2,1)}, u32[]{:S(2)}) copy-start(bf16[3584,64]{0,1:T(8,128)(2,1)} %param.11) | copy-start | bytes 1376260
  0.7 6.2 %copy-start = (bf16[512,3584]{1,0:T(8,128)(2,1)S(1)}, bf16[512,3584]{1,0:T(8,128)(2,1)}, u32[]{:S(2)}) copy-start(bf16[512,3584]{1,0:T(8,128)(2,1)} %grad_ref.1) | copy-start | bytes 11010052
  0.7 10.7 %collective-permute-start.2 = (f32[32,1024]{1,0:T(8,128)}, f32[32,1024]{1,0:T(8,128)S(1)}, u32[]{:S(2)}, u32[]{:S(2)}) collective-permute-start(f32[32,1024]{1,0:T(8,128)} %refs_0_.1), channel_id=1, source_target_pairs={{0,8},{4,12},{8,0},{12,4},{1,9},{5,13},{9,1},{13,5},{2,10},{6,14},... | collective-permute-start | bytes 393224 | tf_op jit(solution)/shard_map/ppermute | solution.py:334
  4.8 3.8 %copy-start.2 = (f32[32,1024]{1,0:T(8,128)S(1)}, f32[32,1024]{1,0:T(8,128)}, u32[]{:S(2)}) copy-start(f32[32,1024]{1,0:T(8,128)} %refs_0_.1) | copy-start | bytes 393220
  4.8 5.4 %copy-start.6 = (s32[1,32]{1,0:T(1,128)S(1)}, s32[1,32]{1,0:T(1,128)}, u32[]{:S(2)}) copy-start(s32[1,32]{1,0:T(1,128)} %lengths_ref.1) | copy-start | bytes 388
  4.8 5.4 %copy-start.7 = (s32[32,1]{0,1:T(1,128)S(1)}, s32[32,1]{0,1:T(1,128)}, u32[]{:S(2)}) copy-start(s32[32,1]{0,1:T(1,128)} %param.13) | copy-start | bytes 388
  5.3 7.1 %collective-permute-start = (f32[64,512]{1,0:T(8,128)S(1)}, f32[64,512]{1,0:T(8,128)S(1)}, u32[]{:S(2)}, u32[]{:S(2)}) collective-permute-start(f32[64,512]{1,0:T(8,128)S(1)} %shard_map.97.refs_0_), channel_id=1, source_target_pairs={{0,2},{1,3},{2,0},{3,1},{4,6},{5,7},{6,4},{7,5},{8,10},{9,11},{10,... | collective-permute-start | bytes 393224 | tf_op jit(solution)/shard_map/ppermute | solution.py:334
  6.8 14.9 %copy-start.3 = (s32[128]{0:T(128)S(1)}, s32[128]{0:T(128)}, u32[]{:S(2)}) copy-start(s32[128]{0:T(128)} %param.15) | copy-start | bytes 1540
  8.0 4.3 %collective-permute-start.1 = (f32[32,512]{1,0:T(8,128)S(1)}, f32[32,512]{1,0:T(8,128)S(1)}, u32[]{:S(2)}, u32[]{:S(2)}) collective-permute-start(f32[32,512]{1,0:T(8,128)S(1)} %get-tuple-element.10), channel_id=1, source_target_pairs={{0,2},{1,3},{2,0},{3,1},{4,6},{5,7},{6,4},{7,5},{8,10},{9,11},{10,... | collective-permute-start | bytes 196616 | tf_op jit(solution)/shard_map/ppermute | solution.py:334
  8.6 10.0 %collective-permute-start.7 = (f32[32,1024]{1,0:T(8,128)S(1)}, f32[32,1024]{1,0:T(8,128)S(1)}, u32[]{:S(2)}, u32[]{:S(2)}) collective-permute-start(f32[32,1024]{1,0:T(8,128)S(1)} %copy-done.2), channel_id=1, source_target_pairs={{0,4},{4,0},{8,12},{12,8},{1,5},{5,1},{9,13},{13,9},{2,6},{6,2},{1... | collective-permute-start | bytes 393224 | tf_op jit(solution)/shard_map/ppermute | solution.py:334
  11.4 7.2 %collective-permute-start.8 = (f32[32,1024]{1,0:T(8,128)S(1)}, f32[32,1024]{1,0:T(8,128)S(1)}, u32[]{:S(2)}, u32[]{:S(2)}) collective-permute-start(f32[32,1024]{1,0:T(8,128)S(1)} %collective-permute-done.2.refs_0_.refs_1_), channel_id=1, source_target_pairs={{0,4},{4,0},{8,12},{12,8},{1,5},{5,1},{9,13},{13,9},{2,6},{6,2},{1... | collective-permute-start | bytes 393224 | tf_op jit(solution)/shard_map/ppermute | solution.py:334
  12.3 1.3 %collective-permute-start.3 = (f32[40,512]{1,0:T(8,128)S(1)}, f32[40,512]{1,0:T(8,128)S(1)}, u32[]{:S(2)}, u32[]{:S(2)}) collective-permute-start(f32[40,512]{1,0:T(8,128)S(1)} %get-tuple-element.12.refs_0_), channel_id=1, source_target_pairs={{0,1},{1,0},{2,3},{3,2},{4,5},{5,4},{6,7},{7,6},{8,9},{9,8},{10,11... | collective-permute-start | bytes 245768 | tf_op jit(solution)/shard_map/ppermute | solution.py:334
  12.4 1.4 %collective-permute-start.4 = (f32[40,512]{1,0:T(8,128)S(1)}, f32[40,512]{1,0:T(8,128)S(1)}, u32[]{:S(2)}, u32[]{:S(2)}) collective-permute-start(f32[40,512]{1,0:T(8,128)S(1)} %get-tuple-element.13.refs_1_), channel_id=1, source_target_pairs={{0,1},{1,0},{2,3},{3,2},{4,5},{5,4},{6,7},{7,6},{8,9},{9,8},{10,11... | collective-permute-start | bytes 245768 | tf_op jit(solution)/shard_map/ppermute | solution.py:334
  14.3 7.4 %collective-permute-start.5 = (f32[16,1024]{1,0:T(8,128)S(1)}, f32[16,1024]{1,0:T(8,128)S(1)}, u32[]{:S(2)}, u32[]{:S(2)}) collective-permute-start(f32[16,1024]{1,0:T(8,128)S(1)} %shard_map.102), channel_id=1, source_target_pairs={{0,4},{4,8},{8,12},{12,0},{1,5},{5,9},{9,13},{13,1},{2,6},{6,10},{... | collective-permute-start | bytes 196616 | tf_op jit(solution)/shard_map/ppermute | solution.py:339
  16.3 6.8 %collective-permute-start.6 = (f32[16,1024]{1,0:T(8,128)S(1)}, f32[16,1024]{1,0:T(8,128)S(1)}, u32[]{:S(2)}, u32[]{:S(2)}) collective-permute-start(f32[16,1024]{1,0:T(8,128)S(1)} %shard_map.103), channel_id=1, source_target_pairs={{0,8},{4,12},{8,0},{12,4},{1,9},{5,13},{9,1},{13,5},{2,10},{6,14},... | collective-permute-start | bytes 196616 | tf_op jit(solution)/shard_map/ppermute | solution.py:339
  18.6 4.9 %collective-permute-start.9 = (f32[16,1024]{1,0:T(8,128)S(1)}, f32[16,1024]{1,0:T(8,128)S(1)}, u32[]{:S(2)}, u32[]{:S(2)}) collective-permute-start(f32[16,1024]{1,0:T(8,128)S(1)} %shard_map.104), channel_id=1, source_target_pairs={{0,12},{4,0},{8,4},{12,8},{1,13},{5,1},{9,5},{13,9},{2,14},{6,2},{... | collective-permute-start | bytes 196616 | tf_op jit(solution)/shard_map/ppermute | solution.py:339
  23.8 3.6 %collective-permute-start.12 = (f32[64,128]{1,0:T(8,128)S(1)}, f32[64,128]{1,0:T(8,128)S(1)}, u32[]{:S(2)}, u32[]{:S(2)}) collective-permute-start(f32[64,128]{1,0:T(8,128)S(1)} %shard_map.109), channel_id=1, source_target_pairs={{0,3},{1,2},{2,1},{3,0},{4,7},{5,6},{6,5},{7,4},{8,11},{9,10},{10,... | collective-permute-start | bytes 98312 | tf_op jit(solution)/shard_map/ppermute | solution.py:334
  24.1 3.9 %collective-permute-start.11 = (f32[64,128]{1,0:T(8,128)S(1)}, f32[64,128]{1,0:T(8,128)S(1)}, u32[]{:S(2)}, u32[]{:S(2)}) collective-permute-start(f32[64,128]{1,0:T(8,128)S(1)} %shard_map.109), channel_id=1, source_target_pairs={{0,2},{1,3},{2,0},{3,1},{4,6},{5,7},{6,4},{7,5},{8,10},{9,11},{10,... | collective-permute-start | bytes 98312 | tf_op jit(solution)/shard_map/ppermute | solution.py:334
  25.4 2.6 %collective-permute-start.10 = (f32[64,128]{1,0:T(8,128)S(1)}, f32[64,128]{1,0:T(8,128)S(1)}, u32[]{:S(2)}, u32[]{:S(2)}) collective-permute-start(f32[64,128]{1,0:T(8,128)S(1)} %shard_map.109), channel_id=1, source_target_pairs={{0,1},{1,0},{2,3},{3,2},{4,5},{5,4},{6,7},{7,6},{8,9},{9,8},{10,11... | collective-permute-start | bytes 98312 | tf_op jit(solution)/shard_map/ppermute | solution.py:334

commit v25 on v24

--- a/solution.py
+++ b/solution.py
@@ -13,7 +13,7 @@
 NT = (((1,), (1,)), ((), ()))
 MOST_DIRECT = 8
 MOST_AT_ONCE = 4
-GROUP = 16
+GROUP = 8
 ROWS = 16
 LANES = 128
 FIRST_FLOPS = 10 * 10**8
@@ -381,7 +381,7 @@
     ids_row = query_ids[None, :]
     if direct:
         split = max(1, data_size // 2)
-        soon = [outer(own, gots, keep, mask, cap, k, 1)[0] for k in range(split)]
+        soon = outer(own, gots, keep, mask, cap, 0, split)
         rows = [shift(block, "dp", k) for k, block in enumerate(soon, 1)]
         *sent, kept = outer(own, gots, keep, mask, cap, split, data_size - split)
         sent[-1] = after(sent[-1], [mate, *passed])

time: 28.8 us -> 29.4 us (1.021)
  waiting for transfers between devices: 5.18 us -> 6.1 us
    ppermute x10, waiting for transfers between devices: 3.73 us -> 4.3 us  [swap(): lax.ppermute(x, axis, [(i, i ^ gap) for i in range(lax.axis_size(axis))])]
    ppermute x3, waiting for transfers between devices: 1.45 us -> 1.8 us  [shift(): return lax.ppermute(x, axis, [(i, (i + by) % size) for i in range(size)])]
    pallas_call x3 -> x2, Pallas kernels: 1.43 us -> 1.15 us  [outer(): pl.pallas_call(functools.partial(outer_kernel, first, owners, len(sent)),...]
  transfers between devices with their start and end apart: 13 -> 13, of which waited for: 8 -> 7; matrix products, arithmetic and copies ran while one was open for 0% -> 0% of each run, Pallas kernels for 15% -> 14%
where the time goes in v25:
time: 29.4 us; the launch traced here: 29.3 us
  starting transfers between devices  17.2 us (59%)
  waiting for transfers between devices  6.1 us (21%)
  Pallas kernels  4.51 us (15%)
  between operations  0.78 us (3%)
  other arithmetic  0.62 us (2%)
    ppermute x10, starting transfers between devices, swap(): lax.ppermute(x, axis, [(i, i ^ gap) for i in range(lax.axis_size(axis))])  11 us
    ppermute x3, starting transfers between devices, shift(): return lax.ppermute(x, axis, [(i, (i + by) % size) for i in range(size)])  6.23 us
    ppermute x10, waiting for transfers between devices, swap(): lax.ppermute(x, axis, [(i, i ^ gap) for i in range(lax.axis_size(axis))])  4.3 us
    ppermute x3, waiting for transfers between devices, shift(): return lax.ppermute(x, axis, [(i, (i + by) % size) for i in range(size)])  1.8 us
    pallas_call x1, Pallas kernels, project_g(): pl.pallas_call(functools.partial(g_kernel, width), out_shape=[part, part]...  1.16 us
    pallas_call x2, Pallas kernels, outer(): pl.pallas_call(functools.partial(outer_kernel, first, owners, len(sent)),...  1.15 us
    pallas_call x1, Pallas kernels, place(): pl.pallas_call(place_kernel, out_shape=jax.ShapeDtypeStruct((slots, feats...  0.72 us
    mul x1, other arithmetic, local(): return (store, scores * (1.0 / (rank * rank)))  0.62 us
  transfers between devices with their start and end apart: 13, of which 7 were waited for; matrix products, arithmetic and copies ran while one was open for 0% of the time, Pallas kernels for 14%

profile of v25, /device:TPU:0, one launch (start us, length us, event | category | flops | bytes accessed | tf_op | source)
XLA Modules:
  0.0 29.3 jit_solution(604330789798212565)
XLA Ops:
  0.7 4.1 %collective-permute-start.2 = (f32[32,1024]{1,0:T(8,128)}, f32[32,1024]{1,0:T(8,128)S(1)}, u32[]{:S(2)}, u32[]{:S(2)}) collective-permute-start(f32[32,1024]{1,0:T(8,128)} %refs_0_.1), channel_id=1, source_target_pairs={{0,8},{4,12},{8,0},{12,4},{1,9},{5,13},{9,1},{13,5},{2,10},{6,14},... | collective-permute-start | bytes 393224 | tf_op jit(solution)/shard_map/ppermute | solution.py:334
  4.8 0.5 %shard_map.97.refs_0_ = f32[64,512]{1,0:T(8,128)S(1)} custom-call(bf16[512,1024]{1,0:T(8,128)(2,1)S(1)} %copy-done.4, bf16[64,1024]{1,0:T(8,128)(2,1)S(1)} %bitcast.7, f32[8,128]{1,0:T(8,128)S(1)} %shard_map.96.refs_0_), custom_call_target="tpu_custom_call" | custom-call | flops 600000000 | tf_op jit(solution)/shard_map/pallas_call | solution.py:91
  5.3 1.5 %collective-permute-start = (f32[64,512]{1,0:T(8,128)S(1)}, f32[64,512]{1,0:T(8,128)S(1)}, u32[]{:S(2)}, u32[]{:S(2)}) collective-permute-start(f32[64,512]{1,0:T(8,128)S(1)} %shard_map.97.refs_0_), channel_id=1, source_target_pairs={{0,2},{1,3},{2,0},{3,1},{4,6},{5,7},{6,4},{7,5},{8,10},{9,11},{10,... | collective-permute-start | bytes 393224 | tf_op jit(solution)/shard_map/ppermute | solution.py:334
  6.8 1.2 %shard_map.95 = (f32[32,512]{1,0:T(8,128)S(1)}, f32[32,512]{1,0:T(8,128)S(1)}) custom-call(bf16[512,3584]{1,0:T(8,128)(2,1)S(1)} %copy-done, bf16[64,3584]{1,0:T(8,128)(2,1)S(1)} %bitcast.4), custom_call_target="tpu_custom_call" | custom-call | tf_op jit(solution)/shard_map/pallas_call | solution.py:114
  8.0 0.6 %collective-permute-start.1 = (f32[32,512]{1,0:T(8,128)S(1)}, f32[32,512]{1,0:T(8,128)S(1)}, u32[]{:S(2)}, u32[]{:S(2)}) collective-permute-start(f32[32,512]{1,0:T(8,128)S(1)} %get-tuple-element.12), channel_id=1, source_target_pairs={{0,2},{1,3},{2,0},{3,1},{4,6},{5,7},{6,4},{7,5},{8,10},{9,11},{10,... | collective-permute-start | bytes 196616 | tf_op jit(solution)/shard_map/ppermute | solution.py:334
  8.6 1.6 %collective-permute-start.7 = (f32[32,1024]{1,0:T(8,128)S(1)}, f32[32,1024]{1,0:T(8,128)S(1)}, u32[]{:S(2)}, u32[]{:S(2)}) collective-permute-start(f32[32,1024]{1,0:T(8,128)S(1)} %copy-done.2), channel_id=1, source_target_pairs={{0,4},{4,0},{8,12},{12,8},{1,5},{5,1},{9,13},{13,9},{2,6},{6,2},{1... | collective-permute-start | bytes 393224 | tf_op jit(solution)/shard_map/ppermute | solution.py:334
  10.4 1.0 %collective-permute-done.2.refs_0_.refs_1_ = f32[32,1024]{1,0:T(8,128)S(1)} collective-permute-done((f32[32,1024]{1,0:T(8,128)}, f32[32,1024]{1,0:T(8,128)S(1)}, u32[]{:S(2)}, u32[]{:S(2)}) %collective-permute-start.2) | collective-permute-done | bytes 131104 | tf_op jit(solution)/shard_map/ppermute | solution.py:334
  11.4 0.7 %collective-permute-start.8 = (f32[32,1024]{1,0:T(8,128)S(1)}, f32[32,1024]{1,0:T(8,128)S(1)}, u32[]{:S(2)}, u32[]{:S(2)}) collective-permute-start(f32[32,1024]{1,0:T(8,128)S(1)} %collective-permute-done.2.refs_0_.refs_1_), channel_id=1, source_target_pairs={{0,4},{4,0},{8,12},{12,8},{1,5},{5,1},{9,13},{13,9},{2,6},{6,2},{1... | collective-permute-start | bytes 393224 | tf_op jit(solution)/shard_map/ppermute | solution.py:334
  12.4 0.5 %collective-permute-start.4 = (f32[40,512]{1,0:T(8,128)S(1)}, f32[40,512]{1,0:T(8,128)S(1)}, u32[]{:S(2)}, u32[]{:S(2)}) collective-permute-start(f32[40,512]{1,0:T(8,128)S(1)} %get-tuple-element.15.refs_1_), channel_id=1, source_target_pairs={{0,1},{1,0},{2,3},{3,2},{4,5},{5,4},{6,7},{7,6},{8,9},{9,8},{10,11... | collective-permute-start | bytes 245768 | tf_op jit(solution)/shard_map/ppermute | solution.py:334
  12.9 0.8 %collective-permute-done.3.refs_2_ = f32[40,512]{1,0:T(8,128)S(1)} collective-permute-done((f32[40,512]{1,0:T(8,128)S(1)}, f32[40,512]{1,0:T(8,128)S(1)}, u32[]{:S(2)}, u32[]{:S(2)}) %collective-permute-start.3) | collective-permute-done | bytes 81952 | tf_op jit(solution)/shard_map/ppermute | solution.py:334
  13.8 0.6 %shard_map.102 = (f32[16,1024]{1,0:T(8,128)S(1)}, f32[16,1024]{1,0:T(8,128)S(1)}) custom-call(f32[16,512]{1,0:T(8,128)S(1)} %get-tuple-element.13.g_ref, bf16[64,512]{1,0:T(8,128)(2,1)S(1)} %shard_map.98.refs_3_.mask_ref, f32[40,512]{1,0:T(8,128)S(1)} %get-tuple-element.14.refs_0_, f32[40,512]{1,0:T(8,128)S(1)} %get-tuple-element.15.refs_1_, ...), custom_call_target="tpu_custom_call" | custom-call | flops 134217728 | tf_op jit(solution)/shard_map/pallas_call | solution.py:202
  14.4 1.6 %collective-permute-start.5 = (f32[16,1024]{1,0:T(8,128)S(1)}, f32[16,1024]{1,0:T(8,128)S(1)}, u32[]{:S(2)}, u32[]{:S(2)}) collective-permute-start(f32[16,1024]{1,0:T(8,128)S(1)} %get-tuple-element.17), channel_id=1, source_target_pairs={{0,4},{4,8},{8,12},{12,0},{1,5},{5,9},{9,13},{13,1},{2,6},{6,10},{... | collective-permute-start | bytes 196616 | tf_op jit(solution)/shard_map/ppermute | solution.py:339
  16.1 1.7 %collective-permute-start.6 = (f32[16,1024]{1,0:T(8,128)S(1)}, f32[16,1024]{1,0:T(8,128)S(1)}, u32[]{:S(2)}, u32[]{:S(2)}) collective-permute-start(f32[16,1024]{1,0:T(8,128)S(1)} %get-tuple-element.18), channel_id=1, source_target_pairs={{0,8},{4,12},{8,0},{12,4},{1,9},{5,13},{9,1},{13,5},{2,10},{6,14},... | collective-permute-start | bytes 196616 | tf_op jit(solution)/shard_map/ppermute | solution.py:339
  17.7 0.6 %shard_map.101 = (f32[16,1024]{1,0:T(8,128)S(1)}, f32[16,1024]{1,0:T(8,128)S(1)}) custom-call(f32[16,512]{1,0:T(8,128)S(1)} %get-tuple-element.13.g_ref, bf16[64,512]{1,0:T(8,128)(2,1)S(1)} %shard_map.98.refs_3_.mask_ref, f32[40,512]{1,0:T(8,128)S(1)} %get-tuple-element.14.refs_0_, f32[40,512]{1,0:T(8,128)S(1)} %get-tuple-element.15.refs_1_, ...), custom_call_target="tpu_custom_call" | custom-call | flops 134217728 | tf_op jit(solution)/shard_map/pallas_call | solution.py:202
  18.4 2.9 %collective-permute-start.9 = (f32[16,1024]{1,0:T(8,128)S(1)}, f32[16,1024]{1,0:T(8,128)S(1)}, u32[]{:S(2)}, u32[]{:S(2)}) collective-permute-start(f32[16,1024]{1,0:T(8,128)S(1)} %shard_map.103), channel_id=1, source_target_pairs={{0,12},{4,0},{8,4},{12,8},{1,13},{5,1},{9,5},{13,9},{2,14},{6,2},{... | collective-permute-start | bytes 196616 | tf_op jit(solution)/shard_map/ppermute | solution.py:339
  21.4 0.3 %shard_map.106.early_ref = f32[32,128]{1,0:T(8,128)S(1)} custom-call(s32[1,128]{1,0:T(1,128)S(1)} %bitcast.5, bf16[256,1024]{1,0:T(8,128)(2,1)S(1)} %shard_map.105.pool_ref, f32[16,1024]{1,0:T(8,128)S(1)} %get-tuple-element.16.refs_0_, f32[16,1024]{1,0:T(8,128)S(1)} %collective-permute-done.5.refs_1_), custom_call_target="tpu_custom_call" | custom-call | tf_op jit(solution)/shard_map/pallas_call | solution.py:280
  21.7 1.8 %collective-permute-done.6.refs_2_.refs_0_ = f32[16,1024]{1,0:T(8,128)S(1)} collective-permute-done((f32[16,1024]{1,0:T(8,128)S(1)}, f32[16,1024]{1,0:T(8,128)S(1)}, u32[]{:S(2)}, u32[]{:S(2)}) %collective-permute-start.6) | collective-permute-done | bytes 65568 | tf_op jit(solution)/shard_map/ppermute | solution.py:339
  23.5 0.3 %shard_map.108 = f32[64,128]{1,0:T(8,128)S(1)} custom-call(s32[1,128]{1,0:T(1,128)S(1)} %bitcast.6, bf16[256,1024]{1,0:T(8,128)(2,1)S(1)} %shard_map.105.pool_ref, f32[32,128]{1,0:T(8,128)S(1)} %shard_map.106.early_ref, f32[16,1024]{1,0:T(8,128)S(1)} %collective-permute-done.6.refs_2_.refs_0_, f32[16,1024]{1,0:T(8,128)S(1)} %collective-permute-done.9.refs_3_.refs_1_, ...), custom_call_target="tpu_custom_call" | custom-call | tf_op jit(solution)/shard_map/pallas_call | solution.py:304
  23.9 1.4 %collective-permute-start.11 = (f32[64,128]{1,0:T(8,128)S(1)}, f32[64,128]{1,0:T(8,128)S(1)}, u32[]{:S(2)}, u32[]{:S(2)}) collective-permute-start(f32[64,128]{1,0:T(8,128)S(1)} %shard_map.108), channel_id=1, source_target_pairs={{0,2},{1,3},{2,0},{3,1},{4,6},{5,7},{6,4},{7,5},{8,10},{9,11},{10,... | collective-permute-start | bytes 98312 | tf_op jit(solution)/shard_map/ppermute | solution.py:334
  25.3 0.4 %collective-permute-start.12 = (f32[64,128]{1,0:T(8,128)S(1)}, f32[64,128]{1,0:T(8,128)S(1)}, u32[]{:S(2)}, u32[]{:S(2)}) collective-permute-start(f32[64,128]{1,0:T(8,128)S(1)} %shard_map.108), channel_id=1, source_target_pairs={{0,3},{1,2},{2,1},{3,0},{4,7},{5,6},{6,5},{7,4},{8,11},{9,10},{10,... | collective-permute-start | bytes 98312 | tf_op jit(solution)/shard_map/ppermute | solution.py:334
  25.7 0.7 %shard_map.104 = f32[64,1024]{1,0:T(8,128)} custom-call(f32[16,1024]{1,0:T(8,128)S(1)} %get-tuple-element.16.refs_0_, f32[16,1024]{1,0:T(8,128)S(1)} %collective-permute-done.5.refs_1_, f32[16,1024]{1,0:T(8,128)S(1)} %collective-permute-done.6.refs_2_.refs_0_, f32[16,1024]{1,0:T(8,128)S(1)} %collective-permute-done.9.refs_3_.refs_1_), custom_call_target="tpu_custom_call" | custom-call | bytes 524288 | tf_op jit(solution)/shard_map/pallas_call | solution.py:325
  26.5 1.4 %collective-permute-done.11 = f32[64,128]{1,0:T(8,128)S(1)} collective-permute-done((f32[64,128]{1,0:T(8,128)S(1)}, f32[64,128]{1,0:T(8,128)S(1)}, u32[]{:S(2)}, u32[]{:S(2)}) %collective-permute-start.11) | collective-permute-done | bytes 32800 | tf_op jit(solution)/shard_map/ppermute | solution.py:334
  27.9 0.8 %collective-permute-done.12 = f32[64,128]{1,0:T(8,128)S(1)} collective-permute-done((f32[64,128]{1,0:T(8,128)S(1)}, f32[64,128]{1,0:T(8,128)S(1)}, u32[]{:S(2)}, u32[]{:S(2)}) %collective-permute-start.12) | collective-permute-done | bytes 32800 | tf_op jit(solution)/shard_map/ppermute | solution.py:334
  28.6 0.6 %add_multiply_fusion = f32[64,128]{1,0:T(8,128)} fusion(f32[64,128]{1,0:T(8,128)S(1)} %collective-permute-done.11, f32[64,128]{1,0:T(8,128)S(1)} %collective-permute-done.12, f32[64,128]{1,0:T(8,128)S(1)} %shard_map.108, f32[64,128]{1,0:T(8,128)S(1)} %collective-permute-done.10), kind=kLoop, calls=%fused_computation | loop fusion | flops 32768 | bytes 163840 | tf_op jit(solution)/shard_map/mul | solution.py:411
  (33 shorter events, 0.8 us)
Async XLA Ops:
  0.6 4.2 %copy-start.5 = (bf16[1024,64]{0,1:T(8,128)(2,1)S(1)}, bf16[1024,64]{0,1:T(8,128)(2,1)}, u32[]{:S(2)}) copy-start(bf16[1024,64]{0,1:T(8,128)(2,1)} %param.10) | copy-start | bytes 393220
  0.6 4.2 %copy-start.4 = (bf16[512,1024]{1,0:T(8,128)(2,1)S(1)}, bf16[512,1024]{1,0:T(8,128)(2,1)}, u32[]{:S(2)}) copy-start(bf16[512,1024]{1,0:T(8,128)(2,1)} %act_ref.1) | copy-start | bytes 3145732
  0.7 6.2 %copy-start.1 = (bf16[3584,64]{0,1:T(8,128)(2,1)S(1)}, bf16[3584,64]{0,1:T(8,128)(2,1)}, u32[]{:S(2)}) copy-start(bf16[3584,64]{0,1:T(8,128)(2,1)} %param.11) | copy-start | bytes 1376260
  0.7 6.2 %copy-start = (bf16[512,3584]{1,0:T(8,128)(2,1)S(1)}, bf16[512,3584]{1,0:T(8,128)(2,1)}, u32[]{:S(2)}) copy-start(bf16[512,3584]{1,0:T(8,128)(2,1)} %grad_ref.1) | copy-start | bytes 11010052
  0.7 10.7 %collective-permute-start.2 = (f32[32,1024]{1,0:T(8,128)}, f32[32,1024]{1,0:T(8,128)S(1)}, u32[]{:S(2)}, u32[]{:S(2)}) collective-permute-start(f32[32,1024]{1,0:T(8,128)} %refs_0_.1), channel_id=1, source_target_pairs={{0,8},{4,12},{8,0},{12,4},{1,9},{5,13},{9,1},{13,5},{2,10},{6,14},... | collective-permute-start | bytes 393224 | tf_op jit(solution)/shard_map/ppermute | solution.py:334
  4.8 3.8 %copy-start.2 = (f32[32,1024]{1,0:T(8,128)S(1)}, f32[32,1024]{1,0:T(8,128)}, u32[]{:S(2)}) copy-start(f32[32,1024]{1,0:T(8,128)} %refs_0_.1) | copy-start | bytes 393220
  4.8 5.4 %copy-start.6 = (s32[1,32]{1,0:T(1,128)S(1)}, s32[1,32]{1,0:T(1,128)}, u32[]{:S(2)}) copy-start(s32[1,32]{1,0:T(1,128)} %lengths_ref.1) | copy-start | bytes 388
  4.8 5.4 %copy-start.7 = (s32[32,1]{0,1:T(1,128)S(1)}, s32[32,1]{0,1:T(1,128)}, u32[]{:S(2)}) copy-start(s32[32,1]{0,1:T(1,128)} %param.13) | copy-start | bytes 388
  5.3 7.1 %collective-permute-start = (f32[64,512]{1,0:T(8,128)S(1)}, f32[64,512]{1,0:T(8,128)S(1)}, u32[]{:S(2)}, u32[]{:S(2)}) collective-permute-start(f32[64,512]{1,0:T(8,128)S(1)} %shard_map.97.refs_0_), channel_id=1, source_target_pairs={{0,2},{1,3},{2,0},{3,1},{4,6},{5,7},{6,4},{7,5},{8,10},{9,11},{10,... | collective-permute-start | bytes 393224 | tf_op jit(solution)/shard_map/ppermute | solution.py:334
  6.8 14.6 %copy-start.3 = (s32[128]{0:T(128)S(1)}, s32[128]{0:T(128)}, u32[]{:S(2)}) copy-start(s32[128]{0:T(128)} %param.15) | copy-start | bytes 1540
  8.0 4.3 %collective-permute-start.1 = (f32[32,512]{1,0:T(8,128)S(1)}, f32[32,512]{1,0:T(8,128)S(1)}, u32[]{:S(2)}, u32[]{:S(2)}) collective-permute-start(f32[32,512]{1,0:T(8,128)S(1)} %get-tuple-element.12), channel_id=1, source_target_pairs={{0,2},{1,3},{2,0},{3,1},{4,6},{5,7},{6,4},{7,5},{8,10},{9,11},{10,... | collective-permute-start | bytes 196616 | tf_op jit(solution)/shard_map/ppermute | solution.py:334
  8.6 9.7 %collective-permute-start.7 = (f32[32,1024]{1,0:T(8,128)S(1)}, f32[32,1024]{1,0:T(8,128)S(1)}, u32[]{:S(2)}, u32[]{:S(2)}) collective-permute-start(f32[32,1024]{1,0:T(8,128)S(1)} %copy-done.2), channel_id=1, source_target_pairs={{0,4},{4,0},{8,12},{12,8},{1,5},{5,1},{9,13},{13,9},{2,6},{6,2},{1... | collective-permute-start | bytes 393224 | tf_op jit(solution)/shard_map/ppermute | solution.py:334
  11.4 6.9 %collective-permute-start.8 = (f32[32,1024]{1,0:T(8,128)S(1)}, f32[32,1024]{1,0:T(8,128)S(1)}, u32[]{:S(2)}, u32[]{:S(2)}) collective-permute-start(f32[32,1024]{1,0:T(8,128)S(1)} %collective-permute-done.2.refs_0_.refs_1_), channel_id=1, source_target_pairs={{0,4},{4,0},{8,12},{12,8},{1,5},{5,1},{9,13},{13,9},{2,6},{6,2},{1... | collective-permute-start | bytes 393224 | tf_op jit(solution)/shard_map/ppermute | solution.py:334
  12.3 1.3 %collective-permute-start.3 = (f32[40,512]{1,0:T(8,128)S(1)}, f32[40,512]{1,0:T(8,128)S(1)}, u32[]{:S(2)}, u32[]{:S(2)}) collective-permute-start(f32[40,512]{1,0:T(8,128)S(1)} %get-tuple-element.14.refs_0_), channel_id=1, source_target_pairs={{0,1},{1,0},{2,3},{3,2},{4,5},{5,4},{6,7},{7,6},{8,9},{9,8},{10,11... | collective-permute-start | bytes 245768 | tf_op jit(solution)/shard_map/ppermute | solution.py:334
  12.4 1.4 %collective-permute-start.4 = (f32[40,512]{1,0:T(8,128)S(1)}, f32[40,512]{1,0:T(8,128)S(1)}, u32[]{:S(2)}, u32[]{:S(2)}) collective-permute-start(f32[40,512]{1,0:T(8,128)S(1)} %get-tuple-element.15.refs_1_), channel_id=1, source_target_pairs={{0,1},{1,0},{2,3},{3,2},{4,5},{5,4},{6,7},{7,6},{8,9},{9,8},{10,11... | collective-permute-start | bytes 245768 | tf_op jit(solution)/shard_map/ppermute | solution.py:334
  14.4 6.9 %collective-permute-start.5 = (f32[16,1024]{1,0:T(8,128)S(1)}, f32[16,1024]{1,0:T(8,128)S(1)}, u32[]{:S(2)}, u32[]{:S(2)}) collective-permute-start(f32[16,1024]{1,0:T(8,128)S(1)} %get-tuple-element.17), channel_id=1, source_target_pairs={{0,4},{4,8},{8,12},{12,0},{1,5},{5,9},{9,13},{13,1},{2,6},{6,10},{... | collective-permute-start | bytes 196616 | tf_op jit(solution)/shard_map/ppermute | solution.py:339
  16.1 7.5 %collective-permute-start.6 = (f32[16,1024]{1,0:T(8,128)S(1)}, f32[16,1024]{1,0:T(8,128)S(1)}, u32[]{:S(2)}, u32[]{:S(2)}) collective-permute-start(f32[16,1024]{1,0:T(8,128)S(1)} %get-tuple-element.18), channel_id=1, source_target_pairs={{0,8},{4,12},{8,0},{12,4},{1,9},{5,13},{9,1},{13,5},{2,10},{6,14},... | collective-permute-start | bytes 196616 | tf_op jit(solution)/shard_map/ppermute | solution.py:339
  18.4 5.2 %collective-permute-start.9 = (f32[16,1024]{1,0:T(8,128)S(1)}, f32[16,1024]{1,0:T(8,128)S(1)}, u32[]{:S(2)}, u32[]{:S(2)}) collective-permute-start(f32[16,1024]{1,0:T(8,128)S(1)} %shard_map.103), channel_id=1, source_target_pairs={{0,12},{4,0},{8,4},{12,8},{1,13},{5,1},{9,5},{13,9},{2,14},{6,2},{... | collective-permute-start | bytes 196616 | tf_op jit(solution)/shard_map/ppermute | solution.py:339
  23.9 2.6 %collective-permute-start.10 = (f32[64,128]{1,0:T(8,128)S(1)}, f32[64,128]{1,0:T(8,128)S(1)}, u32[]{:S(2)}, u32[]{:S(2)}) collective-permute-start(f32[64,128]{1,0:T(8,128)S(1)} %shard_map.108), channel_id=1, source_target_pairs={{0,1},{1,0},{2,3},{3,2},{4,5},{5,4},{6,7},{7,6},{8,9},{9,8},{10,11... | collective-permute-start | bytes 98312 | tf_op jit(solution)/shard_map/ppermute | solution.py:334
  23.9 4.0 %collective-permute-start.11 = (f32[64,128]{1,0:T(8,128)S(1)}, f32[64,128]{1,0:T(8,128)S(1)}, u32[]{:S(2)}, u32[]{:S(2)}) collective-permute-start(f32[64,128]{1,0:T(8,128)S(1)} %shard_map.108), channel_id=1, source_target_pairs={{0,2},{1,3},{2,0},{3,1},{4,6},{5,7},{6,4},{7,5},{8,10},{9,11},{10,... | collective-permute-start | bytes 98312 | tf_op jit(solution)/shard_map/ppermute | solution.py:334
  25.3 3.3 %collective-permute-start.12 = (f32[64,128]{1,0:T(8,128)S(1)}, f32[64,128]{1,0:T(8,128)S(1)}, u32[]{:S(2)}, u32[]{:S(2)}) collective-permute-start(f32[64,128]{1,0:T(8,128)S(1)} %shard_map.108), channel_id=1, source_target_pairs={{0,3},{1,2},{2,1},{3,0},{4,7},{5,6},{6,5},{7,4},{8,11},{9,10},{10,... | collective-permute-start | bytes 98312 | tf_op jit(solution)/shard_map/ppermute | solution.py:334
